TPU v7x, 512 devices: a whole 4x4x16 slice. The times are simulated.
512 devices in a mesh: seq: 64 (over y, z_lo, core), tp: 8 (over x, z_hi).
Axes of the slice: x: 4, y: 4, z: 16 (z_hi: 2, z_lo: 8; z = z_hi * 8 + z_lo), core: 2. Of those that a mesh axis runs over, the one named last changes fastest.
Arguments:
- tokens: bfloat16 [32768, 2048], P('seq', 'tp'), may hold values from -6 to 6
- w_feature: bfloat16 [2048, 16, 32], P(None, 'tp'), may hold values from -0.125 to 0.125
- w_window: bfloat16 [2048, 16, 384], P(None, 'tp'), may hold values from -0.125 to 0.125
- w_out: bfloat16 [16, 128, 2048], P('tp'), may hold values from -0.125 to 0.125
- win_blocks: int32 [16], P('tp'), may hold values from 1 to 4, as said below
Outputs:
- mixed: bfloat16 [32768, 2048], P(('seq', 'tp'))
Inputs may be any that keep to these rules, and one draw needn't show every extreme that they name: `win_blocks`: some head's window spans 4 blocks.
All inputs are finite; a program needn't handle non-finite values.
Results may differ from a plain program's by a relative error of at most 0.017.
Values may be sent and summed in bfloat16 or wider, within the bound.
No kernel may reach another device: no remote copies, remote signals or barrier semaphores. Data moves between devices by JAX's collectives and lax.ppermute only.
A program may use at most 64 MiB of HBM per device.

v0:
```python
import math

import jax
import jax.numpy as jnp
from jax import lax
from jax.sharding import PartitionSpec as P

BLOCK = 128
WMAX = 4


epsilon = 1e-06
score_scale = 12.0
highest = lax.Precision.HIGHEST


def shifted(value, axis, steps):
    count = lax.axis_size(axis)
    leading, last = (max(0, -steps), min(count, count - steps))
    return lax.ppermute(value, axis, [(source, source + steps) for source in range(leading, last)])


def prefix(part, axis, combine, identity):
    place = lax.axis_index(axis)
    gathered = lax.all_gather(part, axis)
    state = jnp.zeros_like(part) + jnp.asarray(identity, part.dtype)

    def one(turn, state):
        return combine(state, lax.dynamic_index_in_dim(gathered, turn, 0, False))

    return lax.fori_loop(0, place, one, state)


def normalize(vector):
    return vector / jnp.sqrt(jnp.mean(vector * vector, axis=-1, keepdims=True) + epsilon)


def full_taylor(vector, feat_dim):
    outer_prod = (vector[..., :, None] * vector[..., None, :]).reshape(
        vector.shape[:-1] + (feat_dim * feat_dim,)
    )
    ones_col = jnp.ones(vector.shape[:-1] + (1,), jnp.float32)
    return jnp.concatenate([ones_col, vector * 0.5, outer_prod * (0.25 / math.sqrt(2.0))], axis=-1)


def add_states(earlier, later):
    return earlier + later


def local(tokens, w_feature, w_window, w_out, win_blocks):
    tok_rows = tokens.shape[0]
    model_width = w_feature.shape[0]
    head_count = w_feature.shape[1]
    feat_dim = w_feature.shape[2] // 2
    head_size = w_window.shape[2] // 3
    halo_rows = (WMAX - 1) * BLOCK
    tail_rows = min(halo_rows, tok_rows)
    first_row = lax.axis_index("seq") * tok_rows
    feature_cols = w_feature.reshape(model_width, head_count * 2 * feat_dim)
    window_cols = w_window.reshape(model_width, head_count * 3 * head_size)
    shard_piece = lax.all_gather(tokens, "tp", axis=1, tiled=True)
    feature_sum = jnp.dot(shard_piece, feature_cols, preferred_element_type=jnp.float32)
    window_sum = jnp.dot(shard_piece, window_cols, preferred_element_type=jnp.float32)
    window_proj = window_sum.astype(jnp.bfloat16).reshape(tok_rows, head_count, 3 * head_size)
    key_norm = normalize(window_proj[..., head_size : 2 * head_size].astype(jnp.float32)).astype(
        jnp.bfloat16
    )
    key_value = jnp.concatenate([key_norm, window_proj[..., 2 * head_size :]], axis=-1)
    tail = key_value[tok_rows - tail_rows :]
    earlier = shifted(tail, "seq", 1)
    halo_keys = earlier[..., :head_size]
    halo_values = earlier[..., head_size:]
    feature_proj = feature_sum.astype(jnp.bfloat16).reshape(tok_rows, head_count, 2 * feat_dim)
    query_feat = feature_proj[..., :feat_dim]
    key_feat = feature_proj[..., feat_dim:]
    values = window_proj[..., 2 * head_size :]
    values_wide = values.astype(jnp.float32)
    inner_dot = jnp.einsum("thf,uhf->htu", query_feat, key_feat, preferred_element_type=jnp.float32)
    pair_weight = 1.0 + inner_dot * 0.25 + inner_dot * inner_dot / 32.0
    causal = jnp.arange(tok_rows)[:, None] >= jnp.arange(tok_rows)[None, :]
    pair_weight = jnp.where(causal[None], pair_weight, 0.0)
    local_term = jnp.einsum("htu,uhd->thd", pair_weight, values_wide, precision=highest)
    query_wide = query_feat.astype(jnp.float32)
    key_wide = key_feat.astype(jnp.float32)
    query_taylor = full_taylor(query_wide, feat_dim)
    key_taylor = full_taylor(key_wide, feat_dim)
    own_state = jnp.einsum("thf,thd->hfd", key_taylor, values_wide, precision=highest)
    earlier_state = prefix(own_state, "seq", add_states, jnp.zeros_like(own_state))
    carried = jnp.einsum("thf,hfd->thd", query_taylor, earlier_state, precision=highest)
    linear_out = local_term + carried
    query_norm = normalize(window_proj[..., :head_size].astype(jnp.float32)).astype(jnp.bfloat16)
    all_keys = jnp.concatenate([halo_keys, key_norm], axis=0)
    all_values = jnp.concatenate([halo_values, values], axis=0)
    scores = jnp.einsum(
        "thd,uhd->htu", query_norm, all_keys, preferred_element_type=jnp.float32
    ) * (score_scale / head_size)
    query_pos = first_row + jnp.arange(tok_rows, dtype=jnp.int32)
    key_pos = first_row - halo_rows + jnp.arange(halo_rows + tok_rows, dtype=jnp.int32)
    later_key = key_pos[None, None, :]
    allowed = (
        (later_key >= 0)
        & (later_key <= query_pos[None, :, None])
        & (later_key // BLOCK >= query_pos[None, :, None] // BLOCK - win_blocks[:, None, None] + 1)
    )
    weights = jnp.where(allowed, jnp.exp(scores), 0.0).astype(jnp.bfloat16)
    window_out = jnp.einsum("htu,uhd->thd", weights, all_values, preferred_element_type=jnp.float32)
    hidden = (
        (normalize(linear_out) + normalize(window_out))
        .astype(jnp.bfloat16)
        .reshape(tok_rows, head_count * head_size)
    )
    out_cols = w_out.reshape(head_count * head_size, model_width)
    return lax.psum_scatter(
        jnp.dot(hidden, out_cols, preferred_element_type=jnp.float32).astype(jnp.bfloat16),
        "tp",
        scatter_dimension=0,
        tiled=True,
    )


def solution(mesh):
    in_specs = (
        P("seq", "tp"),
        P(None, "tp", None),
        P(None, "tp", None),
        P("tp", None, None),
        P("tp"),
    )
    out_specs = P(("seq", "tp"), None)
    return jax.shard_map(local, mesh=mesh, in_specs=in_specs, out_specs=out_specs, check_vma=False)
```

profile of v0, /device:TPU:8, one launch (start us, length us, event | category | flops | bytes accessed | tf_op | source)
XLA Modules:
  0.0 490.1 jit_solution(5376807825300232360)
XLA Ops:
  6.5 0.0 copy-start
  6.5 0.0 all-gather.4.cloned.1.call-start
  6.5 0.7 all-gather.4.cloned.1.call-update
  7.3 0.0 all-gather.6.cloned.1.call-start
  7.3 0.0 copy-start.3
  7.3 4.2 copy.44
  11.5 119.6 %all-gather.4.cloned.1.call-done = bf16[512,2048]{1,0:T(8,128)(2,1)} async-done(((bf16[512,256]{1,0:T(8,128)(2,1)}), bf16[512,2048]{1,0:T(8,128)(2,1)}) %all-gather.4.cloned.1.call-update) | async-done | bytes 2097168 | tf_op jit(solution)/shard_map/all_gather | solution.py:61
  131.2 0.0 copy-start.1
  131.2 0.0 copy-done.3
  131.2 2.5 convolution_convert_fusion.1
  133.7 0.0 copy-done.1
  133.7 3.7 convolution_convert_fusion
  137.4 0.3 copy.32
  137.7 0.0 copy-start.5
  137.7 0.3 multiply_multiply_fusion
  138.0 1.5 fusion.10
  139.5 0.0 all-gather.6.cloned.1.call-update
  139.5 0.0 reduce-scatter.2.cloned.1.call-start
  139.6 0.8 iota_compare_fusion
  140.4 0.0 copy-done.5
  140.4 0.1 subtract_add_fusion
  140.5 1.2 compare_and_fusion
  141.7 0.1 fusion.26
  141.7 0.1 fusion.27
  141.8 0.7 fusion.67
  142.5 0.8 pad_maximum_fusion
  143.3 1.9 collective-permute-start
  145.2 1.8 copy.43
  147.0 0.0 copy-start.4
  147.0 1.2 fusion.28
  148.3 0.5 fusion.45
  148.8 0.0 copy-done.4
  148.8 2.6 fusion
  151.3 9.3 %collective-permute-done = bf16[384,2,256]{0,2,1:T(8,128)(2,1)} collective-permute-done((bf16[384,2,256]{0,2,1:T(8,128)(2,1)}, bf16[384,2,256]{0,2,1:T(8,128)(2,1)}, u32[]{:S(2)}, u32[]{:S(2)}) %collective-permute-start) | collective-permute-done | bytes 393248 | tf_op jit(solution)/shard_map/ppermute | solution.py:20
  160.6 1.1 fusion.68
  161.7 3.5 multiply_reduce_fusion
  165.2 109.8 %all-gather.6.cloned.1.call-done = f32[128,273,128]{2,1,0:T(8,128)} async-done(((f32[2,273,128]{2,1,0:T(8,128)}), f32[128,273,128]{2,1,0:T(8,128)}) %all-gather.6.cloned.1.call-update) | async-done | bytes 17891344 | tf_op jit(solution)/shard_map/all_gather | solution.py:25
  275.0 0.0 copy-start.2
  275.0 16.7 %while.10 = (s32[]{:T(128)}, f32[2,273,128]{2,1,0:T(8,128)S(1)}, s32[]{:T(128)}, f32[64,2,273,128]{3,2,1,0:T(8,128)}, s32[]{:T(128)}, /*index=5*/s32[]{:T(128)}, s32[]{:T(128)}) while((s32[]{:T(128)}, f32[2,273,128]{2,1,0:T(8,128)S(1)}, s32[]{:T(128)}, f32[64,2,273,128]{3,2,1,0:T(8,128)}, s32[]{:T(128)}, /*index=5*/s32[]{:T(128)}, ...), condition=%wide.region_1.2_spmd, body=%wide.region_0.0_spmd.sunk | while | flops 69893 | bytes 838779 | solution.py:31
  275.0 1.1 bitcast_add_fusion.2
  276.1 1.0 bitcast_add_fusion.2
  277.2 1.0 bitcast_add_fusion.2
  278.2 1.0 bitcast_add_fusion.2
  279.2 1.0 bitcast_add_fusion.2
  280.3 1.0 bitcast_add_fusion.2
  281.3 1.0 bitcast_add_fusion.2
  282.3 1.0 bitcast_add_fusion.2
  283.4 1.0 bitcast_add_fusion.2
  284.4 1.0 bitcast_add_fusion.2
  285.5 1.0 bitcast_add_fusion.2
  286.5 1.0 bitcast_add_fusion.2
  287.5 1.0 bitcast_add_fusion.2
  288.6 1.0 bitcast_add_fusion.2
  289.6 1.0 bitcast_add_fusion.2
  290.6 1.0 bitcast_add_fusion.2
  291.7 0.0 copy-start.6
  291.7 0.0 copy-done.2
  291.7 1.3 multiply_reduce_fusion.1
  293.0 0.0 copy-done
  293.0 0.0 copy-done.6
  293.0 2.2 bitcast_convert_fusion
  295.2 0.0 reduce-scatter.2.cloned.1.call-update
  295.2 188.4 %reduce-scatter.2.cloned.1.call-done = bf16[64,2048]{1,0:T(8,128)(2,1)} async-done(((bf16[512,2048]{1,0:T(8,128)(2,1)}), bf16[64,2048]{1,0:T(8,128)(2,1)}) %reduce-scatter.2.cloned.1.call-update) | async-done | bytes 262160 | tf_op jit(solution)/shard_map/reduce_scatter | solution.py:113
  (11 shorter events, 0.1 us)
Async XLA Ops:
  6.5 286.5 %copy-start = (bf16[2,128,2048]{2,1,0:T(8,128)(2,1)S(1)}, bf16[2,128,2048]{2,1,0:T(8,128)(2,1)}, u32[]{:S(2)}) copy-start(bf16[2,128,2048]{2,1,0:T(8,128)(2,1)} %param.10) | copy-start | bytes 3145732
  6.5 124.6 %all-gather.4.cloned.1.call-start = ((), (), s32[]{:S(2)}) async-start(), calls=%async_computation.1 | async-start | bytes 2359296 | tf_op jit(solution)/shard_map/all_gather | solution.py:61
  7.3 267.7 %all-gather.6.cloned.1.call-start = ((), (), s32[]{:S(2)}) async-start(), calls=%async_computation.3 | async-start | bytes 18636800 | tf_op jit(solution)/shard_map/all_gather | solution.py:25
  7.3 123.8 %copy-start.3 = (bf16[2048,2,32]{0,2,1:T(8,128)(2,1)S(1)}, bf16[2048,2,32]{0,2,1:T(8,128)(2,1)}, u32[]{:S(2)}) copy-start(bf16[2048,2,32]{0,2,1:T(8,128)(2,1)} %param.8) | copy-start | bytes 786436
  131.2 2.5 copy-start.1
  137.7 2.7 copy-start.5
  139.5 344.1 %reduce-scatter.2.cloned.1.call-start = ((), (), s32[]{:S(2)}) async-start(), calls=%async_computation.2 | async-start | bytes 2359296 | tf_op jit(solution)/shard_map/reduce_scatter | solution.py:113
  143.3 17.3 %collective-permute-start = (bf16[384,2,256]{0,2,1:T(8,128)(2,1)}, bf16[384,2,256]{0,2,1:T(8,128)(2,1)}, u32[]{:S(2)}, u32[]{:S(2)}) collective-permute-start(bf16[384,2,256]{0,2,1:T(8,128)(2,1)} %pad_maximum_fusion), channel_id=1, source_target_pairs={{0,8},{8,16},{16,24},{24,32},{32,40},{40,48},{48,56},{56,64},{64,7... | collective-permute-start | bytes 1179656 | tf_op jit(solution)/shard_map/ppermute | solution.py:20
  147.0 1.7 copy-start.4
  275.0 16.7 %copy-start.2 = (f32[2,128,512]{2,1,0:T(8,128)S(1)}, f32[2,128,512]{2,1,0:T(8,128)}, u32[]{:S(2)}) copy-start(f32[2,128,512]{2,1,0:T(8,128)} %fusion) | copy-start | bytes 1572868
  291.7 1.4 copy-start.6
Sparse Core Ops, SparseCore 0:
  10.4 120.6 all-gather.3
  139.6 135.2 all-gather.5
  295.3 188.2 reduce-scatter.1
where the time goes:
time: 492 us; the launch traced here: 490 us
  waiting for transfers between devices  428 us (87%)
  other arithmetic  20.8 us (4%)
  matrix products  17.7 us (4%)
  between operations  13.3 us (3%)
  local copies, waits for them, and re-layouts  8.13 us (2%)
    reduce_scatter x1, waiting for transfers between devices, local(): lax.psum_scatter(jnp.dot(hidden, out_cols, preferred_element_type=jnp.flo...  188 us
    all_gather x1, waiting for transfers between devices, local(): shard_piece = lax.all_gather(tokens, 'tp', axis=1, tiled=True)  120 us
    all_gather x1, waiting for transfers between devices, prefix(): gathered = lax.all_gather(part, axis)  110 us
    add x16, other arithmetic, add_states(): return earlier + later  16.3 us
  transfers between devices with their start and end apart: 4, of which 4 were waited for; matrix products, arithmetic and copies ran while one was open for 4% of the time, Pallas kernels for 0%

commit v1 on v0

v1 whole, which is shorter than its diff:
```python
import jax
import jax.numpy as jnp
import numpy as np
from jax import lax
from jax.sharding import PartitionSpec as P

BLOCK = 128
WMAX = 4
NX, NY, NZ = 4, 4, 8
N_TP = 8
EPS = 1e-06
SCALE = 12.0
bf16, f32 = jnp.bfloat16, jnp.float32


def pairs(move):
    out = []
    for x in range(NX):
        for h in range(2):
            for y in range(NY):
                for z in range(NZ):
                    for c in range(2):
                        to = move(x, h, y, z, c)
                        if to is not None:
                            tx, th, ty, tz, tc = to
                            source = ((y * NZ + z) * 2 + c) * N_TP + x * 2 + h
                            target = ((ty * NZ + tz) * 2 + tc) * N_TP + (tx % NX) * 2 + th
                            out.append((source, target))
    return out


def send(value, move):
    return lax.ppermute(value, ("seq", "tp"), pairs(move))


def to_x(steps):
    return lambda x, h, y, z, c: (x + steps, h, y, z, c)


def to_half(x, h, y, z, c):
    return (x, 1 - h, y, z, c)


def to_core(x, h, y, z, c):
    return (x, h, y, z, 1 - c)


def to_z(flip):
    return lambda x, h, y, z, c: (x, h, y, z ^ flip, c)


def to_y(steps):
    return lambda x, h, y, z, c: (x, h, y + steps, z, c) if y + steps < NY else None


def to_next(x, h, y, z, c):
    place = (y * NZ + z) * 2 + c + 1
    if place == NY * NZ * 2:
        return None
    return (x, h, place // (2 * NZ), place // 2 % NZ, place % 2)


def normalize(vector):
    return vector / jnp.sqrt(jnp.mean(vector * vector, axis=-1, keepdims=True) + EPS)


def feature_maps(feat_dim, rows):
    left = np.zeros((rows, feat_dim), np.float32)
    right = np.zeros((rows, feat_dim), np.float32)
    left_one = np.zeros((rows,), np.float32)
    right_one = np.zeros((rows,), np.float32)
    weight = np.zeros((rows,), np.float32)
    at = 0
    for i in range(feat_dim):
        for j in range(i, feat_dim):
            left[at, i] = 1.0
            right[at, j] = 1.0
            weight[at] = 1.0 / 32.0 if i == j else 1.0 / 16.0
            at += 1
    for i in range(feat_dim):
        left[at, i] = 1.0
        right_one[at] = 1.0
        weight[at] = 0.25
        at += 1
    left_one[at] = right_one[at] = weight[at] = 1.0
    return left, right, left_one, right_one, weight


ROWS = 160


def taylor(vector, maps):
    left, right, left_one, right_one, _ = maps
    a = jnp.einsum("thf,rf->thr", vector, left.astype(bf16), preferred_element_type=f32) + left_one
    b = jnp.einsum("thf,rf->thr", vector, right.astype(bf16), preferred_element_type=f32) + right_one
    return a * b


def prefix(state, place):
    x, h, y, z, c = place
    mine = lax.dynamic_index_in_dim(state, c, 0, False)
    other = lax.dynamic_index_in_dim(state, 1 - c, 0, False)
    got = send(other.astype(bf16), to_core).astype(f32)
    total = mine + got
    short = total.astype(bf16)
    quad = [send(short, to_z(flip)).astype(f32) for flip in (1, 2, 3)]
    before = jnp.zeros_like(total)
    for flip, part in zip((1, 2, 3), quad):
        before = before + jnp.where((z ^ flip) < z, part, 0.0)
        total = total + part
    part = send(total.astype(bf16), to_z(4)).astype(f32)
    before = before + jnp.where((z ^ 4) < z, part, 0.0)
    total = total + part
    short = total.astype(bf16)
    for steps in (1, 2, 3):
        before = before + send(short, to_y(steps)).astype(f32)
    theirs = send((before + jnp.where(c == 0, mine, 0.0)).astype(bf16), to_core).astype(f32)
    ours = before + jnp.where(c == 1, got, 0.0)
    first = jnp.where(c == 0, ours, theirs)
    second = jnp.where(c == 0, theirs, ours)
    return jnp.stack([first, second])


def local(tokens, w_feature, w_window, w_out, win_blocks):
    tok_rows = tokens.shape[0]
    model_width, head_count = w_feature.shape[:2]
    feat_dim = w_feature.shape[2] // 2
    head_size = w_window.shape[2] // 3
    halo_rows = (WMAX - 1) * BLOCK
    seq, tp = lax.axis_index("seq"), lax.axis_index("tp")
    x, h, y, z, c = tp // 2, tp % 2, seq // (2 * NZ), seq // 2 % NZ, seq % 2
    place = (x, h, y, z, c)
    first_row = seq * tok_rows

    other = send(tokens, to_half)
    parts = [tokens] + [send(tokens, to_x(s)) for s in (1, 3, 2)]
    parts += [other] + [send(other, to_x(s)) for s in (1, 3, 2)]
    owners = jnp.stack([(x + NX - s) % NX * 2 + half for half in (h, 1 - h) for s in (0, 1, 3, 2)])

    def ordered(w):
        return jnp.take(w.reshape(N_TP, model_width // N_TP, -1), owners, axis=0)

    window_w = ordered(w_window)
    feature_w = ordered(w_feature)
    stacked = jnp.stack(parts)
    window_sum = jnp.einsum("ktd,kdn->tn", stacked, window_w, preferred_element_type=f32)
    feature_sum = jnp.einsum("ktd,kdn->tn", stacked, feature_w, preferred_element_type=f32)
    window_proj = window_sum.astype(bf16).reshape(tok_rows, head_count, 3 * head_size)
    feature_proj = feature_sum.astype(bf16).reshape(tok_rows, head_count, 2 * feat_dim)
    query_feat, key_feat = feature_proj[..., :feat_dim], feature_proj[..., feat_dim:]
    values = window_proj[..., 2 * head_size :]
    values_wide = values.astype(f32)

    maps = feature_maps(feat_dim, ROWS)
    key_map = taylor(key_feat, maps)
    query_map = taylor(query_feat, maps) * maps[4]
    state = jnp.einsum("thr,thd->hrd", key_map, values_wide, precision=lax.Precision.HIGHEST)
    earlier_state = prefix(state, place)

    key_norm = normalize(window_proj[..., head_size : 2 * head_size].astype(f32)).astype(bf16)
    query_norm = normalize(window_proj[..., :head_size].astype(f32)).astype(bf16)
    key_value = jnp.concatenate([key_norm, values], axis=-1)
    halo = send(key_value[tok_rows - halo_rows :], to_next)

    inner = jnp.einsum("thf,uhf->htu", query_feat, key_feat, preferred_element_type=f32)
    pair_weight = 1.0 + inner * 0.25 + inner * inner / 32.0
    causal = jnp.arange(tok_rows)[:, None] >= jnp.arange(tok_rows)[None, :]
    pair_weight = jnp.where(causal[None], pair_weight, 0.0).astype(bf16)
    local_term = jnp.einsum("htu,uhd->thd", pair_weight, values, preferred_element_type=f32)
    all_keys = jnp.concatenate([halo[..., :head_size], key_norm], axis=0)
    all_values = jnp.concatenate([halo[..., head_size:], values], axis=0)
    scores = jnp.einsum("thd,uhd->htu", query_norm, all_keys, preferred_element_type=f32) * (SCALE / head_size)
    query_pos = first_row + jnp.arange(tok_rows, dtype=jnp.int32)
    key_pos = first_row - halo_rows + jnp.arange(halo_rows + tok_rows, dtype=jnp.int32)
    later_key = key_pos[None, None, :]
    allowed = (
        (later_key >= 0)
        & (later_key <= query_pos[None, :, None])
        & (later_key // BLOCK >= query_pos[None, :, None] // BLOCK - win_blocks[:, None, None] + 1)
    )
    weights = jnp.where(allowed, jnp.exp(scores), 0.0).astype(bf16)
    window_out = jnp.einsum("htu,uhd->thd", weights, all_values, preferred_element_type=f32)

    carried = jnp.einsum("thr,hrd->thd", query_map, earlier_state, precision=lax.Precision.HIGHEST)
    hidden = (normalize(local_term + carried) + normalize(window_out)).astype(bf16)
    hidden = hidden.reshape(tok_rows, head_count * head_size)
    out_cols = w_out.reshape(head_count * head_size, -1)

    rows = hidden.reshape(NX, 2, tok_rows // N_TP, -1)

    def summed(half):
        part = jnp.einsum(
            "xtk,kn->xtn", lax.dynamic_index_in_dim(rows, half, 1, False), out_cols, preferred_element_type=f32
        ).astype(bf16)
        total = lax.dynamic_index_in_dim(part, x, 0, False).astype(f32)
        for steps in (1, 3, 2):
            to = lax.dynamic_index_in_dim(part, (x + steps) % NX, 0, False)
            total = total + send(to, to_x(steps)).astype(f32)
        return total

    away = send(summed(1 - h).astype(bf16), to_half)
    return (summed(h) + away.astype(f32)).astype(bf16)


def solution(mesh):
    in_specs = (P("seq", "tp"), P(None, "tp", None), P(None, "tp", None), P("tp", None, None), P("tp"))
    return jax.shard_map(local, mesh=mesh, in_specs=in_specs, out_specs=P(("seq", "tp"), None), check_vma=False)
```

time: 492 us -> 188 us (0.38)
  the two profiles are of different devices: /device:TPU:8 before, /device:TPU:46 now
where the time goes in v1:
time: 188 us; the launch traced here: 187 us
  starting transfers between devices  97.3 us (52%)
  waiting for transfers between devices  39.5 us (21%)
  local copies, waits for them, and re-layouts  25.8 us (14%)
  matrix products  17.2 us (9%)
  other arithmetic  6.23 us (3%)
    ppermute x24, starting transfers between devices, send(): return lax.ppermute(value, ('seq', 'tp'), pairs(move))  97.3 us
    ppermute x24, waiting for transfers between devices, send(): return lax.ppermute(value, ('seq', 'tp'), pairs(move))  39.5 us
    reshape x2, local copies, waits for them, and re-layouts, ordered(): return jnp.take(w.reshape(N_TP, model_width // N_TP, -1), owners, axis=0)  8.16 us
    unnamed x46, local copies, waits for them, and re-layouts  6.93 us
    gather x2, local copies, waits for them, and re-layouts, ordered(): return jnp.take(w.reshape(N_TP, model_width // N_TP, -1), owners, axis=0)  5.54 us
  transfers between devices with their start and end apart: 24, of which 8 were waited for; matrix products, arithmetic and copies ran while one was open for 15% of the time, Pallas kernels for 0%

profile of v1, /device:TPU:46, one launch (start us, length us, event | category | flops | bytes accessed | tf_op | source)
XLA Modules:
  0.0 186.8 jit_solution(5115222716305707272)
XLA Ops:
  0.0 2.5 %collective-permute-start = (bf16[512,256]{1,0:T(8,128)(2,1)}, bf16[512,256]{1,0:T(8,128)(2,1)}, u32[]{:S(2)}, u32[]{:S(2)}) collective-permute-start(bf16[512,256]{1,0:T(8,128)(2,1)} %param.12), channel_id=1, source_target_pairs={{0,2},{8,10},{16,18},{24,26},{32,34},{40,42},{48,50},{56,58},{64,6... | collective-permute-start | bytes 786440 | tf_op jit(solution)/shard_map/ppermute | solution.py:33
  2.5 3.5 %collective-permute-start.1 = (bf16[512,256]{1,0:T(8,128)(2,1)}, bf16[512,256]{1,0:T(8,128)(2,1)}, u32[]{:S(2)}, u32[]{:S(2)}) collective-permute-start(bf16[512,256]{1,0:T(8,128)(2,1)} %param.12), channel_id=1, source_target_pairs={{0,6},{8,14},{16,22},{24,30},{32,38},{40,46},{48,54},{56,62},{64,7... | collective-permute-start | bytes 786440 | tf_op jit(solution)/shard_map/ppermute | solution.py:33
  6.0 3.3 %collective-permute-start.2 = (bf16[512,256]{1,0:T(8,128)(2,1)}, bf16[512,256]{1,0:T(8,128)(2,1)}, u32[]{:S(2)}, u32[]{:S(2)}) collective-permute-start(bf16[512,256]{1,0:T(8,128)(2,1)} %param.12), channel_id=1, source_target_pairs={{0,4},{8,12},{16,20},{24,28},{32,36},{40,44},{48,52},{56,60},{64,6... | collective-permute-start | bytes 786440 | tf_op jit(solution)/shard_map/ppermute | solution.py:33
  9.3 14.8 %collective-permute-start.3 = (bf16[512,256]{1,0:T(8,128)(2,1)}, bf16[512,256]{1,0:T(8,128)(2,1)}, u32[]{:S(2)}, u32[]{:S(2)}) collective-permute-start(bf16[512,256]{1,0:T(8,128)(2,1)} %param.12), channel_id=1, source_target_pairs={{0,1},{8,9},{16,17},{24,25},{32,33},{40,41},{48,49},{56,57},{64,65... | collective-permute-start | bytes 786440 | tf_op jit(solution)/shard_map/ppermute | solution.py:33
  24.2 1.0 bitcast_dynamic-update-slice_fusion.7
  25.4 0.7 subtract_add_fusion
  26.1 1.1 compare_and_fusion
  27.4 0.8 iota_compare_fusion
  28.2 8.1 %reshape.583 = bf16[8,256,768]{2,1,0:T(8,128)(2,1)} reshape(bf16[2048,2,384]{2,1,0:T(2,128)(2,1)} %param.14) | data formatting | bytes 6291456 | tf_op jit(solution)/shard_map/reshape | solution.py:141
  36.4 4.3 %gather_fusion = bf16[8,256,768]{2,1,0:T(8,128)(2,1)} fusion(bf16[8,256,768]{2,1,0:T(8,128)(2,1)} %reshape.583, s32[1024]{0:T(1024)S(1)} %pad_clamp_fusion), kind=kCustom, calls=%fused_computation | custom fusion | bytes 6291488 | tf_op jit(solution)/shard_map/jit(_take)/gather | solution.py:141
  40.6 1.3 gather_fusion.1
  41.9 5.1 %collective-permute-done.3 = bf16[512,256]{1,0:T(8,128)(2,1)} collective-permute-done((bf16[512,256]{1,0:T(8,128)(2,1)}, bf16[512,256]{1,0:T(8,128)(2,1)}, u32[]{:S(2)}, u32[]{:S(2)}) %collective-permute-start.3) | collective-permute-done | bytes 262176 | tf_op jit(solution)/shard_map/ppermute | solution.py:33
  47.0 4.0 %collective-permute-start.4 = (bf16[512,256]{1,0:T(8,128)(2,1)}, bf16[512,256]{1,0:T(8,128)(2,1)S(1)}, u32[]{:S(2)}, u32[]{:S(2)}) collective-permute-start(bf16[512,256]{1,0:T(8,128)(2,1)} %collective-permute-done.3), channel_id=1, source_target_pairs={{0,2},{8,10},{16,18},{24,26},{32,34},{40,42},{48,50},{56,58},{64,6... | collective-permute-start | bytes 786440 | tf_op jit(solution)/shard_map/ppermute | solution.py:33
  51.0 1.9 %collective-permute-start.5 = (bf16[512,256]{1,0:T(8,128)(2,1)}, bf16[512,256]{1,0:T(8,128)(2,1)S(1)}, u32[]{:S(2)}, u32[]{:S(2)}) collective-permute-start(bf16[512,256]{1,0:T(8,128)(2,1)} %collective-permute-done.3), channel_id=1, source_target_pairs={{0,6},{8,14},{16,22},{24,30},{32,38},{40,46},{48,54},{56,62},{64,7... | collective-permute-start | bytes 786440 | tf_op jit(solution)/shard_map/ppermute | solution.py:33
  52.9 4.0 %collective-permute-start.6 = (bf16[512,256]{1,0:T(8,128)(2,1)}, bf16[512,256]{1,0:T(8,128)(2,1)S(1)}, u32[]{:S(2)}, u32[]{:S(2)}) collective-permute-start(bf16[512,256]{1,0:T(8,128)(2,1)} %collective-permute-done.3), channel_id=1, source_target_pairs={{0,4},{8,12},{16,20},{24,28},{32,36},{40,44},{48,52},{56,60},{64,6... | collective-permute-start | bytes 786440 | tf_op jit(solution)/shard_map/ppermute | solution.py:33
  56.9 1.0 bitcast_dynamic-update-slice_fusion.6
  57.9 1.0 bitcast_dynamic-update-slice_fusion.5
  58.9 1.0 bitcast_dynamic-update-slice_fusion.4
  59.8 1.0 bitcast_dynamic-update-slice_fusion.3
  60.9 5.8 %collective-permute-done.5 = bf16[512,256]{1,0:T(8,128)(2,1)S(1)} collective-permute-done((bf16[512,256]{1,0:T(8,128)(2,1)}, bf16[512,256]{1,0:T(8,128)(2,1)S(1)}, u32[]{:S(2)}, u32[]{:S(2)}) %collective-permute-start.5) | collective-permute-done | bytes 262176 | tf_op jit(solution)/shard_map/ppermute | solution.py:33
  66.8 0.8 fusion.13
  67.6 1.1 convolution_add_fusion.1
  68.7 1.1 convolution_add_fusion.3
  69.8 2.8 %bitcast_convert_fusion = bf16[512,768]{1,0:T(8,128)(2,1)} fusion(bf16[8,512,256]{2,1,0:T(8,128)(2,1)S(1)} %bitcast_dynamic-update-slice_fusion, bf16[8,256,768]{2,1,0:T(8,128)(2,1)S(1)} %copy-done.1, pred[8]{0:T(512)(128)(4,1)S(1)} %compare_and_fusion.1), kind=kOutput, calls=%fused_computation.10 | convolution fusion | flops 1612578816 | bytes 6029320 | tf_op jit(solution)/shard_map/ktd,kdn->tn/dot_general | solution.py:146
  72.6 2.1 %reshape.584 = bf16[512,2,384]{2,1,0:T(2,128)(2,1)S(1)} reshape(bf16[512,768]{1,0:T(8,128)(2,1)} %bitcast_convert_fusion) | data formatting | bytes 1572864 | tf_op jit(solution)/shard_map/reshape | solution.py:148
  74.7 1.3 fusion.100
  76.4 1.2 copy.33
  77.6 1.1 fusion.9
  78.6 0.4 fusion.106
  79.1 1.9 %collective-permute-start.7 = (bf16[160,128]{1,0:T(8,128)(2,1)S(1)}, bf16[160,128]{1,0:T(8,128)(2,1)S(1)}, u32[]{:S(2)}, u32[]{:S(2)}) collective-permute-start(bf16[160,128]{1,0:T(8,128)(2,1)S(1)} %fusion.68), channel_id=1, source_target_pairs={{0,8},{8,0},{16,24},{24,16},{32,40},{40,32},{48,56},{56,48},{64,72... | collective-permute-start | bytes 122888 | tf_op jit(solution)/shard_map/ppermute | solution.py:33
  81.0 0.8 pad_maximum_fusion
  81.8 2.4 %collective-permute-start.16 = (bf16[384,2,256]{0,2,1:T(8,128)(2,1)}, bf16[384,2,256]{0,2,1:T(8,128)(2,1)}, u32[]{:S(2)}, u32[]{:S(2)}) collective-permute-start(bf16[384,2,256]{0,2,1:T(8,128)(2,1)} %pad_maximum_fusion), channel_id=1, source_target_pairs={{0,8},{8,16},{16,24},{24,32},{32,40},{40,48},{48,56},{56,64},{64,7... | collective-permute-start | bytes 1179656 | tf_op jit(solution)/shard_map/ppermute | solution.py:33
  84.3 1.9 %collective-permute-start.10 = (bf16[160,128]{1,0:T(8,128)(2,1)S(1)}, bf16[160,128]{1,0:T(8,128)(2,1)S(1)}, u32[]{:S(2)}, u32[]{:S(2)}) collective-permute-start(bf16[160,128]{1,0:T(8,128)(2,1)S(1)} %fusion.67), channel_id=1, source_target_pairs={{0,48},{8,56},{16,32},{24,40},{32,16},{40,24},{48,0},{56,8},{64,11... | collective-permute-start | bytes 122888 | tf_op jit(solution)/shard_map/ppermute | solution.py:33
  86.2 1.9 %collective-permute-start.9 = (bf16[160,128]{1,0:T(8,128)(2,1)S(1)}, bf16[160,128]{1,0:T(8,128)(2,1)S(1)}, u32[]{:S(2)}, u32[]{:S(2)}) collective-permute-start(bf16[160,128]{1,0:T(8,128)(2,1)S(1)} %fusion.67), channel_id=1, source_target_pairs={{0,32},{8,40},{16,48},{24,56},{32,0},{40,8},{48,16},{56,24},{64,96... | collective-permute-start | bytes 122888 | tf_op jit(solution)/shard_map/ppermute | solution.py:33
  88.1 5.4 %collective-permute-start.8 = (bf16[160,128]{1,0:T(8,128)(2,1)S(1)}, bf16[160,128]{1,0:T(8,128)(2,1)S(1)}, u32[]{:S(2)}, u32[]{:S(2)}) collective-permute-start(bf16[160,128]{1,0:T(8,128)(2,1)S(1)} %fusion.67), channel_id=1, source_target_pairs={{0,16},{8,24},{16,0},{24,8},{32,48},{40,56},{48,32},{56,40},{64,80... | collective-permute-start | bytes 122888 | tf_op jit(solution)/shard_map/ppermute | solution.py:33
  93.5 1.1 fusion.10
  94.6 0.8 collective-permute-done.10
  95.4 0.2 collective-permute-done.8
  95.7 0.4 copy-done.9
  96.0 0.2 copy-done.13
  96.3 7.4 %collective-permute-start.11 = (bf16[160,128]{1,0:T(8,128)(2,1)S(1)}, bf16[160,128]{1,0:T(8,128)(2,1)S(1)}, u32[]{:S(2)}, u32[]{:S(2)}) collective-permute-start(bf16[160,128]{1,0:T(8,128)(2,1)S(1)} %get-tuple-element.7), channel_id=1, source_target_pairs={{0,64},{8,72},{16,80},{24,88},{32,96},{40,104},{48,112},{56,120},{... | collective-permute-start | bytes 122888 | tf_op jit(solution)/shard_map/ppermute | solution.py:33
  103.7 2.7 %fusion.6 = f32[2,128,512]{2,1,0:T(8,128)} fusion(bf16[512,2,128]{0,2,1:T(8,128)(2,1)S(1)} %copy.33, pred[512,512]{1,0:T(8,128)(4,1)} %iota_compare_fusion, bf16[512,2,32]{0,2,1:T(8,128)(2,1)S(1)} %bitcast.116), kind=kOutput, calls=%fused_computation.12 | convolution fusion | flops 154664960 | bytes 1114112 | tf_op jit(solution)/shard_map/htu,uhd->thd/dot_general | solution.py:169
  106.4 1.0 collective-permute-done.11
  107.3 0.7 collective-permute-start.14
  108.0 4.7 %collective-permute-start.13 = (bf16[160,128]{1,0:T(8,128)(2,1)S(1)}, bf16[160,128]{1,0:T(8,128)(2,1)S(1)}, u32[]{:S(2)}, u32[]{:S(2)}) collective-permute-start(bf16[160,128]{1,0:T(8,128)(2,1)S(1)} %fusion.62), channel_id=1, source_target_pairs={{0,256},{8,264},{16,272},{24,280},{32,288},{40,296},{48,304},{56,3... | collective-permute-start | bytes 122888 | tf_op jit(solution)/shard_map/ppermute | solution.py:33
  112.8 1.9 %collective-permute-start.12 = (bf16[160,128]{1,0:T(8,128)(2,1)S(1)}, bf16[160,128]{1,0:T(8,128)(2,1)S(1)}, u32[]{:S(2)}, u32[]{:S(2)}) collective-permute-start(bf16[160,128]{1,0:T(8,128)(2,1)S(1)} %fusion.62), channel_id=1, source_target_pairs={{0,128},{8,136},{16,144},{24,152},{32,160},{40,168},{48,176},{56,1... | collective-permute-start | bytes 122888 | tf_op jit(solution)/shard_map/ppermute | solution.py:33
  114.9 3.7 %collective-permute-done.12 = bf16[160,128]{1,0:T(8,128)(2,1)S(1)} collective-permute-done((bf16[160,128]{1,0:T(8,128)(2,1)S(1)}, bf16[160,128]{1,0:T(8,128)(2,1)S(1)}, u32[]{:S(2)}, u32[]{:S(2)}) %collective-permute-start.12) | collective-permute-done | bytes 40992 | tf_op jit(solution)/shard_map/ppermute | solution.py:33
  118.7 2.1 %collective-permute-start.15 = (bf16[160,128]{1,0:T(8,128)(2,1)S(1)}, bf16[160,128]{1,0:T(8,128)(2,1)S(1)}, u32[]{:S(2)}, u32[]{:S(2)}) collective-permute-start(bf16[160,128]{1,0:T(8,128)(2,1)S(1)} %get-tuple-element.5), channel_id=1, source_target_pairs={{0,8},{8,0},{16,24},{24,16},{32,40},{40,32},{48,56},{56,48},{64,72... | collective-permute-start | bytes 122888 | tf_op jit(solution)/shard_map/ppermute | solution.py:33
  120.9 1.0 collective-permute-done.15
  121.9 1.8 multiply_reduce_fusion.1
  123.7 1.1 fusion.101
  124.8 3.4 %multiply_reduce_fusion = (f32[512,2]{0,1:T(2,128)S(1)}, f32[512,2,128]{0,2,1:T(8,128)}) fusion(s32[2,512]{1,0:T(2,128)S(1)} %subtract_add_fusion, s32[896]{0:T(1024)S(1)} %get-tuple-element.28, pred[512,896]{1,0:T(8,128)(4,1)} %compare_and_fusion, bf16[512,2,128]{0,2,1:T(8,128)(2,1)S(1)} %fusion.20, bf16[384,2,128]{0,2,1:T(8,128)(2,1)S(1)} %get-tuple-element.18, ...), kind=kOutput, calls=%fused_computation.50 | convolution fusion | flops 476838912 | bytes 2178560 | tf_op jit(solution)/shard_map/htu,uhd->thd/dot_general | solution.py:182
  128.2 1.2 add_convert_fusion
  129.7 0.4 convolution_convert_fusion
  130.3 2.4 %collective-permute-start.22 = (bf16[64,2048]{1,0:T(8,128)(2,1)S(1)}, bf16[64,2048]{1,0:T(8,128)(2,1)S(1)}, u32[]{:S(2)}, u32[]{:S(2)}) collective-permute-start(bf16[64,2048]{1,0:T(8,128)(2,1)S(1)} %get-tuple-element.13), channel_id=1, source_target_pairs={{0,4},{8,12},{16,20},{24,28},{32,36},{40,44},{48,52},{56,60},{64,6... | collective-permute-start | bytes 786440 | tf_op jit(solution)/shard_map/ppermute | solution.py:33
  132.7 1.9 %collective-permute-start.21 = (bf16[64,2048]{1,0:T(8,128)(2,1)S(1)}, bf16[64,2048]{1,0:T(8,128)(2,1)S(1)}, u32[]{:S(2)}, u32[]{:S(2)}) collective-permute-start(bf16[64,2048]{1,0:T(8,128)(2,1)S(1)} %get-tuple-element.14), channel_id=1, source_target_pairs={{0,6},{8,14},{16,22},{24,30},{32,38},{40,46},{48,54},{56,62},{64,7... | collective-permute-start | bytes 786440 | tf_op jit(solution)/shard_map/ppermute | solution.py:33
  134.6 5.1 %collective-permute-start.20 = (bf16[64,2048]{1,0:T(8,128)(2,1)S(1)}, bf16[64,2048]{1,0:T(8,128)(2,1)S(1)}, u32[]{:S(2)}, u32[]{:S(2)}) collective-permute-start(bf16[64,2048]{1,0:T(8,128)(2,1)S(1)} %get-tuple-element.12), channel_id=1, source_target_pairs={{0,2},{8,10},{16,18},{24,26},{32,34},{40,42},{48,50},{56,58},{64,6... | collective-permute-start | bytes 786440 | tf_op jit(solution)/shard_map/ppermute | solution.py:33
  139.8 0.4 convolution_convert_fusion.1
  140.3 3.7 %collective-permute-start.19 = (bf16[64,2048]{1,0:T(8,128)(2,1)S(1)}, bf16[64,2048]{1,0:T(8,128)(2,1)S(1)}, u32[]{:S(2)}, u32[]{:S(2)}) collective-permute-start(bf16[64,2048]{1,0:T(8,128)(2,1)S(1)} %get-tuple-element.10), channel_id=1, source_target_pairs={{0,4},{8,12},{16,20},{24,28},{32,36},{40,44},{48,52},{56,60},{64,6... | collective-permute-start | bytes 786440 | tf_op jit(solution)/shard_map/ppermute | solution.py:33
  144.0 1.9 %collective-permute-start.18 = (bf16[64,2048]{1,0:T(8,128)(2,1)S(1)}, bf16[64,2048]{1,0:T(8,128)(2,1)S(1)}, u32[]{:S(2)}, u32[]{:S(2)}) collective-permute-start(bf16[64,2048]{1,0:T(8,128)(2,1)S(1)} %get-tuple-element.11), channel_id=1, source_target_pairs={{0,6},{8,14},{16,22},{24,30},{32,38},{40,46},{48,54},{56,62},{64,7... | collective-permute-start | bytes 786440 | tf_op jit(solution)/shard_map/ppermute | solution.py:33
  146.0 5.1 %collective-permute-start.17 = (bf16[64,2048]{1,0:T(8,128)(2,1)S(1)}, bf16[64,2048]{1,0:T(8,128)(2,1)S(1)}, u32[]{:S(2)}, u32[]{:S(2)}) collective-permute-start(bf16[64,2048]{1,0:T(8,128)(2,1)S(1)} %get-tuple-element.9), channel_id=1, source_target_pairs={{0,2},{8,10},{16,18},{24,26},{32,34},{40,42},{48,50},{56,58},{64,6... | collective-permute-start | bytes 786440 | tf_op jit(solution)/shard_map/ppermute | solution.py:33
  151.3 12.8 %collective-permute-start.23 = (bf16[64,2048]{1,0:T(8,128)(2,1)S(1)}, bf16[64,2048]{1,0:T(8,128)(2,1)S(1)}, u32[]{:S(2)}, u32[]{:S(2)}) collective-permute-start(bf16[64,2048]{1,0:T(8,128)(2,1)S(1)} %fusion.25), channel_id=1, source_target_pairs={{0,1},{8,9},{16,17},{24,25},{32,33},{40,41},{48,49},{56,57},{64,65... | collective-permute-start | bytes 786440 | tf_op jit(solution)/shard_map/ppermute | solution.py:33
  164.1 21.9 %collective-permute-done.23 = bf16[64,2048]{1,0:T(8,128)(2,1)S(1)} collective-permute-done((bf16[64,2048]{1,0:T(8,128)(2,1)S(1)}, bf16[64,2048]{1,0:T(8,128)(2,1)S(1)}, u32[]{:S(2)}, u32[]{:S(2)}) %collective-permute-start.23) | collective-permute-done | bytes 262176 | tf_op jit(solution)/shard_map/ppermute | solution.py:33
  186.0 0.9 fusion.29
  (82 shorter events, 1.9 us)
Async XLA Ops:
  0.0 129.7 %copy-start = (bf16[2,128,2048]{2,1,0:T(8,128)(2,1)S(1)}, bf16[2,128,2048]{2,1,0:T(8,128)(2,1)}, u32[]{:S(2)}) copy-start(bf16[2,128,2048]{2,1,0:T(8,128)(2,1)} %param.15) | copy-start | bytes 3145732
  0.0 52.9 %collective-permute-start = (bf16[512,256]{1,0:T(8,128)(2,1)}, bf16[512,256]{1,0:T(8,128)(2,1)}, u32[]{:S(2)}, u32[]{:S(2)}) collective-permute-start(bf16[512,256]{1,0:T(8,128)(2,1)} %param.12), channel_id=1, source_target_pairs={{0,2},{8,10},{16,18},{24,26},{32,34},{40,42},{48,50},{56,58},{64,6... | collective-permute-start | bytes 786440 | tf_op jit(solution)/shard_map/ppermute | solution.py:33
  2.5 55.4 %collective-permute-start.1 = (bf16[512,256]{1,0:T(8,128)(2,1)}, bf16[512,256]{1,0:T(8,128)(2,1)}, u32[]{:S(2)}, u32[]{:S(2)}) collective-permute-start(bf16[512,256]{1,0:T(8,128)(2,1)} %param.12), channel_id=1, source_target_pairs={{0,6},{8,14},{16,22},{24,30},{32,38},{40,46},{48,54},{56,62},{64,7... | collective-permute-start | bytes 786440 | tf_op jit(solution)/shard_map/ppermute | solution.py:33
  6.0 52.9 %collective-permute-start.2 = (bf16[512,256]{1,0:T(8,128)(2,1)}, bf16[512,256]{1,0:T(8,128)(2,1)}, u32[]{:S(2)}, u32[]{:S(2)}) collective-permute-start(bf16[512,256]{1,0:T(8,128)(2,1)} %param.12), channel_id=1, source_target_pairs={{0,4},{8,12},{16,20},{24,28},{32,36},{40,44},{48,52},{56,60},{64,6... | collective-permute-start | bytes 786440 | tf_op jit(solution)/shard_map/ppermute | solution.py:33
  9.3 37.7 %collective-permute-start.3 = (bf16[512,256]{1,0:T(8,128)(2,1)}, bf16[512,256]{1,0:T(8,128)(2,1)}, u32[]{:S(2)}, u32[]{:S(2)}) collective-permute-start(bf16[512,256]{1,0:T(8,128)(2,1)} %param.12), channel_id=1, source_target_pairs={{0,1},{8,9},{16,17},{24,25},{32,33},{40,41},{48,49},{56,57},{64,65... | collective-permute-start | bytes 786440 | tf_op jit(solution)/shard_map/ppermute | solution.py:33
  28.2 8.1 %copy-start.8 = (bf16[2048,2,32]{0,2,1:T(8,128)(2,1)S(1)}, bf16[2048,2,32]{0,2,1:T(8,128)(2,1)}, u32[]{:S(2)}) copy-start(bf16[2048,2,32]{0,2,1:T(8,128)(2,1)} %param.13) | copy-start | bytes 786436
  41.9 24.9 %copy-start.4 = (bf16[8,256,64]{1,2,0:T(8,128)(2,1)S(1)}, bf16[8,256,64]{1,2,0:T(8,128)(2,1)}, u32[]{:S(2)}) copy-start(bf16[8,256,64]{1,2,0:T(8,128)(2,1)} %gather_fusion.1) | copy-start | bytes 786436
  47.0 13.8 %collective-permute-start.4 = (bf16[512,256]{1,0:T(8,128)(2,1)}, bf16[512,256]{1,0:T(8,128)(2,1)S(1)}, u32[]{:S(2)}, u32[]{:S(2)}) collective-permute-start(bf16[512,256]{1,0:T(8,128)(2,1)} %collective-permute-done.3), channel_id=1, source_target_pairs={{0,2},{8,10},{16,18},{24,26},{32,34},{40,42},{48,50},{56,58},{64,6... | collective-permute-start | bytes 786440 | tf_op jit(solution)/shard_map/ppermute | solution.py:33
  51.0 15.7 %collective-permute-start.5 = (bf16[512,256]{1,0:T(8,128)(2,1)}, bf16[512,256]{1,0:T(8,128)(2,1)S(1)}, u32[]{:S(2)}, u32[]{:S(2)}) collective-permute-start(bf16[512,256]{1,0:T(8,128)(2,1)} %collective-permute-done.3), channel_id=1, source_target_pairs={{0,6},{8,14},{16,22},{24,30},{32,38},{40,46},{48,54},{56,62},{64,7... | collective-permute-start | bytes 786440 | tf_op jit(solution)/shard_map/ppermute | solution.py:33
  52.9 13.8 %collective-permute-start.6 = (bf16[512,256]{1,0:T(8,128)(2,1)}, bf16[512,256]{1,0:T(8,128)(2,1)S(1)}, u32[]{:S(2)}, u32[]{:S(2)}) collective-permute-start(bf16[512,256]{1,0:T(8,128)(2,1)} %collective-permute-done.3), channel_id=1, source_target_pairs={{0,4},{8,12},{16,20},{24,28},{32,36},{40,44},{48,52},{56,60},{64,6... | collective-permute-start | bytes 786440 | tf_op jit(solution)/shard_map/ppermute | solution.py:33
  60.8 6.7 %copy-start.16 = (bf16[160,16,1]{0,1,2:T(8,128)(2,1)S(1)}, bf16[160,16,1]{0,1,2:T(8,128)(2,1)}, u32[]{:S(2)}) copy-start(bf16[160,16,1]{0,1,2:T(8,128)(2,1)} %constant.234) | copy-start | bytes 15364
  60.8 6.7 %copy-start.17 = (f32[160]{0:T(256)S(1)}, f32[160]{0:T(256)}, u32[]{:S(2)}) copy-start(f32[160]{0:T(256)} %constant.226.clone) | copy-start | bytes 1924
  66.7 3.1 %copy-start.1 = (bf16[8,256,768]{2,1,0:T(8,128)(2,1)S(1)}, bf16[8,256,768]{2,1,0:T(8,128)(2,1)}, u32[]{:S(2)}) copy-start(bf16[8,256,768]{2,1,0:T(8,128)(2,1)} %gather_fusion) | copy-start | bytes 9437188
  67.5 1.2 copy-start.6
  74.7 2.9 %copy-start.3 = (f32[512,2,160]{0,2,1:T(8,128)S(1)}, f32[512,2,160]{0,2,1:T(8,128)}, u32[]{:S(2)}) copy-start(f32[512,2,160]{0,2,1:T(8,128)} %convolution_add_fusion.3) | copy-start | bytes 1966084
  74.7 2.9 %copy-start.15 = (bf16[160,16,1]{0,1,2:T(8,128)(2,1)S(1)}, bf16[160,16,1]{0,1,2:T(8,128)(2,1)}, u32[]{:S(2)}) copy-start(bf16[160,16,1]{0,1,2:T(8,128)(2,1)} %constant.235) | copy-start | bytes 15364
  76.4 17.2 %copy-start.2 = (f32[512,2,160]{0,2,1:T(8,128)S(1)}, f32[512,2,160]{0,2,1:T(8,128)}, u32[]{:S(2)}) copy-start(f32[512,2,160]{0,2,1:T(8,128)} %convolution_add_fusion.1) | copy-start | bytes 1966084
  78.6 25.0 %copy-start.7 = (bf16[512,64]{0,1:T(8,128)(2,1)S(1)}, bf16[512,64]{0,1:T(8,128)(2,1)}, u32[]{:S(2)}) copy-start(bf16[512,64]{0,1:T(8,128)(2,1)} %copy-done.6) | copy-start | bytes 196612
  79.1 5.1 %collective-permute-start.7 = (bf16[160,128]{1,0:T(8,128)(2,1)S(1)}, bf16[160,128]{1,0:T(8,128)(2,1)S(1)}, u32[]{:S(2)}, u32[]{:S(2)}) collective-permute-start(bf16[160,128]{1,0:T(8,128)(2,1)S(1)} %fusion.68), channel_id=1, source_target_pairs={{0,8},{8,0},{16,24},{24,16},{32,40},{40,32},{48,56},{56,48},{64,72... | collective-permute-start | bytes 122888 | tf_op jit(solution)/shard_map/ppermute | solution.py:33
  81.8 41.8 %collective-permute-start.16 = (bf16[384,2,256]{0,2,1:T(8,128)(2,1)}, bf16[384,2,256]{0,2,1:T(8,128)(2,1)}, u32[]{:S(2)}, u32[]{:S(2)}) collective-permute-start(bf16[384,2,256]{0,2,1:T(8,128)(2,1)} %pad_maximum_fusion), channel_id=1, source_target_pairs={{0,8},{8,16},{16,24},{24,32},{32,40},{40,48},{48,56},{56,64},{64,7... | collective-permute-start | bytes 1179656 | tf_op jit(solution)/shard_map/ppermute | solution.py:33
  84.3 11.1 %collective-permute-start.10 = (bf16[160,128]{1,0:T(8,128)(2,1)S(1)}, bf16[160,128]{1,0:T(8,128)(2,1)S(1)}, u32[]{:S(2)}, u32[]{:S(2)}) collective-permute-start(bf16[160,128]{1,0:T(8,128)(2,1)S(1)} %fusion.67), channel_id=1, source_target_pairs={{0,48},{8,56},{16,32},{24,40},{32,16},{40,24},{48,0},{56,8},{64,11... | collective-permute-start | bytes 122888 | tf_op jit(solution)/shard_map/ppermute | solution.py:33
  86.2 9.2 %collective-permute-start.9 = (bf16[160,128]{1,0:T(8,128)(2,1)S(1)}, bf16[160,128]{1,0:T(8,128)(2,1)S(1)}, u32[]{:S(2)}, u32[]{:S(2)}) collective-permute-start(bf16[160,128]{1,0:T(8,128)(2,1)S(1)} %fusion.67), channel_id=1, source_target_pairs={{0,32},{8,40},{16,48},{24,56},{32,0},{40,8},{48,16},{56,24},{64,96... | collective-permute-start | bytes 122888 | tf_op jit(solution)/shard_map/ppermute | solution.py:33
  88.1 7.5 %collective-permute-start.8 = (bf16[160,128]{1,0:T(8,128)(2,1)S(1)}, bf16[160,128]{1,0:T(8,128)(2,1)S(1)}, u32[]{:S(2)}, u32[]{:S(2)}) collective-permute-start(bf16[160,128]{1,0:T(8,128)(2,1)S(1)} %fusion.67), channel_id=1, source_target_pairs={{0,16},{8,24},{16,0},{24,8},{32,48},{40,56},{48,32},{56,40},{64,80... | collective-permute-start | bytes 122888 | tf_op jit(solution)/shard_map/ppermute | solution.py:33
  95.4 0.6 copy-start.9
  95.4 0.6 copy-start.11
  95.7 0.6 copy-start.13
  96.3 18.4 %copy-start.5 = (bf16[512,2,128]{2,1,0:T(2,128)(2,1)S(1)}, bf16[512,2,128]{2,1,0:T(2,128)(2,1)}, u32[]{:S(2)}) copy-start(bf16[512,2,128]{2,1,0:T(2,128)(2,1)} %get-tuple-element.15) | copy-start | bytes 786436
  96.3 22.4 %copy-start.10 = (bf16[160,128]{1,0:T(8,128)(2,1)S(1)}, bf16[160,128]{1,0:T(8,128)(2,1)}, u32[]{:S(2)}) copy-start(bf16[160,128]{1,0:T(8,128)(2,1)} %copy-done.9) | copy-start | bytes 122884
  96.3 22.4 %copy-start.12 = (bf16[160,128]{1,0:T(8,128)(2,1)S(1)}, bf16[160,128]{1,0:T(8,128)(2,1)}, u32[]{:S(2)}) copy-start(bf16[160,128]{1,0:T(8,128)(2,1)} %copy-done.11) | copy-start | bytes 122884
  96.3 22.4 %copy-start.14 = (bf16[160,128]{1,0:T(8,128)(2,1)S(1)}, bf16[160,128]{1,0:T(8,128)(2,1)}, u32[]{:S(2)}) copy-start(bf16[160,128]{1,0:T(8,128)(2,1)} %copy-done.13) | copy-start | bytes 122884
  96.3 11.0 %collective-permute-start.11 = (bf16[160,128]{1,0:T(8,128)(2,1)S(1)}, bf16[160,128]{1,0:T(8,128)(2,1)S(1)}, u32[]{:S(2)}, u32[]{:S(2)}) collective-permute-start(bf16[160,128]{1,0:T(8,128)(2,1)S(1)} %get-tuple-element.7), channel_id=1, source_target_pairs={{0,64},{8,72},{16,80},{24,88},{32,96},{40,104},{48,112},{56,120},{... | collective-permute-start | bytes 122888 | tf_op jit(solution)/shard_map/ppermute | solution.py:33
  107.3 7.6 %collective-permute-start.14 = (bf16[160,128]{1,0:T(8,128)(2,1)S(1)}, bf16[160,128]{1,0:T(8,128)(2,1)S(1)}, u32[]{:S(2)}, u32[]{:S(2)}) collective-permute-start(bf16[160,128]{1,0:T(8,128)(2,1)S(1)} %fusion.62), channel_id=1, source_target_pairs={{0,384},{8,392},{16,400},{24,408},{32,416},{40,424},{48,432},{56,4... | collective-permute-start | bytes 122888 | tf_op jit(solution)/shard_map/ppermute | solution.py:33
  108.0 6.9 %collective-permute-start.13 = (bf16[160,128]{1,0:T(8,128)(2,1)S(1)}, bf16[160,128]{1,0:T(8,128)(2,1)S(1)}, u32[]{:S(2)}, u32[]{:S(2)}) collective-permute-start(bf16[160,128]{1,0:T(8,128)(2,1)S(1)} %fusion.62), channel_id=1, source_target_pairs={{0,256},{8,264},{16,272},{24,280},{32,288},{40,296},{48,304},{56,3... | collective-permute-start | bytes 122888 | tf_op jit(solution)/shard_map/ppermute | solution.py:33
  112.8 5.9 %collective-permute-start.12 = (bf16[160,128]{1,0:T(8,128)(2,1)S(1)}, bf16[160,128]{1,0:T(8,128)(2,1)S(1)}, u32[]{:S(2)}, u32[]{:S(2)}) collective-permute-start(bf16[160,128]{1,0:T(8,128)(2,1)S(1)} %fusion.62), channel_id=1, source_target_pairs={{0,128},{8,136},{16,144},{24,152},{32,160},{40,168},{48,176},{56,1... | collective-permute-start | bytes 122888 | tf_op jit(solution)/shard_map/ppermute | solution.py:33
  118.7 3.1 %collective-permute-start.15 = (bf16[160,128]{1,0:T(8,128)(2,1)S(1)}, bf16[160,128]{1,0:T(8,128)(2,1)S(1)}, u32[]{:S(2)}, u32[]{:S(2)}) collective-permute-start(bf16[160,128]{1,0:T(8,128)(2,1)S(1)} %get-tuple-element.5), channel_id=1, source_target_pairs={{0,8},{8,0},{16,24},{24,16},{32,40},{40,32},{48,56},{56,48},{64,72... | collective-permute-start | bytes 122888 | tf_op jit(solution)/shard_map/ppermute | solution.py:33
  130.3 15.7 %collective-permute-start.22 = (bf16[64,2048]{1,0:T(8,128)(2,1)S(1)}, bf16[64,2048]{1,0:T(8,128)(2,1)S(1)}, u32[]{:S(2)}, u32[]{:S(2)}) collective-permute-start(bf16[64,2048]{1,0:T(8,128)(2,1)S(1)} %get-tuple-element.13), channel_id=1, source_target_pairs={{0,4},{8,12},{16,20},{24,28},{32,36},{40,44},{48,52},{56,60},{64,6... | collective-permute-start | bytes 786440 | tf_op jit(solution)/shard_map/ppermute | solution.py:33
  132.7 18.4 %collective-permute-start.21 = (bf16[64,2048]{1,0:T(8,128)(2,1)S(1)}, bf16[64,2048]{1,0:T(8,128)(2,1)S(1)}, u32[]{:S(2)}, u32[]{:S(2)}) collective-permute-start(bf16[64,2048]{1,0:T(8,128)(2,1)S(1)} %get-tuple-element.14), channel_id=1, source_target_pairs={{0,6},{8,14},{16,22},{24,30},{32,38},{40,46},{48,54},{56,62},{64,7... | collective-permute-start | bytes 786440 | tf_op jit(solution)/shard_map/ppermute | solution.py:33
  134.6 16.5 %collective-permute-start.20 = (bf16[64,2048]{1,0:T(8,128)(2,1)S(1)}, bf16[64,2048]{1,0:T(8,128)(2,1)S(1)}, u32[]{:S(2)}, u32[]{:S(2)}) collective-permute-start(bf16[64,2048]{1,0:T(8,128)(2,1)S(1)} %get-tuple-element.12), channel_id=1, source_target_pairs={{0,2},{8,10},{16,18},{24,26},{32,34},{40,42},{48,50},{56,58},{64,6... | collective-permute-start | bytes 786440 | tf_op jit(solution)/shard_map/ppermute | solution.py:33
  140.3 23.8 %collective-permute-start.19 = (bf16[64,2048]{1,0:T(8,128)(2,1)S(1)}, bf16[64,2048]{1,0:T(8,128)(2,1)S(1)}, u32[]{:S(2)}, u32[]{:S(2)}) collective-permute-start(bf16[64,2048]{1,0:T(8,128)(2,1)S(1)} %get-tuple-element.10), channel_id=1, source_target_pairs={{0,4},{8,12},{16,20},{24,28},{32,36},{40,44},{48,52},{56,60},{64,6... | collective-permute-start | bytes 786440 | tf_op jit(solution)/shard_map/ppermute | solution.py:33
  144.0 20.1 %collective-permute-start.18 = (bf16[64,2048]{1,0:T(8,128)(2,1)S(1)}, bf16[64,2048]{1,0:T(8,128)(2,1)S(1)}, u32[]{:S(2)}, u32[]{:S(2)}) collective-permute-start(bf16[64,2048]{1,0:T(8,128)(2,1)S(1)} %get-tuple-element.11), channel_id=1, source_target_pairs={{0,6},{8,14},{16,22},{24,30},{32,38},{40,46},{48,54},{56,62},{64,7... | collective-permute-start | bytes 786440 | tf_op jit(solution)/shard_map/ppermute | solution.py:33
  146.0 18.2 %collective-permute-start.17 = (bf16[64,2048]{1,0:T(8,128)(2,1)S(1)}, bf16[64,2048]{1,0:T(8,128)(2,1)S(1)}, u32[]{:S(2)}, u32[]{:S(2)}) collective-permute-start(bf16[64,2048]{1,0:T(8,128)(2,1)S(1)} %get-tuple-element.9), channel_id=1, source_target_pairs={{0,2},{8,10},{16,18},{24,26},{32,34},{40,42},{48,50},{56,58},{64,6... | collective-permute-start | bytes 786440 | tf_op jit(solution)/shard_map/ppermute | solution.py:33
  151.3 34.7 %collective-permute-start.23 = (bf16[64,2048]{1,0:T(8,128)(2,1)S(1)}, bf16[64,2048]{1,0:T(8,128)(2,1)S(1)}, u32[]{:S(2)}, u32[]{:S(2)}) collective-permute-start(bf16[64,2048]{1,0:T(8,128)(2,1)S(1)} %fusion.25), channel_id=1, source_target_pairs={{0,1},{8,9},{16,17},{24,25},{32,33},{40,41},{48,49},{56,57},{64,65... | collective-permute-start | bytes 786440 | tf_op jit(solution)/shard_map/ppermute | solution.py:33

commit v2 on v1

v2 whole, which is shorter than its diff:
```python
import jax
import jax.numpy as jnp
import numpy as np
from jax import lax
from jax.experimental import pallas as pl
from jax.experimental.pallas import tpu as pltpu
from jax.sharding import PartitionSpec as P

BLOCK = 128
WMAX = 4
NX, NY, NZ = 4, 4, 8
N_TP = 8
EPS = 1e-06
SCALE = 12.0
bf16, f32 = jnp.bfloat16, jnp.float32


def pairs(move):
    out = []
    for x in range(NX):
        for h in range(2):
            for y in range(NY):
                for z in range(NZ):
                    for c in range(2):
                        to = move(x, h, y, z, c)
                        if to is not None:
                            tx, th, ty, tz, tc = to
                            source = ((y * NZ + z) * 2 + c) * N_TP + x * 2 + h
                            target = ((ty * NZ + tz) * 2 + tc) * N_TP + (tx % NX) * 2 + th
                            out.append((source, target))
    return out


def send(value, move):
    return lax.ppermute(value, ("seq", "tp"), pairs(move))


def to_x(steps):
    return lambda x, h, y, z, c: (x + steps, h, y, z, c)


def to_half(x, h, y, z, c):
    return (x, 1 - h, y, z, c)


def to_core(x, h, y, z, c):
    return (x, h, y, z, 1 - c)


def to_z(flip):
    return lambda x, h, y, z, c: (x, h, y, z ^ flip, c)


def to_y(steps):
    return lambda x, h, y, z, c: (x, h, y + steps, z, c) if y + steps < NY else None


def to_next(x, h, y, z, c):
    place = (y * NZ + z) * 2 + c + 1
    if place == NY * NZ * 2:
        return None
    return (x, h, place // (2 * NZ), place // 2 % NZ, place % 2)


ROWS = 160
VMEM = pl.BlockSpec(memory_space=pltpu.VMEM)
SMEM = pl.BlockSpec(memory_space=pltpu.SMEM)


def feature_maps(feat_dim, heads):
    width = heads * 2 * feat_dim
    tables = np.zeros((heads, 4, ROWS, width), np.float32)
    ones = np.zeros((4, ROWS), np.float32)
    at = 0
    for i in range(feat_dim):
        for j in range(i, feat_dim):
            for head in range(heads):
                query, key = head * 2 * feat_dim, (head * 2 + 1) * feat_dim
                tables[head, 0, at, query + i] = 1.0 / 32.0 if i == j else 1.0 / 16.0
                tables[head, 1, at, query + j] = 1.0
                tables[head, 2, at, key + i] = 1.0
                tables[head, 3, at, key + j] = 1.0
            at += 1
    for i in range(feat_dim):
        for head in range(heads):
            query, key = head * 2 * feat_dim, (head * 2 + 1) * feat_dim
            tables[head, 0, at, query + i] = 0.25
            tables[head, 2, at, key + i] = 1.0
        ones[1, at] = ones[3, at] = 1.0
        at += 1
    ones[:, at] = 1.0
    return tables, ones


def dot(a, b):
    return jnp.dot(a, b, preferred_element_type=f32)


def dot_t(a, b):
    return lax.dot_general(a, b, (((1,), (1,)), ((), ())), preferred_element_type=f32)


def unit(v):
    return v * lax.rsqrt(jnp.mean(v * v, axis=-1, keepdims=True) + EPS)


def halves(v):
    high = v.astype(bf16)
    return high, (v - high.astype(f32)).astype(bf16)


def project_kernel(where, *refs):
    parts = refs[:N_TP]
    wf, ww, table, ones, feats_ref, qn_ref, kv_ref, tail_ref, mine_ref, other_ref = refs[N_TP:]
    core = where[N_TP]
    width = parts[0].shape[1]
    head = ww.shape[2] // 3
    tokens = jnp.concatenate([p[...] for p in parts], axis=1)
    rows = [pl.ds(pl.multiple_of(where[k] * width, width), width) for k in range(N_TP)]

    def columns(pick):
        return dot(tokens, jnp.concatenate([pick(r) for r in rows], axis=0)).astype(bf16)

    feats = columns(lambda r: wf[r, :])
    feats_ref[...] = feats
    first_tail = kv_ref.shape[0] - tail_ref.shape[0]
    states = []
    for kind in (2, 1, 0):
        out = columns(
            lambda r: jnp.concatenate([ww[h, r, kind * head : (kind + 1) * head] for h in range(2)], axis=1)
        )
        if kind == 2:
            kv_ref[:, 2 * head :] = out
            tail_ref[:, 2 * head :] = out[first_tail:]
            for h in range(2):
                left = dot_t(table[h, 2], feats) + ones[2]
                right = dot_t(table[h, 3], feats) + ones[3]
                high, low = halves(left * right)
                v = out[:, h * head : (h + 1) * head]
                states.append(dot(high, v) + dot(low, v))
            mine_ref[...] = jnp.where(core == 0, states[0], states[1])
            other_ref[...] = jnp.where(core == 0, states[1], states[0]).astype(bf16)
            continue
        for h in range(2):
            cols = slice(h * head, (h + 1) * head)
            normed = unit(out[:, cols].astype(f32)).astype(bf16)
            if kind == 1:
                kv_ref[:, cols] = normed
                tail_ref[:, cols] = normed[first_tail:]
            else:
                qn_ref[:, cols] = normed


def local_kernel(where, win, feats_ref, qn_ref, kv_ref, halo_ref, table, ones, near_ref, win_ref, high_ref, low_ref):
    seq = where[0]
    rows = qn_ref.shape[0]
    heads = win_ref.shape[1] // 128
    head = 128
    halo = halo_ref.shape[0]
    span = halo + BLOCK
    feats = feats_ref[...]
    feat = feats.shape[1] // (2 * heads)
    blocks = rows // BLOCK
    row = lax.broadcasted_iota(jnp.int32, (BLOCK, span), 0)
    col = lax.broadcasted_iota(jnp.int32, (BLOCK, span), 1)
    causal = col <= row + halo
    for h in range(heads):
        cols = slice(h * head, (h + 1) * head)
        vcols = slice((heads + h) * head, (heads + h + 1) * head)
        left = dot_t(feats, table[h, 0]) + ones[0:1]
        right = dot_t(feats, table[h, 1]) + ones[1:2]
        high, low = halves(left * right)
        high_ref[h] = high
        low_ref[h] = low
        key = lax.broadcasted_iota(jnp.int32, (feats.shape[1], feats.shape[1]), 0)
        lane = lax.broadcasted_iota(jnp.int32, (feats.shape[1], feats.shape[1]), 1)
        first = h * 2 * feat
        moved = (lane == key + feat) & (key >= first) & (key < first + feat)
        query = dot(feats, jnp.where(moved, 1.0, 0.0).astype(bf16)).astype(bf16)
        keys = jnp.concatenate([halo_ref[:, cols], kv_ref[:, cols]], axis=0)
        values = jnp.concatenate([halo_ref[:, vcols], kv_ref[:, vcols]], axis=0)
        for b in range(blocks):
            at = slice(b * BLOCK, (b + 1) * BLOCK)
            ahead = (b + 1) * BLOCK
            inner = dot_t(query[at], feats[:ahead])
            pair = 1.0 + inner * (0.25 + inner * (1.0 / 32.0))
            last = jnp.where(causal[:, halo:], pair[:, b * BLOCK :], 0.0)
            pair = jnp.concatenate([pair[:, : b * BLOCK], last], axis=1) if b else last
            near_ref[at, cols] = dot(pair.astype(bf16), values[halo : halo + ahead])
            scores = dot_t(qn_ref[at, cols], keys[b * BLOCK : b * BLOCK + span]) * (SCALE / head)
            least = jnp.maximum(span // BLOCK - win[h], span // BLOCK - 1 - (seq * blocks + b))
            allowed = causal & (col >= least * BLOCK)
            weights = jnp.where(allowed, jnp.exp(scores), 0.0).astype(bf16)
            win_ref[at, cols] = unit(dot(weights, values[b * BLOCK : b * BLOCK + span]))


def output_kernel(where, ours, theirs, near_ref, win_ref, high_ref, low_ref, w_ref, *refs):
    outs, hidden = refs[:-1], refs[-1]
    core, x, half = where[0], where[1], where[2]
    mine, other = ours[...], theirs[...].astype(f32)
    head = mine.shape[1]
    rows = hidden.shape[1]
    for h in range(2):
        cols = slice(h * head, (h + 1) * head)
        state_high, state_low = halves(jnp.where(core == h, mine, other))
        high = high_ref[h]
        far = dot(high, state_high) + dot(low_ref[h], state_high) + dot(high, state_low)
        out = (unit(near_ref[:, cols] + far) + win_ref[:, cols]).astype(bf16)
        for g in range(N_TP):
            hidden[g, :, cols] = out[g * rows : (g + 1) * rows]
    weight = w_ref[...]
    for away in (1, 0):
        want = jnp.where(away == 1, 1 - half, half)
        groups = [hidden[lax.rem(x + s, NX) * 2 + want] for s in range(NX)]
        product = dot(jnp.concatenate(groups, axis=0), weight).astype(bf16)
        for s in range(NX):
            outs[(1 - away) * NX + s][...] = product[s * rows : (s + 1) * rows]


def prefix(mine, other, place):
    x, h, y, z, c = place
    got = send(other, to_core).astype(f32)
    total = mine + got
    short = total.astype(bf16)
    quad = [send(short, to_z(flip)).astype(f32) for flip in (1, 2, 3)]
    before = jnp.zeros_like(total)
    for flip, part in zip((1, 2, 3), quad):
        before = before + jnp.where((z ^ flip) < z, part, 0.0)
        total = total + part
    part = send(total.astype(bf16), to_z(4)).astype(f32)
    before = before + jnp.where((z ^ 4) < z, part, 0.0)
    total = total + part
    short = total.astype(bf16)
    for steps in (1, 2, 3):
        before = before + send(short, to_y(steps)).astype(f32)
    theirs = send((before + jnp.where(c == 0, mine, 0.0)).astype(bf16), to_core)
    ours = before + jnp.where(c == 1, got, 0.0)
    return ours, theirs


def shape(dims, kind):
    return jax.ShapeDtypeStruct(dims, kind)


def project(where, parts, wf, ww, tables, ones):
    tok_rows = parts[0].shape[0]
    wide = 2 * ww.shape[2] // 3
    halo_rows = (WMAX - 1) * BLOCK
    return pl.pallas_call(
        project_kernel,
        out_shape=(
            shape((tok_rows, wf.shape[1]), bf16),
            shape((tok_rows, wide), bf16),
            shape((tok_rows, 2 * wide), bf16),
            shape((halo_rows, 2 * wide), bf16),
            shape((ROWS, wide // 2), f32),
            shape((ROWS, wide // 2), bf16),
        ),
        in_specs=[SMEM] + [VMEM] * (N_TP + 4),
        out_specs=(VMEM,) * 6,
        name="project",
        compiler_params=pltpu.CompilerParams(vmem_limit_bytes=LIMIT),
    )(where, *parts, wf, ww, tables.astype(bf16), ones[:, :, None])


def near(where, win_blocks, feats, qn, kv, halo, tables, ones):
    tok_rows, wide = qn.shape
    return pl.pallas_call(
        local_kernel,
        out_shape=(
            shape((tok_rows, wide), f32),
            shape((tok_rows, wide), f32),
            shape((2, tok_rows, ROWS), bf16),
            shape((2, tok_rows, ROWS), bf16),
        ),
        in_specs=[SMEM, SMEM] + [VMEM] * 6,
        out_specs=(VMEM,) * 4,
        name="near",
        compiler_params=pltpu.CompilerParams(vmem_limit_bytes=LIMIT),
    )(where, win_blocks, feats, qn, kv, halo, tables.astype(bf16), ones)


def output(where, ours, theirs, near_out, win_out, high, low, w_out):
    rows = near_out.shape[0] // N_TP
    return pl.pallas_call(
        output_kernel,
        out_shape=(shape((rows, w_out.shape[1]), bf16),) * N_TP,
        in_specs=[SMEM] + [VMEM] * 7,
        out_specs=(VMEM,) * N_TP,
        scratch_shapes=[pltpu.VMEM((N_TP, rows, w_out.shape[0]), bf16)],
        name="output",
        compiler_params=pltpu.CompilerParams(vmem_limit_bytes=LIMIT),
    )(where, ours, theirs, near_out, win_out, high, low, w_out)


LIMIT = 40 * 2**20


def local(tokens, w_feature, w_window, w_out, win_blocks):
    model_width, head_count = w_feature.shape[:2]
    feat_dim = w_feature.shape[2] // 2
    seq, tp = lax.axis_index("seq"), lax.axis_index("tp")
    x, h, y, z, c = tp // 2, tp % 2, seq // (2 * NZ), seq // 2 % NZ, seq % 2

    other = send(tokens, to_half)
    parts = [tokens] + [send(tokens, to_x(s)) for s in (1, 3, 2)]
    parts += [other] + [send(other, to_x(s)) for s in (1, 3, 2)]
    owners = [(x + NX - s) % NX * 2 + half for half in (h, 1 - h) for s in (0, 1, 3, 2)]
    tables, ones = feature_maps(feat_dim, head_count)

    feats, qn, kv, tail, mine, theirs = project(
        jnp.stack(owners + [c]).astype(jnp.int32),
        parts,
        w_feature.reshape(model_width, -1),
        w_window.transpose(1, 0, 2),
        tables,
        ones,
    )
    ours, theirs = prefix(mine, theirs, (x, h, y, z, c))
    halo = send(tail, to_next)
    near_out, win_out, high, low = near(seq[None], win_blocks, feats, qn, kv, halo, tables[:, :2], ones[:2])
    products = output(
        jnp.stack([c, x, h]), ours, theirs, near_out, win_out, high, low, w_out.reshape(-1, model_width)
    )

    def summed(group):
        total = group[0].astype(f32)
        for steps in (1, 3, 2):
            total = total + send(group[steps], to_x(steps)).astype(f32)
        return total

    away = summed(products[:NX]).astype(bf16)
    away, *own = lax.optimization_barrier((away, *products[NX:]))
    away = send(away, to_half)
    return (summed(own) + away.astype(f32)).astype(bf16)


def solution(mesh):
    in_specs = (P("seq", "tp"), P(None, "tp", None), P(None, "tp", None), P("tp", None, None), P("tp"))
    return jax.shard_map(local, mesh=mesh, in_specs=in_specs, out_specs=P(("seq", "tp"), None), check_vma=False)
```

time: 188 us -> 180 us (0.957)
  the two profiles are of different devices: /device:TPU:46 before, /device:TPU:8 now
where the time goes in v2:
time: 180 us; the launch traced here: 179 us
  starting transfers between devices  111 us (62%)
  waiting for transfers between devices  39.1 us (22%)
  local copies, waits for them, and re-layouts  17.4 us (10%)
  Pallas kernels  10.2 us (6%)
    ppermute x24, starting transfers between devices, send(): return lax.ppermute(value, ('seq', 'tp'), pairs(move))  111 us
    ppermute x24, waiting for transfers between devices, send(): return lax.ppermute(value, ('seq', 'tp'), pairs(move))  39.1 us
    unnamed x37, local copies, waits for them, and re-layouts  14.8 us
    pallas_call x1, Pallas kernels, project(): pl.pallas_call(project_kernel, out_shape=(shape((tok_rows, wf.shape[1]),...  4.5 us
    pallas_call x1, Pallas kernels, near(): pl.pallas_call(local_kernel, out_shape=(shape((tok_rows, wide), f32), sha...  3.78 us
  transfers between devices with their start and end apart: 24, of which 11 were waited for; matrix products, arithmetic and copies ran while one was open for 3% of the time, Pallas kernels for 2%

profile of v2, /device:TPU:8, one launch (start us, length us, event | category | flops | bytes accessed | tf_op | source)
XLA Modules:
  0.0 179.1 jit_solution(11612321327539084697)
XLA Ops:
  0.0 15.7 %collective-permute-start.3 = (bf16[512,256]{1,0:T(8,128)(2,1)}, bf16[512,256]{1,0:T(8,128)(2,1)}, u32[]{:S(2)}, u32[]{:S(2)}) collective-permute-start(bf16[512,256]{1,0:T(8,128)(2,1)} %refs_0_.1), channel_id=1, source_target_pairs={{0,1},{8,9},{16,17},{24,25},{32,33},{40,41},{48,49},{56,57},{64,65... | collective-permute-start | bytes 786440 | tf_op jit(solution)/shard_map/ppermute | solution.py:35
  15.7 3.4 %collective-permute-start = (bf16[512,256]{1,0:T(8,128)(2,1)}, bf16[512,256]{1,0:T(8,128)(2,1)S(1)}, u32[]{:S(2)}, u32[]{:S(2)}) collective-permute-start(bf16[512,256]{1,0:T(8,128)(2,1)} %refs_0_.1), channel_id=1, source_target_pairs={{0,2},{8,10},{16,18},{24,26},{32,34},{40,42},{48,50},{56,58},{64,6... | collective-permute-start | bytes 786440 | tf_op jit(solution)/shard_map/ppermute | solution.py:35
  19.1 3.7 %collective-permute-start.1 = (bf16[512,256]{1,0:T(8,128)(2,1)}, bf16[512,256]{1,0:T(8,128)(2,1)}, u32[]{:S(2)}, u32[]{:S(2)}) collective-permute-start(bf16[512,256]{1,0:T(8,128)(2,1)} %refs_0_.1), channel_id=1, source_target_pairs={{0,6},{8,14},{16,22},{24,30},{32,38},{40,46},{48,54},{56,62},{64,7... | collective-permute-start | bytes 786440 | tf_op jit(solution)/shard_map/ppermute | solution.py:35
  22.8 3.7 %collective-permute-start.2 = (bf16[512,256]{1,0:T(8,128)(2,1)}, bf16[512,256]{1,0:T(8,128)(2,1)}, u32[]{:S(2)}, u32[]{:S(2)}) collective-permute-start(bf16[512,256]{1,0:T(8,128)(2,1)} %refs_0_.1), channel_id=1, source_target_pairs={{0,4},{8,12},{16,20},{24,28},{32,36},{40,44},{48,52},{56,60},{64,6... | collective-permute-start | bytes 786440 | tf_op jit(solution)/shard_map/ppermute | solution.py:35
  26.5 0.0 collective-permute-done.3.refs_4_
  26.5 2.5 %collective-permute-start.4 = (bf16[512,256]{1,0:T(8,128)(2,1)}, bf16[512,256]{1,0:T(8,128)(2,1)}, u32[]{:S(2)}, u32[]{:S(2)}) collective-permute-start(bf16[512,256]{1,0:T(8,128)(2,1)} %collective-permute-done.3.refs_4_), channel_id=1, source_target_pairs={{0,2},{8,10},{16,18},{24,26},{32,34},{40,42},{48,50},{56,58},{64,6... | collective-permute-start | bytes 786440 | tf_op jit(solution)/shard_map/ppermute | solution.py:35
  29.0 4.6 %collective-permute-start.5 = (bf16[512,256]{1,0:T(8,128)(2,1)}, bf16[512,256]{1,0:T(8,128)(2,1)}, u32[]{:S(2)}, u32[]{:S(2)}) collective-permute-start(bf16[512,256]{1,0:T(8,128)(2,1)} %collective-permute-done.3.refs_4_), channel_id=1, source_target_pairs={{0,6},{8,14},{16,22},{24,30},{32,38},{40,46},{48,54},{56,62},{64,7... | collective-permute-start | bytes 786440 | tf_op jit(solution)/shard_map/ppermute | solution.py:35
  33.6 0.0 copy-start.7
  33.6 0.7 copy-done.7
  34.3 2.4 %collective-permute-start.6 = (bf16[512,256]{1,0:T(8,128)(2,1)}, bf16[512,256]{1,0:T(8,128)(2,1)}, u32[]{:S(2)}, u32[]{:S(2)}) collective-permute-start(bf16[512,256]{1,0:T(8,128)(2,1)} %collective-permute-done.3.refs_4_), channel_id=1, source_target_pairs={{0,4},{8,12},{16,20},{24,28},{32,36},{40,44},{48,52},{56,60},{64,6... | collective-permute-start | bytes 786440 | tf_op jit(solution)/shard_map/ppermute | solution.py:35
  36.8 2.0 %copy.13.refs_8_ = bf16[2048,64]{1,0:T(8,128)(2,1)} copy(bf16[2048,64]{0,1:T(8,128)(2,1)} %bitcast.19) | data formatting | bytes 524288 | tf_op jit(solution)/shard_map/reshape | solution.py:314
  38.8 2.3 %copy.15 = bf16[2048,2,384]{2,0,1:T(8,128)(2,1)S(1)} copy(bf16[2048,2,384]{2,1,0:T(2,128)(2,1)} %param.11) | data formatting | bytes 6291456 | tf_op args[2]
  41.1 0.6 stack.52.where
  41.7 0.0 collective-permute-done.1.refs_2_
  41.7 0.0 collective-permute-done.2.refs_3_
  41.8 3.4 %collective-permute-done.5.refs_6_ = bf16[512,256]{1,0:T(8,128)(2,1)} collective-permute-done((bf16[512,256]{1,0:T(8,128)(2,1)}, bf16[512,256]{1,0:T(8,128)(2,1)}, u32[]{:S(2)}, u32[]{:S(2)}) %collective-permute-start.5) | collective-permute-done | bytes 262176 | tf_op jit(solution)/shard_map/ppermute | solution.py:35
  45.1 1.0 copy-done
  46.2 1.0 copy-done.5
  47.1 0.9 copy-done.6
  48.1 0.9 copy-done.8
  49.0 0.6 copy-done.15
  49.6 4.5 %project.1 = (bf16[512,64]{1,0:T(8,128)(2,1)S(1)}, bf16[512,256]{1,0:T(8,128)(2,1)S(1)}, bf16[512,512]{1,0:T(8,128)(2,1)S(1)}, bf16[384,512]{1,0:T(8,128)(2,1)S(...) custom-call(s32[9]{0:T(128)S(1)} %copy-done.15, bf16[512,256]{1,0:T(8,128)(2,1)S(1)} %copy-done.6, ...), custom_call_target="tpu_custom_call" | custom-call | tf_op jit(solution)/shard_map/project/pallas_call | solution.py:249
  54.1 0.8 copy-done.2
  54.9 0.7 copy-done.9
  55.6 0.6 copy-done.12
  56.3 2.0 %collective-permute-start.7 = (bf16[160,128]{1,0:T(8,128)(2,1)S(1)}, bf16[160,128]{1,0:T(8,128)(2,1)S(1)}, u32[]{:S(2)}, u32[]{:S(2)}) collective-permute-start(bf16[160,128]{1,0:T(8,128)(2,1)S(1)} %get-tuple-element.29), channel_id=1, source_target_pairs={{0,8},{8,0},{16,24},{24,16},{32,40},{40,32},{48,56},{56,48},{64,72... | collective-permute-start | bytes 122888 | tf_op jit(solution)/shard_map/ppermute | solution.py:35
  58.3 1.2 collective-permute-done.7
  59.5 6.5 %collective-permute-start.10 = (bf16[160,128]{1,0:T(8,128)(2,1)S(1)}, bf16[160,128]{1,0:T(8,128)(2,1)S(1)}, u32[]{:S(2)}, u32[]{:S(2)}) collective-permute-start(bf16[160,128]{1,0:T(8,128)(2,1)S(1)} %fusion.8), channel_id=1, source_target_pairs={{0,48},{8,56},{16,32},{24,40},{32,16},{40,24},{48,0},{56,8},{64,11... | collective-permute-start | bytes 122888 | tf_op jit(solution)/shard_map/ppermute | solution.py:35
  66.1 12.3 %collective-permute-start.9 = (bf16[160,128]{1,0:T(8,128)(2,1)S(1)}, bf16[160,128]{1,0:T(8,128)(2,1)S(1)}, u32[]{:S(2)}, u32[]{:S(2)}) collective-permute-start(bf16[160,128]{1,0:T(8,128)(2,1)S(1)} %fusion.8), channel_id=1, source_target_pairs={{0,32},{8,40},{16,48},{24,56},{32,0},{40,8},{48,16},{56,24},{64,96... | collective-permute-start | bytes 122888 | tf_op jit(solution)/shard_map/ppermute | solution.py:35
  78.4 1.9 %collective-permute-start.8 = (bf16[160,128]{1,0:T(8,128)(2,1)S(1)}, bf16[160,128]{1,0:T(8,128)(2,1)S(1)}, u32[]{:S(2)}, u32[]{:S(2)}) collective-permute-start(bf16[160,128]{1,0:T(8,128)(2,1)S(1)} %fusion.8), channel_id=1, source_target_pairs={{0,16},{8,24},{16,0},{24,8},{32,48},{40,56},{48,32},{56,40},{64,80... | collective-permute-start | bytes 122888 | tf_op jit(solution)/shard_map/ppermute | solution.py:35
  80.3 0.5 collective-permute-done.9
  80.8 3.5 %collective-permute-done.8 = bf16[160,128]{1,0:T(8,128)(2,1)S(1)} collective-permute-done((bf16[160,128]{1,0:T(8,128)(2,1)S(1)}, bf16[160,128]{1,0:T(8,128)(2,1)S(1)}, u32[]{:S(2)}, u32[]{:S(2)}) %collective-permute-start.8) | collective-permute-done | bytes 40992 | tf_op jit(solution)/shard_map/ppermute | solution.py:35
  84.3 6.3 %collective-permute-start.11 = (bf16[160,128]{1,0:T(8,128)(2,1)S(1)}, bf16[160,128]{1,0:T(8,128)(2,1)S(1)}, u32[]{:S(2)}, u32[]{:S(2)}) collective-permute-start(bf16[160,128]{1,0:T(8,128)(2,1)S(1)} %fusion.9), channel_id=1, source_target_pairs={{0,64},{8,72},{16,80},{24,88},{32,96},{40,104},{48,112},{56,120},{... | collective-permute-start | bytes 122888 | tf_op jit(solution)/shard_map/ppermute | solution.py:35
  90.6 3.8 %collective-permute-done.11 = bf16[160,128]{1,0:T(8,128)(2,1)S(1)} collective-permute-done((bf16[160,128]{1,0:T(8,128)(2,1)S(1)}, bf16[160,128]{1,0:T(8,128)(2,1)S(1)}, u32[]{:S(2)}, u32[]{:S(2)}) %collective-permute-start.11) | collective-permute-done | bytes 40992 | tf_op jit(solution)/shard_map/ppermute | solution.py:35
  94.5 0.7 collective-permute-start.14
  95.1 4.8 %collective-permute-start.13 = (bf16[160,128]{1,0:T(8,128)(2,1)S(1)}, bf16[160,128]{1,0:T(8,128)(2,1)S(1)}, u32[]{:S(2)}, u32[]{:S(2)}) collective-permute-start(bf16[160,128]{1,0:T(8,128)(2,1)S(1)} %fusion.7), channel_id=1, source_target_pairs={{0,256},{8,264},{16,272},{24,280},{32,288},{40,296},{48,304},{56,3... | collective-permute-start | bytes 122888 | tf_op jit(solution)/shard_map/ppermute | solution.py:35
  100.0 1.9 %collective-permute-start.12 = (bf16[160,128]{1,0:T(8,128)(2,1)S(1)}, bf16[160,128]{1,0:T(8,128)(2,1)S(1)}, u32[]{:S(2)}, u32[]{:S(2)}) collective-permute-start(bf16[160,128]{1,0:T(8,128)(2,1)S(1)} %fusion.7), channel_id=1, source_target_pairs={{0,128},{8,136},{16,144},{24,152},{32,160},{40,168},{48,176},{56,1... | collective-permute-start | bytes 122888 | tf_op jit(solution)/shard_map/ppermute | solution.py:35
  101.9 0.1 pad_add_fusion.where
  102.0 1.9 %collective-permute-start.16 = (bf16[384,512]{1,0:T(8,128)(2,1)}, bf16[384,512]{1,0:T(8,128)(2,1)S(1)}, u32[]{:S(2)}, u32[]{:S(2)}) collective-permute-start(bf16[384,512]{1,0:T(8,128)(2,1)} %copy-done.17), channel_id=1, source_target_pairs={{0,8},{8,16},{16,24},{24,32},{32,40},{40,48},{48,56},{56,64},{64,7... | collective-permute-start | bytes 1179656 | tf_op jit(solution)/shard_map/ppermute | solution.py:35
  103.9 1.9 %collective-permute-done.12 = bf16[160,128]{1,0:T(8,128)(2,1)S(1)} collective-permute-done((bf16[160,128]{1,0:T(8,128)(2,1)S(1)}, bf16[160,128]{1,0:T(8,128)(2,1)S(1)}, u32[]{:S(2)}, u32[]{:S(2)}) %collective-permute-start.12) | collective-permute-done | bytes 40992 | tf_op jit(solution)/shard_map/ppermute | solution.py:35
  105.9 0.1 add_convert_fusion.2
  105.9 1.9 %collective-permute-start.15 = (bf16[160,128]{1,0:T(8,128)(2,1)S(1)}, bf16[160,128]{1,0:T(8,128)(2,1)S(1)}, u32[]{:S(2)}, u32[]{:S(2)}) collective-permute-start(bf16[160,128]{1,0:T(8,128)(2,1)S(1)} %get-tuple-element.51), channel_id=1, source_target_pairs={{0,8},{8,0},{16,24},{24,16},{32,40},{40,32},{48,56},{56,48},{64,72... | collective-permute-start | bytes 122888 | tf_op jit(solution)/shard_map/ppermute | solution.py:35
  107.9 10.9 %collective-permute-done.16.halo_ref = bf16[384,512]{1,0:T(8,128)(2,1)S(1)} collective-permute-done((bf16[384,512]{1,0:T(8,128)(2,1)}, bf16[384,512]{1,0:T(8,128)(2,1)S(1)}, u32[]{:S(2)}, u32[]{:S(2)}) %collective-permute-start.16) | collective-permute-done | bytes 393248 | tf_op jit(solution)/shard_map/ppermute | solution.py:35
  118.8 1.0 copy-done.3
  119.8 0.9 copy-done.10
  120.8 0.9 copy-done.11
  121.7 0.9 copy-done.13
  122.6 0.7 copy-done.14
  123.3 0.7 copy-done.16
  123.9 3.8 %near.1 = (f32[512,256]{1,0:T(8,128)S(1)}, f32[512,256]{1,0:T(8,128)S(1)}, bf16[2,512,160]{2,1,0:T(8,128)(2,1)S(1)}, bf16[2,512,160]{2,1,0:T(8,128)(2,1)S(1)}) custom-call(s32[1]{0:T(128)} %bitcast.13.where, s32[2]{0:T(128)S(1)} %copy-done.16, bf16[512,64]{1,0:T(8,128)(2,1)S(1)} %copy-done.13, bf16[512,256]{1,0:T(8,128)(2,1)S(1)} %copy-done.10, ...), custom_call_target="tpu_custom_call" | custom-call | tf_op jit(solution)/shard_map/near/pallas_call | solution.py:268
  127.7 1.9 %output.1 = (bf16[64,2048]{1,0:T(8,128)(2,1)S(1)}, bf16[64,2048]{1,0:T(8,128)(2,1)S(1)}, bf16[64,2048]{1,0:T(8,128)(2,1)S(1)}, bf16[64,2048]{1,0:T(8,128)(2,1)S(...) custom-call(s32[3]{0:T(128)S(1)} %pad_add_fusion.where, ...), custom_call_target="tpu_custom_call" | custom-call | tf_op jit(solution)/shard_map/output/pallas_call | solution.py:285
  129.6 3.7 %collective-permute-start.19 = (bf16[64,2048]{1,0:T(8,128)(2,1)S(1)}, bf16[64,2048]{1,0:T(8,128)(2,1)S(1)}, u32[]{:S(2)}, u32[]{:S(2)}) collective-permute-start(bf16[64,2048]{1,0:T(8,128)(2,1)S(1)} %get-tuple-element.41), channel_id=1, source_target_pairs={{0,4},{8,12},{16,20},{24,28},{32,36},{40,44},{48,52},{56,60},{64,6... | collective-permute-start | bytes 786440 | tf_op jit(solution)/shard_map/ppermute | solution.py:35
  133.4 4.9 %collective-permute-start.18 = (bf16[64,2048]{1,0:T(8,128)(2,1)S(1)}, bf16[64,2048]{1,0:T(8,128)(2,1)S(1)}, u32[]{:S(2)}, u32[]{:S(2)}) collective-permute-start(bf16[64,2048]{1,0:T(8,128)(2,1)S(1)} %get-tuple-element.40), channel_id=1, source_target_pairs={{0,6},{8,14},{16,22},{24,30},{32,38},{40,46},{48,54},{56,62},{64,7... | collective-permute-start | bytes 786440 | tf_op jit(solution)/shard_map/ppermute | solution.py:35
  138.3 1.9 %collective-permute-start.17 = (bf16[64,2048]{1,0:T(8,128)(2,1)S(1)}, bf16[64,2048]{1,0:T(8,128)(2,1)S(1)}, u32[]{:S(2)}, u32[]{:S(2)}) collective-permute-start(bf16[64,2048]{1,0:T(8,128)(2,1)S(1)} %get-tuple-element.39), channel_id=1, source_target_pairs={{0,2},{8,10},{16,18},{24,26},{32,34},{40,42},{48,50},{56,58},{64,6... | collective-permute-start | bytes 786440 | tf_op jit(solution)/shard_map/ppermute | solution.py:35
  140.2 2.3 %collective-permute-done.18 = bf16[64,2048]{1,0:T(8,128)(2,1)S(1)} collective-permute-done((bf16[64,2048]{1,0:T(8,128)(2,1)S(1)}, bf16[64,2048]{1,0:T(8,128)(2,1)S(1)}, u32[]{:S(2)}, u32[]{:S(2)}) %collective-permute-start.18) | collective-permute-done | bytes 262176 | tf_op jit(solution)/shard_map/ppermute | solution.py:35
  142.5 5.2 %collective-permute-done.17 = bf16[64,2048]{1,0:T(8,128)(2,1)S(1)} collective-permute-done((bf16[64,2048]{1,0:T(8,128)(2,1)S(1)}, bf16[64,2048]{1,0:T(8,128)(2,1)S(1)}, u32[]{:S(2)}, u32[]{:S(2)}) %collective-permute-start.17) | collective-permute-done | bytes 262176 | tf_op jit(solution)/shard_map/ppermute | solution.py:35
  147.8 0.1 add_convert_fusion.1
  147.9 16.2 %collective-permute-start.23 = (bf16[64,2048]{1,0:T(8,128)(2,1)S(1)}, bf16[64,2048]{1,0:T(8,128)(2,1)S(1)}, u32[]{:S(2)}, u32[]{:S(2)}) collective-permute-start(bf16[64,2048]{1,0:T(8,128)(2,1)S(1)} %add_convert_fusion.1), channel_id=1, source_target_pairs={{0,1},{8,9},{16,17},{24,25},{32,33},{40,41},{48,49},{56,57},{64,65... | collective-permute-start | bytes 786440 | tf_op jit(solution)/shard_map/ppermute | solution.py:35
  164.1 1.9 %collective-permute-start.22 = (bf16[64,2048]{1,0:T(8,128)(2,1)S(1)}, bf16[64,2048]{1,0:T(8,128)(2,1)S(1)}, u32[]{:S(2)}, u32[]{:S(2)}) collective-permute-start(bf16[64,2048]{1,0:T(8,128)(2,1)S(1)} %get-tuple-element.49), channel_id=1, source_target_pairs={{0,4},{8,12},{16,20},{24,28},{32,36},{40,44},{48,52},{56,60},{64,6... | collective-permute-start | bytes 786440 | tf_op jit(solution)/shard_map/ppermute | solution.py:35
  166.0 2.1 %collective-permute-start.21 = (bf16[64,2048]{1,0:T(8,128)(2,1)S(1)}, bf16[64,2048]{1,0:T(8,128)(2,1)S(1)}, u32[]{:S(2)}, u32[]{:S(2)}) collective-permute-start(bf16[64,2048]{1,0:T(8,128)(2,1)S(1)} %get-tuple-element.48), channel_id=1, source_target_pairs={{0,6},{8,14},{16,22},{24,30},{32,38},{40,46},{48,54},{56,62},{64,7... | collective-permute-start | bytes 786440 | tf_op jit(solution)/shard_map/ppermute | solution.py:35
  168.1 3.7 %collective-permute-start.20 = (bf16[64,2048]{1,0:T(8,128)(2,1)S(1)}, bf16[64,2048]{1,0:T(8,128)(2,1)S(1)}, u32[]{:S(2)}, u32[]{:S(2)}) collective-permute-start(bf16[64,2048]{1,0:T(8,128)(2,1)S(1)} %get-tuple-element.47), channel_id=1, source_target_pairs={{0,2},{8,10},{16,18},{24,26},{32,34},{40,42},{48,50},{56,58},{64,6... | collective-permute-start | bytes 786440 | tf_op jit(solution)/shard_map/ppermute | solution.py:35
  171.9 6.3 %collective-permute-done.23 = bf16[64,2048]{1,0:T(8,128)(2,1)S(1)} collective-permute-done((bf16[64,2048]{1,0:T(8,128)(2,1)S(1)}, bf16[64,2048]{1,0:T(8,128)(2,1)S(1)}, u32[]{:S(2)}, u32[]{:S(2)}) %collective-permute-start.23) | collective-permute-done | bytes 262176 | tf_op jit(solution)/shard_map/ppermute | solution.py:35
  178.1 0.1 collective-permute-done.20
  178.3 0.9 add_convert_fusion
  (34 shorter events, 0.2 us)
Async XLA Ops:
  0.0 26.5 %collective-permute-start.3 = (bf16[512,256]{1,0:T(8,128)(2,1)}, bf16[512,256]{1,0:T(8,128)(2,1)}, u32[]{:S(2)}, u32[]{:S(2)}) collective-permute-start(bf16[512,256]{1,0:T(8,128)(2,1)} %refs_0_.1), channel_id=1, source_target_pairs={{0,1},{8,9},{16,17},{24,25},{32,33},{40,41},{48,49},{56,57},{64,65... | collective-permute-start | bytes 786440 | tf_op jit(solution)/shard_map/ppermute | solution.py:35
  15.7 17.9 %collective-permute-start = (bf16[512,256]{1,0:T(8,128)(2,1)}, bf16[512,256]{1,0:T(8,128)(2,1)S(1)}, u32[]{:S(2)}, u32[]{:S(2)}) collective-permute-start(bf16[512,256]{1,0:T(8,128)(2,1)} %refs_0_.1), channel_id=1, source_target_pairs={{0,2},{8,10},{16,18},{24,26},{32,34},{40,42},{48,50},{56,58},{64,6... | collective-permute-start | bytes 786440 | tf_op jit(solution)/shard_map/ppermute | solution.py:35
  19.1 22.6 %collective-permute-start.1 = (bf16[512,256]{1,0:T(8,128)(2,1)}, bf16[512,256]{1,0:T(8,128)(2,1)}, u32[]{:S(2)}, u32[]{:S(2)}) collective-permute-start(bf16[512,256]{1,0:T(8,128)(2,1)} %refs_0_.1), channel_id=1, source_target_pairs={{0,6},{8,14},{16,22},{24,30},{32,38},{40,46},{48,54},{56,62},{64,7... | collective-permute-start | bytes 786440 | tf_op jit(solution)/shard_map/ppermute | solution.py:35
  22.8 18.9 %collective-permute-start.2 = (bf16[512,256]{1,0:T(8,128)(2,1)}, bf16[512,256]{1,0:T(8,128)(2,1)}, u32[]{:S(2)}, u32[]{:S(2)}) collective-permute-start(bf16[512,256]{1,0:T(8,128)(2,1)} %refs_0_.1), channel_id=1, source_target_pairs={{0,4},{8,12},{16,20},{24,28},{32,36},{40,44},{48,52},{56,60},{64,6... | collective-permute-start | bytes 786440 | tf_op jit(solution)/shard_map/ppermute | solution.py:35
  26.5 15.2 %collective-permute-start.4 = (bf16[512,256]{1,0:T(8,128)(2,1)}, bf16[512,256]{1,0:T(8,128)(2,1)}, u32[]{:S(2)}, u32[]{:S(2)}) collective-permute-start(bf16[512,256]{1,0:T(8,128)(2,1)} %collective-permute-done.3.refs_4_), channel_id=1, source_target_pairs={{0,2},{8,10},{16,18},{24,26},{32,34},{40,42},{48,50},{56,58},{64,6... | collective-permute-start | bytes 786440 | tf_op jit(solution)/shard_map/ppermute | solution.py:35
  29.0 16.1 %collective-permute-start.5 = (bf16[512,256]{1,0:T(8,128)(2,1)}, bf16[512,256]{1,0:T(8,128)(2,1)}, u32[]{:S(2)}, u32[]{:S(2)}) collective-permute-start(bf16[512,256]{1,0:T(8,128)(2,1)} %collective-permute-done.3.refs_4_), channel_id=1, source_target_pairs={{0,6},{8,14},{16,22},{24,30},{32,38},{40,46},{48,54},{56,62},{64,7... | collective-permute-start | bytes 786440 | tf_op jit(solution)/shard_map/ppermute | solution.py:35
  33.6 0.7 copy-start.7
  34.3 10.8 %collective-permute-start.6 = (bf16[512,256]{1,0:T(8,128)(2,1)}, bf16[512,256]{1,0:T(8,128)(2,1)}, u32[]{:S(2)}, u32[]{:S(2)}) collective-permute-start(bf16[512,256]{1,0:T(8,128)(2,1)} %collective-permute-done.3.refs_4_), channel_id=1, source_target_pairs={{0,4},{8,12},{16,20},{24,28},{32,36},{40,44},{48,52},{56,60},{64,6... | collective-permute-start | bytes 786440 | tf_op jit(solution)/shard_map/ppermute | solution.py:35
  38.8 6.3 %copy-start.4 = (bf16[2,4,160,64]{3,2,1,0:T(8,128)(2,1)S(1)}, bf16[2,4,160,64]{3,2,1,0:T(8,128)(2,1)}, u32[]{:S(2)}) copy-start(bf16[2,4,160,64]{3,2,1,0:T(8,128)(2,1)} %constant.103.clone.refs_10_) | copy-start | bytes 491524
  45.1 1.0 copy-start
  46.2 1.0 copy-start.5
  47.1 0.9 copy-start.6
  48.1 0.9 copy-start.8
  49.0 0.6 copy-start.15
  54.1 0.8 copy-start.2
  54.9 0.7 copy-start.9
  55.6 0.6 copy-start.12
  56.3 45.6 %copy-start.17 = (bf16[384,512]{1,0:T(8,128)(2,1)}, bf16[384,512]{1,0:T(8,128)(2,1)S(1)}, u32[]{:S(2)}) copy-start(bf16[384,512]{1,0:T(8,128)(2,1)S(1)} %get-tuple-element.33) | copy-start | bytes 1179652
  56.3 71.4 %copy-start.1 = (bf16[2,128,2048]{2,1,0:T(8,128)(2,1)S(1)}, bf16[2,128,2048]{2,1,0:T(8,128)(2,1)}, u32[]{:S(2)}) copy-start(bf16[2,128,2048]{2,1,0:T(8,128)(2,1)} %param.12) | copy-start | bytes 3145732
  56.3 3.2 %collective-permute-start.7 = (bf16[160,128]{1,0:T(8,128)(2,1)S(1)}, bf16[160,128]{1,0:T(8,128)(2,1)S(1)}, u32[]{:S(2)}, u32[]{:S(2)}) collective-permute-start(bf16[160,128]{1,0:T(8,128)(2,1)S(1)} %get-tuple-element.29), channel_id=1, source_target_pairs={{0,8},{8,0},{16,24},{24,16},{32,40},{40,32},{48,56},{56,48},{64,72... | collective-permute-start | bytes 122888 | tf_op jit(solution)/shard_map/ppermute | solution.py:35
  59.5 20.8 %collective-permute-start.10 = (bf16[160,128]{1,0:T(8,128)(2,1)S(1)}, bf16[160,128]{1,0:T(8,128)(2,1)S(1)}, u32[]{:S(2)}, u32[]{:S(2)}) collective-permute-start(bf16[160,128]{1,0:T(8,128)(2,1)S(1)} %fusion.8), channel_id=1, source_target_pairs={{0,48},{8,56},{16,32},{24,40},{32,16},{40,24},{48,0},{56,8},{64,11... | collective-permute-start | bytes 122888 | tf_op jit(solution)/shard_map/ppermute | solution.py:35
  66.1 14.7 %collective-permute-start.9 = (bf16[160,128]{1,0:T(8,128)(2,1)S(1)}, bf16[160,128]{1,0:T(8,128)(2,1)S(1)}, u32[]{:S(2)}, u32[]{:S(2)}) collective-permute-start(bf16[160,128]{1,0:T(8,128)(2,1)S(1)} %fusion.8), channel_id=1, source_target_pairs={{0,32},{8,40},{16,48},{24,56},{32,0},{40,8},{48,16},{56,24},{64,96... | collective-permute-start | bytes 122888 | tf_op jit(solution)/shard_map/ppermute | solution.py:35
  78.4 5.9 %collective-permute-start.8 = (bf16[160,128]{1,0:T(8,128)(2,1)S(1)}, bf16[160,128]{1,0:T(8,128)(2,1)S(1)}, u32[]{:S(2)}, u32[]{:S(2)}) collective-permute-start(bf16[160,128]{1,0:T(8,128)(2,1)S(1)} %fusion.8), channel_id=1, source_target_pairs={{0,16},{8,24},{16,0},{24,8},{32,48},{40,56},{48,32},{56,40},{64,80... | collective-permute-start | bytes 122888 | tf_op jit(solution)/shard_map/ppermute | solution.py:35
  84.3 10.1 %collective-permute-start.11 = (bf16[160,128]{1,0:T(8,128)(2,1)S(1)}, bf16[160,128]{1,0:T(8,128)(2,1)S(1)}, u32[]{:S(2)}, u32[]{:S(2)}) collective-permute-start(bf16[160,128]{1,0:T(8,128)(2,1)S(1)} %fusion.9), channel_id=1, source_target_pairs={{0,64},{8,72},{16,80},{24,88},{32,96},{40,104},{48,112},{56,120},{... | collective-permute-start | bytes 122888 | tf_op jit(solution)/shard_map/ppermute | solution.py:35
  94.5 9.4 %collective-permute-start.14 = (bf16[160,128]{1,0:T(8,128)(2,1)S(1)}, bf16[160,128]{1,0:T(8,128)(2,1)S(1)}, u32[]{:S(2)}, u32[]{:S(2)}) collective-permute-start(bf16[160,128]{1,0:T(8,128)(2,1)S(1)} %fusion.7), channel_id=1, source_target_pairs={{0,384},{8,392},{16,400},{24,408},{32,416},{40,424},{48,432},{56,4... | collective-permute-start | bytes 122888 | tf_op jit(solution)/shard_map/ppermute | solution.py:35
  95.1 8.8 %collective-permute-start.13 = (bf16[160,128]{1,0:T(8,128)(2,1)S(1)}, bf16[160,128]{1,0:T(8,128)(2,1)S(1)}, u32[]{:S(2)}, u32[]{:S(2)}) collective-permute-start(bf16[160,128]{1,0:T(8,128)(2,1)S(1)} %fusion.7), channel_id=1, source_target_pairs={{0,256},{8,264},{16,272},{24,280},{32,288},{40,296},{48,304},{56,3... | collective-permute-start | bytes 122888 | tf_op jit(solution)/shard_map/ppermute | solution.py:35
  100.0 5.9 %collective-permute-start.12 = (bf16[160,128]{1,0:T(8,128)(2,1)S(1)}, bf16[160,128]{1,0:T(8,128)(2,1)S(1)}, u32[]{:S(2)}, u32[]{:S(2)}) collective-permute-start(bf16[160,128]{1,0:T(8,128)(2,1)S(1)} %fusion.7), channel_id=1, source_target_pairs={{0,128},{8,136},{16,144},{24,152},{32,160},{40,168},{48,176},{56,1... | collective-permute-start | bytes 122888 | tf_op jit(solution)/shard_map/ppermute | solution.py:35
  102.0 16.8 %collective-permute-start.16 = (bf16[384,512]{1,0:T(8,128)(2,1)}, bf16[384,512]{1,0:T(8,128)(2,1)S(1)}, u32[]{:S(2)}, u32[]{:S(2)}) collective-permute-start(bf16[384,512]{1,0:T(8,128)(2,1)} %copy-done.17), channel_id=1, source_target_pairs={{0,8},{8,16},{16,24},{24,32},{32,40},{40,48},{48,56},{56,64},{64,7... | collective-permute-start | bytes 1179656 | tf_op jit(solution)/shard_map/ppermute | solution.py:35
  105.9 21.8 %collective-permute-start.15 = (bf16[160,128]{1,0:T(8,128)(2,1)S(1)}, bf16[160,128]{1,0:T(8,128)(2,1)S(1)}, u32[]{:S(2)}, u32[]{:S(2)}) collective-permute-start(bf16[160,128]{1,0:T(8,128)(2,1)S(1)} %get-tuple-element.51), channel_id=1, source_target_pairs={{0,8},{8,0},{16,24},{24,16},{32,40},{40,32},{48,56},{56,48},{64,72... | collective-permute-start | bytes 122888 | tf_op jit(solution)/shard_map/ppermute | solution.py:35
  118.8 1.0 copy-start.3
  119.8 0.9 copy-start.10
  120.8 0.9 copy-start.11
  121.7 0.9 copy-start.13
  122.6 0.7 copy-start.14
  123.3 0.7 copy-start.16
  129.6 10.6 %collective-permute-start.19 = (bf16[64,2048]{1,0:T(8,128)(2,1)S(1)}, bf16[64,2048]{1,0:T(8,128)(2,1)S(1)}, u32[]{:S(2)}, u32[]{:S(2)}) collective-permute-start(bf16[64,2048]{1,0:T(8,128)(2,1)S(1)} %get-tuple-element.41), channel_id=1, source_target_pairs={{0,4},{8,12},{16,20},{24,28},{32,36},{40,44},{48,52},{56,60},{64,6... | collective-permute-start | bytes 786440 | tf_op jit(solution)/shard_map/ppermute | solution.py:35
  133.4 9.2 %collective-permute-start.18 = (bf16[64,2048]{1,0:T(8,128)(2,1)S(1)}, bf16[64,2048]{1,0:T(8,128)(2,1)S(1)}, u32[]{:S(2)}, u32[]{:S(2)}) collective-permute-start(bf16[64,2048]{1,0:T(8,128)(2,1)S(1)} %get-tuple-element.40), channel_id=1, source_target_pairs={{0,6},{8,14},{16,22},{24,30},{32,38},{40,46},{48,54},{56,62},{64,7... | collective-permute-start | bytes 786440 | tf_op jit(solution)/shard_map/ppermute | solution.py:35
  138.3 9.5 %collective-permute-start.17 = (bf16[64,2048]{1,0:T(8,128)(2,1)S(1)}, bf16[64,2048]{1,0:T(8,128)(2,1)S(1)}, u32[]{:S(2)}, u32[]{:S(2)}) collective-permute-start(bf16[64,2048]{1,0:T(8,128)(2,1)S(1)} %get-tuple-element.39), channel_id=1, source_target_pairs={{0,2},{8,10},{16,18},{24,26},{32,34},{40,42},{48,50},{56,58},{64,6... | collective-permute-start | bytes 786440 | tf_op jit(solution)/shard_map/ppermute | solution.py:35
  147.9 30.2 %collective-permute-start.23 = (bf16[64,2048]{1,0:T(8,128)(2,1)S(1)}, bf16[64,2048]{1,0:T(8,128)(2,1)S(1)}, u32[]{:S(2)}, u32[]{:S(2)}) collective-permute-start(bf16[64,2048]{1,0:T(8,128)(2,1)S(1)} %add_convert_fusion.1), channel_id=1, source_target_pairs={{0,1},{8,9},{16,17},{24,25},{32,33},{40,41},{48,49},{56,57},{64,65... | collective-permute-start | bytes 786440 | tf_op jit(solution)/shard_map/ppermute | solution.py:35
  164.1 14.1 %collective-permute-start.22 = (bf16[64,2048]{1,0:T(8,128)(2,1)S(1)}, bf16[64,2048]{1,0:T(8,128)(2,1)S(1)}, u32[]{:S(2)}, u32[]{:S(2)}) collective-permute-start(bf16[64,2048]{1,0:T(8,128)(2,1)S(1)} %get-tuple-element.49), channel_id=1, source_target_pairs={{0,4},{8,12},{16,20},{24,28},{32,36},{40,44},{48,52},{56,60},{64,6... | collective-permute-start | bytes 786440 | tf_op jit(solution)/shard_map/ppermute | solution.py:35
  166.0 12.1 %collective-permute-start.21 = (bf16[64,2048]{1,0:T(8,128)(2,1)S(1)}, bf16[64,2048]{1,0:T(8,128)(2,1)S(1)}, u32[]{:S(2)}, u32[]{:S(2)}) collective-permute-start(bf16[64,2048]{1,0:T(8,128)(2,1)S(1)} %get-tuple-element.48), channel_id=1, source_target_pairs={{0,6},{8,14},{16,22},{24,30},{32,38},{40,46},{48,54},{56,62},{64,7... | collective-permute-start | bytes 786440 | tf_op jit(solution)/shard_map/ppermute | solution.py:35
  168.1 10.1 %collective-permute-start.20 = (bf16[64,2048]{1,0:T(8,128)(2,1)S(1)}, bf16[64,2048]{1,0:T(8,128)(2,1)S(1)}, u32[]{:S(2)}, u32[]{:S(2)}) collective-permute-start(bf16[64,2048]{1,0:T(8,128)(2,1)S(1)} %get-tuple-element.47), channel_id=1, source_target_pairs={{0,2},{8,10},{16,18},{24,26},{32,34},{40,42},{48,50},{56,58},{64,6... | collective-permute-start | bytes 786440 | tf_op jit(solution)/shard_map/ppermute | solution.py:35

commit v3 on v2

--- a/solution.py
+++ b/solution.py
@@ -69,8 +69,7 @@
 
 def feature_maps(feat_dim, heads):
     width = heads * 2 * feat_dim
-    tables = np.zeros((heads, 4, ROWS, width), np.float32)
-    ones = np.zeros((4, ROWS), np.float32)
+    tables = np.zeros((heads, 4, ROWS, 2 * width), np.float32)
     at = 0
     for i in range(feat_dim):
         for j in range(i, feat_dim):
@@ -86,10 +85,10 @@
             query, key = head * 2 * feat_dim, (head * 2 + 1) * feat_dim
             tables[head, 0, at, query + i] = 0.25
             tables[head, 2, at, key + i] = 1.0
-        ones[1, at] = ones[3, at] = 1.0
+        tables[:, 1::2, at, width] = 1.0
         at += 1
-    ones[:, at] = 1.0
-    return tables, ones
+    tables[:, :, at, width] = 1.0
+    return tables
 
 
 def dot(a, b):
@@ -109,19 +108,27 @@
     return high, (v - high.astype(f32)).astype(bf16)
 
 
-def project_kernel(where, *refs):
+def position():
+    seq, tp = lax.axis_index("seq"), lax.axis_index("tp")
+    return lax.div(tp, 2), lax.rem(tp, 2), lax.rem(seq, 2), seq
+
+
+def project_kernel(*refs):
     parts = refs[:N_TP]
-    wf, ww, table, ones, feats_ref, qn_ref, kv_ref, tail_ref, mine_ref, other_ref = refs[N_TP:]
-    core = where[N_TP]
+    wf, ww, table, feats_ref, qn_ref, kv_ref, tail_ref, mine_ref, other_ref = refs[N_TP:]
+    x, half, core, _ = position()
+    owners = [lax.rem(x + NX - s, NX) * 2 + side for side in (half, 1 - half) for s in (0, 1, 3, 2)]
     width = parts[0].shape[1]
     head = ww.shape[2] // 3
     tokens = jnp.concatenate([p[...] for p in parts], axis=1)
-    rows = [pl.ds(pl.multiple_of(where[k] * width, width), width) for k in range(N_TP)]
+    rows = [pl.ds(pl.multiple_of(owner * width, width), width) for owner in owners]
 
     def columns(pick):
         return dot(tokens, jnp.concatenate([pick(r) for r in rows], axis=0)).astype(bf16)
 
     feats = columns(lambda r: wf[r, :])
+    ones = lax.broadcasted_iota(jnp.int32, feats.shape, 1) == 0
+    feats = jnp.concatenate([feats, jnp.where(ones, 1.0, 0.0).astype(bf16)], axis=1)
     feats_ref[...] = feats
     first_tail = kv_ref.shape[0] - tail_ref.shape[0]
     states = []
@@ -133,8 +140,8 @@
             kv_ref[:, 2 * head :] = out
             tail_ref[:, 2 * head :] = out[first_tail:]
             for h in range(2):
-                left = dot_t(table[h, 2], feats) + ones[2]
-                right = dot_t(table[h, 3], feats) + ones[3]
+                left = dot_t(table[h, 2], feats)
+                right = dot_t(table[h, 3], feats)
                 high, low = halves(left * right)
                 v = out[:, h * head : (h + 1) * head]
                 states.append(dot(high, v) + dot(low, v))
@@ -151,15 +158,15 @@
                 qn_ref[:, cols] = normed
 
 
-def local_kernel(where, win, feats_ref, qn_ref, kv_ref, halo_ref, table, ones, near_ref, win_ref, high_ref, low_ref):
-    seq = where[0]
+def local_kernel(win, feats_ref, qn_ref, kv_ref, halo_ref, table, near_ref, win_ref, high_ref, low_ref):
+    seq = position()[3]
     rows = qn_ref.shape[0]
     heads = win_ref.shape[1] // 128
     head = 128
     halo = halo_ref.shape[0]
     span = halo + BLOCK
     feats = feats_ref[...]
-    feat = feats.shape[1] // (2 * heads)
+    feat = feats.shape[1] // (4 * heads)
     blocks = rows // BLOCK
     row = lax.broadcasted_iota(jnp.int32, (BLOCK, span), 0)
     col = lax.broadcasted_iota(jnp.int32, (BLOCK, span), 1)
@@ -167,8 +174,8 @@
     for h in range(heads):
         cols = slice(h * head, (h + 1) * head)
         vcols = slice((heads + h) * head, (heads + h + 1) * head)
-        left = dot_t(feats, table[h, 0]) + ones[0:1]
-        right = dot_t(feats, table[h, 1]) + ones[1:2]
+        left = dot_t(feats, table[h, 0])
+        right = dot_t(feats, table[h, 1])
         high, low = halves(left * right)
         high_ref[h] = high
         low_ref[h] = low
@@ -194,9 +201,9 @@
             win_ref[at, cols] = unit(dot(weights, values[b * BLOCK : b * BLOCK + span]))
 
 
-def output_kernel(where, ours, theirs, near_ref, win_ref, high_ref, low_ref, w_ref, *refs):
+def output_kernel(ours, theirs, near_ref, win_ref, high_ref, low_ref, w_ref, *refs):
     outs, hidden = refs[:-1], refs[-1]
-    core, x, half = where[0], where[1], where[2]
+    x, half, core, _ = position()
     mine, other = ours[...], theirs[...].astype(f32)
     head = mine.shape[1]
     rows = hidden.shape[1]
@@ -217,53 +224,53 @@
             outs[(1 - away) * NX + s][...] = product[s * rows : (s + 1) * rows]
 
 
-def prefix(mine, other, place):
+def prefix(mine, other, place, beside):
     x, h, y, z, c = place
     got = send(other, to_core).astype(f32)
     total = mine + got
-    short = total.astype(bf16)
-    quad = [send(short, to_z(flip)).astype(f32) for flip in (1, 2, 3)]
     before = jnp.zeros_like(total)
-    for flip, part in zip((1, 2, 3), quad):
+    done = None
+    for flip in (1, 2, 4):
+        part = send(total.astype(bf16), to_z(flip)).astype(f32)
         before = before + jnp.where((z ^ flip) < z, part, 0.0)
         total = total + part
-    part = send(total.astype(bf16), to_z(4)).astype(f32)
-    before = before + jnp.where((z ^ 4) < z, part, 0.0)
-    total = total + part
+        if flip == 1:
+            done = beside(total)
+    total, done = lax.optimization_barrier((total, done))
     short = total.astype(bf16)
     for steps in (1, 2, 3):
         before = before + send(short, to_y(steps)).astype(f32)
     theirs = send((before + jnp.where(c == 0, mine, 0.0)).astype(bf16), to_core)
     ours = before + jnp.where(c == 1, got, 0.0)
-    return ours, theirs
+    return ours, theirs, done
 
 
 def shape(dims, kind):
     return jax.ShapeDtypeStruct(dims, kind)
 
 
-def project(where, parts, wf, ww, tables, ones):
+def project(parts, wf, ww, tables):
     tok_rows = parts[0].shape[0]
     wide = 2 * ww.shape[2] // 3
     halo_rows = (WMAX - 1) * BLOCK
     return pl.pallas_call(
         project_kernel,
         out_shape=(
-            shape((tok_rows, wf.shape[1]), bf16),
+            shape((tok_rows, 2 * wf.shape[1]), bf16),
             shape((tok_rows, wide), bf16),
             shape((tok_rows, 2 * wide), bf16),
             shape((halo_rows, 2 * wide), bf16),
             shape((ROWS, wide // 2), f32),
             shape((ROWS, wide // 2), bf16),
         ),
-        in_specs=[SMEM] + [VMEM] * (N_TP + 4),
+        in_specs=[VMEM] * (N_TP + 3),
         out_specs=(VMEM,) * 6,
         name="project",
         compiler_params=pltpu.CompilerParams(vmem_limit_bytes=LIMIT),
-    )(where, *parts, wf, ww, tables.astype(bf16), ones[:, :, None])
-
-
-def near(where, win_blocks, feats, qn, kv, halo, tables, ones):
+    )(*parts, wf, ww, tables.astype(bf16))
+
+
+def near(win_blocks, feats, qn, kv, halo, tables):
     tok_rows, wide = qn.shape
     return pl.pallas_call(
         local_kernel,
@@ -273,27 +280,27 @@
             shape((2, tok_rows, ROWS), bf16),
             shape((2, tok_rows, ROWS), bf16),
         ),
-        in_specs=[SMEM, SMEM] + [VMEM] * 6,
+        in_specs=[SMEM] + [VMEM] * 5,
         out_specs=(VMEM,) * 4,
         name="near",
         compiler_params=pltpu.CompilerParams(vmem_limit_bytes=LIMIT),
-    )(where, win_blocks, feats, qn, kv, halo, tables.astype(bf16), ones)
-
-
-def output(where, ours, theirs, near_out, win_out, high, low, w_out):
+    )(win_blocks, feats, qn, kv, halo, tables.astype(bf16))
+
+
+def output(ours, theirs, near_out, win_out, high, low, w_out):
     rows = near_out.shape[0] // N_TP
     return pl.pallas_call(
         output_kernel,
         out_shape=(shape((rows, w_out.shape[1]), bf16),) * N_TP,
-        in_specs=[SMEM] + [VMEM] * 7,
+        in_specs=[VMEM] * 7,
         out_specs=(VMEM,) * N_TP,
         scratch_shapes=[pltpu.VMEM((N_TP, rows, w_out.shape[0]), bf16)],
         name="output",
         compiler_params=pltpu.CompilerParams(vmem_limit_bytes=LIMIT),
-    )(where, ours, theirs, near_out, win_out, high, low, w_out)
-
-
-LIMIT = 40 * 2**20
+    )(ours, theirs, near_out, win_out, high, low, w_out)
+
+
+LIMIT = 16 * 2**20
 
 
 def local(tokens, w_feature, w_window, w_out, win_blocks):
@@ -305,23 +312,17 @@
     other = send(tokens, to_half)
     parts = [tokens] + [send(tokens, to_x(s)) for s in (1, 3, 2)]
     parts += [other] + [send(other, to_x(s)) for s in (1, 3, 2)]
-    owners = [(x + NX - s) % NX * 2 + half for half in (h, 1 - h) for s in (0, 1, 3, 2)]
-    tables, ones = feature_maps(feat_dim, head_count)
-
+    tables = feature_maps(feat_dim, head_count)
     feats, qn, kv, tail, mine, theirs = project(
-        jnp.stack(owners + [c]).astype(jnp.int32),
-        parts,
-        w_feature.reshape(model_width, -1),
-        w_window.transpose(1, 0, 2),
-        tables,
-        ones,
+        parts, w_feature.reshape(model_width, -1), w_window.transpose(1, 0, 2), tables
     )
-    ours, theirs = prefix(mine, theirs, (x, h, y, z, c))
-    halo = send(tail, to_next)
-    near_out, win_out, high, low = near(seq[None], win_blocks, feats, qn, kv, halo, tables[:, :2], ones[:2])
-    products = output(
-        jnp.stack([c, x, h]), ours, theirs, near_out, win_out, high, low, w_out.reshape(-1, model_width)
-    )
+
+    def beside(total):
+        halo, _ = lax.optimization_barrier((send(tail, to_next), total))
+        return near(win_blocks, feats, qn, kv, halo, tables[:, :2])
+
+    ours, theirs, attended = prefix(mine, theirs, (x, h, y, z, c), beside)
+    products = output(ours, theirs, *attended, w_out.reshape(-1, model_width))
 
     def summed(group):
         total = group[0].astype(f32)

time: 180 us -> 177 us (0.983)
  the two profiles are of different devices: /device:TPU:8 before, /device:TPU:57 now
where the time goes in v3:
time: 177 us; the launch traced here: 176 us
  starting transfers between devices  94.3 us (53%)
  waiting for transfers between devices  62.9 us (36%)
  Pallas kernels  9.61 us (5%)
  local copies, waits for them, and re-layouts  7.89 us (4%)
    ppermute x23, starting transfers between devices, send(): return lax.ppermute(value, ('seq', 'tp'), pairs(move))  94.3 us
    ppermute x23, waiting for transfers between devices, send(): return lax.ppermute(value, ('seq', 'tp'), pairs(move))  62.9 us
    unnamed x17, local copies, waits for them, and re-layouts  5.95 us
    pallas_call x1, Pallas kernels, project(): pl.pallas_call(project_kernel, out_shape=(shape((tok_rows, 2 * wf.shape[1...  4.5 us
    pallas_call x1, Pallas kernels, near(): pl.pallas_call(local_kernel, out_shape=(shape((tok_rows, wide), f32), sha...  3.77 us
  transfers between devices with their start and end apart: 23, of which 13 were waited for; matrix products, arithmetic and copies ran while one was open for 2% of the time, Pallas kernels for 0%

profile of v3, /device:TPU:57, one launch (start us, length us, event | category | flops | bytes accessed | tf_op | source)
XLA Modules:
  0.0 176.2 jit_solution(5962604563909348895)
XLA Ops:
  0.0 14.7 %collective-permute-start.3 = (bf16[512,256]{1,0:T(8,128)(2,1)}, bf16[512,256]{1,0:T(8,128)(2,1)}, u32[]{:S(2)}, u32[]{:S(2)}) collective-permute-start(bf16[512,256]{1,0:T(8,128)(2,1)} %refs_0_.1), channel_id=1, source_target_pairs={{0,1},{8,9},{16,17},{24,25},{32,33},{40,41},{48,49},{56,57},{64,65... | collective-permute-start | bytes 786440 | tf_op jit(solution)/shard_map/ppermute | solution.py:35
  14.7 3.1 %collective-permute-start = (bf16[512,256]{1,0:T(8,128)(2,1)}, bf16[512,256]{1,0:T(8,128)(2,1)S(1)}, u32[]{:S(2)}, u32[]{:S(2)}) collective-permute-start(bf16[512,256]{1,0:T(8,128)(2,1)} %refs_0_.1), channel_id=1, source_target_pairs={{0,2},{8,10},{16,18},{24,26},{32,34},{40,42},{48,50},{56,58},{64,6... | collective-permute-start | bytes 786440 | tf_op jit(solution)/shard_map/ppermute | solution.py:35
  17.8 3.4 %collective-permute-start.1 = (bf16[512,256]{1,0:T(8,128)(2,1)}, bf16[512,256]{1,0:T(8,128)(2,1)}, u32[]{:S(2)}, u32[]{:S(2)}) collective-permute-start(bf16[512,256]{1,0:T(8,128)(2,1)} %refs_0_.1), channel_id=1, source_target_pairs={{0,6},{8,14},{16,22},{24,30},{32,38},{40,46},{48,54},{56,62},{64,7... | collective-permute-start | bytes 786440 | tf_op jit(solution)/shard_map/ppermute | solution.py:35
  21.2 3.4 %collective-permute-start.2 = (bf16[512,256]{1,0:T(8,128)(2,1)}, bf16[512,256]{1,0:T(8,128)(2,1)}, u32[]{:S(2)}, u32[]{:S(2)}) collective-permute-start(bf16[512,256]{1,0:T(8,128)(2,1)} %refs_0_.1), channel_id=1, source_target_pairs={{0,4},{8,12},{16,20},{24,28},{32,36},{40,44},{48,52},{56,60},{64,6... | collective-permute-start | bytes 786440 | tf_op jit(solution)/shard_map/ppermute | solution.py:35
  24.6 13.2 %collective-permute-done.3.refs_4_ = bf16[512,256]{1,0:T(8,128)(2,1)} collective-permute-done((bf16[512,256]{1,0:T(8,128)(2,1)}, bf16[512,256]{1,0:T(8,128)(2,1)}, u32[]{:S(2)}, u32[]{:S(2)}) %collective-permute-start.3) | collective-permute-done | bytes 262176 | tf_op jit(solution)/shard_map/ppermute | solution.py:35
  37.9 3.1 %collective-permute-start.4 = (bf16[512,256]{1,0:T(8,128)(2,1)}, bf16[512,256]{1,0:T(8,128)(2,1)}, u32[]{:S(2)}, u32[]{:S(2)}) collective-permute-start(bf16[512,256]{1,0:T(8,128)(2,1)} %collective-permute-done.3.refs_4_), channel_id=1, source_target_pairs={{0,2},{8,10},{16,18},{24,26},{32,34},{40,42},{48,50},{56,58},{64,6... | collective-permute-start | bytes 786440 | tf_op jit(solution)/shard_map/ppermute | solution.py:35
  41.0 3.4 %collective-permute-start.5 = (bf16[512,256]{1,0:T(8,128)(2,1)}, bf16[512,256]{1,0:T(8,128)(2,1)}, u32[]{:S(2)}, u32[]{:S(2)}) collective-permute-start(bf16[512,256]{1,0:T(8,128)(2,1)} %collective-permute-done.3.refs_4_), channel_id=1, source_target_pairs={{0,6},{8,14},{16,22},{24,30},{32,38},{40,46},{48,54},{56,62},{64,7... | collective-permute-start | bytes 786440 | tf_op jit(solution)/shard_map/ppermute | solution.py:35
  44.4 0.0 collective-permute-done.refs_1_
  44.4 0.0 copy-start.4
  44.4 0.7 copy-done.4
  45.1 3.4 %collective-permute-start.6 = (bf16[512,256]{1,0:T(8,128)(2,1)}, bf16[512,256]{1,0:T(8,128)(2,1)}, u32[]{:S(2)}, u32[]{:S(2)}) collective-permute-start(bf16[512,256]{1,0:T(8,128)(2,1)} %collective-permute-done.3.refs_4_), channel_id=1, source_target_pairs={{0,4},{8,12},{16,20},{24,28},{32,36},{40,44},{48,52},{56,60},{64,6... | collective-permute-start | bytes 786440 | tf_op jit(solution)/shard_map/ppermute | solution.py:35
  48.5 2.3 %copy.13 = bf16[2048,2,384]{2,0,1:T(8,128)(2,1)S(1)} copy(bf16[2048,2,384]{2,1,0:T(2,128)(2,1)} %param.9) | data formatting | bytes 6291456 | tf_op args[2]
  50.8 1.9 %copy.11.refs_8_ = bf16[2048,64]{1,0:T(8,128)(2,1)} copy(bf16[2048,64]{0,1:T(8,128)(2,1)} %bitcast.7) | data formatting | bytes 524288 | tf_op jit(solution)/shard_map/reshape | solution.py:317
  52.8 0.0 collective-permute-done.1.refs_2_
  52.8 0.0 collective-permute-done.2.refs_3_
  52.8 0.0 collective-permute-done.4.refs_5_
  52.8 0.0 collective-permute-done.5.refs_6_
  52.8 1.8 %collective-permute-done.6.refs_7_ = bf16[512,256]{1,0:T(8,128)(2,1)} collective-permute-done((bf16[512,256]{1,0:T(8,128)(2,1)}, bf16[512,256]{1,0:T(8,128)(2,1)}, u32[]{:S(2)}, u32[]{:S(2)}) %collective-permute-start.6) | collective-permute-done | bytes 262176 | tf_op jit(solution)/shard_map/ppermute | solution.py:35
  54.6 0.0 copy-done.2
  54.6 1.0 copy-done
  55.7 0.9 copy-done.3
  56.6 0.9 copy-done.5
  57.6 4.5 %project.1 = (bf16[512,128]{1,0:T(8,128)(2,1)S(1)}, bf16[512,256]{1,0:T(8,128)(2,1)S(1)}, bf16[512,512]{1,0:T(8,128)(2,1)S(1)}, bf16[384,512]{1,0:T(8,128)(2,1)S...) custom-call(bf16[512,256]{1,0:T(8,128)(2,1)S(1)} %copy-done.3, bf16[512,256]{1,0:T(8,128)(2,1)S(1)} %copy-done.5, ...), custom_call_target="tpu_custom_call" | custom-call | tf_op jit(solution)/shard_map/project/pallas_call | solution.py:256
  62.1 0.0 copy-start.1
  62.1 5.0 %collective-permute-start.7 = (bf16[160,128]{1,0:T(8,128)(2,1)S(1)}, bf16[160,128]{1,0:T(8,128)(2,1)S(1)}, u32[]{:S(2)}, u32[]{:S(2)}) collective-permute-start(bf16[160,128]{1,0:T(8,128)(2,1)S(1)} %get-tuple-element.35), channel_id=1, source_target_pairs={{0,8},{8,0},{16,24},{24,16},{32,40},{40,32},{48,56},{56,48},{64,72... | collective-permute-start | bytes 122888 | tf_op jit(solution)/shard_map/ppermute | solution.py:35
  67.1 0.8 collective-permute-done.7
  67.9 1.9 %collective-permute-start.8 = (bf16[160,128]{1,0:T(8,128)(2,1)S(1)}, bf16[160,128]{1,0:T(8,128)(2,1)S(1)}, u32[]{:S(2)}, u32[]{:S(2)}) collective-permute-start(bf16[160,128]{1,0:T(8,128)(2,1)S(1)} %fusion.6), channel_id=1, source_target_pairs={{0,16},{8,24},{16,0},{24,8},{32,48},{40,56},{48,32},{56,40},{64,80... | collective-permute-start | bytes 122888 | tf_op jit(solution)/shard_map/ppermute | solution.py:35
  69.9 2.8 %collective-permute-done.8 = bf16[160,128]{1,0:T(8,128)(2,1)S(1)} collective-permute-done((bf16[160,128]{1,0:T(8,128)(2,1)S(1)}, bf16[160,128]{1,0:T(8,128)(2,1)S(1)}, u32[]{:S(2)}, u32[]{:S(2)}) %collective-permute-start.8) | collective-permute-done | bytes 40992 | tf_op jit(solution)/shard_map/ppermute | solution.py:35
  72.7 1.9 %collective-permute-start.9 = (bf16[160,128]{1,0:T(8,128)(2,1)S(1)}, bf16[160,128]{1,0:T(8,128)(2,1)S(1)}, u32[]{:S(2)}, u32[]{:S(2)}) collective-permute-start(bf16[160,128]{1,0:T(8,128)(2,1)S(1)} %get-tuple-element.65), channel_id=1, source_target_pairs={{0,32},{8,40},{16,48},{24,56},{32,0},{40,8},{48,16},{56,24},{64,96... | collective-permute-start | bytes 122888 | tf_op jit(solution)/shard_map/ppermute | solution.py:35
  74.6 4.5 %collective-permute-start.11 = (bf16[384,512]{1,0:T(8,128)(2,1)S(1)}, bf16[384,512]{1,0:T(8,128)(2,1)S(1)}, u32[]{:S(2)}, u32[]{:S(2)}) collective-permute-start(bf16[384,512]{1,0:T(8,128)(2,1)S(1)} %get-tuple-element.39), channel_id=1, source_target_pairs={{0,8},{8,16},{16,24},{24,32},{32,40},{40,48},{48,56},{56,64},{64,7... | collective-permute-start | bytes 1179656 | tf_op jit(solution)/shard_map/ppermute | solution.py:35
  79.1 0.0 collective-permute-done.9
  79.2 6.6 %collective-permute-start.10 = (bf16[160,128]{1,0:T(8,128)(2,1)S(1)}, bf16[160,128]{1,0:T(8,128)(2,1)S(1)}, u32[]{:S(2)}, u32[]{:S(2)}) collective-permute-start(bf16[160,128]{1,0:T(8,128)(2,1)S(1)} %fusion.7), channel_id=1, source_target_pairs={{0,64},{8,72},{16,80},{24,88},{32,96},{40,104},{48,112},{56,120},{... | collective-permute-start | bytes 122888 | tf_op jit(solution)/shard_map/ppermute | solution.py:35
  85.7 2.1 %collective-permute-done.10 = bf16[160,128]{1,0:T(8,128)(2,1)S(1)} collective-permute-done((bf16[160,128]{1,0:T(8,128)(2,1)S(1)}, bf16[160,128]{1,0:T(8,128)(2,1)S(1)}, u32[]{:S(2)}, u32[]{:S(2)}) %collective-permute-start.10) | collective-permute-done | bytes 40992 | tf_op jit(solution)/shard_map/ppermute | solution.py:35
  87.8 0.0 collective-permute-done.11.halo_ref
  87.8 0.0 copy-done.6
  87.9 0.0 copy-done.7
  87.9 3.8 %near.1 = (f32[512,256]{1,0:T(8,128)S(1)}, f32[512,256]{1,0:T(8,128)S(1)}, bf16[2,512,160]{2,1,0:T(8,128)(2,1)S(1)}, bf16[2,512,160]{2,1,0:T(8,128)(2,1)S(1)}) custom-call(s32[2]{0:T(128)S(1)} %copy-done.7, bf16[512,128]{1,0:T(8,128)(2,1)S(1)} %get-tuple-element.36.feats_ref, bf16[512,256]{1,0:T(8,128)(2,1)S(1)} %get-tuple-element.37.qn_ref, ...), custom_call_target="tpu_custom_call" | custom-call | tf_op jit(solution)/shard_map/near/pallas_call | solution.py:275
  91.6 1.3 collective-permute-start.12
  92.9 1.3 collective-permute-start.13
  94.2 1.3 collective-permute-start.14
  95.6 5.3 %collective-permute-done.12 = bf16[160,128]{1,0:T(8,128)(2,1)S(1)} collective-permute-done((bf16[160,128]{1,0:T(8,128)(2,1)S(1)}, bf16[160,128]{1,0:T(8,128)(2,1)S(1)}, u32[]{:S(2)}, u32[]{:S(2)}) %collective-permute-start.12) | collective-permute-done | bytes 40992 | tf_op jit(solution)/shard_map/ppermute | solution.py:35
  100.9 3.1 %collective-permute-done.13 = bf16[160,128]{1,0:T(8,128)(2,1)S(1)} collective-permute-done((bf16[160,128]{1,0:T(8,128)(2,1)S(1)}, bf16[160,128]{1,0:T(8,128)(2,1)S(1)}, u32[]{:S(2)}, u32[]{:S(2)}) %collective-permute-start.13) | collective-permute-done | bytes 40992 | tf_op jit(solution)/shard_map/ppermute | solution.py:35
  104.0 2.5 %collective-permute-done.14 = bf16[160,128]{1,0:T(8,128)(2,1)S(1)} collective-permute-done((bf16[160,128]{1,0:T(8,128)(2,1)S(1)}, bf16[160,128]{1,0:T(8,128)(2,1)S(1)}, u32[]{:S(2)}, u32[]{:S(2)}) %collective-permute-start.14) | collective-permute-done | bytes 40992 | tf_op jit(solution)/shard_map/ppermute | solution.py:35
  106.5 0.1 add_convert_fusion.2
  106.5 3.6 %collective-permute-start.15 = (bf16[160,128]{1,0:T(8,128)(2,1)S(1)}, bf16[160,128]{1,0:T(8,128)(2,1)S(1)}, u32[]{:S(2)}, u32[]{:S(2)}) collective-permute-start(bf16[160,128]{1,0:T(8,128)(2,1)S(1)} %get-tuple-element.63), channel_id=1, source_target_pairs={{0,8},{8,0},{16,24},{24,16},{32,40},{40,32},{48,56},{56,48},{64,72... | collective-permute-start | bytes 122888 | tf_op jit(solution)/shard_map/ppermute | solution.py:35
  110.2 0.8 collective-permute-done.15.theirs
  111.0 0.0 copy-done.1
  111.0 1.3 output.1
  112.4 3.8 %collective-permute-start.16 = (bf16[64,2048]{1,0:T(8,128)(2,1)S(1)}, bf16[64,2048]{1,0:T(8,128)(2,1)S(1)}, u32[]{:S(2)}, u32[]{:S(2)}) collective-permute-start(bf16[64,2048]{1,0:T(8,128)(2,1)S(1)} %get-tuple-element.51), channel_id=1, source_target_pairs={{0,2},{8,10},{16,18},{24,26},{32,34},{40,42},{48,50},{56,58},{64,6... | collective-permute-start | bytes 786440 | tf_op jit(solution)/shard_map/ppermute | solution.py:35
  116.1 2.8 %collective-permute-start.17 = (bf16[64,2048]{1,0:T(8,128)(2,1)S(1)}, bf16[64,2048]{1,0:T(8,128)(2,1)S(1)}, u32[]{:S(2)}, u32[]{:S(2)}) collective-permute-start(bf16[64,2048]{1,0:T(8,128)(2,1)S(1)} %get-tuple-element.52), channel_id=1, source_target_pairs={{0,6},{8,14},{16,22},{24,30},{32,38},{40,46},{48,54},{56,62},{64,7... | collective-permute-start | bytes 786440 | tf_op jit(solution)/shard_map/ppermute | solution.py:35
  118.9 3.1 %collective-permute-start.18 = (bf16[64,2048]{1,0:T(8,128)(2,1)S(1)}, bf16[64,2048]{1,0:T(8,128)(2,1)S(1)}, u32[]{:S(2)}, u32[]{:S(2)}) collective-permute-start(bf16[64,2048]{1,0:T(8,128)(2,1)S(1)} %get-tuple-element.53), channel_id=1, source_target_pairs={{0,4},{8,12},{16,20},{24,28},{32,36},{40,44},{48,52},{56,60},{64,6... | collective-permute-start | bytes 786440 | tf_op jit(solution)/shard_map/ppermute | solution.py:35
  122.0 1.1 collective-permute-done.16
  123.1 2.2 %collective-permute-done.17 = bf16[64,2048]{1,0:T(8,128)(2,1)S(1)} collective-permute-done((bf16[64,2048]{1,0:T(8,128)(2,1)S(1)}, bf16[64,2048]{1,0:T(8,128)(2,1)S(1)}, u32[]{:S(2)}, u32[]{:S(2)}) %collective-permute-start.17) | collective-permute-done | bytes 262176 | tf_op jit(solution)/shard_map/ppermute | solution.py:35
  125.2 4.0 %collective-permute-done.18 = bf16[64,2048]{1,0:T(8,128)(2,1)S(1)} collective-permute-done((bf16[64,2048]{1,0:T(8,128)(2,1)S(1)}, bf16[64,2048]{1,0:T(8,128)(2,1)S(1)}, u32[]{:S(2)}, u32[]{:S(2)}) %collective-permute-start.18) | collective-permute-done | bytes 262176 | tf_op jit(solution)/shard_map/ppermute | solution.py:35
  129.3 0.1 add_convert_fusion.1
  129.4 4.9 %collective-permute-start.19 = (bf16[64,2048]{1,0:T(8,128)(2,1)S(1)}, bf16[64,2048]{1,0:T(8,128)(2,1)S(1)}, u32[]{:S(2)}, u32[]{:S(2)}) collective-permute-start(bf16[64,2048]{1,0:T(8,128)(2,1)S(1)} %get-tuple-element.59), channel_id=1, source_target_pairs={{0,2},{8,10},{16,18},{24,26},{32,34},{40,42},{48,50},{56,58},{64,6... | collective-permute-start | bytes 786440 | tf_op jit(solution)/shard_map/ppermute | solution.py:35
  134.3 2.9 %collective-permute-start.20 = (bf16[64,2048]{1,0:T(8,128)(2,1)S(1)}, bf16[64,2048]{1,0:T(8,128)(2,1)S(1)}, u32[]{:S(2)}, u32[]{:S(2)}) collective-permute-start(bf16[64,2048]{1,0:T(8,128)(2,1)S(1)} %get-tuple-element.60), channel_id=1, source_target_pairs={{0,6},{8,14},{16,22},{24,30},{32,38},{40,46},{48,54},{56,62},{64,7... | collective-permute-start | bytes 786440 | tf_op jit(solution)/shard_map/ppermute | solution.py:35
  137.2 3.1 %collective-permute-start.21 = (bf16[64,2048]{1,0:T(8,128)(2,1)S(1)}, bf16[64,2048]{1,0:T(8,128)(2,1)S(1)}, u32[]{:S(2)}, u32[]{:S(2)}) collective-permute-start(bf16[64,2048]{1,0:T(8,128)(2,1)S(1)} %get-tuple-element.61), channel_id=1, source_target_pairs={{0,4},{8,12},{16,20},{24,28},{32,36},{40,44},{48,52},{56,60},{64,6... | collective-permute-start | bytes 786440 | tf_op jit(solution)/shard_map/ppermute | solution.py:35
  140.3 11.8 %collective-permute-start.22 = (bf16[64,2048]{1,0:T(8,128)(2,1)S(1)}, bf16[64,2048]{1,0:T(8,128)(2,1)S(1)}, u32[]{:S(2)}, u32[]{:S(2)}) collective-permute-start(bf16[64,2048]{1,0:T(8,128)(2,1)S(1)} %add_convert_fusion.1), channel_id=1, source_target_pairs={{0,1},{8,9},{16,17},{24,25},{32,33},{40,41},{48,49},{56,57},{64,65... | collective-permute-start | bytes 786440 | tf_op jit(solution)/shard_map/ppermute | solution.py:35
  152.2 0.0 collective-permute-done.19
  152.2 0.0 collective-permute-done.20
  152.2 0.0 collective-permute-done.21
  152.2 23.1 %collective-permute-done.22 = bf16[64,2048]{1,0:T(8,128)(2,1)S(1)} collective-permute-done((bf16[64,2048]{1,0:T(8,128)(2,1)S(1)}, bf16[64,2048]{1,0:T(8,128)(2,1)S(1)}, u32[]{:S(2)}, u32[]{:S(2)}) %collective-permute-start.22) | collective-permute-done | bytes 262176 | tf_op jit(solution)/shard_map/ppermute | solution.py:35
  175.4 0.9 add_convert_fusion
  (11 shorter events, 0.1 us)
Async XLA Ops:
  0.0 54.6 %copy-start.2 = (bf16[2,4,160,128]{3,2,1,0:T(8,128)(2,1)S(1)}, bf16[2,4,160,128]{3,2,1,0:T(8,128)(2,1)}, u32[]{:S(2)}) copy-start(bf16[2,4,160,128]{3,2,1,0:T(8,128)(2,1)} %constant.50.clone.refs_10_) | copy-start | bytes 983044
  0.0 37.9 %collective-permute-start.3 = (bf16[512,256]{1,0:T(8,128)(2,1)}, bf16[512,256]{1,0:T(8,128)(2,1)}, u32[]{:S(2)}, u32[]{:S(2)}) collective-permute-start(bf16[512,256]{1,0:T(8,128)(2,1)} %refs_0_.1), channel_id=1, source_target_pairs={{0,1},{8,9},{16,17},{24,25},{32,33},{40,41},{48,49},{56,57},{64,65... | collective-permute-start | bytes 786440 | tf_op jit(solution)/shard_map/ppermute | solution.py:35
  14.7 29.7 %collective-permute-start = (bf16[512,256]{1,0:T(8,128)(2,1)}, bf16[512,256]{1,0:T(8,128)(2,1)S(1)}, u32[]{:S(2)}, u32[]{:S(2)}) collective-permute-start(bf16[512,256]{1,0:T(8,128)(2,1)} %refs_0_.1), channel_id=1, source_target_pairs={{0,2},{8,10},{16,18},{24,26},{32,34},{40,42},{48,50},{56,58},{64,6... | collective-permute-start | bytes 786440 | tf_op jit(solution)/shard_map/ppermute | solution.py:35
  17.8 35.0 %collective-permute-start.1 = (bf16[512,256]{1,0:T(8,128)(2,1)}, bf16[512,256]{1,0:T(8,128)(2,1)}, u32[]{:S(2)}, u32[]{:S(2)}) collective-permute-start(bf16[512,256]{1,0:T(8,128)(2,1)} %refs_0_.1), channel_id=1, source_target_pairs={{0,6},{8,14},{16,22},{24,30},{32,38},{40,46},{48,54},{56,62},{64,7... | collective-permute-start | bytes 786440 | tf_op jit(solution)/shard_map/ppermute | solution.py:35
  21.2 31.6 %collective-permute-start.2 = (bf16[512,256]{1,0:T(8,128)(2,1)}, bf16[512,256]{1,0:T(8,128)(2,1)}, u32[]{:S(2)}, u32[]{:S(2)}) collective-permute-start(bf16[512,256]{1,0:T(8,128)(2,1)} %refs_0_.1), channel_id=1, source_target_pairs={{0,4},{8,12},{16,20},{24,28},{32,36},{40,44},{48,52},{56,60},{64,6... | collective-permute-start | bytes 786440 | tf_op jit(solution)/shard_map/ppermute | solution.py:35
  37.9 14.9 %collective-permute-start.4 = (bf16[512,256]{1,0:T(8,128)(2,1)}, bf16[512,256]{1,0:T(8,128)(2,1)}, u32[]{:S(2)}, u32[]{:S(2)}) collective-permute-start(bf16[512,256]{1,0:T(8,128)(2,1)} %collective-permute-done.3.refs_4_), channel_id=1, source_target_pairs={{0,2},{8,10},{16,18},{24,26},{32,34},{40,42},{48,50},{56,58},{64,6... | collective-permute-start | bytes 786440 | tf_op jit(solution)/shard_map/ppermute | solution.py:35
  41.0 11.8 %collective-permute-start.5 = (bf16[512,256]{1,0:T(8,128)(2,1)}, bf16[512,256]{1,0:T(8,128)(2,1)}, u32[]{:S(2)}, u32[]{:S(2)}) collective-permute-start(bf16[512,256]{1,0:T(8,128)(2,1)} %collective-permute-done.3.refs_4_), channel_id=1, source_target_pairs={{0,6},{8,14},{16,22},{24,30},{32,38},{40,46},{48,54},{56,62},{64,7... | collective-permute-start | bytes 786440 | tf_op jit(solution)/shard_map/ppermute | solution.py:35
  44.4 0.7 copy-start.4
  45.1 9.5 %collective-permute-start.6 = (bf16[512,256]{1,0:T(8,128)(2,1)}, bf16[512,256]{1,0:T(8,128)(2,1)}, u32[]{:S(2)}, u32[]{:S(2)}) collective-permute-start(bf16[512,256]{1,0:T(8,128)(2,1)} %collective-permute-done.3.refs_4_), channel_id=1, source_target_pairs={{0,4},{8,12},{16,20},{24,28},{32,36},{40,44},{48,52},{56,60},{64,6... | collective-permute-start | bytes 786440 | tf_op jit(solution)/shard_map/ppermute | solution.py:35
  54.6 1.0 copy-start
  55.7 0.9 copy-start.3
  56.6 0.9 copy-start.5
  57.6 30.3 %copy-start.6 = (bf16[2,2,160,128]{3,2,1,0:T(8,128)(2,1)S(1)}, bf16[2,2,160,128]{3,2,1,0:T(8,128)(2,1)}, u32[]{:S(2)}) copy-start(bf16[2,2,160,128]{3,2,1,0:T(8,128)(2,1)} %constant.51.clone.table) | copy-start | bytes 491524
  57.6 30.3 %copy-start.7 = (s32[2]{0:T(128)S(1)}, s32[2]{0:T(128)}, u32[]{:S(2)}) copy-start(s32[2]{0:T(128)} %win.1) | copy-start | bytes 28
  62.1 48.9 %copy-start.1 = (bf16[2,128,2048]{2,1,0:T(8,128)(2,1)S(1)}, bf16[2,128,2048]{2,1,0:T(8,128)(2,1)}, u32[]{:S(2)}) copy-start(bf16[2,128,2048]{2,1,0:T(8,128)(2,1)} %param.10) | copy-start | bytes 3145732
  62.1 5.8 %collective-permute-start.7 = (bf16[160,128]{1,0:T(8,128)(2,1)S(1)}, bf16[160,128]{1,0:T(8,128)(2,1)S(1)}, u32[]{:S(2)}, u32[]{:S(2)}) collective-permute-start(bf16[160,128]{1,0:T(8,128)(2,1)S(1)} %get-tuple-element.35), channel_id=1, source_target_pairs={{0,8},{8,0},{16,24},{24,16},{32,40},{40,32},{48,56},{56,48},{64,72... | collective-permute-start | bytes 122888 | tf_op jit(solution)/shard_map/ppermute | solution.py:35
  67.9 4.7 %collective-permute-start.8 = (bf16[160,128]{1,0:T(8,128)(2,1)S(1)}, bf16[160,128]{1,0:T(8,128)(2,1)S(1)}, u32[]{:S(2)}, u32[]{:S(2)}) collective-permute-start(bf16[160,128]{1,0:T(8,128)(2,1)S(1)} %fusion.6), channel_id=1, source_target_pairs={{0,16},{8,24},{16,0},{24,8},{32,48},{40,56},{48,32},{56,40},{64,80... | collective-permute-start | bytes 122888 | tf_op jit(solution)/shard_map/ppermute | solution.py:35
  72.7 6.4 %collective-permute-start.9 = (bf16[160,128]{1,0:T(8,128)(2,1)S(1)}, bf16[160,128]{1,0:T(8,128)(2,1)S(1)}, u32[]{:S(2)}, u32[]{:S(2)}) collective-permute-start(bf16[160,128]{1,0:T(8,128)(2,1)S(1)} %get-tuple-element.65), channel_id=1, source_target_pairs={{0,32},{8,40},{16,48},{24,56},{32,0},{40,8},{48,16},{56,24},{64,96... | collective-permute-start | bytes 122888 | tf_op jit(solution)/shard_map/ppermute | solution.py:35
  74.6 13.2 %collective-permute-start.11 = (bf16[384,512]{1,0:T(8,128)(2,1)S(1)}, bf16[384,512]{1,0:T(8,128)(2,1)S(1)}, u32[]{:S(2)}, u32[]{:S(2)}) collective-permute-start(bf16[384,512]{1,0:T(8,128)(2,1)S(1)} %get-tuple-element.39), channel_id=1, source_target_pairs={{0,8},{8,16},{16,24},{24,32},{32,40},{40,48},{48,56},{56,64},{64,7... | collective-permute-start | bytes 1179656 | tf_op jit(solution)/shard_map/ppermute | solution.py:35
  79.2 8.7 %collective-permute-start.10 = (bf16[160,128]{1,0:T(8,128)(2,1)S(1)}, bf16[160,128]{1,0:T(8,128)(2,1)S(1)}, u32[]{:S(2)}, u32[]{:S(2)}) collective-permute-start(bf16[160,128]{1,0:T(8,128)(2,1)S(1)} %fusion.7), channel_id=1, source_target_pairs={{0,64},{8,72},{16,80},{24,88},{32,96},{40,104},{48,112},{56,120},{... | collective-permute-start | bytes 122888 | tf_op jit(solution)/shard_map/ppermute | solution.py:35
  91.6 9.2 %collective-permute-start.12 = (bf16[160,128]{1,0:T(8,128)(2,1)S(1)}, bf16[160,128]{1,0:T(8,128)(2,1)S(1)}, u32[]{:S(2)}, u32[]{:S(2)}) collective-permute-start(bf16[160,128]{1,0:T(8,128)(2,1)S(1)} %convert_add_fusion), channel_id=1, source_target_pairs={{0,128},{8,136},{16,144},{24,152},{32,160},{40,168},{48,176},{56,1... | collective-permute-start | bytes 122888 | tf_op jit(solution)/shard_map/ppermute | solution.py:35
  92.9 11.0 %collective-permute-start.13 = (bf16[160,128]{1,0:T(8,128)(2,1)S(1)}, bf16[160,128]{1,0:T(8,128)(2,1)S(1)}, u32[]{:S(2)}, u32[]{:S(2)}) collective-permute-start(bf16[160,128]{1,0:T(8,128)(2,1)S(1)} %convert_add_fusion), channel_id=1, source_target_pairs={{0,256},{8,264},{16,272},{24,280},{32,288},{40,296},{48,304},{56,3... | collective-permute-start | bytes 122888 | tf_op jit(solution)/shard_map/ppermute | solution.py:35
  94.2 12.2 %collective-permute-start.14 = (bf16[160,128]{1,0:T(8,128)(2,1)S(1)}, bf16[160,128]{1,0:T(8,128)(2,1)S(1)}, u32[]{:S(2)}, u32[]{:S(2)}) collective-permute-start(bf16[160,128]{1,0:T(8,128)(2,1)S(1)} %convert_add_fusion), channel_id=1, source_target_pairs={{0,384},{8,392},{16,400},{24,408},{32,416},{40,424},{48,432},{56,4... | collective-permute-start | bytes 122888 | tf_op jit(solution)/shard_map/ppermute | solution.py:35
  106.5 4.5 %collective-permute-start.15 = (bf16[160,128]{1,0:T(8,128)(2,1)S(1)}, bf16[160,128]{1,0:T(8,128)(2,1)S(1)}, u32[]{:S(2)}, u32[]{:S(2)}) collective-permute-start(bf16[160,128]{1,0:T(8,128)(2,1)S(1)} %get-tuple-element.63), channel_id=1, source_target_pairs={{0,8},{8,0},{16,24},{24,16},{32,40},{40,32},{48,56},{56,48},{64,72... | collective-permute-start | bytes 122888 | tf_op jit(solution)/shard_map/ppermute | solution.py:35
  112.4 10.7 %collective-permute-start.16 = (bf16[64,2048]{1,0:T(8,128)(2,1)S(1)}, bf16[64,2048]{1,0:T(8,128)(2,1)S(1)}, u32[]{:S(2)}, u32[]{:S(2)}) collective-permute-start(bf16[64,2048]{1,0:T(8,128)(2,1)S(1)} %get-tuple-element.51), channel_id=1, source_target_pairs={{0,2},{8,10},{16,18},{24,26},{32,34},{40,42},{48,50},{56,58},{64,6... | collective-permute-start | bytes 786440 | tf_op jit(solution)/shard_map/ppermute | solution.py:35
  116.1 9.1 %collective-permute-start.17 = (bf16[64,2048]{1,0:T(8,128)(2,1)S(1)}, bf16[64,2048]{1,0:T(8,128)(2,1)S(1)}, u32[]{:S(2)}, u32[]{:S(2)}) collective-permute-start(bf16[64,2048]{1,0:T(8,128)(2,1)S(1)} %get-tuple-element.52), channel_id=1, source_target_pairs={{0,6},{8,14},{16,22},{24,30},{32,38},{40,46},{48,54},{56,62},{64,7... | collective-permute-start | bytes 786440 | tf_op jit(solution)/shard_map/ppermute | solution.py:35
  118.9 10.3 %collective-permute-start.18 = (bf16[64,2048]{1,0:T(8,128)(2,1)S(1)}, bf16[64,2048]{1,0:T(8,128)(2,1)S(1)}, u32[]{:S(2)}, u32[]{:S(2)}) collective-permute-start(bf16[64,2048]{1,0:T(8,128)(2,1)S(1)} %get-tuple-element.53), channel_id=1, source_target_pairs={{0,4},{8,12},{16,20},{24,28},{32,36},{40,44},{48,52},{56,60},{64,6... | collective-permute-start | bytes 786440 | tf_op jit(solution)/shard_map/ppermute | solution.py:35
  129.4 22.8 %collective-permute-start.19 = (bf16[64,2048]{1,0:T(8,128)(2,1)S(1)}, bf16[64,2048]{1,0:T(8,128)(2,1)S(1)}, u32[]{:S(2)}, u32[]{:S(2)}) collective-permute-start(bf16[64,2048]{1,0:T(8,128)(2,1)S(1)} %get-tuple-element.59), channel_id=1, source_target_pairs={{0,2},{8,10},{16,18},{24,26},{32,34},{40,42},{48,50},{56,58},{64,6... | collective-permute-start | bytes 786440 | tf_op jit(solution)/shard_map/ppermute | solution.py:35
  134.3 17.9 %collective-permute-start.20 = (bf16[64,2048]{1,0:T(8,128)(2,1)S(1)}, bf16[64,2048]{1,0:T(8,128)(2,1)S(1)}, u32[]{:S(2)}, u32[]{:S(2)}) collective-permute-start(bf16[64,2048]{1,0:T(8,128)(2,1)S(1)} %get-tuple-element.60), channel_id=1, source_target_pairs={{0,6},{8,14},{16,22},{24,30},{32,38},{40,46},{48,54},{56,62},{64,7... | collective-permute-start | bytes 786440 | tf_op jit(solution)/shard_map/ppermute | solution.py:35
  137.2 15.0 %collective-permute-start.21 = (bf16[64,2048]{1,0:T(8,128)(2,1)S(1)}, bf16[64,2048]{1,0:T(8,128)(2,1)S(1)}, u32[]{:S(2)}, u32[]{:S(2)}) collective-permute-start(bf16[64,2048]{1,0:T(8,128)(2,1)S(1)} %get-tuple-element.61), channel_id=1, source_target_pairs={{0,4},{8,12},{16,20},{24,28},{32,36},{40,44},{48,52},{56,60},{64,6... | collective-permute-start | bytes 786440 | tf_op jit(solution)/shard_map/ppermute | solution.py:35
  140.3 35.0 %collective-permute-start.22 = (bf16[64,2048]{1,0:T(8,128)(2,1)S(1)}, bf16[64,2048]{1,0:T(8,128)(2,1)S(1)}, u32[]{:S(2)}, u32[]{:S(2)}) collective-permute-start(bf16[64,2048]{1,0:T(8,128)(2,1)S(1)} %add_convert_fusion.1), channel_id=1, source_target_pairs={{0,1},{8,9},{16,17},{24,25},{32,33},{40,41},{48,49},{56,57},{64,65... | collective-permute-start | bytes 786440 | tf_op jit(solution)/shard_map/ppermute | solution.py:35

commit v4 on v3

--- a/solution.py
+++ b/solution.py
@@ -64,6 +64,7 @@
 
 ROWS = 160
 VMEM = pl.BlockSpec(memory_space=pltpu.VMEM)
+ANY = pl.BlockSpec(memory_space=pl.ANY)
 SMEM = pl.BlockSpec(memory_space=pltpu.SMEM)
 
 
@@ -115,27 +116,32 @@
 
 def project_kernel(*refs):
     parts = refs[:N_TP]
-    wf, ww, table, feats_ref, qn_ref, kv_ref, tail_ref, mine_ref, other_ref = refs[N_TP:]
+    wf, ww, table, feats_ref, qn_ref, kv_ref, tail_ref, mine_ref, other_ref, held, sems = refs[N_TP:]
     x, half, core, _ = position()
     owners = [lax.rem(x + NX - s, NX) * 2 + side for side in (half, 1 - half) for s in (0, 1, 3, 2)]
     width = parts[0].shape[1]
     head = ww.shape[2] // 3
-    tokens = jnp.concatenate([p[...] for p in parts], axis=1)
-    rows = [pl.ds(pl.multiple_of(owner * width, width), width) for owner in owners]
-
-    def columns(pick):
-        return dot(tokens, jnp.concatenate([pick(r) for r in rows], axis=0)).astype(bf16)
-
-    feats = columns(lambda r: wf[r, :])
+    copies = [
+        pltpu.make_async_copy(part, held.at[:, pl.ds(pl.multiple_of(owner * width, width), width)], sems.at[k])
+        for k, (part, owner) in enumerate(zip(parts, owners))
+    ]
+    for copy in copies:
+        copy.start()
+    for copy in copies:
+        copy.wait()
+    tokens = held[...]
+
+    def columns(weight):
+        return dot(tokens, weight).astype(bf16)
+
+    feats = columns(wf[...])
     ones = lax.broadcasted_iota(jnp.int32, feats.shape, 1) == 0
     feats = jnp.concatenate([feats, jnp.where(ones, 1.0, 0.0).astype(bf16)], axis=1)
     feats_ref[...] = feats
     first_tail = kv_ref.shape[0] - tail_ref.shape[0]
     states = []
     for kind in (2, 1, 0):
-        out = columns(
-            lambda r: jnp.concatenate([ww[h, r, kind * head : (kind + 1) * head] for h in range(2)], axis=1)
-        )
+        out = columns(jnp.concatenate([ww[h, :, kind * head : (kind + 1) * head] for h in range(2)], axis=1))
         if kind == 2:
             kv_ref[:, 2 * head :] = out
             tail_ref[:, 2 * head :] = out[first_tail:]
@@ -201,8 +207,7 @@
             win_ref[at, cols] = unit(dot(weights, values[b * BLOCK : b * BLOCK + span]))
 
 
-def output_kernel(ours, theirs, near_ref, win_ref, high_ref, low_ref, w_ref, *refs):
-    outs, hidden = refs[:-1], refs[-1]
+def hidden_kernel(ours, theirs, near_ref, win_ref, high_ref, low_ref, keep_ref, away_ref, hidden):
     x, half, core, _ = position()
     mine, other = ours[...], theirs[...].astype(f32)
     head = mine.shape[1]
@@ -215,13 +220,17 @@
         out = (unit(near_ref[:, cols] + far) + win_ref[:, cols]).astype(bf16)
         for g in range(N_TP):
             hidden[g, :, cols] = out[g * rows : (g + 1) * rows]
-    weight = w_ref[...]
-    for away in (1, 0):
-        want = jnp.where(away == 1, 1 - half, half)
-        groups = [hidden[lax.rem(x + s, NX) * 2 + want] for s in range(NX)]
-        product = dot(jnp.concatenate(groups, axis=0), weight).astype(bf16)
-        for s in range(NX):
-            outs[(1 - away) * NX + s][...] = product[s * rows : (s + 1) * rows]
+    for s in range(NX):
+        group = lax.rem(x + s, NX) * 2
+        keep_ref[s * rows : (s + 1) * rows] = hidden[group + half]
+        away_ref[s * rows : (s + 1) * rows] = hidden[group + 1 - half]
+
+
+def product_kernel(keep_ref, got_ref, w_ref, w_got_ref, *outs):
+    rows = outs[0].shape[0]
+    product = (dot(keep_ref[...], w_ref[...]) + dot(got_ref[...], w_got_ref[...])).astype(bf16)
+    for s, out in enumerate(outs):
+        out[...] = product[s * rows : (s + 1) * rows]
 
 
 def prefix(mine, other, place, beside):
@@ -231,12 +240,14 @@
     before = jnp.zeros_like(total)
     done = None
     for flip in (1, 2, 4):
-        part = send(total.astype(bf16), to_z(flip)).astype(f32)
+        part = send(total.astype(bf16), to_z(flip))
+        if flip == 4:
+            part, done = lax.optimization_barrier((part, done))
+        part = part.astype(f32)
         before = before + jnp.where((z ^ flip) < z, part, 0.0)
         total = total + part
         if flip == 1:
             done = beside(total)
-    total, done = lax.optimization_barrier((total, done))
     short = total.astype(bf16)
     for steps in (1, 2, 3):
         before = before + send(short, to_y(steps)).astype(f32)
@@ -263,8 +274,9 @@
             shape((ROWS, wide // 2), f32),
             shape((ROWS, wide // 2), bf16),
         ),
-        in_specs=[VMEM] * (N_TP + 3),
+        in_specs=[ANY] * N_TP + [VMEM] * 3,
         out_specs=(VMEM,) * 6,
+        scratch_shapes=[pltpu.VMEM((tok_rows, wf.shape[0]), bf16), pltpu.SemaphoreType.DMA((N_TP,))],
         name="project",
         compiler_params=pltpu.CompilerParams(vmem_limit_bytes=LIMIT),
     )(*parts, wf, ww, tables.astype(bf16))
@@ -287,17 +299,28 @@
     )(win_blocks, feats, qn, kv, halo, tables.astype(bf16))
 
 
-def output(ours, theirs, near_out, win_out, high, low, w_out):
-    rows = near_out.shape[0] // N_TP
+def hidden_rows(ours, theirs, near_out, win_out, high, low):
+    tok_rows, wide = near_out.shape
     return pl.pallas_call(
-        output_kernel,
-        out_shape=(shape((rows, w_out.shape[1]), bf16),) * N_TP,
-        in_specs=[VMEM] * 7,
-        out_specs=(VMEM,) * N_TP,
-        scratch_shapes=[pltpu.VMEM((N_TP, rows, w_out.shape[0]), bf16)],
-        name="output",
+        hidden_kernel,
+        out_shape=(shape((tok_rows // 2, wide), bf16),) * 2,
+        in_specs=[VMEM] * 6,
+        out_specs=(VMEM,) * 2,
+        scratch_shapes=[pltpu.VMEM((N_TP, tok_rows // N_TP, wide), bf16)],
+        name="hidden",
         compiler_params=pltpu.CompilerParams(vmem_limit_bytes=LIMIT),
-    )(ours, theirs, near_out, win_out, high, low, w_out)
+    )(ours, theirs, near_out, win_out, high, low)
+
+
+def product(keep, got, w_out, w_got):
+    return pl.pallas_call(
+        product_kernel,
+        out_shape=(shape((keep.shape[0] // NX, w_out.shape[1]), bf16),) * NX,
+        in_specs=[VMEM] * 4,
+        out_specs=(VMEM,) * NX,
+        name="product",
+        compiler_params=pltpu.CompilerParams(vmem_limit_bytes=LIMIT),
+    )(keep, got, w_out, w_got)
 
 
 LIMIT = 16 * 2**20
@@ -311,7 +334,12 @@
 
     other = send(tokens, to_half)
     parts = [tokens] + [send(tokens, to_x(s)) for s in (1, 3, 2)]
+    w_out = w_out.reshape(-1, model_width)
+    piece_rows = w_out.shape[0] // (2 * NY)
+    piece = lax.dynamic_slice_in_dim(w_out, (y * 2 + c) * piece_rows, piece_rows, 0)
+    other, piece = lax.optimization_barrier((other, piece))
     parts += [other] + [send(other, to_x(s)) for s in (1, 3, 2)]
+    piece = send(piece, to_half)
     tables = feature_maps(feat_dim, head_count)
     feats, qn, kv, tail, mine, theirs = project(
         parts, w_feature.reshape(model_width, -1), w_window.transpose(1, 0, 2), tables
@@ -321,19 +349,16 @@
         halo, _ = lax.optimization_barrier((send(tail, to_next), total))
         return near(win_blocks, feats, qn, kv, halo, tables[:, :2])
 
+    mine, piece = lax.optimization_barrier((mine, piece))
+    alike = [[(row * NZ + at) * 2 + core for row in range(NY) for core in range(2)] for at in range(NZ)]
+    w_got = lax.all_gather(piece, "seq", axis=0, axis_index_groups=alike, tiled=True)
     ours, theirs, attended = prefix(mine, theirs, (x, h, y, z, c), beside)
-    products = output(ours, theirs, *attended, w_out.reshape(-1, model_width))
-
-    def summed(group):
-        total = group[0].astype(f32)
-        for steps in (1, 3, 2):
-            total = total + send(group[steps], to_x(steps)).astype(f32)
-        return total
-
-    away = summed(products[:NX]).astype(bf16)
-    away, *own = lax.optimization_barrier((away, *products[NX:]))
-    away = send(away, to_half)
-    return (summed(own) + away.astype(f32)).astype(bf16)
+    keep, away = hidden_rows(ours, theirs, *attended)
+    products = product(keep, send(away, to_half), w_out, w_got)
+    total = products[0].astype(f32)
+    for steps in (1, 3, 2):
+        total = total + send(products[steps], to_x(steps)).astype(f32)
+    return total.astype(bf16)
 
 
 def solution(mesh):

time: 177 us -> 179 us (1.011)
  the two profiles are of different devices: /device:TPU:57 before, /device:TPU:10 now
where the time goes in v4:
time: 179 us; the launch traced here: 178 us
  starting transfers between devices  103 us (58%)
  waiting for transfers between devices  39 us (22%)
  between operations  13.8 us (8%)
  local copies, waits for them, and re-layouts  13.1 us (7%)
  Pallas kernels  8.69 us (5%)
    ppermute x21, starting transfers between devices, send(): return lax.ppermute(value, ('seq', 'tp'), pairs(move))  103 us
    ppermute x21, waiting for transfers between devices, send(): return lax.ppermute(value, ('seq', 'tp'), pairs(move))  39 us
    unnamed x29, local copies, waits for them, and re-layouts  11 us
    pallas_call x1, Pallas kernels, near(): pl.pallas_call(local_kernel, out_shape=(shape((tok_rows, wide), f32), sha...  3.76 us
  transfers between devices with their start and end apart: 22, of which 8 were waited for; matrix products, arithmetic and copies ran while one was open for 3% of the time, Pallas kernels for 4%

profile of v4, /device:TPU:10, one launch (start us, length us, event | category | flops | bytes accessed | tf_op | source)
XLA Modules:
  0.0 178.2 jit_solution(14882796713719726117)
XLA Ops:
  6.5 15.7 %collective-permute-start.3 = (bf16[512,256]{1,0:T(8,128)(2,1)}, bf16[512,256]{1,0:T(8,128)(2,1)S(1)}, u32[]{:S(2)}, u32[]{:S(2)}) collective-permute-start(bf16[512,256]{1,0:T(8,128)(2,1)} %refs_0_.1), channel_id=1, source_target_pairs={{0,1},{8,9},{16,17},{24,25},{32,33},{40,41},{48,49},{56,57},{64,65... | collective-permute-start | bytes 786440 | tf_op jit(solution)/shard_map/ppermute | solution.py:35
  22.3 4.0 %collective-permute-start.2 = (bf16[512,256]{1,0:T(8,128)(2,1)}, bf16[512,256]{1,0:T(8,128)(2,1)S(1)}, u32[]{:S(2)}, u32[]{:S(2)}) collective-permute-start(bf16[512,256]{1,0:T(8,128)(2,1)} %refs_0_.1), channel_id=1, source_target_pairs={{0,4},{8,12},{16,20},{24,28},{32,36},{40,44},{48,52},{56,60},{64,6... | collective-permute-start | bytes 786440 | tf_op jit(solution)/shard_map/ppermute | solution.py:35
  26.3 3.3 %collective-permute-start.1 = (bf16[512,256]{1,0:T(8,128)(2,1)}, bf16[512,256]{1,0:T(8,128)(2,1)S(1)}, u32[]{:S(2)}, u32[]{:S(2)}) collective-permute-start(bf16[512,256]{1,0:T(8,128)(2,1)} %refs_0_.1), channel_id=1, source_target_pairs={{0,6},{8,14},{16,22},{24,30},{32,38},{40,46},{48,54},{56,62},{64,7... | collective-permute-start | bytes 786440 | tf_op jit(solution)/shard_map/ppermute | solution.py:35
  29.7 2.5 %collective-permute-start = (bf16[512,256]{1,0:T(8,128)(2,1)}, bf16[512,256]{1,0:T(8,128)(2,1)S(1)}, u32[]{:S(2)}, u32[]{:S(2)}) collective-permute-start(bf16[512,256]{1,0:T(8,128)(2,1)} %refs_0_.1), channel_id=1, source_target_pairs={{0,2},{8,10},{16,18},{24,26},{32,34},{40,42},{48,50},{56,58},{64,6... | collective-permute-start | bytes 786440 | tf_op jit(solution)/shard_map/ppermute | solution.py:35
  32.2 0.9 constant_dynamic-slice_fusion
  33.1 0.0 collective-permute-done.3.refs_4_
  33.1 4.5 %collective-permute-start.6 = (bf16[512,256]{1,0:T(8,128)(2,1)S(1)}, bf16[512,256]{1,0:T(8,128)(2,1)S(1)}, u32[]{:S(2)}, u32[]{:S(2)}) collective-permute-start(bf16[512,256]{1,0:T(8,128)(2,1)S(1)} %collective-permute-done.3.refs_4_), channel_id=1, source_target_pairs={{0,4},{8,12},{16,20},{24,28},{32,36},{40,44},{48,52},{56,60},{64,6... | collective-permute-start | bytes 786440 | tf_op jit(solution)/shard_map/ppermute | solution.py:35
  37.7 1.9 %collective-permute-start.5 = (bf16[512,256]{1,0:T(8,128)(2,1)S(1)}, bf16[512,256]{1,0:T(8,128)(2,1)S(1)}, u32[]{:S(2)}, u32[]{:S(2)}) collective-permute-start(bf16[512,256]{1,0:T(8,128)(2,1)S(1)} %collective-permute-done.3.refs_4_), channel_id=1, source_target_pairs={{0,6},{8,14},{16,22},{24,30},{32,38},{40,46},{48,54},{56,62},{64,7... | collective-permute-start | bytes 786440 | tf_op jit(solution)/shard_map/ppermute | solution.py:35
  39.6 0.0 collective-permute-done.2.refs_3_
  39.6 3.9 %collective-permute-start.4 = (bf16[512,256]{1,0:T(8,128)(2,1)S(1)}, bf16[512,256]{1,0:T(8,128)(2,1)S(1)}, u32[]{:S(2)}, u32[]{:S(2)}) collective-permute-start(bf16[512,256]{1,0:T(8,128)(2,1)S(1)} %collective-permute-done.3.refs_4_), channel_id=1, source_target_pairs={{0,2},{8,10},{16,18},{24,26},{32,34},{40,42},{48,50},{56,58},{64,6... | collective-permute-start | bytes 786440 | tf_op jit(solution)/shard_map/ppermute | solution.py:35
  43.5 0.0 collective-permute-done.1.refs_2_
  43.5 7.8 %collective-permute-start.7 = (bf16[32,2048]{1,0:T(8,128)(2,1)S(1)}, bf16[32,2048]{1,0:T(8,128)(2,1)S(1)}, u32[]{:S(2)}, u32[]{:S(2)}) collective-permute-start(bf16[32,2048]{1,0:T(8,128)(2,1)S(1)} %constant_dynamic-slice_fusion), channel_id=1, source_target_pairs={{0,1},{8,9},{16,17},{24,25},{32,33},{40,41},{48,49},{56,57},{64,65... | collective-permute-start | bytes 393224 | tf_op jit(solution)/shard_map/ppermute | solution.py:35
  51.3 1.2 copy.11.refs_8_
  52.5 0.0 copy-start.4
  52.6 0.0 copy-start.5
  52.6 2.4 %copy.13 = bf16[2048,2,384]{2,0,1:T(8,128)(2,1)S(1)} copy(bf16[2048,2,384]{2,1,0:T(2,128)(2,1)} %param.9) | data formatting | bytes 6291456 | tf_op args[2]
  54.9 0.0 collective-permute-done.refs_1_
  54.9 0.0 collective-permute-done.6.refs_7_
  55.0 0.0 collective-permute-done.5.refs_6_
  55.0 0.0 collective-permute-done.4.refs_5_
  55.0 0.0 copy-start.11
  55.0 3.6 %project.1 = (bf16[512,128]{1,0:T(8,128)(2,1)S(1)}, bf16[512,256]{1,0:T(8,128)(2,1)S(1)}, bf16[512,512]{1,0:T(8,128)(2,1)S(1)}, bf16[384,512]{1,0:T(8,128)(2,1)S...) custom-call(bf16[512,256]{1,0:T(8,128)(2,1)S(1)} %copy-done.5, ...), custom_call_target="tpu_custom_call" | custom-call | tf_op jit(solution)/shard_map/project/pallas_call | solution.py:267
  58.6 0.0 copy-start.6
  58.6 0.7 copy-done.6
  59.3 0.6 copy-done.9
  59.9 0.7 copy-done.12
  60.7 0.0 collective-permute-done.7
  60.7 0.7 copy-done.13
  61.3 0.0 all-gather.2.cloned.1.call-update
  61.3 1.9 %collective-permute-start.8 = (bf16[160,128]{1,0:T(8,128)(2,1)S(1)}, bf16[160,128]{1,0:T(8,128)(2,1)S(1)}, u32[]{:S(2)}, u32[]{:S(2)}) collective-permute-start(bf16[160,128]{1,0:T(8,128)(2,1)S(1)} %get-tuple-element.35), channel_id=1, source_target_pairs={{0,8},{8,0},{16,24},{24,16},{32,40},{40,32},{48,56},{56,48},{64,72... | collective-permute-start | bytes 122888 | tf_op jit(solution)/shard_map/ppermute | solution.py:35
  63.3 1.2 collective-permute-done.8
  64.5 19.5 %collective-permute-start.9 = (bf16[160,128]{1,0:T(8,128)(2,1)S(1)}, bf16[160,128]{1,0:T(8,128)(2,1)S(1)}, u32[]{:S(2)}, u32[]{:S(2)}) collective-permute-start(bf16[160,128]{1,0:T(8,128)(2,1)S(1)} %fusion.7), channel_id=1, source_target_pairs={{0,16},{8,24},{16,0},{24,8},{32,48},{40,56},{48,32},{56,40},{64,80... | collective-permute-start | bytes 122888 | tf_op jit(solution)/shard_map/ppermute | solution.py:35
  84.0 1.9 %collective-permute-start.12 = (bf16[384,512]{1,0:T(8,128)(2,1)}, bf16[384,512]{1,0:T(8,128)(2,1)S(1)}, u32[]{:S(2)}, u32[]{:S(2)}) collective-permute-start(bf16[384,512]{1,0:T(8,128)(2,1)} %copy-done.12), channel_id=1, source_target_pairs={{0,8},{8,16},{16,24},{24,32},{32,40},{40,48},{48,56},{56,64},{64,7... | collective-permute-start | bytes 1179656 | tf_op jit(solution)/shard_map/ppermute | solution.py:35
  85.9 0.0 collective-permute-done.9
  86.0 3.7 %collective-permute-start.10 = (bf16[160,128]{1,0:T(8,128)(2,1)S(1)}, bf16[160,128]{1,0:T(8,128)(2,1)S(1)}, u32[]{:S(2)}, u32[]{:S(2)}) collective-permute-start(bf16[160,128]{1,0:T(8,128)(2,1)S(1)} %get-tuple-element.59), channel_id=1, source_target_pairs={{0,32},{8,40},{16,48},{24,56},{32,0},{40,8},{48,16},{56,24},{64,96... | collective-permute-start | bytes 122888 | tf_op jit(solution)/shard_map/ppermute | solution.py:35
  89.6 3.3 %collective-permute-done.10 = bf16[160,128]{1,0:T(8,128)(2,1)S(1)} collective-permute-done((bf16[160,128]{1,0:T(8,128)(2,1)S(1)}, bf16[160,128]{1,0:T(8,128)(2,1)S(1)}, u32[]{:S(2)}, u32[]{:S(2)}) %collective-permute-start.10) | collective-permute-done | bytes 40992 | tf_op jit(solution)/shard_map/ppermute | solution.py:35
  92.9 4.0 %collective-permute-start.11 = (bf16[160,128]{1,0:T(8,128)(2,1)S(1)}, bf16[160,128]{1,0:T(8,128)(2,1)S(1)}, u32[]{:S(2)}, u32[]{:S(2)}) collective-permute-start(bf16[160,128]{1,0:T(8,128)(2,1)S(1)} %fusion.8), channel_id=1, source_target_pairs={{0,64},{8,72},{16,80},{24,88},{32,96},{40,104},{48,112},{56,120},{... | collective-permute-start | bytes 122888 | tf_op jit(solution)/shard_map/ppermute | solution.py:35
  96.9 4.1 %collective-permute-done.12.halo_ref = bf16[384,512]{1,0:T(8,128)(2,1)S(1)} collective-permute-done((bf16[384,512]{1,0:T(8,128)(2,1)}, bf16[384,512]{1,0:T(8,128)(2,1)S(1)}, u32[]{:S(2)}, u32[]{:S(2)}) %collective-permute-start.12) | collective-permute-done | bytes 393248 | tf_op jit(solution)/shard_map/ppermute | solution.py:35
  101.0 0.9 copy-done.7
  101.9 0.9 copy-done.8
  102.8 0.9 copy-done.10
  103.7 3.8 %near.1 = (f32[512,256]{1,0:T(8,128)S(1)}, f32[512,256]{1,0:T(8,128)S(1)}, bf16[2,512,160]{2,1,0:T(8,128)(2,1)S(1)}, bf16[2,512,160]{2,1,0:T(8,128)(2,1)S(1)}) custom-call(s32[2]{0:T(128)S(1)} %copy-done.11, bf16[512,128]{1,0:T(8,128)(2,1)S(1)} %copy-done.10, bf16[512,256]{1,0:T(8,128)(2,1)S(1)} %copy-done.7, bf16[512,512]{1,0:T(8,128)(2,1)S(1)} %get-tuple-element.38.kv_ref, ...), custom_call_target="tpu_custom_call" | custom-call | tf_op jit(solution)/shard_map/near/pallas_call | solution.py:287
  107.5 0.8 copy-done.2
  108.3 0.7 collective-permute-start.15
  109.0 4.8 %collective-permute-start.14 = (bf16[160,128]{1,0:T(8,128)(2,1)S(1)}, bf16[160,128]{1,0:T(8,128)(2,1)S(1)}, u32[]{:S(2)}, u32[]{:S(2)}) collective-permute-start(bf16[160,128]{1,0:T(8,128)(2,1)S(1)} %fusion.6), channel_id=1, source_target_pairs={{0,256},{8,264},{16,272},{24,280},{32,288},{40,296},{48,304},{56,3... | collective-permute-start | bytes 122888 | tf_op jit(solution)/shard_map/ppermute | solution.py:35
  113.8 1.9 %collective-permute-start.13 = (bf16[160,128]{1,0:T(8,128)(2,1)S(1)}, bf16[160,128]{1,0:T(8,128)(2,1)S(1)}, u32[]{:S(2)}, u32[]{:S(2)}) collective-permute-start(bf16[160,128]{1,0:T(8,128)(2,1)S(1)} %fusion.6), channel_id=1, source_target_pairs={{0,128},{8,136},{16,144},{24,152},{32,160},{40,168},{48,176},{56,1... | collective-permute-start | bytes 122888 | tf_op jit(solution)/shard_map/ppermute | solution.py:35
  115.8 0.0 collective-permute-done.15
  115.8 3.9 %collective-permute-done.13 = bf16[160,128]{1,0:T(8,128)(2,1)S(1)} collective-permute-done((bf16[160,128]{1,0:T(8,128)(2,1)S(1)}, bf16[160,128]{1,0:T(8,128)(2,1)S(1)}, u32[]{:S(2)}, u32[]{:S(2)}) %collective-permute-start.13) | collective-permute-done | bytes 40992 | tf_op jit(solution)/shard_map/ppermute | solution.py:35
  119.7 0.1 add_convert_fusion.1
  119.8 1.9 %collective-permute-start.16 = (bf16[160,128]{1,0:T(8,128)(2,1)S(1)}, bf16[160,128]{1,0:T(8,128)(2,1)S(1)}, u32[]{:S(2)}, u32[]{:S(2)}) collective-permute-start(bf16[160,128]{1,0:T(8,128)(2,1)S(1)} %get-tuple-element.57), channel_id=1, source_target_pairs={{0,8},{8,0},{16,24},{24,16},{32,40},{40,32},{48,56},{56,48},{64,72... | collective-permute-start | bytes 122888 | tf_op jit(solution)/shard_map/ppermute | solution.py:35
  121.7 1.2 collective-permute-done.16.theirs
  122.9 1.0 copy-done.3
  123.9 0.7 hidden.1
  124.6 8.2 %collective-permute-start.17 = (bf16[256,256]{1,0:T(8,128)(2,1)S(1)}, bf16[256,256]{1,0:T(8,128)(2,1)S(1)}, u32[]{:S(2)}, u32[]{:S(2)}) collective-permute-start(bf16[256,256]{1,0:T(8,128)(2,1)S(1)} %get-tuple-element.51), channel_id=1, source_target_pairs={{0,1},{8,9},{16,17},{24,25},{32,33},{40,41},{48,49},{56,57},{64,65... | collective-permute-start | bytes 393224 | tf_op jit(solution)/shard_map/ppermute | solution.py:35
  132.9 15.7 %collective-permute-done.17.got_ref = bf16[256,256]{1,0:T(8,128)(2,1)S(1)} collective-permute-done((bf16[256,256]{1,0:T(8,128)(2,1)S(1)}, bf16[256,256]{1,0:T(8,128)(2,1)S(1)}, u32[]{:S(2)}, u32[]{:S(2)}) %collective-permute-start.17) | collective-permute-done | bytes 131104 | tf_op jit(solution)/shard_map/ppermute | solution.py:35
  148.6 1.2 copy-done.1
  149.8 0.7 product.1
  150.5 2.1 %collective-permute-start.18 = (bf16[64,2048]{1,0:T(8,128)(2,1)S(1)}, bf16[64,2048]{1,0:T(8,128)(2,1)S(1)}, u32[]{:S(2)}, u32[]{:S(2)}) collective-permute-start(bf16[64,2048]{1,0:T(8,128)(2,1)S(1)} %get-tuple-element.54), channel_id=1, source_target_pairs={{0,2},{8,10},{16,18},{24,26},{32,34},{40,42},{48,50},{56,58},{64,6... | collective-permute-start | bytes 786440 | tf_op jit(solution)/shard_map/ppermute | solution.py:35
  152.7 3.7 %collective-permute-start.19 = (bf16[64,2048]{1,0:T(8,128)(2,1)S(1)}, bf16[64,2048]{1,0:T(8,128)(2,1)S(1)}, u32[]{:S(2)}, u32[]{:S(2)}) collective-permute-start(bf16[64,2048]{1,0:T(8,128)(2,1)S(1)} %get-tuple-element.55), channel_id=1, source_target_pairs={{0,6},{8,14},{16,22},{24,30},{32,38},{40,46},{48,54},{56,62},{64,7... | collective-permute-start | bytes 786440 | tf_op jit(solution)/shard_map/ppermute | solution.py:35
  156.4 4.5 %collective-permute-start.20 = (bf16[64,2048]{1,0:T(8,128)(2,1)S(1)}, bf16[64,2048]{1,0:T(8,128)(2,1)S(1)}, u32[]{:S(2)}, u32[]{:S(2)}) collective-permute-start(bf16[64,2048]{1,0:T(8,128)(2,1)S(1)} %get-tuple-element.56), channel_id=1, source_target_pairs={{0,4},{8,12},{16,20},{24,28},{32,36},{40,44},{48,52},{56,60},{64,6... | collective-permute-start | bytes 786440 | tf_op jit(solution)/shard_map/ppermute | solution.py:35
  160.9 0.0 collective-permute-done.18
  160.9 2.9 %collective-permute-done.19 = bf16[64,2048]{1,0:T(8,128)(2,1)S(1)} collective-permute-done((bf16[64,2048]{1,0:T(8,128)(2,1)S(1)}, bf16[64,2048]{1,0:T(8,128)(2,1)S(1)}, u32[]{:S(2)}, u32[]{:S(2)}) %collective-permute-start.19) | collective-permute-done | bytes 262176 | tf_op jit(solution)/shard_map/ppermute | solution.py:35
  163.8 6.7 %collective-permute-done.20 = bf16[64,2048]{1,0:T(8,128)(2,1)S(1)} collective-permute-done((bf16[64,2048]{1,0:T(8,128)(2,1)S(1)}, bf16[64,2048]{1,0:T(8,128)(2,1)S(1)}, u32[]{:S(2)}, u32[]{:S(2)}) %collective-permute-start.20) | collective-permute-done | bytes 262176 | tf_op jit(solution)/shard_map/ppermute | solution.py:35
  170.6 0.8 add_convert_fusion
  (23 shorter events, 0.1 us)
Async XLA Ops:
  6.5 142.1 %all-gather.2.cloned.1.call-start = ((), (), s32[]{:S(2)}) async-start(), calls=%async_computation | async-start | bytes 1179648 | tf_op jit(solution)/shard_map/all_gather | solution.py:354
  6.5 26.6 %collective-permute-start.3 = (bf16[512,256]{1,0:T(8,128)(2,1)}, bf16[512,256]{1,0:T(8,128)(2,1)S(1)}, u32[]{:S(2)}, u32[]{:S(2)}) collective-permute-start(bf16[512,256]{1,0:T(8,128)(2,1)} %refs_0_.1), channel_id=1, source_target_pairs={{0,1},{8,9},{16,17},{24,25},{32,33},{40,41},{48,49},{56,57},{64,65... | collective-permute-start | bytes 786440 | tf_op jit(solution)/shard_map/ppermute | solution.py:35
  22.3 17.3 %collective-permute-start.2 = (bf16[512,256]{1,0:T(8,128)(2,1)}, bf16[512,256]{1,0:T(8,128)(2,1)S(1)}, u32[]{:S(2)}, u32[]{:S(2)}) collective-permute-start(bf16[512,256]{1,0:T(8,128)(2,1)} %refs_0_.1), channel_id=1, source_target_pairs={{0,4},{8,12},{16,20},{24,28},{32,36},{40,44},{48,52},{56,60},{64,6... | collective-permute-start | bytes 786440 | tf_op jit(solution)/shard_map/ppermute | solution.py:35
  26.3 17.2 %collective-permute-start.1 = (bf16[512,256]{1,0:T(8,128)(2,1)}, bf16[512,256]{1,0:T(8,128)(2,1)S(1)}, u32[]{:S(2)}, u32[]{:S(2)}) collective-permute-start(bf16[512,256]{1,0:T(8,128)(2,1)} %refs_0_.1), channel_id=1, source_target_pairs={{0,6},{8,14},{16,22},{24,30},{32,38},{40,46},{48,54},{56,62},{64,7... | collective-permute-start | bytes 786440 | tf_op jit(solution)/shard_map/ppermute | solution.py:35
  29.7 25.3 %collective-permute-start = (bf16[512,256]{1,0:T(8,128)(2,1)}, bf16[512,256]{1,0:T(8,128)(2,1)S(1)}, u32[]{:S(2)}, u32[]{:S(2)}) collective-permute-start(bf16[512,256]{1,0:T(8,128)(2,1)} %refs_0_.1), channel_id=1, source_target_pairs={{0,2},{8,10},{16,18},{24,26},{32,34},{40,42},{48,50},{56,58},{64,6... | collective-permute-start | bytes 786440 | tf_op jit(solution)/shard_map/ppermute | solution.py:35
  33.1 21.8 %collective-permute-start.6 = (bf16[512,256]{1,0:T(8,128)(2,1)S(1)}, bf16[512,256]{1,0:T(8,128)(2,1)S(1)}, u32[]{:S(2)}, u32[]{:S(2)}) collective-permute-start(bf16[512,256]{1,0:T(8,128)(2,1)S(1)} %collective-permute-done.3.refs_4_), channel_id=1, source_target_pairs={{0,4},{8,12},{16,20},{24,28},{32,36},{40,44},{48,52},{56,60},{64,6... | collective-permute-start | bytes 786440 | tf_op jit(solution)/shard_map/ppermute | solution.py:35
  37.7 17.3 %collective-permute-start.5 = (bf16[512,256]{1,0:T(8,128)(2,1)S(1)}, bf16[512,256]{1,0:T(8,128)(2,1)S(1)}, u32[]{:S(2)}, u32[]{:S(2)}) collective-permute-start(bf16[512,256]{1,0:T(8,128)(2,1)S(1)} %collective-permute-done.3.refs_4_), channel_id=1, source_target_pairs={{0,6},{8,14},{16,22},{24,30},{32,38},{40,46},{48,54},{56,62},{64,7... | collective-permute-start | bytes 786440 | tf_op jit(solution)/shard_map/ppermute | solution.py:35
  39.6 15.4 %collective-permute-start.4 = (bf16[512,256]{1,0:T(8,128)(2,1)S(1)}, bf16[512,256]{1,0:T(8,128)(2,1)S(1)}, u32[]{:S(2)}, u32[]{:S(2)}) collective-permute-start(bf16[512,256]{1,0:T(8,128)(2,1)S(1)} %collective-permute-done.3.refs_4_), channel_id=1, source_target_pairs={{0,2},{8,10},{16,18},{24,26},{32,34},{40,42},{48,50},{56,58},{64,6... | collective-permute-start | bytes 786440 | tf_op jit(solution)/shard_map/ppermute | solution.py:35
  43.5 17.1 %collective-permute-start.7 = (bf16[32,2048]{1,0:T(8,128)(2,1)S(1)}, bf16[32,2048]{1,0:T(8,128)(2,1)S(1)}, u32[]{:S(2)}, u32[]{:S(2)}) collective-permute-start(bf16[32,2048]{1,0:T(8,128)(2,1)S(1)} %constant_dynamic-slice_fusion), channel_id=1, source_target_pairs={{0,1},{8,9},{16,17},{24,25},{32,33},{40,41},{48,49},{56,57},{64,65... | collective-permute-start | bytes 393224 | tf_op jit(solution)/shard_map/ppermute | solution.py:35
  52.5 2.4 %copy-start.4 = (bf16[2,4,160,128]{3,2,1,0:T(8,128)(2,1)S(1)}, bf16[2,4,160,128]{3,2,1,0:T(8,128)(2,1)}, u32[]{:S(2)}) copy-start(bf16[2,4,160,128]{3,2,1,0:T(8,128)(2,1)} %constant.64.clone.refs_10_) | copy-start | bytes 983044
  52.6 2.4 %copy-start.5 = (bf16[512,256]{1,0:T(8,128)(2,1)S(1)}, bf16[512,256]{1,0:T(8,128)(2,1)}, u32[]{:S(2)}) copy-start(bf16[512,256]{1,0:T(8,128)(2,1)} %refs_0_.1) | copy-start | bytes 786436
  55.0 46.0 %copy-start.11 = (s32[2]{0:T(128)S(1)}, s32[2]{0:T(128)}, u32[]{:S(2)}) copy-start(s32[2]{0:T(128)} %win.1) | copy-start | bytes 28
  58.6 0.7 copy-start.6
  59.3 0.6 copy-start.9
  59.9 0.7 copy-start.12
  60.7 87.9 %copy-start = (bf16[2,128,2048]{2,1,0:T(8,128)(2,1)S(1)}, bf16[2,128,2048]{2,1,0:T(8,128)(2,1)}, u32[]{:S(2)}) copy-start(bf16[2,128,2048]{2,1,0:T(8,128)(2,1)} %param.10) | copy-start | bytes 3145732
  60.7 0.7 copy-start.13
  61.3 3.1 %collective-permute-start.8 = (bf16[160,128]{1,0:T(8,128)(2,1)S(1)}, bf16[160,128]{1,0:T(8,128)(2,1)S(1)}, u32[]{:S(2)}, u32[]{:S(2)}) collective-permute-start(bf16[160,128]{1,0:T(8,128)(2,1)S(1)} %get-tuple-element.35), channel_id=1, source_target_pairs={{0,8},{8,0},{16,24},{24,16},{32,40},{40,32},{48,56},{56,48},{64,72... | collective-permute-start | bytes 122888 | tf_op jit(solution)/shard_map/ppermute | solution.py:35
  64.5 21.5 %collective-permute-start.9 = (bf16[160,128]{1,0:T(8,128)(2,1)S(1)}, bf16[160,128]{1,0:T(8,128)(2,1)S(1)}, u32[]{:S(2)}, u32[]{:S(2)}) collective-permute-start(bf16[160,128]{1,0:T(8,128)(2,1)S(1)} %fusion.7), channel_id=1, source_target_pairs={{0,16},{8,24},{16,0},{24,8},{32,48},{40,56},{48,32},{56,40},{64,80... | collective-permute-start | bytes 122888 | tf_op jit(solution)/shard_map/ppermute | solution.py:35
  84.0 17.0 %collective-permute-start.12 = (bf16[384,512]{1,0:T(8,128)(2,1)}, bf16[384,512]{1,0:T(8,128)(2,1)S(1)}, u32[]{:S(2)}, u32[]{:S(2)}) collective-permute-start(bf16[384,512]{1,0:T(8,128)(2,1)} %copy-done.12), channel_id=1, source_target_pairs={{0,8},{8,16},{16,24},{24,32},{32,40},{40,48},{48,56},{56,64},{64,7... | collective-permute-start | bytes 1179656 | tf_op jit(solution)/shard_map/ppermute | solution.py:35
  86.0 6.9 %collective-permute-start.10 = (bf16[160,128]{1,0:T(8,128)(2,1)S(1)}, bf16[160,128]{1,0:T(8,128)(2,1)S(1)}, u32[]{:S(2)}, u32[]{:S(2)}) collective-permute-start(bf16[160,128]{1,0:T(8,128)(2,1)S(1)} %get-tuple-element.59), channel_id=1, source_target_pairs={{0,32},{8,40},{16,48},{24,56},{32,0},{40,8},{48,16},{56,24},{64,96... | collective-permute-start | bytes 122888 | tf_op jit(solution)/shard_map/ppermute | solution.py:35
  92.9 15.4 %collective-permute-start.11 = (bf16[160,128]{1,0:T(8,128)(2,1)S(1)}, bf16[160,128]{1,0:T(8,128)(2,1)S(1)}, u32[]{:S(2)}, u32[]{:S(2)}) collective-permute-start(bf16[160,128]{1,0:T(8,128)(2,1)S(1)} %fusion.8), channel_id=1, source_target_pairs={{0,64},{8,72},{16,80},{24,88},{32,96},{40,104},{48,112},{56,120},{... | collective-permute-start | bytes 122888 | tf_op jit(solution)/shard_map/ppermute | solution.py:35
  101.0 1.0 copy-start.7
  101.9 0.9 copy-start.8
  102.8 0.9 copy-start.10
  107.5 0.8 copy-start.2
  108.3 7.5 %collective-permute-start.15 = (bf16[160,128]{1,0:T(8,128)(2,1)S(1)}, bf16[160,128]{1,0:T(8,128)(2,1)S(1)}, u32[]{:S(2)}, u32[]{:S(2)}) collective-permute-start(bf16[160,128]{1,0:T(8,128)(2,1)S(1)} %fusion.6), channel_id=1, source_target_pairs={{0,384},{8,392},{16,400},{24,408},{32,416},{40,424},{48,432},{56,4... | collective-permute-start | bytes 122888 | tf_op jit(solution)/shard_map/ppermute | solution.py:35
  109.0 6.8 %collective-permute-start.14 = (bf16[160,128]{1,0:T(8,128)(2,1)S(1)}, bf16[160,128]{1,0:T(8,128)(2,1)S(1)}, u32[]{:S(2)}, u32[]{:S(2)}) collective-permute-start(bf16[160,128]{1,0:T(8,128)(2,1)S(1)} %fusion.6), channel_id=1, source_target_pairs={{0,256},{8,264},{16,272},{24,280},{32,288},{40,296},{48,304},{56,3... | collective-permute-start | bytes 122888 | tf_op jit(solution)/shard_map/ppermute | solution.py:35
  113.8 5.9 %collective-permute-start.13 = (bf16[160,128]{1,0:T(8,128)(2,1)S(1)}, bf16[160,128]{1,0:T(8,128)(2,1)S(1)}, u32[]{:S(2)}, u32[]{:S(2)}) collective-permute-start(bf16[160,128]{1,0:T(8,128)(2,1)S(1)} %fusion.6), channel_id=1, source_target_pairs={{0,128},{8,136},{16,144},{24,152},{32,160},{40,168},{48,176},{56,1... | collective-permute-start | bytes 122888 | tf_op jit(solution)/shard_map/ppermute | solution.py:35
  119.8 3.1 %collective-permute-start.16 = (bf16[160,128]{1,0:T(8,128)(2,1)S(1)}, bf16[160,128]{1,0:T(8,128)(2,1)S(1)}, u32[]{:S(2)}, u32[]{:S(2)}) collective-permute-start(bf16[160,128]{1,0:T(8,128)(2,1)S(1)} %get-tuple-element.57), channel_id=1, source_target_pairs={{0,8},{8,0},{16,24},{24,16},{32,40},{40,32},{48,56},{56,48},{64,72... | collective-permute-start | bytes 122888 | tf_op jit(solution)/shard_map/ppermute | solution.py:35
  122.9 1.0 copy-start.3
  124.6 24.0 %collective-permute-start.17 = (bf16[256,256]{1,0:T(8,128)(2,1)S(1)}, bf16[256,256]{1,0:T(8,128)(2,1)S(1)}, u32[]{:S(2)}, u32[]{:S(2)}) collective-permute-start(bf16[256,256]{1,0:T(8,128)(2,1)S(1)} %get-tuple-element.51), channel_id=1, source_target_pairs={{0,1},{8,9},{16,17},{24,25},{32,33},{40,41},{48,49},{56,57},{64,65... | collective-permute-start | bytes 393224 | tf_op jit(solution)/shard_map/ppermute | solution.py:35
  148.6 1.2 copy-start.1
  150.5 10.4 %collective-permute-start.18 = (bf16[64,2048]{1,0:T(8,128)(2,1)S(1)}, bf16[64,2048]{1,0:T(8,128)(2,1)S(1)}, u32[]{:S(2)}, u32[]{:S(2)}) collective-permute-start(bf16[64,2048]{1,0:T(8,128)(2,1)S(1)} %get-tuple-element.54), channel_id=1, source_target_pairs={{0,2},{8,10},{16,18},{24,26},{32,34},{40,42},{48,50},{56,58},{64,6... | collective-permute-start | bytes 786440 | tf_op jit(solution)/shard_map/ppermute | solution.py:35
  152.7 11.1 %collective-permute-start.19 = (bf16[64,2048]{1,0:T(8,128)(2,1)S(1)}, bf16[64,2048]{1,0:T(8,128)(2,1)S(1)}, u32[]{:S(2)}, u32[]{:S(2)}) collective-permute-start(bf16[64,2048]{1,0:T(8,128)(2,1)S(1)} %get-tuple-element.55), channel_id=1, source_target_pairs={{0,6},{8,14},{16,22},{24,30},{32,38},{40,46},{48,54},{56,62},{64,7... | collective-permute-start | bytes 786440 | tf_op jit(solution)/shard_map/ppermute | solution.py:35
  156.4 14.2 %collective-permute-start.20 = (bf16[64,2048]{1,0:T(8,128)(2,1)S(1)}, bf16[64,2048]{1,0:T(8,128)(2,1)S(1)}, u32[]{:S(2)}, u32[]{:S(2)}) collective-permute-start(bf16[64,2048]{1,0:T(8,128)(2,1)S(1)} %get-tuple-element.56), channel_id=1, source_target_pairs={{0,4},{8,12},{16,20},{24,28},{32,36},{40,44},{48,52},{56,60},{64,6... | collective-permute-start | bytes 786440 | tf_op jit(solution)/shard_map/ppermute | solution.py:35
Sparse Core Ops, SparseCore 0:
  61.5 45.3 all-gather.1

commit v5 on v4

--- a/solution.py
+++ b/solution.py
@@ -64,7 +64,7 @@
 
 ROWS = 160
 VMEM = pl.BlockSpec(memory_space=pltpu.VMEM)
-ANY = pl.BlockSpec(memory_space=pl.ANY)
+HBM = pl.BlockSpec(memory_space=pltpu.HBM)
 SMEM = pl.BlockSpec(memory_space=pltpu.SMEM)
 
 
@@ -116,7 +116,7 @@
 
 def project_kernel(*refs):
     parts = refs[:N_TP]
-    wf, ww, table, feats_ref, qn_ref, kv_ref, tail_ref, mine_ref, other_ref, held, sems = refs[N_TP:]
+    wf, ww, table, qf_ref, kv_ref, tail_ref, mine_ref, other_ref, held, held_wf, qf, tail, sems = refs[N_TP:]
     x, half, core, _ = position()
     owners = [lax.rem(x + NX - s, NX) * 2 + side for side in (half, 1 - half) for s in (0, 1, 3, 2)]
     width = parts[0].shape[1]
@@ -125,6 +125,7 @@
         pltpu.make_async_copy(part, held.at[:, pl.ds(pl.multiple_of(owner * width, width), width)], sems.at[k])
         for k, (part, owner) in enumerate(zip(parts, owners))
     ]
+    copies.append(pltpu.make_async_copy(wf, held_wf, sems.at[N_TP]))
     for copy in copies:
         copy.start()
     for copy in copies:
@@ -134,44 +135,52 @@
     def columns(weight):
         return dot(tokens, weight).astype(bf16)
 
-    feats = columns(wf[...])
+    feats = columns(held_wf[...])
     ones = lax.broadcasted_iota(jnp.int32, feats.shape, 1) == 0
     feats = jnp.concatenate([feats, jnp.where(ones, 1.0, 0.0).astype(bf16)], axis=1)
-    feats_ref[...] = feats
-    first_tail = kv_ref.shape[0] - tail_ref.shape[0]
-    states = []
+    qf[:, 2 * head :] = feats
+    first_tail = kv_ref.shape[0] - tail.shape[0]
+    leave = [pltpu.make_async_copy(tail, tail_ref, sems.at[0]), pltpu.make_async_copy(qf, qf_ref, sems.at[1])]
     for kind in (2, 1, 0):
         out = columns(jnp.concatenate([ww[h, :, kind * head : (kind + 1) * head] for h in range(2)], axis=1))
         if kind == 2:
+            values = out
             kv_ref[:, 2 * head :] = out
-            tail_ref[:, 2 * head :] = out[first_tail:]
-            for h in range(2):
-                left = dot_t(table[h, 2], feats)
-                right = dot_t(table[h, 3], feats)
-                high, low = halves(left * right)
-                v = out[:, h * head : (h + 1) * head]
-                states.append(dot(high, v) + dot(low, v))
-            mine_ref[...] = jnp.where(core == 0, states[0], states[1])
-            other_ref[...] = jnp.where(core == 0, states[1], states[0]).astype(bf16)
+            tail[:, 2 * head :] = out[first_tail:]
             continue
         for h in range(2):
             cols = slice(h * head, (h + 1) * head)
             normed = unit(out[:, cols].astype(f32)).astype(bf16)
             if kind == 1:
                 kv_ref[:, cols] = normed
-                tail_ref[:, cols] = normed[first_tail:]
+                tail[:, cols] = normed[first_tail:]
             else:
-                qn_ref[:, cols] = normed
-
-
-def local_kernel(win, feats_ref, qn_ref, kv_ref, halo_ref, table, near_ref, win_ref, high_ref, low_ref):
+                qf[:, cols] = normed
+        leave[1 - kind].start()
+    states = []
+    for h in range(2):
+        left = dot_t(table[h, 2], feats)
+        right = dot_t(table[h, 3], feats)
+        high, low = halves(left * right)
+        v = values[:, h * head : (h + 1) * head]
+        states.append(dot(high, v) + dot(low, v))
+    mine_ref[...] = jnp.where(core == 0, states[0], states[1])
+    other_ref[...] = jnp.where(core == 0, states[1], states[0]).astype(bf16)
+    for copy in leave:
+        copy.wait()
+
+
+def local_kernel(win, qf_ref, kv_ref, halo_ref, table, near_ref, win_ref, high_ref, low_ref, qn_ref, sem):
+    copy = pltpu.make_async_copy(qf_ref, qn_ref, sem)
+    copy.start()
+    copy.wait()
     seq = position()[3]
     rows = qn_ref.shape[0]
     heads = win_ref.shape[1] // 128
     head = 128
     halo = halo_ref.shape[0]
     span = halo + BLOCK
-    feats = feats_ref[...]
+    feats = qn_ref[:, heads * head :]
     feat = feats.shape[1] // (4 * heads)
     blocks = rows // BLOCK
     row = lax.broadcasted_iota(jnp.int32, (BLOCK, span), 0)
@@ -226,17 +235,19 @@
         away_ref[s * rows : (s + 1) * rows] = hidden[group + 1 - half]
 
 
-def product_kernel(keep_ref, got_ref, w_ref, w_got_ref, *outs):
+def product_kernel(hidden_ref, w_ref, *outs):
     rows = outs[0].shape[0]
-    product = (dot(keep_ref[...], w_ref[...]) + dot(got_ref[...], w_got_ref[...])).astype(bf16)
+    product = dot(hidden_ref[...], w_ref[...]).astype(bf16)
     for s, out in enumerate(outs):
         out[...] = product[s * rows : (s + 1) * rows]
 
 
-def prefix(mine, other, place, beside):
+def prefix(mine, other, place, halo, beside):
     x, h, y, z, c = place
     got = send(other, to_core).astype(f32)
     total = mine + got
+    add = (jnp.where(c == 0, mine, 0.0), jnp.where(c == 1, got, 0.0))
+    total, add = lax.optimization_barrier((total, add))
     before = jnp.zeros_like(total)
     done = None
     for flip in (1, 2, 4):
@@ -245,14 +256,17 @@
             part, done = lax.optimization_barrier((part, done))
         part = part.astype(f32)
         before = before + jnp.where((z ^ flip) < z, part, 0.0)
-        total = total + part
+        total, before = lax.optimization_barrier((total + part, before))
         if flip == 1:
-            done = beside(total)
+            total, halo = lax.optimization_barrier((total, halo))
+        if flip == 2:
+            total, halo = lax.optimization_barrier((total, halo))
+            done = beside(halo)
     short = total.astype(bf16)
     for steps in (1, 2, 3):
         before = before + send(short, to_y(steps)).astype(f32)
-    theirs = send((before + jnp.where(c == 0, mine, 0.0)).astype(bf16), to_core)
-    ours = before + jnp.where(c == 1, got, 0.0)
+    theirs = send((before + add[0]).astype(bf16), to_core)
+    ours = before + add[1]
     return ours, theirs, done
 
 
@@ -263,27 +277,33 @@
 def project(parts, wf, ww, tables):
     tok_rows = parts[0].shape[0]
     wide = 2 * ww.shape[2] // 3
-    halo_rows = (WMAX - 1) * BLOCK
+    queries = shape((tok_rows, wide + 2 * wf.shape[1]), bf16)
+    tail = shape(((WMAX - 1) * BLOCK, 2 * wide), bf16)
     return pl.pallas_call(
         project_kernel,
         out_shape=(
-            shape((tok_rows, 2 * wf.shape[1]), bf16),
-            shape((tok_rows, wide), bf16),
+            queries,
             shape((tok_rows, 2 * wide), bf16),
-            shape((halo_rows, 2 * wide), bf16),
+            tail,
             shape((ROWS, wide // 2), f32),
             shape((ROWS, wide // 2), bf16),
         ),
-        in_specs=[ANY] * N_TP + [VMEM] * 3,
-        out_specs=(VMEM,) * 6,
-        scratch_shapes=[pltpu.VMEM((tok_rows, wf.shape[0]), bf16), pltpu.SemaphoreType.DMA((N_TP,))],
+        in_specs=[HBM] * (N_TP + 1) + [VMEM] * 2,
+        out_specs=(HBM, VMEM, HBM, VMEM, VMEM),
+        scratch_shapes=[
+            pltpu.VMEM((tok_rows, wf.shape[0]), bf16),
+            pltpu.VMEM(wf.shape, bf16),
+            pltpu.VMEM(queries.shape, bf16),
+            pltpu.VMEM(tail.shape, bf16),
+            pltpu.SemaphoreType.DMA((N_TP + 1,)),
+        ],
         name="project",
         compiler_params=pltpu.CompilerParams(vmem_limit_bytes=LIMIT),
     )(*parts, wf, ww, tables.astype(bf16))
 
 
-def near(win_blocks, feats, qn, kv, halo, tables):
-    tok_rows, wide = qn.shape
+def near(win_blocks, qf, kv, halo, tables):
+    tok_rows, wide = kv.shape[0], kv.shape[1] // 2
     return pl.pallas_call(
         local_kernel,
         out_shape=(
@@ -292,11 +312,12 @@
             shape((2, tok_rows, ROWS), bf16),
             shape((2, tok_rows, ROWS), bf16),
         ),
-        in_specs=[SMEM] + [VMEM] * 5,
+        in_specs=[SMEM, HBM, VMEM, VMEM, VMEM],
         out_specs=(VMEM,) * 4,
+        scratch_shapes=[pltpu.VMEM(qf.shape, bf16), pltpu.SemaphoreType.DMA],
         name="near",
         compiler_params=pltpu.CompilerParams(vmem_limit_bytes=LIMIT),
-    )(win_blocks, feats, qn, kv, halo, tables.astype(bf16))
+    )(win_blocks, qf, kv, halo, tables.astype(bf16))
 
 
 def hidden_rows(ours, theirs, near_out, win_out, high, low):
@@ -312,18 +333,18 @@
     )(ours, theirs, near_out, win_out, high, low)
 
 
-def product(keep, got, w_out, w_got):
+def product(hidden, w_out):
     return pl.pallas_call(
         product_kernel,
-        out_shape=(shape((keep.shape[0] // NX, w_out.shape[1]), bf16),) * NX,
-        in_specs=[VMEM] * 4,
+        out_shape=(shape((hidden.shape[0] // NX, w_out.shape[1]), bf16),) * NX,
+        in_specs=[VMEM] * 2,
         out_specs=(VMEM,) * NX,
         name="product",
         compiler_params=pltpu.CompilerParams(vmem_limit_bytes=LIMIT),
-    )(keep, got, w_out, w_got)
-
-
-LIMIT = 16 * 2**20
+    )(hidden, w_out)
+
+
+LIMIT = 12 * 2**20
 
 
 def local(tokens, w_feature, w_window, w_out, win_blocks):
@@ -335,30 +356,28 @@
     other = send(tokens, to_half)
     parts = [tokens] + [send(tokens, to_x(s)) for s in (1, 3, 2)]
     w_out = w_out.reshape(-1, model_width)
-    piece_rows = w_out.shape[0] // (2 * NY)
-    piece = lax.dynamic_slice_in_dim(w_out, (y * 2 + c) * piece_rows, piece_rows, 0)
-    other, piece = lax.optimization_barrier((other, piece))
     parts += [other] + [send(other, to_x(s)) for s in (1, 3, 2)]
-    piece = send(piece, to_half)
     tables = feature_maps(feat_dim, head_count)
-    feats, qn, kv, tail, mine, theirs = project(
+    qf, kv, tail, mine, theirs = project(
         parts, w_feature.reshape(model_width, -1), w_window.transpose(1, 0, 2), tables
     )
 
-    def beside(total):
-        halo, _ = lax.optimization_barrier((send(tail, to_next), total))
-        return near(win_blocks, feats, qn, kv, halo, tables[:, :2])
-
-    mine, piece = lax.optimization_barrier((mine, piece))
-    alike = [[(row * NZ + at) * 2 + core for row in range(NY) for core in range(2)] for at in range(NZ)]
-    w_got = lax.all_gather(piece, "seq", axis=0, axis_index_groups=alike, tiled=True)
-    ours, theirs, attended = prefix(mine, theirs, (x, h, y, z, c), beside)
+    def beside(halo):
+        return near(win_blocks, qf, kv, halo, tables)
+
+    ours, theirs, attended = prefix(mine, theirs, (x, h, y, z, c), send(tail, to_next), beside)
     keep, away = hidden_rows(ours, theirs, *attended)
-    products = product(keep, send(away, to_half), w_out, w_got)
-    total = products[0].astype(f32)
-    for steps in (1, 3, 2):
-        total = total + send(products[steps], to_x(steps)).astype(f32)
-    return total.astype(bf16)
+
+    def summed(total, group):
+        for steps in (1, 3, 2):
+            total = total + send(group[steps], to_x(steps)).astype(f32)
+        return total.astype(bf16)
+
+    group = product(away, w_out)
+    away, keep = lax.optimization_barrier((summed(group[0].astype(f32), group), keep))
+    group = product(keep, w_out)
+    total = lax.optimization_barrier(group[0].astype(f32) + send(away, to_half).astype(f32))
+    return summed(total, group)
 
 
 def solution(mesh):

time: 179 us -> 165 us (0.922)
  the two profiles are of different devices: /device:TPU:10 before, /device:TPU:46 now
where the time goes in v5:
time: 165 us
  starting transfers between devices  88.3 us (54%)
  waiting for transfers between devices  56.3 us (34%)
  Pallas kernels  10.8 us (7%)
  local copies, waits for them, and re-layouts  7.65 us (5%)
    ppermute x23, starting transfers between devices, send(): return lax.ppermute(value, ('seq', 'tp'), pairs(move))  88.3 us
    ppermute x23, waiting for transfers between devices, send(): return lax.ppermute(value, ('seq', 'tp'), pairs(move))  56.3 us
    unnamed x19, local copies, waits for them, and re-layouts  6.43 us
    pallas_call x1, Pallas kernels, project(): pl.pallas_call(project_kernel, out_shape=(queries, shape((tok_rows, 2 * w...  5.3 us
    pallas_call x1, Pallas kernels, near(): pl.pallas_call(local_kernel, out_shape=(shape((tok_rows, wide), f32), sha...  3.98 us
  transfers between devices with their start and end apart: 23, of which 11 were waited for; matrix products, arithmetic and copies ran while one was open for 2% of the time, Pallas kernels for 3%

profile of v5, /device:TPU:46, one launch (start us, length us, event | category | flops | bytes accessed | tf_op | source)
XLA Modules:
  0.0 164.7 jit_solution(3822321157995050507)
XLA Ops:
  0.0 14.8 %collective-permute-start.3 = (bf16[512,256]{1,0:T(8,128)(2,1)}, bf16[512,256]{1,0:T(8,128)(2,1)S(1)}, u32[]{:S(2)}, u32[]{:S(2)}) collective-permute-start(bf16[512,256]{1,0:T(8,128)(2,1)} %refs_0_.1), channel_id=1, source_target_pairs={{0,1},{8,9},{16,17},{24,25},{32,33},{40,41},{48,49},{56,57},{64,65... | collective-permute-start | bytes 786440 | tf_op jit(solution)/shard_map/ppermute | solution.py:35
  14.8 2.4 %collective-permute-start = (bf16[512,256]{1,0:T(8,128)(2,1)}, bf16[512,256]{1,0:T(8,128)(2,1)S(1)}, u32[]{:S(2)}, u32[]{:S(2)}) collective-permute-start(bf16[512,256]{1,0:T(8,128)(2,1)} %refs_0_.1), channel_id=1, source_target_pairs={{0,2},{8,10},{16,18},{24,26},{32,34},{40,42},{48,50},{56,58},{64,6... | collective-permute-start | bytes 786440 | tf_op jit(solution)/shard_map/ppermute | solution.py:35
  17.2 3.5 %collective-permute-start.1 = (bf16[512,256]{1,0:T(8,128)(2,1)}, bf16[512,256]{1,0:T(8,128)(2,1)S(1)}, u32[]{:S(2)}, u32[]{:S(2)}) collective-permute-start(bf16[512,256]{1,0:T(8,128)(2,1)} %refs_0_.1), channel_id=1, source_target_pairs={{0,6},{8,14},{16,22},{24,30},{32,38},{40,46},{48,54},{56,62},{64,7... | collective-permute-start | bytes 786440 | tf_op jit(solution)/shard_map/ppermute | solution.py:35
  20.7 3.3 %collective-permute-start.2 = (bf16[512,256]{1,0:T(8,128)(2,1)}, bf16[512,256]{1,0:T(8,128)(2,1)S(1)}, u32[]{:S(2)}, u32[]{:S(2)}) collective-permute-start(bf16[512,256]{1,0:T(8,128)(2,1)} %refs_0_.1), channel_id=1, source_target_pairs={{0,4},{8,12},{16,20},{24,28},{32,36},{40,44},{48,52},{56,60},{64,6... | collective-permute-start | bytes 786440 | tf_op jit(solution)/shard_map/ppermute | solution.py:35
  24.0 14.4 %collective-permute-done.3.refs_4_ = bf16[512,256]{1,0:T(8,128)(2,1)S(1)} collective-permute-done((bf16[512,256]{1,0:T(8,128)(2,1)}, bf16[512,256]{1,0:T(8,128)(2,1)S(1)}, u32[]{:S(2)}, u32[]{:S(2)}) %collective-permute-start.3) | collective-permute-done | bytes 262176 | tf_op jit(solution)/shard_map/ppermute | solution.py:35
  38.4 2.4 %collective-permute-start.4 = (bf16[512,256]{1,0:T(8,128)(2,1)S(1)}, bf16[512,256]{1,0:T(8,128)(2,1)S(1)}, u32[]{:S(2)}, u32[]{:S(2)}) collective-permute-start(bf16[512,256]{1,0:T(8,128)(2,1)S(1)} %collective-permute-done.3.refs_4_), channel_id=1, source_target_pairs={{0,2},{8,10},{16,18},{24,26},{32,34},{40,42},{48,50},{56,58},{64,6... | collective-permute-start | bytes 786440 | tf_op jit(solution)/shard_map/ppermute | solution.py:35
  40.8 3.5 %collective-permute-start.5 = (bf16[512,256]{1,0:T(8,128)(2,1)S(1)}, bf16[512,256]{1,0:T(8,128)(2,1)S(1)}, u32[]{:S(2)}, u32[]{:S(2)}) collective-permute-start(bf16[512,256]{1,0:T(8,128)(2,1)S(1)} %collective-permute-done.3.refs_4_), channel_id=1, source_target_pairs={{0,6},{8,14},{16,22},{24,30},{32,38},{40,46},{48,54},{56,62},{64,7... | collective-permute-start | bytes 786440 | tf_op jit(solution)/shard_map/ppermute | solution.py:35
  44.3 0.0 collective-permute-done.refs_1_
  44.3 3.3 %collective-permute-start.6 = (bf16[512,256]{1,0:T(8,128)(2,1)S(1)}, bf16[512,256]{1,0:T(8,128)(2,1)S(1)}, u32[]{:S(2)}, u32[]{:S(2)}) collective-permute-start(bf16[512,256]{1,0:T(8,128)(2,1)S(1)} %collective-permute-done.3.refs_4_), channel_id=1, source_target_pairs={{0,4},{8,12},{16,20},{24,28},{32,36},{40,44},{48,52},{56,60},{64,6... | collective-permute-start | bytes 786440 | tf_op jit(solution)/shard_map/ppermute | solution.py:35
  47.6 1.2 copy.11.refs_8_
  48.8 0.0 copy-start.1
  48.8 0.0 copy-start.2
  48.8 2.4 %copy.13 = bf16[2048,2,384]{2,0,1:T(8,128)(2,1)S(1)} copy(bf16[2048,2,384]{2,1,0:T(2,128)(2,1)} %param.9) | data formatting | bytes 6291456 | tf_op args[2]
  51.2 0.0 collective-permute-done.1.refs_2_
  51.2 0.0 collective-permute-done.2.refs_3_
  51.2 0.0 collective-permute-done.4.refs_5_
  51.2 5.3 %collective-permute-done.5.refs_6_ = bf16[512,256]{1,0:T(8,128)(2,1)S(1)} collective-permute-done((bf16[512,256]{1,0:T(8,128)(2,1)S(1)}, bf16[512,256]{1,0:T(8,128)(2,1)S(1)}, u32[]{:S(2)}, u32[]{:S(2)}) %collective-permute-start.5) | collective-permute-done | bytes 262176 | tf_op jit(solution)/shard_map/ppermute | solution.py:35
  56.5 0.7 copy-done.3
  57.2 0.0 collective-permute-done.6.refs_7_
  57.2 0.7 copy-done.5
  57.9 0.0 copy-done.1
  57.9 0.9 copy-done.4
  58.9 0.9 copy-done.6
  59.8 5.3 %project.1 = (bf16[512,384]{1,0:T(8,128)(2,1)S(1)}, bf16[512,512]{1,0:T(8,128)(2,1)S(1)}, bf16[384,512]{1,0:T(8,128)(2,1)S(1)}, f32[160,128]{1,0:T(8,128)S(1)}, bf16[160,128]{1,0:T(8,128)(2,1)S(1)}) custom-call(bf16[512,256]{1,0:T(8,128)(2,1)S(1)} %copy-done.2, bf16[512,256]{1,0:T(8,128)(2,1)S(1)} %collective-permute-done.refs_1_, ...), custom_call_target="tpu_custom_call" | custom-call | tf_op jit(solution)/shard_map/project/pallas_call | solution.py:282
  65.2 0.7 copy-done.8
  65.9 2.0 %collective-permute-start.7 = (bf16[160,128]{1,0:T(8,128)(2,1)S(1)}, bf16[160,128]{1,0:T(8,128)(2,1)S(1)}, u32[]{:S(2)}, u32[]{:S(2)}) collective-permute-start(bf16[160,128]{1,0:T(8,128)(2,1)S(1)} %get-tuple-element.45), channel_id=1, source_target_pairs={{0,8},{8,0},{16,24},{24,16},{32,40},{40,32},{48,56},{56,48},{64,72... | collective-permute-start | bytes 122888 | tf_op jit(solution)/shard_map/ppermute | solution.py:35
  68.0 2.4 %collective-permute-start.9 = (bf16[384,512]{1,0:T(8,128)(2,1)}, bf16[384,512]{1,0:T(8,128)(2,1)S(1)}, u32[]{:S(2)}, u32[]{:S(2)}) collective-permute-start(bf16[384,512]{1,0:T(8,128)(2,1)} %copy-done.8), channel_id=1, source_target_pairs={{0,8},{8,16},{16,24},{24,32},{32,40},{40,48},{48,56},{56,64},{64,7... | collective-permute-start | bytes 1179656 | tf_op jit(solution)/shard_map/ppermute | solution.py:35
  70.4 0.0 collective-permute-done.7
  70.4 1.9 %collective-permute-start.8 = (bf16[160,128]{1,0:T(8,128)(2,1)S(1)}, bf16[160,128]{1,0:T(8,128)(2,1)S(1)}, u32[]{:S(2)}, u32[]{:S(2)}) collective-permute-start(bf16[160,128]{1,0:T(8,128)(2,1)S(1)} %convert_element_type.70), channel_id=1, source_target_pairs={{0,16},{8,24},{16,0},{24,8},{32,48},{40,56},{48,32},{56,40},{64,80... | collective-permute-start | bytes 122888 | tf_op jit(solution)/shard_map/ppermute | solution.py:35
  72.4 4.4 %collective-permute-done.8 = bf16[160,128]{1,0:T(8,128)(2,1)S(1)} collective-permute-done((bf16[160,128]{1,0:T(8,128)(2,1)S(1)}, bf16[160,128]{1,0:T(8,128)(2,1)S(1)}, u32[]{:S(2)}, u32[]{:S(2)}) %collective-permute-start.8) | collective-permute-done | bytes 40992 | tf_op jit(solution)/shard_map/ppermute | solution.py:35
  76.9 0.9 collective-permute-done.9.halo_ref
  77.7 1.9 %collective-permute-start.10 = (bf16[160,128]{1,0:T(8,128)(2,1)S(1)}, bf16[160,128]{1,0:T(8,128)(2,1)S(1)}, u32[]{:S(2)}, u32[]{:S(2)}) collective-permute-start(bf16[160,128]{1,0:T(8,128)(2,1)S(1)} %convert_element_type.72), channel_id=1, source_target_pairs={{0,32},{8,40},{16,48},{24,56},{32,0},{40,8},{48,16},{56,24},{64,96... | collective-permute-start | bytes 122888 | tf_op jit(solution)/shard_map/ppermute | solution.py:35
  79.6 4.9 %collective-permute-done.10 = bf16[160,128]{1,0:T(8,128)(2,1)S(1)} collective-permute-done((bf16[160,128]{1,0:T(8,128)(2,1)S(1)}, bf16[160,128]{1,0:T(8,128)(2,1)S(1)}, u32[]{:S(2)}, u32[]{:S(2)}) %collective-permute-start.10) | collective-permute-done | bytes 40992 | tf_op jit(solution)/shard_map/ppermute | solution.py:35
  84.5 5.4 %collective-permute-start.11 = (bf16[160,128]{1,0:T(8,128)(2,1)S(1)}, bf16[160,128]{1,0:T(8,128)(2,1)S(1)}, u32[]{:S(2)}, u32[]{:S(2)}) collective-permute-start(bf16[160,128]{1,0:T(8,128)(2,1)S(1)} %convert_element_type.74), channel_id=1, source_target_pairs={{0,64},{8,72},{16,80},{24,88},{32,96},{40,104},{48,112},{56,120},{... | collective-permute-start | bytes 122888 | tf_op jit(solution)/shard_map/ppermute | solution.py:35
  90.0 4.0 %near.1 = (f32[512,256]{1,0:T(8,128)S(1)}, f32[512,256]{1,0:T(8,128)S(1)}, bf16[2,512,160]{2,1,0:T(8,128)(2,1)S(1)}, bf16[2,512,160]{2,1,0:T(8,128)(2,1)S(1)}) custom-call(s32[2]{0:T(128)S(1)} %copy-done.7, bf16[512,384]{1,0:T(8,128)(2,1)S(1)} %get-tuple-element.54.qf_ref, bf16[512,512]{1,0:T(8,128)(2,1)S(1)} %get-tuple-element.55.kv_ref, ...), custom_call_target="tpu_custom_call" | custom-call | tf_op jit(solution)/shard_map/near/pallas_call | solution.py:307
  94.0 0.8 collective-permute-done.11
  94.8 0.7 collective-permute-start.14
  95.4 4.8 %collective-permute-start.13 = (bf16[160,128]{1,0:T(8,128)(2,1)S(1)}, bf16[160,128]{1,0:T(8,128)(2,1)S(1)}, u32[]{:S(2)}, u32[]{:S(2)}) collective-permute-start(bf16[160,128]{1,0:T(8,128)(2,1)S(1)} %convert_add_fusion.1), channel_id=1, source_target_pairs={{0,256},{8,264},{16,272},{24,280},{32,288},{40,296},{48,304},{56,3... | collective-permute-start | bytes 122888 | tf_op jit(solution)/shard_map/ppermute | solution.py:35
  100.3 1.9 %collective-permute-start.12 = (bf16[160,128]{1,0:T(8,128)(2,1)S(1)}, bf16[160,128]{1,0:T(8,128)(2,1)S(1)}, u32[]{:S(2)}, u32[]{:S(2)}) collective-permute-start(bf16[160,128]{1,0:T(8,128)(2,1)S(1)} %convert_add_fusion.1), channel_id=1, source_target_pairs={{0,128},{8,136},{16,144},{24,152},{32,160},{40,168},{48,176},{56,1... | collective-permute-start | bytes 122888 | tf_op jit(solution)/shard_map/ppermute | solution.py:35
  102.2 0.0 collective-permute-done.14
  102.2 0.0 collective-permute-done.13
  102.2 3.9 %collective-permute-done.12 = bf16[160,128]{1,0:T(8,128)(2,1)S(1)} collective-permute-done((bf16[160,128]{1,0:T(8,128)(2,1)S(1)}, bf16[160,128]{1,0:T(8,128)(2,1)S(1)}, u32[]{:S(2)}, u32[]{:S(2)}) %collective-permute-start.12) | collective-permute-done | bytes 40992 | tf_op jit(solution)/shard_map/ppermute | solution.py:35
  106.2 1.9 %collective-permute-start.15 = (bf16[160,128]{1,0:T(8,128)(2,1)S(1)}, bf16[160,128]{1,0:T(8,128)(2,1)S(1)}, u32[]{:S(2)}, u32[]{:S(2)}) collective-permute-start(bf16[160,128]{1,0:T(8,128)(2,1)S(1)} %get-tuple-element.83), channel_id=1, source_target_pairs={{0,8},{8,0},{16,24},{24,16},{32,40},{40,32},{48,56},{56,48},{64,72... | collective-permute-start | bytes 122888 | tf_op jit(solution)/shard_map/ppermute | solution.py:35
  108.1 1.2 collective-permute-done.15.theirs
  109.3 0.7 hidden.1
  110.0 0.4 product.2
  110.5 3.1 %collective-permute-start.18 = (bf16[64,2048]{1,0:T(8,128)(2,1)S(1)}, bf16[64,2048]{1,0:T(8,128)(2,1)S(1)}, u32[]{:S(2)}, u32[]{:S(2)}) collective-permute-start(bf16[64,2048]{1,0:T(8,128)(2,1)S(1)} %get-tuple-element.75), channel_id=1, source_target_pairs={{0,4},{8,12},{16,20},{24,28},{32,36},{40,44},{48,52},{56,60},{64,6... | collective-permute-start | bytes 786440 | tf_op jit(solution)/shard_map/ppermute | solution.py:35
  113.5 1.9 %collective-permute-start.17 = (bf16[64,2048]{1,0:T(8,128)(2,1)S(1)}, bf16[64,2048]{1,0:T(8,128)(2,1)S(1)}, u32[]{:S(2)}, u32[]{:S(2)}) collective-permute-start(bf16[64,2048]{1,0:T(8,128)(2,1)S(1)} %get-tuple-element.74), channel_id=1, source_target_pairs={{0,6},{8,14},{16,22},{24,30},{32,38},{40,46},{48,54},{56,62},{64,7... | collective-permute-start | bytes 786440 | tf_op jit(solution)/shard_map/ppermute | solution.py:35
  115.5 5.1 %collective-permute-start.16 = (bf16[64,2048]{1,0:T(8,128)(2,1)S(1)}, bf16[64,2048]{1,0:T(8,128)(2,1)S(1)}, u32[]{:S(2)}, u32[]{:S(2)}) collective-permute-start(bf16[64,2048]{1,0:T(8,128)(2,1)S(1)} %get-tuple-element.73), channel_id=1, source_target_pairs={{0,2},{8,10},{16,18},{24,26},{32,34},{40,42},{48,50},{56,58},{64,6... | collective-permute-start | bytes 786440 | tf_op jit(solution)/shard_map/ppermute | solution.py:35
  120.6 2.5 %collective-permute-done.18 = bf16[64,2048]{1,0:T(8,128)(2,1)S(1)} collective-permute-done((bf16[64,2048]{1,0:T(8,128)(2,1)S(1)}, bf16[64,2048]{1,0:T(8,128)(2,1)S(1)}, u32[]{:S(2)}, u32[]{:S(2)}) %collective-permute-start.18) | collective-permute-done | bytes 262176 | tf_op jit(solution)/shard_map/ppermute | solution.py:35
  123.1 4.8 %collective-permute-done.17 = bf16[64,2048]{1,0:T(8,128)(2,1)S(1)} collective-permute-done((bf16[64,2048]{1,0:T(8,128)(2,1)S(1)}, bf16[64,2048]{1,0:T(8,128)(2,1)S(1)}, u32[]{:S(2)}, u32[]{:S(2)}) %collective-permute-start.17) | collective-permute-done | bytes 262176 | tf_op jit(solution)/shard_map/ppermute | solution.py:35
  127.9 0.0 collective-permute-done.16
  127.9 0.1 add_convert_fusion.1
  128.0 12.0 %collective-permute-start.19 = (bf16[64,2048]{1,0:T(8,128)(2,1)S(1)}, bf16[64,2048]{1,0:T(8,128)(2,1)S(1)}, u32[]{:S(2)}, u32[]{:S(2)}) collective-permute-start(bf16[64,2048]{1,0:T(8,128)(2,1)S(1)} %add_convert_fusion.1), channel_id=1, source_target_pairs={{0,1},{8,9},{16,17},{24,25},{32,33},{40,41},{48,49},{56,57},{64,65... | collective-permute-start | bytes 786440 | tf_op jit(solution)/shard_map/ppermute | solution.py:35
  140.0 0.4 product.3
  140.4 3.0 %collective-permute-start.22 = (bf16[64,2048]{1,0:T(8,128)(2,1)S(1)}, bf16[64,2048]{1,0:T(8,128)(2,1)S(1)}, u32[]{:S(2)}, u32[]{:S(2)}) collective-permute-start(bf16[64,2048]{1,0:T(8,128)(2,1)S(1)} %get-tuple-element.82), channel_id=1, source_target_pairs={{0,4},{8,12},{16,20},{24,28},{32,36},{40,44},{48,52},{56,60},{64,6... | collective-permute-start | bytes 786440 | tf_op jit(solution)/shard_map/ppermute | solution.py:35
  143.5 3.4 %collective-permute-start.21 = (bf16[64,2048]{1,0:T(8,128)(2,1)S(1)}, bf16[64,2048]{1,0:T(8,128)(2,1)S(1)}, u32[]{:S(2)}, u32[]{:S(2)}) collective-permute-start(bf16[64,2048]{1,0:T(8,128)(2,1)S(1)} %get-tuple-element.81), channel_id=1, source_target_pairs={{0,6},{8,14},{16,22},{24,30},{32,38},{40,46},{48,54},{56,62},{64,7... | collective-permute-start | bytes 786440 | tf_op jit(solution)/shard_map/ppermute | solution.py:35
  146.8 3.7 %collective-permute-start.20 = (bf16[64,2048]{1,0:T(8,128)(2,1)S(1)}, bf16[64,2048]{1,0:T(8,128)(2,1)S(1)}, u32[]{:S(2)}, u32[]{:S(2)}) collective-permute-start(bf16[64,2048]{1,0:T(8,128)(2,1)S(1)} %get-tuple-element.80), channel_id=1, source_target_pairs={{0,2},{8,10},{16,18},{24,26},{32,34},{40,42},{48,50},{56,58},{64,6... | collective-permute-start | bytes 786440 | tf_op jit(solution)/shard_map/ppermute | solution.py:35
  150.5 13.2 %collective-permute-done.19 = bf16[64,2048]{1,0:T(8,128)(2,1)S(1)} collective-permute-done((bf16[64,2048]{1,0:T(8,128)(2,1)S(1)}, bf16[64,2048]{1,0:T(8,128)(2,1)S(1)}, u32[]{:S(2)}, u32[]{:S(2)}) %collective-permute-start.19) | collective-permute-done | bytes 262176 | tf_op jit(solution)/shard_map/ppermute | solution.py:35
  163.8 0.1 convert_add_fusion
  163.8 0.0 collective-permute-done.22
  163.8 0.0 collective-permute-done.21
  163.8 0.0 collective-permute-done.20
  163.9 0.8 add_convert_fusion
  (19 shorter events, 0.2 us)
Async XLA Ops:
  0.0 38.4 %collective-permute-start.3 = (bf16[512,256]{1,0:T(8,128)(2,1)}, bf16[512,256]{1,0:T(8,128)(2,1)S(1)}, u32[]{:S(2)}, u32[]{:S(2)}) collective-permute-start(bf16[512,256]{1,0:T(8,128)(2,1)} %refs_0_.1), channel_id=1, source_target_pairs={{0,1},{8,9},{16,17},{24,25},{32,33},{40,41},{48,49},{56,57},{64,65... | collective-permute-start | bytes 786440 | tf_op jit(solution)/shard_map/ppermute | solution.py:35
  14.8 29.4 %collective-permute-start = (bf16[512,256]{1,0:T(8,128)(2,1)}, bf16[512,256]{1,0:T(8,128)(2,1)S(1)}, u32[]{:S(2)}, u32[]{:S(2)}) collective-permute-start(bf16[512,256]{1,0:T(8,128)(2,1)} %refs_0_.1), channel_id=1, source_target_pairs={{0,2},{8,10},{16,18},{24,26},{32,34},{40,42},{48,50},{56,58},{64,6... | collective-permute-start | bytes 786440 | tf_op jit(solution)/shard_map/ppermute | solution.py:35
  17.2 34.0 %collective-permute-start.1 = (bf16[512,256]{1,0:T(8,128)(2,1)}, bf16[512,256]{1,0:T(8,128)(2,1)S(1)}, u32[]{:S(2)}, u32[]{:S(2)}) collective-permute-start(bf16[512,256]{1,0:T(8,128)(2,1)} %refs_0_.1), channel_id=1, source_target_pairs={{0,6},{8,14},{16,22},{24,30},{32,38},{40,46},{48,54},{56,62},{64,7... | collective-permute-start | bytes 786440 | tf_op jit(solution)/shard_map/ppermute | solution.py:35
  20.7 30.5 %collective-permute-start.2 = (bf16[512,256]{1,0:T(8,128)(2,1)}, bf16[512,256]{1,0:T(8,128)(2,1)S(1)}, u32[]{:S(2)}, u32[]{:S(2)}) collective-permute-start(bf16[512,256]{1,0:T(8,128)(2,1)} %refs_0_.1), channel_id=1, source_target_pairs={{0,4},{8,12},{16,20},{24,28},{32,36},{40,44},{48,52},{56,60},{64,6... | collective-permute-start | bytes 786440 | tf_op jit(solution)/shard_map/ppermute | solution.py:35
  38.4 12.8 %collective-permute-start.4 = (bf16[512,256]{1,0:T(8,128)(2,1)S(1)}, bf16[512,256]{1,0:T(8,128)(2,1)S(1)}, u32[]{:S(2)}, u32[]{:S(2)}) collective-permute-start(bf16[512,256]{1,0:T(8,128)(2,1)S(1)} %collective-permute-done.3.refs_4_), channel_id=1, source_target_pairs={{0,2},{8,10},{16,18},{24,26},{32,34},{40,42},{48,50},{56,58},{64,6... | collective-permute-start | bytes 786440 | tf_op jit(solution)/shard_map/ppermute | solution.py:35
  40.8 15.7 %collective-permute-start.5 = (bf16[512,256]{1,0:T(8,128)(2,1)S(1)}, bf16[512,256]{1,0:T(8,128)(2,1)S(1)}, u32[]{:S(2)}, u32[]{:S(2)}) collective-permute-start(bf16[512,256]{1,0:T(8,128)(2,1)S(1)} %collective-permute-done.3.refs_4_), channel_id=1, source_target_pairs={{0,6},{8,14},{16,22},{24,30},{32,38},{40,46},{48,54},{56,62},{64,7... | collective-permute-start | bytes 786440 | tf_op jit(solution)/shard_map/ppermute | solution.py:35
  44.3 13.0 %collective-permute-start.6 = (bf16[512,256]{1,0:T(8,128)(2,1)S(1)}, bf16[512,256]{1,0:T(8,128)(2,1)S(1)}, u32[]{:S(2)}, u32[]{:S(2)}) collective-permute-start(bf16[512,256]{1,0:T(8,128)(2,1)S(1)} %collective-permute-done.3.refs_4_), channel_id=1, source_target_pairs={{0,4},{8,12},{16,20},{24,28},{32,36},{40,44},{48,52},{56,60},{64,6... | collective-permute-start | bytes 786440 | tf_op jit(solution)/shard_map/ppermute | solution.py:35
  48.8 9.1 %copy-start.1 = (bf16[2,4,160,128]{3,2,1,0:T(8,128)(2,1)S(1)}, bf16[2,4,160,128]{3,2,1,0:T(8,128)(2,1)}, u32[]{:S(2)}) copy-start(bf16[2,4,160,128]{3,2,1,0:T(8,128)(2,1)} %constant.48.clone.refs_10_.table) | copy-start | bytes 983044
  48.8 9.1 %copy-start.2 = (bf16[512,256]{1,0:T(8,128)(2,1)S(1)}, bf16[512,256]{1,0:T(8,128)(2,1)}, u32[]{:S(2)}) copy-start(bf16[512,256]{1,0:T(8,128)(2,1)} %refs_0_.1) | copy-start | bytes 786436
  56.5 0.7 copy-start.3
  57.2 0.7 copy-start.5
  57.9 1.0 copy-start.4
  58.9 0.9 copy-start.6
  59.8 30.1 %copy-start.7 = (s32[2]{0:T(128)S(1)}, s32[2]{0:T(128)}, u32[]{:S(2)}) copy-start(s32[2]{0:T(128)} %win.1) | copy-start | bytes 28
  65.2 0.8 copy-start.8
  65.9 44.1 %copy-start = (bf16[2,128,2048]{2,1,0:T(8,128)(2,1)S(1)}, bf16[2,128,2048]{2,1,0:T(8,128)(2,1)}, u32[]{:S(2)}) copy-start(bf16[2,128,2048]{2,1,0:T(8,128)(2,1)} %param.10) | copy-start | bytes 3145732
  65.9 4.5 %collective-permute-start.7 = (bf16[160,128]{1,0:T(8,128)(2,1)S(1)}, bf16[160,128]{1,0:T(8,128)(2,1)S(1)}, u32[]{:S(2)}, u32[]{:S(2)}) collective-permute-start(bf16[160,128]{1,0:T(8,128)(2,1)S(1)} %get-tuple-element.45), channel_id=1, source_target_pairs={{0,8},{8,0},{16,24},{24,16},{32,40},{40,32},{48,56},{56,48},{64,72... | collective-permute-start | bytes 122888 | tf_op jit(solution)/shard_map/ppermute | solution.py:35
  68.0 9.7 %collective-permute-start.9 = (bf16[384,512]{1,0:T(8,128)(2,1)}, bf16[384,512]{1,0:T(8,128)(2,1)S(1)}, u32[]{:S(2)}, u32[]{:S(2)}) collective-permute-start(bf16[384,512]{1,0:T(8,128)(2,1)} %copy-done.8), channel_id=1, source_target_pairs={{0,8},{8,16},{16,24},{24,32},{32,40},{40,48},{48,56},{56,64},{64,7... | collective-permute-start | bytes 1179656 | tf_op jit(solution)/shard_map/ppermute | solution.py:35
  70.4 6.4 %collective-permute-start.8 = (bf16[160,128]{1,0:T(8,128)(2,1)S(1)}, bf16[160,128]{1,0:T(8,128)(2,1)S(1)}, u32[]{:S(2)}, u32[]{:S(2)}) collective-permute-start(bf16[160,128]{1,0:T(8,128)(2,1)S(1)} %convert_element_type.70), channel_id=1, source_target_pairs={{0,16},{8,24},{16,0},{24,8},{32,48},{40,56},{48,32},{56,40},{64,80... | collective-permute-start | bytes 122888 | tf_op jit(solution)/shard_map/ppermute | solution.py:35
  77.7 6.8 %collective-permute-start.10 = (bf16[160,128]{1,0:T(8,128)(2,1)S(1)}, bf16[160,128]{1,0:T(8,128)(2,1)S(1)}, u32[]{:S(2)}, u32[]{:S(2)}) collective-permute-start(bf16[160,128]{1,0:T(8,128)(2,1)S(1)} %convert_element_type.72), channel_id=1, source_target_pairs={{0,32},{8,40},{16,48},{24,56},{32,0},{40,8},{48,16},{56,24},{64,96... | collective-permute-start | bytes 122888 | tf_op jit(solution)/shard_map/ppermute | solution.py:35
  84.5 10.2 %collective-permute-start.11 = (bf16[160,128]{1,0:T(8,128)(2,1)S(1)}, bf16[160,128]{1,0:T(8,128)(2,1)S(1)}, u32[]{:S(2)}, u32[]{:S(2)}) collective-permute-start(bf16[160,128]{1,0:T(8,128)(2,1)S(1)} %convert_element_type.74), channel_id=1, source_target_pairs={{0,64},{8,72},{16,80},{24,88},{32,96},{40,104},{48,112},{56,120},{... | collective-permute-start | bytes 122888 | tf_op jit(solution)/shard_map/ppermute | solution.py:35
  94.8 7.4 %collective-permute-start.14 = (bf16[160,128]{1,0:T(8,128)(2,1)S(1)}, bf16[160,128]{1,0:T(8,128)(2,1)S(1)}, u32[]{:S(2)}, u32[]{:S(2)}) collective-permute-start(bf16[160,128]{1,0:T(8,128)(2,1)S(1)} %convert_add_fusion.1), channel_id=1, source_target_pairs={{0,384},{8,392},{16,400},{24,408},{32,416},{40,424},{48,432},{56,4... | collective-permute-start | bytes 122888 | tf_op jit(solution)/shard_map/ppermute | solution.py:35
  95.4 6.8 %collective-permute-start.13 = (bf16[160,128]{1,0:T(8,128)(2,1)S(1)}, bf16[160,128]{1,0:T(8,128)(2,1)S(1)}, u32[]{:S(2)}, u32[]{:S(2)}) collective-permute-start(bf16[160,128]{1,0:T(8,128)(2,1)S(1)} %convert_add_fusion.1), channel_id=1, source_target_pairs={{0,256},{8,264},{16,272},{24,280},{32,288},{40,296},{48,304},{56,3... | collective-permute-start | bytes 122888 | tf_op jit(solution)/shard_map/ppermute | solution.py:35
  100.3 5.9 %collective-permute-start.12 = (bf16[160,128]{1,0:T(8,128)(2,1)S(1)}, bf16[160,128]{1,0:T(8,128)(2,1)S(1)}, u32[]{:S(2)}, u32[]{:S(2)}) collective-permute-start(bf16[160,128]{1,0:T(8,128)(2,1)S(1)} %convert_add_fusion.1), channel_id=1, source_target_pairs={{0,128},{8,136},{16,144},{24,152},{32,160},{40,168},{48,176},{56,1... | collective-permute-start | bytes 122888 | tf_op jit(solution)/shard_map/ppermute | solution.py:35
  106.2 3.1 %collective-permute-start.15 = (bf16[160,128]{1,0:T(8,128)(2,1)S(1)}, bf16[160,128]{1,0:T(8,128)(2,1)S(1)}, u32[]{:S(2)}, u32[]{:S(2)}) collective-permute-start(bf16[160,128]{1,0:T(8,128)(2,1)S(1)} %get-tuple-element.83), channel_id=1, source_target_pairs={{0,8},{8,0},{16,24},{24,16},{32,40},{40,32},{48,56},{56,48},{64,72... | collective-permute-start | bytes 122888 | tf_op jit(solution)/shard_map/ppermute | solution.py:35
  110.5 12.6 %collective-permute-start.18 = (bf16[64,2048]{1,0:T(8,128)(2,1)S(1)}, bf16[64,2048]{1,0:T(8,128)(2,1)S(1)}, u32[]{:S(2)}, u32[]{:S(2)}) collective-permute-start(bf16[64,2048]{1,0:T(8,128)(2,1)S(1)} %get-tuple-element.75), channel_id=1, source_target_pairs={{0,4},{8,12},{16,20},{24,28},{32,36},{40,44},{48,52},{56,60},{64,6... | collective-permute-start | bytes 786440 | tf_op jit(solution)/shard_map/ppermute | solution.py:35
  113.5 14.3 %collective-permute-start.17 = (bf16[64,2048]{1,0:T(8,128)(2,1)S(1)}, bf16[64,2048]{1,0:T(8,128)(2,1)S(1)}, u32[]{:S(2)}, u32[]{:S(2)}) collective-permute-start(bf16[64,2048]{1,0:T(8,128)(2,1)S(1)} %get-tuple-element.74), channel_id=1, source_target_pairs={{0,6},{8,14},{16,22},{24,30},{32,38},{40,46},{48,54},{56,62},{64,7... | collective-permute-start | bytes 786440 | tf_op jit(solution)/shard_map/ppermute | solution.py:35
  115.5 12.4 %collective-permute-start.16 = (bf16[64,2048]{1,0:T(8,128)(2,1)S(1)}, bf16[64,2048]{1,0:T(8,128)(2,1)S(1)}, u32[]{:S(2)}, u32[]{:S(2)}) collective-permute-start(bf16[64,2048]{1,0:T(8,128)(2,1)S(1)} %get-tuple-element.73), channel_id=1, source_target_pairs={{0,2},{8,10},{16,18},{24,26},{32,34},{40,42},{48,50},{56,58},{64,6... | collective-permute-start | bytes 786440 | tf_op jit(solution)/shard_map/ppermute | solution.py:35
  128.0 35.8 %collective-permute-start.19 = (bf16[64,2048]{1,0:T(8,128)(2,1)S(1)}, bf16[64,2048]{1,0:T(8,128)(2,1)S(1)}, u32[]{:S(2)}, u32[]{:S(2)}) collective-permute-start(bf16[64,2048]{1,0:T(8,128)(2,1)S(1)} %add_convert_fusion.1), channel_id=1, source_target_pairs={{0,1},{8,9},{16,17},{24,25},{32,33},{40,41},{48,49},{56,57},{64,65... | collective-permute-start | bytes 786440 | tf_op jit(solution)/shard_map/ppermute | solution.py:35
  140.4 23.4 %collective-permute-start.22 = (bf16[64,2048]{1,0:T(8,128)(2,1)S(1)}, bf16[64,2048]{1,0:T(8,128)(2,1)S(1)}, u32[]{:S(2)}, u32[]{:S(2)}) collective-permute-start(bf16[64,2048]{1,0:T(8,128)(2,1)S(1)} %get-tuple-element.82), channel_id=1, source_target_pairs={{0,4},{8,12},{16,20},{24,28},{32,36},{40,44},{48,52},{56,60},{64,6... | collective-permute-start | bytes 786440 | tf_op jit(solution)/shard_map/ppermute | solution.py:35
  143.5 20.4 %collective-permute-start.21 = (bf16[64,2048]{1,0:T(8,128)(2,1)S(1)}, bf16[64,2048]{1,0:T(8,128)(2,1)S(1)}, u32[]{:S(2)}, u32[]{:S(2)}) collective-permute-start(bf16[64,2048]{1,0:T(8,128)(2,1)S(1)} %get-tuple-element.81), channel_id=1, source_target_pairs={{0,6},{8,14},{16,22},{24,30},{32,38},{40,46},{48,54},{56,62},{64,7... | collective-permute-start | bytes 786440 | tf_op jit(solution)/shard_map/ppermute | solution.py:35
  146.8 17.0 %collective-permute-start.20 = (bf16[64,2048]{1,0:T(8,128)(2,1)S(1)}, bf16[64,2048]{1,0:T(8,128)(2,1)S(1)}, u32[]{:S(2)}, u32[]{:S(2)}) collective-permute-start(bf16[64,2048]{1,0:T(8,128)(2,1)S(1)} %get-tuple-element.80), channel_id=1, source_target_pairs={{0,2},{8,10},{16,18},{24,26},{32,34},{40,42},{48,50},{56,58},{64,6... | collective-permute-start | bytes 786440 | tf_op jit(solution)/shard_map/ppermute | solution.py:35

commit v6 on v5

--- a/solution.py
+++ b/solution.py
@@ -63,6 +63,8 @@
 
 
 ROWS = 160
+EARLY = 256
+PARTS = 2 * NX
 VMEM = pl.BlockSpec(memory_space=pltpu.VMEM)
 HBM = pl.BlockSpec(memory_space=pltpu.HBM)
 SMEM = pl.BlockSpec(memory_space=pltpu.SMEM)
@@ -115,17 +117,24 @@
 
 
 def project_kernel(*refs):
-    parts = refs[:N_TP]
-    wf, ww, table, qf_ref, kv_ref, tail_ref, mine_ref, other_ref, held, held_wf, qf, tail, sems = refs[N_TP:]
+    parts = refs[:PARTS]
+    wf, ww, table, qf_ref, kv_ref, tail_ref, mine_ref, other_ref, held, held_wf, qf, tail, sems = refs[PARTS:]
     x, half, core, _ = position()
-    owners = [lax.rem(x + NX - s, NX) * 2 + side for side in (half, 1 - half) for s in (0, 1, 3, 2)]
     width = parts[0].shape[1]
     head = ww.shape[2] // 3
-    copies = [
-        pltpu.make_async_copy(part, held.at[:, pl.ds(pl.multiple_of(owner * width, width), width)], sems.at[k])
-        for k, (part, owner) in enumerate(zip(parts, owners))
-    ]
-    copies.append(pltpu.make_async_copy(wf, held_wf, sems.at[N_TP]))
+    rows = held.shape[0]
+    copies = []
+    for k, s in enumerate((0, 1, 3, 2)):
+        column = lax.rem(x + NX - s, NX) * 2
+        for part, first, count, side, to in (
+            (parts[k], 0, rows, half, 0),
+            (parts[k], rows, EARLY, 1 - half, 0),
+            (parts[NX + k], 0, rows - EARLY, 1 - half, EARLY),
+        ):
+            cols = pl.ds(pl.multiple_of((column + side) * width, width), width)
+            target = held.at[pl.ds(to, count), cols]
+            copies.append(pltpu.make_async_copy(part.at[pl.ds(first, count)], target, sems.at[len(copies)]))
+    copies.append(pltpu.make_async_copy(wf, held_wf, sems.at[len(copies)]))
     for copy in copies:
         copy.start()
     for copy in copies:
@@ -275,7 +284,7 @@
 
 
 def project(parts, wf, ww, tables):
-    tok_rows = parts[0].shape[0]
+    tok_rows = parts[0].shape[0] - EARLY
     wide = 2 * ww.shape[2] // 3
     queries = shape((tok_rows, wide + 2 * wf.shape[1]), bf16)
     tail = shape(((WMAX - 1) * BLOCK, 2 * wide), bf16)
@@ -288,14 +297,14 @@
             shape((ROWS, wide // 2), f32),
             shape((ROWS, wide // 2), bf16),
         ),
-        in_specs=[HBM] * (N_TP + 1) + [VMEM] * 2,
+        in_specs=[HBM] * (PARTS + 1) + [VMEM] * 2,
         out_specs=(HBM, VMEM, HBM, VMEM, VMEM),
         scratch_shapes=[
             pltpu.VMEM((tok_rows, wf.shape[0]), bf16),
             pltpu.VMEM(wf.shape, bf16),
             pltpu.VMEM(queries.shape, bf16),
             pltpu.VMEM(tail.shape, bf16),
-            pltpu.SemaphoreType.DMA((N_TP + 1,)),
+            pltpu.SemaphoreType.DMA((3 * NX + 1,)),
         ],
         name="project",
         compiler_params=pltpu.CompilerParams(vmem_limit_bytes=LIMIT),
@@ -353,13 +362,14 @@
     seq, tp = lax.axis_index("seq"), lax.axis_index("tp")
     x, h, y, z, c = tp // 2, tp % 2, seq // (2 * NZ), seq // 2 % NZ, seq % 2
 
-    other = send(tokens, to_half)
-    parts = [tokens] + [send(tokens, to_x(s)) for s in (1, 3, 2)]
+    first, second = [send(piece, to_half) for piece in jnp.split(tokens, [EARLY])]
+    first = jnp.concatenate([tokens, first], axis=0)
+    wf, ww = w_feature.reshape(model_width, -1), w_window.transpose(1, 0, 2)
+    parts = [part for source in (first, second) for part in [source] + [send(source, to_x(s)) for s in (1, 3, 2)]]
     w_out = w_out.reshape(-1, model_width)
-    parts += [other] + [send(other, to_x(s)) for s in (1, 3, 2)]
     tables = feature_maps(feat_dim, head_count)
     qf, kv, tail, mine, theirs = project(
-        parts, w_feature.reshape(model_width, -1), w_window.transpose(1, 0, 2), tables
+        parts, wf, ww, tables
     )
 
     def beside(halo):

time: 165 us -> 177 us (1.073)
  the two profiles are of different devices: /device:TPU:46 before, /device:TPU:8 now
where the time goes in v6:
time: 177 us; the launch traced here: 176 us
  starting transfers between devices  92.4 us (52%)
  waiting for transfers between devices  59.7 us (34%)
  Pallas kernels  11.5 us (6%)
  local copies, waits for them, and re-layouts  10.7 us (6%)
    ppermute x24, starting transfers between devices, send(): return lax.ppermute(value, ('seq', 'tp'), pairs(move))  92.4 us
    ppermute x24, waiting for transfers between devices, send(): return lax.ppermute(value, ('seq', 'tp'), pairs(move))  59.7 us
    unnamed x22, local copies, waits for them, and re-layouts  8.45 us
    pallas_call x1, Pallas kernels, project(): pl.pallas_call(project_kernel, out_shape=(queries, shape((tok_rows, 2 * w...  5.95 us
    pallas_call x1, Pallas kernels, near(): pl.pallas_call(local_kernel, out_shape=(shape((tok_rows, wide), f32), sha...  3.98 us
  transfers between devices with their start and end apart: 24, of which 13 were waited for; matrix products, arithmetic and copies ran while one was open for 3% of the time, Pallas kernels for 3%

profile of v6, /device:TPU:8, one launch (start us, length us, event | category | flops | bytes accessed | tf_op | source)
XLA Modules:
  0.0 175.9 jit_solution(16258219899691282431)
XLA Ops:
  0.0 1.0 fusion.3
  1.0 15.7 %collective-permute-start = (bf16[256,256]{1,0:T(8,128)(2,1)S(1)}, bf16[256,256]{1,0:T(8,128)(2,1)S(1)}, u32[]{:S(2)}, u32[]{:S(2)}) collective-permute-start(bf16[256,256]{1,0:T(8,128)(2,1)S(1)} %get-tuple-element.84), channel_id=1, source_target_pairs={{0,1},{8,9},{16,17},{24,25},{32,33},{40,41},{48,49},{56,57},{64,65... | collective-permute-start | bytes 393224 | tf_op jit(solution)/shard_map/ppermute | solution.py:35
  16.7 1.9 %collective-permute-start.4 = (bf16[256,256]{1,0:T(8,128)(2,1)S(1)}, bf16[256,256]{1,0:T(8,128)(2,1)S(1)}, u32[]{:S(2)}, u32[]{:S(2)}) collective-permute-start(bf16[256,256]{1,0:T(8,128)(2,1)S(1)} %get-tuple-element.83), channel_id=1, source_target_pairs={{0,1},{8,9},{16,17},{24,25},{32,33},{40,41},{48,49},{56,57},{64,65... | collective-permute-start | bytes 393224 | tf_op jit(solution)/shard_map/ppermute | solution.py:35
  18.6 1.0 constant_dynamic-update-slice_fusion.1
  19.6 10.1 %collective-permute-done = bf16[256,256]{1,0:T(8,128)(2,1)S(1)} collective-permute-done((bf16[256,256]{1,0:T(8,128)(2,1)S(1)}, bf16[256,256]{1,0:T(8,128)(2,1)S(1)}, u32[]{:S(2)}, u32[]{:S(2)}) %collective-permute-start) | collective-permute-done | bytes 131104 | tf_op jit(solution)/shard_map/ppermute | solution.py:35
  29.7 3.4 %collective-permute-start.1 = (bf16[768,256]{1,0:T(8,128)(2,1)S(1)}, bf16[768,256]{1,0:T(8,128)(2,1)S(1)}, u32[]{:S(2)}, u32[]{:S(2)}) collective-permute-start(bf16[768,256]{1,0:T(8,128)(2,1)S(1)} %constant_dynamic-update-slice_fusion.refs_0_), channel_id=1, source_target_pairs={{0,2},{8,10},{16,18},{24,26},{32,34},{40,42},{48,50},{56,58},{64,6... | collective-permute-start | bytes 1179656 | tf_op jit(solution)/shard_map/ppermute | solution.py:35
  33.1 3.7 %collective-permute-start.2 = (bf16[768,256]{1,0:T(8,128)(2,1)S(1)}, bf16[768,256]{1,0:T(8,128)(2,1)S(1)}, u32[]{:S(2)}, u32[]{:S(2)}) collective-permute-start(bf16[768,256]{1,0:T(8,128)(2,1)S(1)} %constant_dynamic-update-slice_fusion.refs_0_), channel_id=1, source_target_pairs={{0,6},{8,14},{16,22},{24,30},{32,38},{40,46},{48,54},{56,62},{64,7... | collective-permute-start | bytes 1179656 | tf_op jit(solution)/shard_map/ppermute | solution.py:35
  36.8 3.7 %collective-permute-start.3 = (bf16[768,256]{1,0:T(8,128)(2,1)S(1)}, bf16[768,256]{1,0:T(8,128)(2,1)S(1)}, u32[]{:S(2)}, u32[]{:S(2)}) collective-permute-start(bf16[768,256]{1,0:T(8,128)(2,1)S(1)} %constant_dynamic-update-slice_fusion.refs_0_), channel_id=1, source_target_pairs={{0,4},{8,12},{16,20},{24,28},{32,36},{40,44},{48,52},{56,60},{64,6... | collective-permute-start | bytes 1179656 | tf_op jit(solution)/shard_map/ppermute | solution.py:35
  40.5 4.5 %collective-permute-done.4.refs_4_ = bf16[256,256]{1,0:T(8,128)(2,1)S(1)} collective-permute-done((bf16[256,256]{1,0:T(8,128)(2,1)S(1)}, bf16[256,256]{1,0:T(8,128)(2,1)S(1)}, u32[]{:S(2)}, u32[]{:S(2)}) %collective-permute-start.4) | collective-permute-done | bytes 131104 | tf_op jit(solution)/shard_map/ppermute | solution.py:35
  45.0 3.4 %collective-permute-start.5 = (bf16[256,256]{1,0:T(8,128)(2,1)S(1)}, bf16[256,256]{1,0:T(8,128)(2,1)S(1)}, u32[]{:S(2)}, u32[]{:S(2)}) collective-permute-start(bf16[256,256]{1,0:T(8,128)(2,1)S(1)} %collective-permute-done.4.refs_4_), channel_id=1, source_target_pairs={{0,2},{8,10},{16,18},{24,26},{32,34},{40,42},{48,50},{56,58},{64,6... | collective-permute-start | bytes 393224 | tf_op jit(solution)/shard_map/ppermute | solution.py:35
  48.4 3.7 %collective-permute-start.6 = (bf16[256,256]{1,0:T(8,128)(2,1)S(1)}, bf16[256,256]{1,0:T(8,128)(2,1)S(1)}, u32[]{:S(2)}, u32[]{:S(2)}) collective-permute-start(bf16[256,256]{1,0:T(8,128)(2,1)S(1)} %collective-permute-done.4.refs_4_), channel_id=1, source_target_pairs={{0,6},{8,14},{16,22},{24,30},{32,38},{40,46},{48,54},{56,62},{64,7... | collective-permute-start | bytes 393224 | tf_op jit(solution)/shard_map/ppermute | solution.py:35
  52.1 1.0 collective-permute-done.5.refs_5_
  53.1 0.7 copy-done.2
  53.7 3.7 %collective-permute-start.7 = (bf16[256,256]{1,0:T(8,128)(2,1)S(1)}, bf16[256,256]{1,0:T(8,128)(2,1)S(1)}, u32[]{:S(2)}, u32[]{:S(2)}) collective-permute-start(bf16[256,256]{1,0:T(8,128)(2,1)S(1)} %collective-permute-done.4.refs_4_), channel_id=1, source_target_pairs={{0,4},{8,12},{16,20},{24,28},{32,36},{40,44},{48,52},{56,60},{64,6... | collective-permute-start | bytes 393224 | tf_op jit(solution)/shard_map/ppermute | solution.py:35
  57.4 1.2 copy.11.refs_8_
  58.7 0.0 copy-start.1
  58.7 0.0 copy-start.3
  58.7 2.3 %copy.13 = bf16[2048,2,384]{2,0,1:T(8,128)(2,1)S(1)} copy(bf16[2048,2,384]{2,1,0:T(2,128)(2,1)} %param.9) | data formatting | bytes 6291456 | tf_op args[2]
  61.0 0.0 collective-permute-done.6.refs_6_
  61.1 0.6 copy-done.4
  61.7 0.4 collective-permute-done.7.refs_7_
  62.1 0.6 copy-done.6
  62.7 0.0 collective-permute-done.2.refs_2_
  62.7 0.0 collective-permute-done.3.refs_3_
  62.8 0.9 copy-done.5
  63.7 0.9 copy-done.7
  64.6 6.0 %project.1 = (bf16[512,384]{1,0:T(8,128)(2,1)S(1)}, bf16[512,512]{1,0:T(8,128)(2,1)S(1)}, bf16[384,512]{1,0:T(8,128)(2,1)S(1)}, f32[160,128]{1,0:T(8,128)S(1)}, bf16[160,128]{1,0:T(8,128)(2,1)}) custom-call(bf16[768,256]{1,0:T(8,128)(2,1)S(1)} %constant_dynamic-update-slice_fusion.refs_0_, bf16[768,256]{1,0:T(8,128)(2,1)S(1)} %collective-permute-done.1.refs_1_, ...), custom_call_target="tpu_custom_call" | custom-call | tf_op jit(solution)/shard_map/project/pallas_call | solution.py:291
  70.5 0.7 copy-done.9
  71.3 2.0 %collective-permute-start.8 = (bf16[160,128]{1,0:T(8,128)(2,1)}, bf16[160,128]{1,0:T(8,128)(2,1)S(1)}, u32[]{:S(2)}, u32[]{:S(2)}) collective-permute-start(bf16[160,128]{1,0:T(8,128)(2,1)} %get-tuple-element.45), channel_id=1, source_target_pairs={{0,8},{8,0},{16,24},{24,16},{32,40},{40,32},{48,56},{56,48},{64,72... | collective-permute-start | bytes 122888 | tf_op jit(solution)/shard_map/ppermute | solution.py:35
  73.3 2.4 %collective-permute-start.10 = (bf16[384,512]{1,0:T(8,128)(2,1)}, bf16[384,512]{1,0:T(8,128)(2,1)S(1)}, u32[]{:S(2)}, u32[]{:S(2)}) collective-permute-start(bf16[384,512]{1,0:T(8,128)(2,1)} %copy-done.9), channel_id=1, source_target_pairs={{0,8},{8,16},{16,24},{24,32},{32,40},{40,48},{48,56},{56,64},{64,7... | collective-permute-start | bytes 1179656 | tf_op jit(solution)/shard_map/ppermute | solution.py:35
  75.7 0.0 collective-permute-done.8
  75.8 3.2 %collective-permute-start.9 = (bf16[160,128]{1,0:T(8,128)(2,1)S(1)}, bf16[160,128]{1,0:T(8,128)(2,1)S(1)}, u32[]{:S(2)}, u32[]{:S(2)}) collective-permute-start(bf16[160,128]{1,0:T(8,128)(2,1)S(1)} %convert_element_type.70), channel_id=1, source_target_pairs={{0,16},{8,24},{16,0},{24,8},{32,48},{40,56},{48,32},{56,40},{64,80... | collective-permute-start | bytes 122888 | tf_op jit(solution)/shard_map/ppermute | solution.py:35
  79.1 3.0 %collective-permute-done.9 = bf16[160,128]{1,0:T(8,128)(2,1)S(1)} collective-permute-done((bf16[160,128]{1,0:T(8,128)(2,1)S(1)}, bf16[160,128]{1,0:T(8,128)(2,1)S(1)}, u32[]{:S(2)}, u32[]{:S(2)}) %collective-permute-start.9) | collective-permute-done | bytes 40992 | tf_op jit(solution)/shard_map/ppermute | solution.py:35
  82.1 8.2 %collective-permute-done.10.halo_ref = bf16[384,512]{1,0:T(8,128)(2,1)S(1)} collective-permute-done((bf16[384,512]{1,0:T(8,128)(2,1)}, bf16[384,512]{1,0:T(8,128)(2,1)S(1)}, u32[]{:S(2)}, u32[]{:S(2)}) %collective-permute-start.10) | collective-permute-done | bytes 393248 | tf_op jit(solution)/shard_map/ppermute | solution.py:35
  90.3 1.9 %collective-permute-start.11 = (bf16[160,128]{1,0:T(8,128)(2,1)S(1)}, bf16[160,128]{1,0:T(8,128)(2,1)S(1)}, u32[]{:S(2)}, u32[]{:S(2)}) collective-permute-start(bf16[160,128]{1,0:T(8,128)(2,1)S(1)} %convert_element_type.72), channel_id=1, source_target_pairs={{0,32},{8,40},{16,48},{24,56},{32,0},{40,8},{48,16},{56,24},{64,96... | collective-permute-start | bytes 122888 | tf_op jit(solution)/shard_map/ppermute | solution.py:35
  92.2 4.9 %collective-permute-done.11 = bf16[160,128]{1,0:T(8,128)(2,1)S(1)} collective-permute-done((bf16[160,128]{1,0:T(8,128)(2,1)S(1)}, bf16[160,128]{1,0:T(8,128)(2,1)S(1)}, u32[]{:S(2)}, u32[]{:S(2)}) %collective-permute-start.11) | collective-permute-done | bytes 40992 | tf_op jit(solution)/shard_map/ppermute | solution.py:35
  97.1 6.5 %collective-permute-start.12 = (bf16[160,128]{1,0:T(8,128)(2,1)S(1)}, bf16[160,128]{1,0:T(8,128)(2,1)S(1)}, u32[]{:S(2)}, u32[]{:S(2)}) collective-permute-start(bf16[160,128]{1,0:T(8,128)(2,1)S(1)} %convert_element_type.74), channel_id=1, source_target_pairs={{0,64},{8,72},{16,80},{24,88},{32,96},{40,104},{48,112},{56,120},{... | collective-permute-start | bytes 122888 | tf_op jit(solution)/shard_map/ppermute | solution.py:35
  103.7 0.0 copy-start.8
  103.7 0.6 copy-done.8
  104.3 4.0 %near.1 = (f32[512,256]{1,0:T(8,128)S(1)}, f32[512,256]{1,0:T(8,128)S(1)}, bf16[2,512,160]{2,1,0:T(8,128)(2,1)S(1)}, bf16[2,512,160]{2,1,0:T(8,128)(2,1)S(1)}) custom-call(s32[2]{0:T(128)S(1)} %copy-done.8, bf16[512,384]{1,0:T(8,128)(2,1)S(1)} %get-tuple-element.54.qf_ref, bf16[512,512]{1,0:T(8,128)(2,1)S(1)} %get-tuple-element.55.kv_ref, ...), custom_call_target="tpu_custom_call" | custom-call | tf_op jit(solution)/shard_map/near/pallas_call | solution.py:316
  108.3 0.0 collective-permute-done.12
  108.4 0.7 collective-permute-start.15
  109.0 4.8 %collective-permute-start.14 = (bf16[160,128]{1,0:T(8,128)(2,1)S(1)}, bf16[160,128]{1,0:T(8,128)(2,1)S(1)}, u32[]{:S(2)}, u32[]{:S(2)}) collective-permute-start(bf16[160,128]{1,0:T(8,128)(2,1)S(1)} %convert_add_fusion.1), channel_id=1, source_target_pairs={{0,256},{8,264},{16,272},{24,280},{32,288},{40,296},{48,304},{56,3... | collective-permute-start | bytes 122888 | tf_op jit(solution)/shard_map/ppermute | solution.py:35
  113.9 1.9 %collective-permute-start.13 = (bf16[160,128]{1,0:T(8,128)(2,1)S(1)}, bf16[160,128]{1,0:T(8,128)(2,1)S(1)}, u32[]{:S(2)}, u32[]{:S(2)}) collective-permute-start(bf16[160,128]{1,0:T(8,128)(2,1)S(1)} %convert_add_fusion.1), channel_id=1, source_target_pairs={{0,128},{8,136},{16,144},{24,152},{32,160},{40,168},{48,176},{56,1... | collective-permute-start | bytes 122888 | tf_op jit(solution)/shard_map/ppermute | solution.py:35
  115.8 3.9 %collective-permute-done.13 = bf16[160,128]{1,0:T(8,128)(2,1)S(1)} collective-permute-done((bf16[160,128]{1,0:T(8,128)(2,1)S(1)}, bf16[160,128]{1,0:T(8,128)(2,1)S(1)}, u32[]{:S(2)}, u32[]{:S(2)}) %collective-permute-start.13) | collective-permute-done | bytes 40992 | tf_op jit(solution)/shard_map/ppermute | solution.py:35
  119.8 1.9 %collective-permute-start.16 = (bf16[160,128]{1,0:T(8,128)(2,1)S(1)}, bf16[160,128]{1,0:T(8,128)(2,1)S(1)}, u32[]{:S(2)}, u32[]{:S(2)}) collective-permute-start(bf16[160,128]{1,0:T(8,128)(2,1)S(1)} %get-tuple-element.85), channel_id=1, source_target_pairs={{0,8},{8,0},{16,24},{24,16},{32,40},{40,32},{48,56},{56,48},{64,72... | collective-permute-start | bytes 122888 | tf_op jit(solution)/shard_map/ppermute | solution.py:35
  121.7 1.2 collective-permute-done.16.theirs
  122.9 0.7 hidden.1
  123.6 0.4 product.2
  124.1 3.3 %collective-permute-start.19 = (bf16[64,2048]{1,0:T(8,128)(2,1)S(1)}, bf16[64,2048]{1,0:T(8,128)(2,1)S(1)}, u32[]{:S(2)}, u32[]{:S(2)}) collective-permute-start(bf16[64,2048]{1,0:T(8,128)(2,1)S(1)} %get-tuple-element.75), channel_id=1, source_target_pairs={{0,4},{8,12},{16,20},{24,28},{32,36},{40,44},{48,52},{56,60},{64,6... | collective-permute-start | bytes 786440 | tf_op jit(solution)/shard_map/ppermute | solution.py:35
  127.3 3.0 %collective-permute-start.18 = (bf16[64,2048]{1,0:T(8,128)(2,1)S(1)}, bf16[64,2048]{1,0:T(8,128)(2,1)S(1)}, u32[]{:S(2)}, u32[]{:S(2)}) collective-permute-start(bf16[64,2048]{1,0:T(8,128)(2,1)S(1)} %get-tuple-element.74), channel_id=1, source_target_pairs={{0,6},{8,14},{16,22},{24,30},{32,38},{40,46},{48,54},{56,62},{64,7... | collective-permute-start | bytes 786440 | tf_op jit(solution)/shard_map/ppermute | solution.py:35
  130.3 2.9 %collective-permute-start.17 = (bf16[64,2048]{1,0:T(8,128)(2,1)S(1)}, bf16[64,2048]{1,0:T(8,128)(2,1)S(1)}, u32[]{:S(2)}, u32[]{:S(2)}) collective-permute-start(bf16[64,2048]{1,0:T(8,128)(2,1)S(1)} %get-tuple-element.73), channel_id=1, source_target_pairs={{0,2},{8,10},{16,18},{24,26},{32,34},{40,42},{48,50},{56,58},{64,6... | collective-permute-start | bytes 786440 | tf_op jit(solution)/shard_map/ppermute | solution.py:35
  133.2 2.9 %collective-permute-done.19 = bf16[64,2048]{1,0:T(8,128)(2,1)S(1)} collective-permute-done((bf16[64,2048]{1,0:T(8,128)(2,1)S(1)}, bf16[64,2048]{1,0:T(8,128)(2,1)S(1)}, u32[]{:S(2)}, u32[]{:S(2)}) %collective-permute-start.19) | collective-permute-done | bytes 262176 | tf_op jit(solution)/shard_map/ppermute | solution.py:35
  136.1 3.8 %collective-permute-done.18 = bf16[64,2048]{1,0:T(8,128)(2,1)S(1)} collective-permute-done((bf16[64,2048]{1,0:T(8,128)(2,1)S(1)}, bf16[64,2048]{1,0:T(8,128)(2,1)S(1)}, u32[]{:S(2)}, u32[]{:S(2)}) %collective-permute-start.18) | collective-permute-done | bytes 262176 | tf_op jit(solution)/shard_map/ppermute | solution.py:35
  139.8 1.6 collective-permute-done.17
  141.5 0.1 add_convert_fusion.1
  141.6 9.6 %collective-permute-start.20 = (bf16[64,2048]{1,0:T(8,128)(2,1)S(1)}, bf16[64,2048]{1,0:T(8,128)(2,1)S(1)}, u32[]{:S(2)}, u32[]{:S(2)}) collective-permute-start(bf16[64,2048]{1,0:T(8,128)(2,1)S(1)} %add_convert_fusion.1), channel_id=1, source_target_pairs={{0,1},{8,9},{16,17},{24,25},{32,33},{40,41},{48,49},{56,57},{64,65... | collective-permute-start | bytes 786440 | tf_op jit(solution)/shard_map/ppermute | solution.py:35
  151.2 0.4 product.3
  151.6 3.3 %collective-permute-start.23 = (bf16[64,2048]{1,0:T(8,128)(2,1)S(1)}, bf16[64,2048]{1,0:T(8,128)(2,1)S(1)}, u32[]{:S(2)}, u32[]{:S(2)}) collective-permute-start(bf16[64,2048]{1,0:T(8,128)(2,1)S(1)} %get-tuple-element.82), channel_id=1, source_target_pairs={{0,4},{8,12},{16,20},{24,28},{32,36},{40,44},{48,52},{56,60},{64,6... | collective-permute-start | bytes 786440 | tf_op jit(solution)/shard_map/ppermute | solution.py:35
  154.9 3.1 %collective-permute-start.22 = (bf16[64,2048]{1,0:T(8,128)(2,1)S(1)}, bf16[64,2048]{1,0:T(8,128)(2,1)S(1)}, u32[]{:S(2)}, u32[]{:S(2)}) collective-permute-start(bf16[64,2048]{1,0:T(8,128)(2,1)S(1)} %get-tuple-element.81), channel_id=1, source_target_pairs={{0,6},{8,14},{16,22},{24,30},{32,38},{40,46},{48,54},{56,62},{64,7... | collective-permute-start | bytes 786440 | tf_op jit(solution)/shard_map/ppermute | solution.py:35
  158.0 2.8 %collective-permute-start.21 = (bf16[64,2048]{1,0:T(8,128)(2,1)S(1)}, bf16[64,2048]{1,0:T(8,128)(2,1)S(1)}, u32[]{:S(2)}, u32[]{:S(2)}) collective-permute-start(bf16[64,2048]{1,0:T(8,128)(2,1)S(1)} %get-tuple-element.80), channel_id=1, source_target_pairs={{0,2},{8,10},{16,18},{24,26},{32,34},{40,42},{48,50},{56,58},{64,6... | collective-permute-start | bytes 786440 | tf_op jit(solution)/shard_map/ppermute | solution.py:35
  160.8 14.2 %collective-permute-done.20 = bf16[64,2048]{1,0:T(8,128)(2,1)S(1)} collective-permute-done((bf16[64,2048]{1,0:T(8,128)(2,1)S(1)}, bf16[64,2048]{1,0:T(8,128)(2,1)S(1)}, u32[]{:S(2)}, u32[]{:S(2)}) %collective-permute-start.20) | collective-permute-done | bytes 262176 | tf_op jit(solution)/shard_map/ppermute | solution.py:35
  175.0 0.1 convert_add_fusion
  175.0 0.8 add_convert_fusion
  (26 shorter events, 0.2 us)
Async XLA Ops:
  1.0 28.7 %collective-permute-start = (bf16[256,256]{1,0:T(8,128)(2,1)S(1)}, bf16[256,256]{1,0:T(8,128)(2,1)S(1)}, u32[]{:S(2)}, u32[]{:S(2)}) collective-permute-start(bf16[256,256]{1,0:T(8,128)(2,1)S(1)} %get-tuple-element.84), channel_id=1, source_target_pairs={{0,1},{8,9},{16,17},{24,25},{32,33},{40,41},{48,49},{56,57},{64,65... | collective-permute-start | bytes 393224 | tf_op jit(solution)/shard_map/ppermute | solution.py:35
  16.7 28.3 %collective-permute-start.4 = (bf16[256,256]{1,0:T(8,128)(2,1)S(1)}, bf16[256,256]{1,0:T(8,128)(2,1)S(1)}, u32[]{:S(2)}, u32[]{:S(2)}) collective-permute-start(bf16[256,256]{1,0:T(8,128)(2,1)S(1)} %get-tuple-element.83), channel_id=1, source_target_pairs={{0,1},{8,9},{16,17},{24,25},{32,33},{40,41},{48,49},{56,57},{64,65... | collective-permute-start | bytes 393224 | tf_op jit(solution)/shard_map/ppermute | solution.py:35
  29.7 33.0 %collective-permute-start.1 = (bf16[768,256]{1,0:T(8,128)(2,1)S(1)}, bf16[768,256]{1,0:T(8,128)(2,1)S(1)}, u32[]{:S(2)}, u32[]{:S(2)}) collective-permute-start(bf16[768,256]{1,0:T(8,128)(2,1)S(1)} %constant_dynamic-update-slice_fusion.refs_0_), channel_id=1, source_target_pairs={{0,2},{8,10},{16,18},{24,26},{32,34},{40,42},{48,50},{56,58},{64,6... | collective-permute-start | bytes 1179656 | tf_op jit(solution)/shard_map/ppermute | solution.py:35
  33.1 29.6 %collective-permute-start.2 = (bf16[768,256]{1,0:T(8,128)(2,1)S(1)}, bf16[768,256]{1,0:T(8,128)(2,1)S(1)}, u32[]{:S(2)}, u32[]{:S(2)}) collective-permute-start(bf16[768,256]{1,0:T(8,128)(2,1)S(1)} %constant_dynamic-update-slice_fusion.refs_0_), channel_id=1, source_target_pairs={{0,6},{8,14},{16,22},{24,30},{32,38},{40,46},{48,54},{56,62},{64,7... | collective-permute-start | bytes 1179656 | tf_op jit(solution)/shard_map/ppermute | solution.py:35
  36.8 25.9 %collective-permute-start.3 = (bf16[768,256]{1,0:T(8,128)(2,1)S(1)}, bf16[768,256]{1,0:T(8,128)(2,1)S(1)}, u32[]{:S(2)}, u32[]{:S(2)}) collective-permute-start(bf16[768,256]{1,0:T(8,128)(2,1)S(1)} %constant_dynamic-update-slice_fusion.refs_0_), channel_id=1, source_target_pairs={{0,4},{8,12},{16,20},{24,28},{32,36},{40,44},{48,52},{56,60},{64,6... | collective-permute-start | bytes 1179656 | tf_op jit(solution)/shard_map/ppermute | solution.py:35
  45.0 8.1 %collective-permute-start.5 = (bf16[256,256]{1,0:T(8,128)(2,1)S(1)}, bf16[256,256]{1,0:T(8,128)(2,1)S(1)}, u32[]{:S(2)}, u32[]{:S(2)}) collective-permute-start(bf16[256,256]{1,0:T(8,128)(2,1)S(1)} %collective-permute-done.4.refs_4_), channel_id=1, source_target_pairs={{0,2},{8,10},{16,18},{24,26},{32,34},{40,42},{48,50},{56,58},{64,6... | collective-permute-start | bytes 393224 | tf_op jit(solution)/shard_map/ppermute | solution.py:35
  48.4 12.6 %collective-permute-start.6 = (bf16[256,256]{1,0:T(8,128)(2,1)S(1)}, bf16[256,256]{1,0:T(8,128)(2,1)S(1)}, u32[]{:S(2)}, u32[]{:S(2)}) collective-permute-start(bf16[256,256]{1,0:T(8,128)(2,1)S(1)} %collective-permute-done.4.refs_4_), channel_id=1, source_target_pairs={{0,6},{8,14},{16,22},{24,30},{32,38},{40,46},{48,54},{56,62},{64,7... | collective-permute-start | bytes 393224 | tf_op jit(solution)/shard_map/ppermute | solution.py:35
  53.1 0.7 copy-start.2
  53.7 8.4 %collective-permute-start.7 = (bf16[256,256]{1,0:T(8,128)(2,1)S(1)}, bf16[256,256]{1,0:T(8,128)(2,1)S(1)}, u32[]{:S(2)}, u32[]{:S(2)}) collective-permute-start(bf16[256,256]{1,0:T(8,128)(2,1)S(1)} %collective-permute-done.4.refs_4_), channel_id=1, source_target_pairs={{0,4},{8,12},{16,20},{24,28},{32,36},{40,44},{48,52},{56,60},{64,6... | collective-permute-start | bytes 393224 | tf_op jit(solution)/shard_map/ppermute | solution.py:35
  58.7 4.1 %copy-start.1 = (bf16[2,4,160,128]{3,2,1,0:T(8,128)(2,1)S(1)}, bf16[2,4,160,128]{3,2,1,0:T(8,128)(2,1)}, u32[]{:S(2)}) copy-start(bf16[2,4,160,128]{3,2,1,0:T(8,128)(2,1)} %constant.48.clone.refs_10_.table) | copy-start | bytes 983044
  58.7 4.1 %copy-start.3 = (bf16[256,256]{1,0:T(8,128)(2,1)S(1)}, bf16[256,256]{1,0:T(8,128)(2,1)}, u32[]{:S(2)}) copy-start(bf16[256,256]{1,0:T(8,128)(2,1)} %copy-done.2) | copy-start | bytes 393220
  61.1 0.6 copy-start.4
  62.1 0.6 copy-start.6
  62.8 0.9 copy-start.5
  63.7 0.9 copy-start.7
  70.5 0.7 copy-start.9
  71.3 52.3 %copy-start = (bf16[2,128,2048]{2,1,0:T(8,128)(2,1)S(1)}, bf16[2,128,2048]{2,1,0:T(8,128)(2,1)}, u32[]{:S(2)}) copy-start(bf16[2,128,2048]{2,1,0:T(8,128)(2,1)} %param.10) | copy-start | bytes 3145732
  71.3 4.5 %collective-permute-start.8 = (bf16[160,128]{1,0:T(8,128)(2,1)}, bf16[160,128]{1,0:T(8,128)(2,1)S(1)}, u32[]{:S(2)}, u32[]{:S(2)}) collective-permute-start(bf16[160,128]{1,0:T(8,128)(2,1)} %get-tuple-element.45), channel_id=1, source_target_pairs={{0,8},{8,0},{16,24},{24,16},{32,40},{40,32},{48,56},{56,48},{64,72... | collective-permute-start | bytes 122888 | tf_op jit(solution)/shard_map/ppermute | solution.py:35
  73.3 17.0 %collective-permute-start.10 = (bf16[384,512]{1,0:T(8,128)(2,1)}, bf16[384,512]{1,0:T(8,128)(2,1)S(1)}, u32[]{:S(2)}, u32[]{:S(2)}) collective-permute-start(bf16[384,512]{1,0:T(8,128)(2,1)} %copy-done.9), channel_id=1, source_target_pairs={{0,8},{8,16},{16,24},{24,32},{32,40},{40,48},{48,56},{56,64},{64,7... | collective-permute-start | bytes 1179656 | tf_op jit(solution)/shard_map/ppermute | solution.py:35
  75.8 6.3 %collective-permute-start.9 = (bf16[160,128]{1,0:T(8,128)(2,1)S(1)}, bf16[160,128]{1,0:T(8,128)(2,1)S(1)}, u32[]{:S(2)}, u32[]{:S(2)}) collective-permute-start(bf16[160,128]{1,0:T(8,128)(2,1)S(1)} %convert_element_type.70), channel_id=1, source_target_pairs={{0,16},{8,24},{16,0},{24,8},{32,48},{40,56},{48,32},{56,40},{64,80... | collective-permute-start | bytes 122888 | tf_op jit(solution)/shard_map/ppermute | solution.py:35
  90.3 6.8 %collective-permute-start.11 = (bf16[160,128]{1,0:T(8,128)(2,1)S(1)}, bf16[160,128]{1,0:T(8,128)(2,1)S(1)}, u32[]{:S(2)}, u32[]{:S(2)}) collective-permute-start(bf16[160,128]{1,0:T(8,128)(2,1)S(1)} %convert_element_type.72), channel_id=1, source_target_pairs={{0,32},{8,40},{16,48},{24,56},{32,0},{40,8},{48,16},{56,24},{64,96... | collective-permute-start | bytes 122888 | tf_op jit(solution)/shard_map/ppermute | solution.py:35
  97.1 11.2 %collective-permute-start.12 = (bf16[160,128]{1,0:T(8,128)(2,1)S(1)}, bf16[160,128]{1,0:T(8,128)(2,1)S(1)}, u32[]{:S(2)}, u32[]{:S(2)}) collective-permute-start(bf16[160,128]{1,0:T(8,128)(2,1)S(1)} %convert_element_type.74), channel_id=1, source_target_pairs={{0,64},{8,72},{16,80},{24,88},{32,96},{40,104},{48,112},{56,120},{... | collective-permute-start | bytes 122888 | tf_op jit(solution)/shard_map/ppermute | solution.py:35
  103.7 0.7 copy-start.8
  108.4 7.4 %collective-permute-start.15 = (bf16[160,128]{1,0:T(8,128)(2,1)S(1)}, bf16[160,128]{1,0:T(8,128)(2,1)S(1)}, u32[]{:S(2)}, u32[]{:S(2)}) collective-permute-start(bf16[160,128]{1,0:T(8,128)(2,1)S(1)} %convert_add_fusion.1), channel_id=1, source_target_pairs={{0,384},{8,392},{16,400},{24,408},{32,416},{40,424},{48,432},{56,4... | collective-permute-start | bytes 122888 | tf_op jit(solution)/shard_map/ppermute | solution.py:35
  109.0 6.8 %collective-permute-start.14 = (bf16[160,128]{1,0:T(8,128)(2,1)S(1)}, bf16[160,128]{1,0:T(8,128)(2,1)S(1)}, u32[]{:S(2)}, u32[]{:S(2)}) collective-permute-start(bf16[160,128]{1,0:T(8,128)(2,1)S(1)} %convert_add_fusion.1), channel_id=1, source_target_pairs={{0,256},{8,264},{16,272},{24,280},{32,288},{40,296},{48,304},{56,3... | collective-permute-start | bytes 122888 | tf_op jit(solution)/shard_map/ppermute | solution.py:35
  113.9 5.9 %collective-permute-start.13 = (bf16[160,128]{1,0:T(8,128)(2,1)S(1)}, bf16[160,128]{1,0:T(8,128)(2,1)S(1)}, u32[]{:S(2)}, u32[]{:S(2)}) collective-permute-start(bf16[160,128]{1,0:T(8,128)(2,1)S(1)} %convert_add_fusion.1), channel_id=1, source_target_pairs={{0,128},{8,136},{16,144},{24,152},{32,160},{40,168},{48,176},{56,1... | collective-permute-start | bytes 122888 | tf_op jit(solution)/shard_map/ppermute | solution.py:35
  119.8 3.1 %collective-permute-start.16 = (bf16[160,128]{1,0:T(8,128)(2,1)S(1)}, bf16[160,128]{1,0:T(8,128)(2,1)S(1)}, u32[]{:S(2)}, u32[]{:S(2)}) collective-permute-start(bf16[160,128]{1,0:T(8,128)(2,1)S(1)} %get-tuple-element.85), channel_id=1, source_target_pairs={{0,8},{8,0},{16,24},{24,16},{32,40},{40,32},{48,56},{56,48},{64,72... | collective-permute-start | bytes 122888 | tf_op jit(solution)/shard_map/ppermute | solution.py:35
  124.1 12.0 %collective-permute-start.19 = (bf16[64,2048]{1,0:T(8,128)(2,1)S(1)}, bf16[64,2048]{1,0:T(8,128)(2,1)S(1)}, u32[]{:S(2)}, u32[]{:S(2)}) collective-permute-start(bf16[64,2048]{1,0:T(8,128)(2,1)S(1)} %get-tuple-element.75), channel_id=1, source_target_pairs={{0,4},{8,12},{16,20},{24,28},{32,36},{40,44},{48,52},{56,60},{64,6... | collective-permute-start | bytes 786440 | tf_op jit(solution)/shard_map/ppermute | solution.py:35
  127.3 12.5 %collective-permute-start.18 = (bf16[64,2048]{1,0:T(8,128)(2,1)S(1)}, bf16[64,2048]{1,0:T(8,128)(2,1)S(1)}, u32[]{:S(2)}, u32[]{:S(2)}) collective-permute-start(bf16[64,2048]{1,0:T(8,128)(2,1)S(1)} %get-tuple-element.74), channel_id=1, source_target_pairs={{0,6},{8,14},{16,22},{24,30},{32,38},{40,46},{48,54},{56,62},{64,7... | collective-permute-start | bytes 786440 | tf_op jit(solution)/shard_map/ppermute | solution.py:35
  130.3 11.1 %collective-permute-start.17 = (bf16[64,2048]{1,0:T(8,128)(2,1)S(1)}, bf16[64,2048]{1,0:T(8,128)(2,1)S(1)}, u32[]{:S(2)}, u32[]{:S(2)}) collective-permute-start(bf16[64,2048]{1,0:T(8,128)(2,1)S(1)} %get-tuple-element.73), channel_id=1, source_target_pairs={{0,2},{8,10},{16,18},{24,26},{32,34},{40,42},{48,50},{56,58},{64,6... | collective-permute-start | bytes 786440 | tf_op jit(solution)/shard_map/ppermute | solution.py:35
  141.6 33.4 %collective-permute-start.20 = (bf16[64,2048]{1,0:T(8,128)(2,1)S(1)}, bf16[64,2048]{1,0:T(8,128)(2,1)S(1)}, u32[]{:S(2)}, u32[]{:S(2)}) collective-permute-start(bf16[64,2048]{1,0:T(8,128)(2,1)S(1)} %add_convert_fusion.1), channel_id=1, source_target_pairs={{0,1},{8,9},{16,17},{24,25},{32,33},{40,41},{48,49},{56,57},{64,65... | collective-permute-start | bytes 786440 | tf_op jit(solution)/shard_map/ppermute | solution.py:35
  151.6 23.4 %collective-permute-start.23 = (bf16[64,2048]{1,0:T(8,128)(2,1)S(1)}, bf16[64,2048]{1,0:T(8,128)(2,1)S(1)}, u32[]{:S(2)}, u32[]{:S(2)}) collective-permute-start(bf16[64,2048]{1,0:T(8,128)(2,1)S(1)} %get-tuple-element.82), channel_id=1, source_target_pairs={{0,4},{8,12},{16,20},{24,28},{32,36},{40,44},{48,52},{56,60},{64,6... | collective-permute-start | bytes 786440 | tf_op jit(solution)/shard_map/ppermute | solution.py:35
  154.9 20.1 %collective-permute-start.22 = (bf16[64,2048]{1,0:T(8,128)(2,1)S(1)}, bf16[64,2048]{1,0:T(8,128)(2,1)S(1)}, u32[]{:S(2)}, u32[]{:S(2)}) collective-permute-start(bf16[64,2048]{1,0:T(8,128)(2,1)S(1)} %get-tuple-element.81), channel_id=1, source_target_pairs={{0,6},{8,14},{16,22},{24,30},{32,38},{40,46},{48,54},{56,62},{64,7... | collective-permute-start | bytes 786440 | tf_op jit(solution)/shard_map/ppermute | solution.py:35
  158.0 17.0 %collective-permute-start.21 = (bf16[64,2048]{1,0:T(8,128)(2,1)S(1)}, bf16[64,2048]{1,0:T(8,128)(2,1)S(1)}, u32[]{:S(2)}, u32[]{:S(2)}) collective-permute-start(bf16[64,2048]{1,0:T(8,128)(2,1)S(1)} %get-tuple-element.80), channel_id=1, source_target_pairs={{0,2},{8,10},{16,18},{24,26},{32,34},{40,42},{48,50},{56,58},{64,6... | collective-permute-start | bytes 786440 | tf_op jit(solution)/shard_map/ppermute | solution.py:35

commit v7 on v5

--- a/solution.py
+++ b/solution.py
@@ -116,7 +116,7 @@
 
 def project_kernel(*refs):
     parts = refs[:N_TP]
-    wf, ww, table, qf_ref, kv_ref, tail_ref, mine_ref, other_ref, held, held_wf, qf, tail, sems = refs[N_TP:]
+    wf, ww, table, qf_ref, kv_ref, tail_ref, mine_ref, short_ref, other_ref, held, held_wf, qf, tail, sems = refs[N_TP:]
     x, half, core, _ = position()
     owners = [lax.rem(x + NX - s, NX) * 2 + side for side in (half, 1 - half) for s in (0, 1, 3, 2)]
     width = parts[0].shape[1]
@@ -135,7 +135,7 @@
     def columns(weight):
         return dot(tokens, weight).astype(bf16)
 
-    feats = columns(held_wf[...])
+    feats = dot_t(tokens, held_wf[...]).astype(bf16)
     ones = lax.broadcasted_iota(jnp.int32, feats.shape, 1) == 0
     feats = jnp.concatenate([feats, jnp.where(ones, 1.0, 0.0).astype(bf16)], axis=1)
     qf[:, 2 * head :] = feats
@@ -164,7 +164,9 @@
         high, low = halves(left * right)
         v = values[:, h * head : (h + 1) * head]
         states.append(dot(high, v) + dot(low, v))
-    mine_ref[...] = jnp.where(core == 0, states[0], states[1])
+    mine = jnp.where(core == 0, states[0], states[1])
+    mine_ref[...] = mine
+    short_ref[...] = mine.astype(bf16)
     other_ref[...] = jnp.where(core == 0, states[1], states[0]).astype(bf16)
     for copy in leave:
         copy.wait()
@@ -242,23 +244,23 @@
         out[...] = product[s * rows : (s + 1) * rows]
 
 
-def prefix(mine, other, place, halo, beside):
+def prefix(mine, short, other, place, halo, beside):
     x, h, y, z, c = place
+    across = send(other, lambda x, h, y, z, c: (x, h, y, z ^ 1, 1 - c)).astype(f32)
+    beyond = send(short, to_z(1)).astype(f32)
     got = send(other, to_core).astype(f32)
-    total = mine + got
+    total = mine + got + across + beyond
     add = (jnp.where(c == 0, mine, 0.0), jnp.where(c == 1, got, 0.0))
-    total, add = lax.optimization_barrier((total, add))
-    before = jnp.zeros_like(total)
+    before = jnp.where(z % 2 == 1, across + beyond, 0.0)
+    total, before, add = lax.optimization_barrier((total, before, add))
     done = None
-    for flip in (1, 2, 4):
+    for flip in (2, 4):
         part = send(total.astype(bf16), to_z(flip))
         if flip == 4:
             part, done = lax.optimization_barrier((part, done))
         part = part.astype(f32)
         before = before + jnp.where((z ^ flip) < z, part, 0.0)
         total, before = lax.optimization_barrier((total + part, before))
-        if flip == 1:
-            total, halo = lax.optimization_barrier((total, halo))
         if flip == 2:
             total, halo = lax.optimization_barrier((total, halo))
             done = beside(halo)
@@ -277,7 +279,7 @@
 def project(parts, wf, ww, tables):
     tok_rows = parts[0].shape[0]
     wide = 2 * ww.shape[2] // 3
-    queries = shape((tok_rows, wide + 2 * wf.shape[1]), bf16)
+    queries = shape((tok_rows, wide + 2 * wf.shape[0]), bf16)
     tail = shape(((WMAX - 1) * BLOCK, 2 * wide), bf16)
     return pl.pallas_call(
         project_kernel,
@@ -287,11 +289,12 @@
             tail,
             shape((ROWS, wide // 2), f32),
             shape((ROWS, wide // 2), bf16),
+            shape((ROWS, wide // 2), bf16),
         ),
         in_specs=[HBM] * (N_TP + 1) + [VMEM] * 2,
-        out_specs=(HBM, VMEM, HBM, VMEM, VMEM),
+        out_specs=(HBM, VMEM, HBM, VMEM, VMEM, VMEM),
         scratch_shapes=[
-            pltpu.VMEM((tok_rows, wf.shape[0]), bf16),
+            pltpu.VMEM((tok_rows, wf.shape[1]), bf16),
             pltpu.VMEM(wf.shape, bf16),
             pltpu.VMEM(queries.shape, bf16),
             pltpu.VMEM(tail.shape, bf16),
@@ -358,14 +361,14 @@
     w_out = w_out.reshape(-1, model_width)
     parts += [other] + [send(other, to_x(s)) for s in (1, 3, 2)]
     tables = feature_maps(feat_dim, head_count)
-    qf, kv, tail, mine, theirs = project(
-        parts, w_feature.reshape(model_width, -1), w_window.transpose(1, 0, 2), tables
+    qf, kv, tail, mine, short, theirs = project(
+        parts, w_feature.transpose(1, 2, 0).reshape(-1, model_width), w_window.transpose(1, 0, 2), tables
     )
 
     def beside(halo):
         return near(win_blocks, qf, kv, halo, tables)
 
-    ours, theirs, attended = prefix(mine, theirs, (x, h, y, z, c), send(tail, to_next), beside)
+    ours, theirs, attended = prefix(mine, short, theirs, (x, h, y, z, c), send(tail, to_next), beside)
     keep, away = hidden_rows(ours, theirs, *attended)
 
     def summed(total, group):

time: 165 us -> 169 us (1.024)
  the two profiles are of different devices: /device:TPU:46 before, /device:TPU:1 now
where the time goes in v7:
time: 169 us; the launch traced here: 168 us
  starting transfers between devices  116 us (69%)
  waiting for transfers between devices  36.2 us (21%)
  Pallas kernels  10.8 us (6%)
  other arithmetic  2.66 us (2%)
  local copies, waits for them, and re-layouts  2.32 us (1%)
    ppermute x24, starting transfers between devices, send(): return lax.ppermute(value, ('seq', 'tp'), pairs(move))  116 us
    ppermute x24, waiting for transfers between devices, send(): return lax.ppermute(value, ('seq', 'tp'), pairs(move))  36.2 us
    pallas_call x1, Pallas kernels, project(): pl.pallas_call(project_kernel, out_shape=(queries, shape((tok_rows, 2 * w...  5.31 us
    pallas_call x1, Pallas kernels, near(): pl.pallas_call(local_kernel, out_shape=(shape((tok_rows, wide), f32), sha...  3.98 us
  transfers between devices with their start and end apart: 24, of which 9 were waited for; matrix products, arithmetic and copies ran while one was open for 2% of the time, Pallas kernels for 3%

profile of v7, /device:TPU:1, one launch (start us, length us, event | category | flops | bytes accessed | tf_op | source)
XLA Modules:
  0.0 168.4 jit_solution(9988617080097894912)
XLA Ops:
  0.0 16.4 %collective-permute-start.3 = (bf16[512,256]{1,0:T(8,128)(2,1)}, bf16[512,256]{1,0:T(8,128)(2,1)S(1)}, u32[]{:S(2)}, u32[]{:S(2)}) collective-permute-start(bf16[512,256]{1,0:T(8,128)(2,1)} %refs_0_.1), channel_id=1, source_target_pairs={{0,1},{8,9},{16,17},{24,25},{32,33},{40,41},{48,49},{56,57},{64,65... | collective-permute-start | bytes 786440 | tf_op jit(solution)/shard_map/ppermute | solution.py:35
  16.4 3.1 %collective-permute-start = (bf16[512,256]{1,0:T(8,128)(2,1)}, bf16[512,256]{1,0:T(8,128)(2,1)S(1)}, u32[]{:S(2)}, u32[]{:S(2)}) collective-permute-start(bf16[512,256]{1,0:T(8,128)(2,1)} %refs_0_.1), channel_id=1, source_target_pairs={{0,2},{8,10},{16,18},{24,26},{32,34},{40,42},{48,50},{56,58},{64,6... | collective-permute-start | bytes 786440 | tf_op jit(solution)/shard_map/ppermute | solution.py:35
  19.5 3.4 %collective-permute-start.1 = (bf16[512,256]{1,0:T(8,128)(2,1)}, bf16[512,256]{1,0:T(8,128)(2,1)S(1)}, u32[]{:S(2)}, u32[]{:S(2)}) collective-permute-start(bf16[512,256]{1,0:T(8,128)(2,1)} %refs_0_.1), channel_id=1, source_target_pairs={{0,6},{8,14},{16,22},{24,30},{32,38},{40,46},{48,54},{56,62},{64,7... | collective-permute-start | bytes 786440 | tf_op jit(solution)/shard_map/ppermute | solution.py:35
  22.9 3.4 %collective-permute-start.2 = (bf16[512,256]{1,0:T(8,128)(2,1)}, bf16[512,256]{1,0:T(8,128)(2,1)S(1)}, u32[]{:S(2)}, u32[]{:S(2)}) collective-permute-start(bf16[512,256]{1,0:T(8,128)(2,1)} %refs_0_.1), channel_id=1, source_target_pairs={{0,4},{8,12},{16,20},{24,28},{32,36},{40,44},{48,52},{56,60},{64,6... | collective-permute-start | bytes 786440 | tf_op jit(solution)/shard_map/ppermute | solution.py:35
  26.4 0.0 collective-permute-done.3.refs_4_
  26.4 2.2 %collective-permute-start.4 = (bf16[512,256]{1,0:T(8,128)(2,1)S(1)}, bf16[512,256]{1,0:T(8,128)(2,1)S(1)}, u32[]{:S(2)}, u32[]{:S(2)}) collective-permute-start(bf16[512,256]{1,0:T(8,128)(2,1)S(1)} %collective-permute-done.3.refs_4_), channel_id=1, source_target_pairs={{0,2},{8,10},{16,18},{24,26},{32,34},{40,42},{48,50},{56,58},{64,6... | collective-permute-start | bytes 786440 | tf_op jit(solution)/shard_map/ppermute | solution.py:35
  28.6 4.3 %collective-permute-start.5 = (bf16[512,256]{1,0:T(8,128)(2,1)S(1)}, bf16[512,256]{1,0:T(8,128)(2,1)S(1)}, u32[]{:S(2)}, u32[]{:S(2)}) collective-permute-start(bf16[512,256]{1,0:T(8,128)(2,1)S(1)} %collective-permute-done.3.refs_4_), channel_id=1, source_target_pairs={{0,6},{8,14},{16,22},{24,30},{32,38},{40,46},{48,54},{56,62},{64,7... | collective-permute-start | bytes 786440 | tf_op jit(solution)/shard_map/ppermute | solution.py:35
  32.9 0.0 collective-permute-done.refs_1_
  32.9 2.1 %collective-permute-start.6 = (bf16[512,256]{1,0:T(8,128)(2,1)S(1)}, bf16[512,256]{1,0:T(8,128)(2,1)S(1)}, u32[]{:S(2)}, u32[]{:S(2)}) collective-permute-start(bf16[512,256]{1,0:T(8,128)(2,1)S(1)} %collective-permute-done.3.refs_4_), channel_id=1, source_target_pairs={{0,4},{8,12},{16,20},{24,28},{32,36},{40,44},{48,52},{56,60},{64,6... | collective-permute-start | bytes 786440 | tf_op jit(solution)/shard_map/ppermute | solution.py:35
  35.0 2.3 %copy.10 = bf16[2048,2,384]{2,0,1:T(8,128)(2,1)S(1)} copy(bf16[2048,2,384]{2,1,0:T(2,128)(2,1)} %param.9) | data formatting | bytes 6291456 | tf_op args[2]
  37.3 0.0 collective-permute-done.1.refs_2_
  37.4 0.0 collective-permute-done.2.refs_3_
  37.4 2.7 %collective-permute-done.4.refs_5_ = bf16[512,256]{1,0:T(8,128)(2,1)S(1)} collective-permute-done((bf16[512,256]{1,0:T(8,128)(2,1)S(1)}, bf16[512,256]{1,0:T(8,128)(2,1)S(1)}, u32[]{:S(2)}, u32[]{:S(2)}) %collective-permute-start.4) | collective-permute-done | bytes 262176 | tf_op jit(solution)/shard_map/ppermute | solution.py:35
  40.1 0.0 collective-permute-done.5.refs_6_
  40.1 4.6 %collective-permute-done.6.refs_7_ = bf16[512,256]{1,0:T(8,128)(2,1)S(1)} collective-permute-done((bf16[512,256]{1,0:T(8,128)(2,1)S(1)}, bf16[512,256]{1,0:T(8,128)(2,1)S(1)}, u32[]{:S(2)}, u32[]{:S(2)}) %collective-permute-start.6) | collective-permute-done | bytes 262176 | tf_op jit(solution)/shard_map/ppermute | solution.py:35
  44.7 0.0 copy-done.3
  44.7 0.0 copy-start.4
  44.7 5.3 %project.1 = (bf16[512,384]{1,0:T(8,128)(2,1)S(1)}, bf16[512,512]{1,0:T(8,128)(2,1)S(1)}, bf16[384,512]{1,0:T(8,128)(2,1)S(1)}, f32[160,128]{1,0:T(8,128)S(1)}, ...) custom-call(bf16[512,256]{1,0:T(8,128)(2,1)S(1)} %copy-done.2, ...), custom_call_target="tpu_custom_call" | custom-call | tf_op jit(solution)/shard_map/project/pallas_call | solution.py:284
  50.0 0.0 copy-start
  50.0 13.3 %collective-permute-start.9 = (bf16[160,128]{1,0:T(8,128)(2,1)S(1)}, bf16[160,128]{1,0:T(8,128)(2,1)S(1)}, u32[]{:S(2)}, u32[]{:S(2)}) collective-permute-start(bf16[160,128]{1,0:T(8,128)(2,1)S(1)} %get-tuple-element.44), channel_id=1, source_target_pairs={{0,16},{8,24},{16,0},{24,8},{32,48},{40,56},{48,32},{56,40},{64,80... | collective-permute-start | bytes 122888 | tf_op jit(solution)/shard_map/ppermute | solution.py:35
  63.4 4.7 %collective-permute-start.8 = (bf16[160,128]{1,0:T(8,128)(2,1)S(1)}, bf16[160,128]{1,0:T(8,128)(2,1)S(1)}, u32[]{:S(2)}, u32[]{:S(2)}) collective-permute-start(bf16[160,128]{1,0:T(8,128)(2,1)S(1)} %get-tuple-element.43), channel_id=1, source_target_pairs={{0,24},{8,16},{16,8},{24,0},{32,56},{40,48},{48,40},{56,32},{64,88... | collective-permute-start | bytes 122888 | tf_op jit(solution)/shard_map/ppermute | solution.py:35
  68.1 2.3 %collective-permute-start.7 = (bf16[160,128]{1,0:T(8,128)(2,1)S(1)}, bf16[160,128]{1,0:T(8,128)(2,1)S(1)}, u32[]{:S(2)}, u32[]{:S(2)}) collective-permute-start(bf16[160,128]{1,0:T(8,128)(2,1)S(1)} %get-tuple-element.43), channel_id=1, source_target_pairs={{0,8},{8,0},{16,24},{24,16},{32,40},{40,32},{48,56},{56,48},{64,72... | collective-permute-start | bytes 122888 | tf_op jit(solution)/shard_map/ppermute | solution.py:35
  70.5 3.6 %collective-permute-start.11 = (bf16[384,512]{1,0:T(8,128)(2,1)S(1)}, bf16[384,512]{1,0:T(8,128)(2,1)S(1)}, u32[]{:S(2)}, u32[]{:S(2)}) collective-permute-start(bf16[384,512]{1,0:T(8,128)(2,1)S(1)} %get-tuple-element.48), channel_id=1, source_target_pairs={{0,8},{8,16},{16,24},{24,32},{32,40},{40,48},{48,56},{56,64},{64,7... | collective-permute-start | bytes 1179656 | tf_op jit(solution)/shard_map/ppermute | solution.py:35
  74.1 0.0 collective-permute-done.9
  74.2 0.0 collective-permute-done.8
  74.2 0.0 collective-permute-done.7
  74.2 0.7 broadcast_select_fusion
  74.9 1.9 %collective-permute-start.10 = (bf16[160,128]{1,0:T(8,128)(2,1)S(1)}, bf16[160,128]{1,0:T(8,128)(2,1)S(1)}, u32[]{:S(2)}, u32[]{:S(2)}) collective-permute-start(bf16[160,128]{1,0:T(8,128)(2,1)S(1)} %convert_element_type.72), channel_id=1, source_target_pairs={{0,32},{8,40},{16,48},{24,56},{32,0},{40,8},{48,16},{56,24},{64,96... | collective-permute-start | bytes 122888 | tf_op jit(solution)/shard_map/ppermute | solution.py:35
  76.8 4.3 %collective-permute-done.10 = bf16[160,128]{1,0:T(8,128)(2,1)S(1)} collective-permute-done((bf16[160,128]{1,0:T(8,128)(2,1)S(1)}, bf16[160,128]{1,0:T(8,128)(2,1)S(1)}, u32[]{:S(2)}, u32[]{:S(2)}) %collective-permute-start.10) | collective-permute-done | bytes 40992 | tf_op jit(solution)/shard_map/ppermute | solution.py:35
  81.1 0.0 collective-permute-done.11.halo_ref
  81.1 9.8 %collective-permute-start.12 = (bf16[160,128]{1,0:T(8,128)(2,1)S(1)}, bf16[160,128]{1,0:T(8,128)(2,1)S(1)}, u32[]{:S(2)}, u32[]{:S(2)}) collective-permute-start(bf16[160,128]{1,0:T(8,128)(2,1)S(1)} %convert_element_type.74), channel_id=1, source_target_pairs={{0,64},{8,72},{16,80},{24,88},{32,96},{40,104},{48,112},{56,120},{... | collective-permute-start | bytes 122888 | tf_op jit(solution)/shard_map/ppermute | solution.py:35
  90.9 0.0 copy-done.4
  90.9 4.0 %near.1 = (f32[512,256]{1,0:T(8,128)S(1)}, f32[512,256]{1,0:T(8,128)S(1)}, bf16[2,512,160]{2,1,0:T(8,128)(2,1)S(1)}, bf16[2,512,160]{2,1,0:T(8,128)(2,1)S(1)}) custom-call(s32[2]{0:T(128)S(1)} %copy-done.4, bf16[512,384]{1,0:T(8,128)(2,1)S(1)} %get-tuple-element.50.qf_ref, bf16[512,512]{1,0:T(8,128)(2,1)S(1)} %get-tuple-element.51.kv_ref, ...), custom_call_target="tpu_custom_call" | custom-call | tf_op jit(solution)/shard_map/near/pallas_call | solution.py:310
  94.9 0.0 collective-permute-done.12
  94.9 1.3 collective-permute-start.15
  96.2 3.9 %collective-permute-start.14 = (bf16[160,128]{1,0:T(8,128)(2,1)S(1)}, bf16[160,128]{1,0:T(8,128)(2,1)S(1)}, u32[]{:S(2)}, u32[]{:S(2)}) collective-permute-start(bf16[160,128]{1,0:T(8,128)(2,1)S(1)} %convert_add_fusion.1), channel_id=1, source_target_pairs={{0,256},{8,264},{16,272},{24,280},{32,288},{40,296},{48,304},{56,3... | collective-permute-start | bytes 122888 | tf_op jit(solution)/shard_map/ppermute | solution.py:35
  100.1 1.3 collective-permute-start.13
  101.4 0.0 collective-permute-done.15
  101.4 0.0 collective-permute-done.14
  101.5 1.1 collective-permute-done.13
  102.5 0.9 add_convert_fusion.2
  103.4 7.6 %collective-permute-start.16 = (bf16[160,128]{1,0:T(8,128)(2,1)S(1)}, bf16[160,128]{1,0:T(8,128)(2,1)S(1)}, u32[]{:S(2)}, u32[]{:S(2)}) collective-permute-start(bf16[160,128]{1,0:T(8,128)(2,1)S(1)} %get-tuple-element.79), channel_id=1, source_target_pairs={{0,8},{8,0},{16,24},{24,16},{32,40},{40,32},{48,56},{56,48},{64,72... | collective-permute-start | bytes 122888 | tf_op jit(solution)/shard_map/ppermute | solution.py:35
  111.1 0.8 collective-permute-done.16.theirs
  111.9 0.7 hidden.1
  112.6 0.0 copy-done
  112.6 0.4 product.2
  113.1 3.4 %collective-permute-start.19 = (bf16[64,2048]{1,0:T(8,128)(2,1)S(1)}, bf16[64,2048]{1,0:T(8,128)(2,1)S(1)}, u32[]{:S(2)}, u32[]{:S(2)}) collective-permute-start(bf16[64,2048]{1,0:T(8,128)(2,1)S(1)} %get-tuple-element.71), channel_id=1, source_target_pairs={{0,4},{8,12},{16,20},{24,28},{32,36},{40,44},{48,52},{56,60},{64,6... | collective-permute-start | bytes 786440 | tf_op jit(solution)/shard_map/ppermute | solution.py:35
  116.5 5.3 %collective-permute-start.18 = (bf16[64,2048]{1,0:T(8,128)(2,1)S(1)}, bf16[64,2048]{1,0:T(8,128)(2,1)S(1)}, u32[]{:S(2)}, u32[]{:S(2)}) collective-permute-start(bf16[64,2048]{1,0:T(8,128)(2,1)S(1)} %get-tuple-element.70), channel_id=1, source_target_pairs={{0,6},{8,14},{16,22},{24,30},{32,38},{40,46},{48,54},{56,62},{64,7... | collective-permute-start | bytes 786440 | tf_op jit(solution)/shard_map/ppermute | solution.py:35
  121.8 1.9 %collective-permute-start.17 = (bf16[64,2048]{1,0:T(8,128)(2,1)S(1)}, bf16[64,2048]{1,0:T(8,128)(2,1)S(1)}, u32[]{:S(2)}, u32[]{:S(2)}) collective-permute-start(bf16[64,2048]{1,0:T(8,128)(2,1)S(1)} %get-tuple-element.69), channel_id=1, source_target_pairs={{0,2},{8,10},{16,18},{24,26},{32,34},{40,42},{48,50},{56,58},{64,6... | collective-permute-start | bytes 786440 | tf_op jit(solution)/shard_map/ppermute | solution.py:35
  123.8 0.2 collective-permute-done.19
  124.0 6.6 %collective-permute-done.18 = bf16[64,2048]{1,0:T(8,128)(2,1)S(1)} collective-permute-done((bf16[64,2048]{1,0:T(8,128)(2,1)S(1)}, bf16[64,2048]{1,0:T(8,128)(2,1)S(1)}, u32[]{:S(2)}, u32[]{:S(2)}) %collective-permute-start.18) | collective-permute-done | bytes 262176 | tf_op jit(solution)/shard_map/ppermute | solution.py:35
  130.6 1.2 collective-permute-done.17
  131.8 0.1 add_convert_fusion.1
  132.0 11.3 %collective-permute-start.20 = (bf16[64,2048]{1,0:T(8,128)(2,1)S(1)}, bf16[64,2048]{1,0:T(8,128)(2,1)S(1)}, u32[]{:S(2)}, u32[]{:S(2)}) collective-permute-start(bf16[64,2048]{1,0:T(8,128)(2,1)S(1)} %add_convert_fusion.1), channel_id=1, source_target_pairs={{0,1},{8,9},{16,17},{24,25},{32,33},{40,41},{48,49},{56,57},{64,65... | collective-permute-start | bytes 786440 | tf_op jit(solution)/shard_map/ppermute | solution.py:35
  143.3 0.4 product.3
  143.7 2.9 %collective-permute-start.23 = (bf16[64,2048]{1,0:T(8,128)(2,1)S(1)}, bf16[64,2048]{1,0:T(8,128)(2,1)S(1)}, u32[]{:S(2)}, u32[]{:S(2)}) collective-permute-start(bf16[64,2048]{1,0:T(8,128)(2,1)S(1)} %get-tuple-element.78), channel_id=1, source_target_pairs={{0,4},{8,12},{16,20},{24,28},{32,36},{40,44},{48,52},{56,60},{64,6... | collective-permute-start | bytes 786440 | tf_op jit(solution)/shard_map/ppermute | solution.py:35
  146.6 4.3 %collective-permute-start.22 = (bf16[64,2048]{1,0:T(8,128)(2,1)S(1)}, bf16[64,2048]{1,0:T(8,128)(2,1)S(1)}, u32[]{:S(2)}, u32[]{:S(2)}) collective-permute-start(bf16[64,2048]{1,0:T(8,128)(2,1)S(1)} %get-tuple-element.77), channel_id=1, source_target_pairs={{0,6},{8,14},{16,22},{24,30},{32,38},{40,46},{48,54},{56,62},{64,7... | collective-permute-start | bytes 786440 | tf_op jit(solution)/shard_map/ppermute | solution.py:35
  150.9 1.9 %collective-permute-start.21 = (bf16[64,2048]{1,0:T(8,128)(2,1)S(1)}, bf16[64,2048]{1,0:T(8,128)(2,1)S(1)}, u32[]{:S(2)}, u32[]{:S(2)}) collective-permute-start(bf16[64,2048]{1,0:T(8,128)(2,1)S(1)} %get-tuple-element.76), channel_id=1, source_target_pairs={{0,2},{8,10},{16,18},{24,26},{32,34},{40,42},{48,50},{56,58},{64,6... | collective-permute-start | bytes 786440 | tf_op jit(solution)/shard_map/ppermute | solution.py:35
  152.9 14.6 %collective-permute-done.20 = bf16[64,2048]{1,0:T(8,128)(2,1)S(1)} collective-permute-done((bf16[64,2048]{1,0:T(8,128)(2,1)S(1)}, bf16[64,2048]{1,0:T(8,128)(2,1)S(1)}, u32[]{:S(2)}, u32[]{:S(2)}) %collective-permute-start.20) | collective-permute-done | bytes 262176 | tf_op jit(solution)/shard_map/ppermute | solution.py:35
  167.5 0.1 convert_add_fusion
  167.5 0.0 collective-permute-done.23
  167.5 0.0 collective-permute-done.22
  167.6 0.0 collective-permute-done.21
  167.6 0.8 add_convert_fusion
  (10 shorter events, 0.1 us)
Async XLA Ops:
  0.0 44.7 %copy-start.1 = (bf16[2,4,160,128]{3,2,1,0:T(8,128)(2,1)S(1)}, bf16[2,4,160,128]{3,2,1,0:T(8,128)(2,1)}, u32[]{:S(2)}) copy-start(bf16[2,4,160,128]{3,2,1,0:T(8,128)(2,1)} %constant.52.clone.refs_10_.table) | copy-start | bytes 983044
  0.0 44.7 %copy-start.2 = (bf16[512,256]{1,0:T(8,128)(2,1)S(1)}, bf16[512,256]{1,0:T(8,128)(2,1)}, u32[]{:S(2)}) copy-start(bf16[512,256]{1,0:T(8,128)(2,1)} %refs_0_.1) | copy-start | bytes 786436
  0.0 44.7 %copy-start.3 = (bf16[2048,2,32]{0,2,1:T(8,128)(2,1)S(1)}, bf16[2048,2,32]{0,2,1:T(8,128)(2,1)}, u32[]{:S(2)}) copy-start(bf16[2048,2,32]{0,2,1:T(8,128)(2,1)} %param.8) | copy-start | bytes 786436
  0.0 26.4 %collective-permute-start.3 = (bf16[512,256]{1,0:T(8,128)(2,1)}, bf16[512,256]{1,0:T(8,128)(2,1)S(1)}, u32[]{:S(2)}, u32[]{:S(2)}) collective-permute-start(bf16[512,256]{1,0:T(8,128)(2,1)} %refs_0_.1), channel_id=1, source_target_pairs={{0,1},{8,9},{16,17},{24,25},{32,33},{40,41},{48,49},{56,57},{64,65... | collective-permute-start | bytes 786440 | tf_op jit(solution)/shard_map/ppermute | solution.py:35
  16.4 16.5 %collective-permute-start = (bf16[512,256]{1,0:T(8,128)(2,1)}, bf16[512,256]{1,0:T(8,128)(2,1)S(1)}, u32[]{:S(2)}, u32[]{:S(2)}) collective-permute-start(bf16[512,256]{1,0:T(8,128)(2,1)} %refs_0_.1), channel_id=1, source_target_pairs={{0,2},{8,10},{16,18},{24,26},{32,34},{40,42},{48,50},{56,58},{64,6... | collective-permute-start | bytes 786440 | tf_op jit(solution)/shard_map/ppermute | solution.py:35
  19.5 17.8 %collective-permute-start.1 = (bf16[512,256]{1,0:T(8,128)(2,1)}, bf16[512,256]{1,0:T(8,128)(2,1)S(1)}, u32[]{:S(2)}, u32[]{:S(2)}) collective-permute-start(bf16[512,256]{1,0:T(8,128)(2,1)} %refs_0_.1), channel_id=1, source_target_pairs={{0,6},{8,14},{16,22},{24,30},{32,38},{40,46},{48,54},{56,62},{64,7... | collective-permute-start | bytes 786440 | tf_op jit(solution)/shard_map/ppermute | solution.py:35
  22.9 14.4 %collective-permute-start.2 = (bf16[512,256]{1,0:T(8,128)(2,1)}, bf16[512,256]{1,0:T(8,128)(2,1)S(1)}, u32[]{:S(2)}, u32[]{:S(2)}) collective-permute-start(bf16[512,256]{1,0:T(8,128)(2,1)} %refs_0_.1), channel_id=1, source_target_pairs={{0,4},{8,12},{16,20},{24,28},{32,36},{40,44},{48,52},{56,60},{64,6... | collective-permute-start | bytes 786440 | tf_op jit(solution)/shard_map/ppermute | solution.py:35
  26.4 13.7 %collective-permute-start.4 = (bf16[512,256]{1,0:T(8,128)(2,1)S(1)}, bf16[512,256]{1,0:T(8,128)(2,1)S(1)}, u32[]{:S(2)}, u32[]{:S(2)}) collective-permute-start(bf16[512,256]{1,0:T(8,128)(2,1)S(1)} %collective-permute-done.3.refs_4_), channel_id=1, source_target_pairs={{0,2},{8,10},{16,18},{24,26},{32,34},{40,42},{48,50},{56,58},{64,6... | collective-permute-start | bytes 786440 | tf_op jit(solution)/shard_map/ppermute | solution.py:35
  28.6 11.5 %collective-permute-start.5 = (bf16[512,256]{1,0:T(8,128)(2,1)S(1)}, bf16[512,256]{1,0:T(8,128)(2,1)S(1)}, u32[]{:S(2)}, u32[]{:S(2)}) collective-permute-start(bf16[512,256]{1,0:T(8,128)(2,1)S(1)} %collective-permute-done.3.refs_4_), channel_id=1, source_target_pairs={{0,6},{8,14},{16,22},{24,30},{32,38},{40,46},{48,54},{56,62},{64,7... | collective-permute-start | bytes 786440 | tf_op jit(solution)/shard_map/ppermute | solution.py:35
  32.9 11.8 %collective-permute-start.6 = (bf16[512,256]{1,0:T(8,128)(2,1)S(1)}, bf16[512,256]{1,0:T(8,128)(2,1)S(1)}, u32[]{:S(2)}, u32[]{:S(2)}) collective-permute-start(bf16[512,256]{1,0:T(8,128)(2,1)S(1)} %collective-permute-done.3.refs_4_), channel_id=1, source_target_pairs={{0,4},{8,12},{16,20},{24,28},{32,36},{40,44},{48,52},{56,60},{64,6... | collective-permute-start | bytes 786440 | tf_op jit(solution)/shard_map/ppermute | solution.py:35
  44.7 46.2 %copy-start.4 = (s32[2]{0:T(128)S(1)}, s32[2]{0:T(128)}, u32[]{:S(2)}) copy-start(s32[2]{0:T(128)} %win.1) | copy-start | bytes 28
  50.0 62.6 %copy-start = (bf16[2,128,2048]{2,1,0:T(8,128)(2,1)S(1)}, bf16[2,128,2048]{2,1,0:T(8,128)(2,1)}, u32[]{:S(2)}) copy-start(bf16[2,128,2048]{2,1,0:T(8,128)(2,1)} %param.10) | copy-start | bytes 3145732
  50.0 24.1 %collective-permute-start.9 = (bf16[160,128]{1,0:T(8,128)(2,1)S(1)}, bf16[160,128]{1,0:T(8,128)(2,1)S(1)}, u32[]{:S(2)}, u32[]{:S(2)}) collective-permute-start(bf16[160,128]{1,0:T(8,128)(2,1)S(1)} %get-tuple-element.44), channel_id=1, source_target_pairs={{0,16},{8,24},{16,0},{24,8},{32,48},{40,56},{48,32},{56,40},{64,80... | collective-permute-start | bytes 122888 | tf_op jit(solution)/shard_map/ppermute | solution.py:35
  63.4 10.8 %collective-permute-start.8 = (bf16[160,128]{1,0:T(8,128)(2,1)S(1)}, bf16[160,128]{1,0:T(8,128)(2,1)S(1)}, u32[]{:S(2)}, u32[]{:S(2)}) collective-permute-start(bf16[160,128]{1,0:T(8,128)(2,1)S(1)} %get-tuple-element.43), channel_id=1, source_target_pairs={{0,24},{8,16},{16,8},{24,0},{32,56},{40,48},{48,40},{56,32},{64,88... | collective-permute-start | bytes 122888 | tf_op jit(solution)/shard_map/ppermute | solution.py:35
  68.1 6.0 %collective-permute-start.7 = (bf16[160,128]{1,0:T(8,128)(2,1)S(1)}, bf16[160,128]{1,0:T(8,128)(2,1)S(1)}, u32[]{:S(2)}, u32[]{:S(2)}) collective-permute-start(bf16[160,128]{1,0:T(8,128)(2,1)S(1)} %get-tuple-element.43), channel_id=1, source_target_pairs={{0,8},{8,0},{16,24},{24,16},{32,40},{40,32},{48,56},{56,48},{64,72... | collective-permute-start | bytes 122888 | tf_op jit(solution)/shard_map/ppermute | solution.py:35
  70.5 10.6 %collective-permute-start.11 = (bf16[384,512]{1,0:T(8,128)(2,1)S(1)}, bf16[384,512]{1,0:T(8,128)(2,1)S(1)}, u32[]{:S(2)}, u32[]{:S(2)}) collective-permute-start(bf16[384,512]{1,0:T(8,128)(2,1)S(1)} %get-tuple-element.48), channel_id=1, source_target_pairs={{0,8},{8,16},{16,24},{24,32},{32,40},{40,48},{48,56},{56,64},{64,7... | collective-permute-start | bytes 1179656 | tf_op jit(solution)/shard_map/ppermute | solution.py:35
  74.9 6.2 %collective-permute-start.10 = (bf16[160,128]{1,0:T(8,128)(2,1)S(1)}, bf16[160,128]{1,0:T(8,128)(2,1)S(1)}, u32[]{:S(2)}, u32[]{:S(2)}) collective-permute-start(bf16[160,128]{1,0:T(8,128)(2,1)S(1)} %convert_element_type.72), channel_id=1, source_target_pairs={{0,32},{8,40},{16,48},{24,56},{32,0},{40,8},{48,16},{56,24},{64,96... | collective-permute-start | bytes 122888 | tf_op jit(solution)/shard_map/ppermute | solution.py:35
  81.1 13.8 %collective-permute-start.12 = (bf16[160,128]{1,0:T(8,128)(2,1)S(1)}, bf16[160,128]{1,0:T(8,128)(2,1)S(1)}, u32[]{:S(2)}, u32[]{:S(2)}) collective-permute-start(bf16[160,128]{1,0:T(8,128)(2,1)S(1)} %convert_element_type.74), channel_id=1, source_target_pairs={{0,64},{8,72},{16,80},{24,88},{32,96},{40,104},{48,112},{56,120},{... | collective-permute-start | bytes 122888 | tf_op jit(solution)/shard_map/ppermute | solution.py:35
  94.9 6.5 %collective-permute-start.15 = (bf16[160,128]{1,0:T(8,128)(2,1)S(1)}, bf16[160,128]{1,0:T(8,128)(2,1)S(1)}, u32[]{:S(2)}, u32[]{:S(2)}) collective-permute-start(bf16[160,128]{1,0:T(8,128)(2,1)S(1)} %convert_add_fusion.1), channel_id=1, source_target_pairs={{0,384},{8,392},{16,400},{24,408},{32,416},{40,424},{48,432},{56,4... | collective-permute-start | bytes 122888 | tf_op jit(solution)/shard_map/ppermute | solution.py:35
  96.2 5.2 %collective-permute-start.14 = (bf16[160,128]{1,0:T(8,128)(2,1)S(1)}, bf16[160,128]{1,0:T(8,128)(2,1)S(1)}, u32[]{:S(2)}, u32[]{:S(2)}) collective-permute-start(bf16[160,128]{1,0:T(8,128)(2,1)S(1)} %convert_add_fusion.1), channel_id=1, source_target_pairs={{0,256},{8,264},{16,272},{24,280},{32,288},{40,296},{48,304},{56,3... | collective-permute-start | bytes 122888 | tf_op jit(solution)/shard_map/ppermute | solution.py:35
  100.1 2.4 %collective-permute-start.13 = (bf16[160,128]{1,0:T(8,128)(2,1)S(1)}, bf16[160,128]{1,0:T(8,128)(2,1)S(1)}, u32[]{:S(2)}, u32[]{:S(2)}) collective-permute-start(bf16[160,128]{1,0:T(8,128)(2,1)S(1)} %convert_add_fusion.1), channel_id=1, source_target_pairs={{0,128},{8,136},{16,144},{24,152},{32,160},{40,168},{48,176},{56,1... | collective-permute-start | bytes 122888 | tf_op jit(solution)/shard_map/ppermute | solution.py:35
  103.4 8.5 %collective-permute-start.16 = (bf16[160,128]{1,0:T(8,128)(2,1)S(1)}, bf16[160,128]{1,0:T(8,128)(2,1)S(1)}, u32[]{:S(2)}, u32[]{:S(2)}) collective-permute-start(bf16[160,128]{1,0:T(8,128)(2,1)S(1)} %get-tuple-element.79), channel_id=1, source_target_pairs={{0,8},{8,0},{16,24},{24,16},{32,40},{40,32},{48,56},{56,48},{64,72... | collective-permute-start | bytes 122888 | tf_op jit(solution)/shard_map/ppermute | solution.py:35
  113.1 10.9 %collective-permute-start.19 = (bf16[64,2048]{1,0:T(8,128)(2,1)S(1)}, bf16[64,2048]{1,0:T(8,128)(2,1)S(1)}, u32[]{:S(2)}, u32[]{:S(2)}) collective-permute-start(bf16[64,2048]{1,0:T(8,128)(2,1)S(1)} %get-tuple-element.71), channel_id=1, source_target_pairs={{0,4},{8,12},{16,20},{24,28},{32,36},{40,44},{48,52},{56,60},{64,6... | collective-permute-start | bytes 786440 | tf_op jit(solution)/shard_map/ppermute | solution.py:35
  116.5 14.1 %collective-permute-start.18 = (bf16[64,2048]{1,0:T(8,128)(2,1)S(1)}, bf16[64,2048]{1,0:T(8,128)(2,1)S(1)}, u32[]{:S(2)}, u32[]{:S(2)}) collective-permute-start(bf16[64,2048]{1,0:T(8,128)(2,1)S(1)} %get-tuple-element.70), channel_id=1, source_target_pairs={{0,6},{8,14},{16,22},{24,30},{32,38},{40,46},{48,54},{56,62},{64,7... | collective-permute-start | bytes 786440 | tf_op jit(solution)/shard_map/ppermute | solution.py:35
  121.8 10.0 %collective-permute-start.17 = (bf16[64,2048]{1,0:T(8,128)(2,1)S(1)}, bf16[64,2048]{1,0:T(8,128)(2,1)S(1)}, u32[]{:S(2)}, u32[]{:S(2)}) collective-permute-start(bf16[64,2048]{1,0:T(8,128)(2,1)S(1)} %get-tuple-element.69), channel_id=1, source_target_pairs={{0,2},{8,10},{16,18},{24,26},{32,34},{40,42},{48,50},{56,58},{64,6... | collective-permute-start | bytes 786440 | tf_op jit(solution)/shard_map/ppermute | solution.py:35
  132.0 35.5 %collective-permute-start.20 = (bf16[64,2048]{1,0:T(8,128)(2,1)S(1)}, bf16[64,2048]{1,0:T(8,128)(2,1)S(1)}, u32[]{:S(2)}, u32[]{:S(2)}) collective-permute-start(bf16[64,2048]{1,0:T(8,128)(2,1)S(1)} %add_convert_fusion.1), channel_id=1, source_target_pairs={{0,1},{8,9},{16,17},{24,25},{32,33},{40,41},{48,49},{56,57},{64,65... | collective-permute-start | bytes 786440 | tf_op jit(solution)/shard_map/ppermute | solution.py:35
  143.7 23.8 %collective-permute-start.23 = (bf16[64,2048]{1,0:T(8,128)(2,1)S(1)}, bf16[64,2048]{1,0:T(8,128)(2,1)S(1)}, u32[]{:S(2)}, u32[]{:S(2)}) collective-permute-start(bf16[64,2048]{1,0:T(8,128)(2,1)S(1)} %get-tuple-element.78), channel_id=1, source_target_pairs={{0,4},{8,12},{16,20},{24,28},{32,36},{40,44},{48,52},{56,60},{64,6... | collective-permute-start | bytes 786440 | tf_op jit(solution)/shard_map/ppermute | solution.py:35
  146.6 21.0 %collective-permute-start.22 = (bf16[64,2048]{1,0:T(8,128)(2,1)S(1)}, bf16[64,2048]{1,0:T(8,128)(2,1)S(1)}, u32[]{:S(2)}, u32[]{:S(2)}) collective-permute-start(bf16[64,2048]{1,0:T(8,128)(2,1)S(1)} %get-tuple-element.77), channel_id=1, source_target_pairs={{0,6},{8,14},{16,22},{24,30},{32,38},{40,46},{48,54},{56,62},{64,7... | collective-permute-start | bytes 786440 | tf_op jit(solution)/shard_map/ppermute | solution.py:35
  150.9 16.6 %collective-permute-start.21 = (bf16[64,2048]{1,0:T(8,128)(2,1)S(1)}, bf16[64,2048]{1,0:T(8,128)(2,1)S(1)}, u32[]{:S(2)}, u32[]{:S(2)}) collective-permute-start(bf16[64,2048]{1,0:T(8,128)(2,1)S(1)} %get-tuple-element.76), channel_id=1, source_target_pairs={{0,2},{8,10},{16,18},{24,26},{32,34},{40,42},{48,50},{56,58},{64,6... | collective-permute-start | bytes 786440 | tf_op jit(solution)/shard_map/ppermute | solution.py:35

commit v8 on v7

--- a/solution.py
+++ b/solution.py
@@ -172,22 +172,17 @@
         copy.wait()
 
 
-def local_kernel(win, qf_ref, kv_ref, halo_ref, table, near_ref, win_ref, high_ref, low_ref, qn_ref, sem):
+def near_kernel(qf_ref, kv_ref, table, near_ref, high_ref, low_ref, qn_ref, sem):
     copy = pltpu.make_async_copy(qf_ref, qn_ref, sem)
     copy.start()
     copy.wait()
-    seq = position()[3]
     rows = qn_ref.shape[0]
-    heads = win_ref.shape[1] // 128
+    heads = near_ref.shape[1] // 128
     head = 128
-    halo = halo_ref.shape[0]
-    span = halo + BLOCK
     feats = qn_ref[:, heads * head :]
     feat = feats.shape[1] // (4 * heads)
-    blocks = rows // BLOCK
-    row = lax.broadcasted_iota(jnp.int32, (BLOCK, span), 0)
-    col = lax.broadcasted_iota(jnp.int32, (BLOCK, span), 1)
-    causal = col <= row + halo
+    row = lax.broadcasted_iota(jnp.int32, (BLOCK, BLOCK), 0)
+    col = lax.broadcasted_iota(jnp.int32, (BLOCK, BLOCK), 1)
     for h in range(heads):
         cols = slice(h * head, (h + 1) * head)
         vcols = slice((heads + h) * head, (heads + h + 1) * head)
@@ -201,16 +196,37 @@
         first = h * 2 * feat
         moved = (lane == key + feat) & (key >= first) & (key < first + feat)
         query = dot(feats, jnp.where(moved, 1.0, 0.0).astype(bf16)).astype(bf16)
+        for b in range(rows // BLOCK):
+            at = slice(b * BLOCK, (b + 1) * BLOCK)
+            ahead = (b + 1) * BLOCK
+            inner = dot_t(query[at], feats[:ahead])
+            pair = 1.0 + inner * (0.25 + inner * (1.0 / 32.0))
+            last = jnp.where(col <= row, pair[:, b * BLOCK :], 0.0)
+            pair = jnp.concatenate([pair[:, : b * BLOCK], last], axis=1) if b else last
+            near_ref[at, cols] = dot(pair.astype(bf16), kv_ref[:ahead, vcols])
+
+
+def window_kernel(win, qf_ref, kv_ref, halo_ref, win_ref, qn_ref, sem):
+    copy = pltpu.make_async_copy(qf_ref, qn_ref, sem)
+    copy.start()
+    copy.wait()
+    seq = position()[3]
+    rows = qn_ref.shape[0]
+    heads = win_ref.shape[1] // 128
+    head = 128
+    halo = halo_ref.shape[0]
+    span = halo + BLOCK
+    blocks = rows // BLOCK
+    row = lax.broadcasted_iota(jnp.int32, (BLOCK, span), 0)
+    col = lax.broadcasted_iota(jnp.int32, (BLOCK, span), 1)
+    causal = col <= row + halo
+    for h in range(heads):
+        cols = slice(h * head, (h + 1) * head)
+        vcols = slice((heads + h) * head, (heads + h + 1) * head)
         keys = jnp.concatenate([halo_ref[:, cols], kv_ref[:, cols]], axis=0)
         values = jnp.concatenate([halo_ref[:, vcols], kv_ref[:, vcols]], axis=0)
         for b in range(blocks):
             at = slice(b * BLOCK, (b + 1) * BLOCK)
-            ahead = (b + 1) * BLOCK
-            inner = dot_t(query[at], feats[:ahead])
-            pair = 1.0 + inner * (0.25 + inner * (1.0 / 32.0))
-            last = jnp.where(causal[:, halo:], pair[:, b * BLOCK :], 0.0)
-            pair = jnp.concatenate([pair[:, : b * BLOCK], last], axis=1) if b else last
-            near_ref[at, cols] = dot(pair.astype(bf16), values[halo : halo + ahead])
             scores = dot_t(qn_ref[at, cols], keys[b * BLOCK : b * BLOCK + span]) * (SCALE / head)
             least = jnp.maximum(span // BLOCK - win[h], span // BLOCK - 1 - (seq * blocks + b))
             allowed = causal & (col >= least * BLOCK)
@@ -244,7 +260,7 @@
         out[...] = product[s * rows : (s + 1) * rows]
 
 
-def prefix(mine, short, other, place, halo, beside):
+def prefix(mine, short, other, place, beside):
     x, h, y, z, c = place
     across = send(other, lambda x, h, y, z, c: (x, h, y, z ^ 1, 1 - c)).astype(f32)
     beyond = send(short, to_z(1)).astype(f32)
@@ -257,13 +273,14 @@
     for flip in (2, 4):
         part = send(total.astype(bf16), to_z(flip))
         if flip == 4:
-            part, done = lax.optimization_barrier((part, done))
+            *behind, halo = done
+            part, *behind = lax.optimization_barrier((part, *behind))
+            done = (*behind, halo)
         part = part.astype(f32)
         before = before + jnp.where((z ^ flip) < z, part, 0.0)
         total, before = lax.optimization_barrier((total + part, before))
         if flip == 2:
-            total, halo = lax.optimization_barrier((total, halo))
-            done = beside(halo)
+            done = beside(total)
     short = total.astype(bf16)
     for steps in (1, 2, 3):
         before = before + send(short, to_y(steps)).astype(f32)
@@ -305,22 +322,33 @@
     )(*parts, wf, ww, tables.astype(bf16))
 
 
-def near(win_blocks, qf, kv, halo, tables):
+def near(qf, kv, tables):
     tok_rows, wide = kv.shape[0], kv.shape[1] // 2
     return pl.pallas_call(
-        local_kernel,
+        near_kernel,
         out_shape=(
-            shape((tok_rows, wide), f32),
             shape((tok_rows, wide), f32),
             shape((2, tok_rows, ROWS), bf16),
             shape((2, tok_rows, ROWS), bf16),
         ),
-        in_specs=[SMEM, HBM, VMEM, VMEM, VMEM],
-        out_specs=(VMEM,) * 4,
+        in_specs=[HBM, VMEM, VMEM],
+        out_specs=(VMEM,) * 3,
         scratch_shapes=[pltpu.VMEM(qf.shape, bf16), pltpu.SemaphoreType.DMA],
         name="near",
         compiler_params=pltpu.CompilerParams(vmem_limit_bytes=LIMIT),
-    )(win_blocks, qf, kv, halo, tables.astype(bf16))
+    )(qf, kv, tables.astype(bf16))
+
+
+def window(win_blocks, qf, kv, halo):
+    return pl.pallas_call(
+        window_kernel,
+        out_shape=shape((kv.shape[0], kv.shape[1] // 2), f32),
+        in_specs=[SMEM, HBM, VMEM, VMEM],
+        out_specs=VMEM,
+        scratch_shapes=[pltpu.VMEM(qf.shape, bf16), pltpu.SemaphoreType.DMA],
+        name="window",
+        compiler_params=pltpu.CompilerParams(vmem_limit_bytes=LIMIT),
+    )(win_blocks, qf, kv, halo)
 
 
 def hidden_rows(ours, theirs, near_out, win_out, high, low):
@@ -365,11 +393,13 @@
         parts, w_feature.transpose(1, 2, 0).reshape(-1, model_width), w_window.transpose(1, 0, 2), tables
     )
 
-    def beside(halo):
-        return near(win_blocks, qf, kv, halo, tables)
-
-    ours, theirs, attended = prefix(mine, short, theirs, (x, h, y, z, c), send(tail, to_next), beside)
-    keep, away = hidden_rows(ours, theirs, *attended)
+    def beside(total):
+        early, kept, _ = lax.optimization_barrier((qf, tail, total))
+        return *near(early, kv, tables), send(kept, to_next)
+
+    ours, theirs, (near_out, high, low, halo) = prefix(mine, short, theirs, (x, h, y, z, c), beside)
+    win_out = window(win_blocks, qf, kv, halo)
+    keep, away = hidden_rows(ours, theirs, near_out, win_out, high, low)
 
     def summed(total, group):
         for steps in (1, 3, 2):

time: 169 us -> 165 us (0.976)
  the two profiles are of different devices: /device:TPU:1 before, /device:TPU:16 now
where the time goes in v8:
time: 165 us; the launch traced here: 164 us
  starting transfers between devices  102 us (62%)
  waiting for transfers between devices  47.4 us (29%)
  Pallas kernels  11.4 us (7%)
  local copies, waits for them, and re-layouts  2.32 us (1%)
    ppermute x24, starting transfers between devices, send(): return lax.ppermute(value, ('seq', 'tp'), pairs(move))  102 us
    ppermute x24, waiting for transfers between devices, send(): return lax.ppermute(value, ('seq', 'tp'), pairs(move))  47.4 us
    pallas_call x1, Pallas kernels, project(): pl.pallas_call(project_kernel, out_shape=(queries, shape((tok_rows, 2 * w...  5.32 us
  transfers between devices with their start and end apart: 24, of which 12 were waited for; matrix products, arithmetic and copies ran while one was open for 1% of the time, Pallas kernels for 3%

profile of v8, /device:TPU:16, one launch (start us, length us, event | category | flops | bytes accessed | tf_op | source)
XLA Modules:
  0.0 164.2 jit_solution(9864717099302373671)
XLA Ops:
  0.0 15.9 %collective-permute-start.3 = (bf16[512,256]{1,0:T(8,128)(2,1)}, bf16[512,256]{1,0:T(8,128)(2,1)S(1)}, u32[]{:S(2)}, u32[]{:S(2)}) collective-permute-start(bf16[512,256]{1,0:T(8,128)(2,1)} %refs_0_.1), channel_id=1, source_target_pairs={{0,1},{8,9},{16,17},{24,25},{32,33},{40,41},{48,49},{56,57},{64,65... | collective-permute-start | bytes 786440 | tf_op jit(solution)/shard_map/ppermute | solution.py:35
  15.9 3.4 %collective-permute-start = (bf16[512,256]{1,0:T(8,128)(2,1)}, bf16[512,256]{1,0:T(8,128)(2,1)S(1)}, u32[]{:S(2)}, u32[]{:S(2)}) collective-permute-start(bf16[512,256]{1,0:T(8,128)(2,1)} %refs_0_.1), channel_id=1, source_target_pairs={{0,2},{8,10},{16,18},{24,26},{32,34},{40,42},{48,50},{56,58},{64,6... | collective-permute-start | bytes 786440 | tf_op jit(solution)/shard_map/ppermute | solution.py:35
  19.3 3.7 %collective-permute-start.1 = (bf16[512,256]{1,0:T(8,128)(2,1)}, bf16[512,256]{1,0:T(8,128)(2,1)S(1)}, u32[]{:S(2)}, u32[]{:S(2)}) collective-permute-start(bf16[512,256]{1,0:T(8,128)(2,1)} %refs_0_.1), channel_id=1, source_target_pairs={{0,6},{8,14},{16,22},{24,30},{32,38},{40,46},{48,54},{56,62},{64,7... | collective-permute-start | bytes 786440 | tf_op jit(solution)/shard_map/ppermute | solution.py:35
  22.9 3.7 %collective-permute-start.2 = (bf16[512,256]{1,0:T(8,128)(2,1)}, bf16[512,256]{1,0:T(8,128)(2,1)S(1)}, u32[]{:S(2)}, u32[]{:S(2)}) collective-permute-start(bf16[512,256]{1,0:T(8,128)(2,1)} %refs_0_.1), channel_id=1, source_target_pairs={{0,4},{8,12},{16,20},{24,28},{32,36},{40,44},{48,52},{56,60},{64,6... | collective-permute-start | bytes 786440 | tf_op jit(solution)/shard_map/ppermute | solution.py:35
  26.7 0.0 collective-permute-done.3.refs_4_
  26.7 2.5 %collective-permute-start.4 = (bf16[512,256]{1,0:T(8,128)(2,1)S(1)}, bf16[512,256]{1,0:T(8,128)(2,1)S(1)}, u32[]{:S(2)}, u32[]{:S(2)}) collective-permute-start(bf16[512,256]{1,0:T(8,128)(2,1)S(1)} %collective-permute-done.3.refs_4_), channel_id=1, source_target_pairs={{0,2},{8,10},{16,18},{24,26},{32,34},{40,42},{48,50},{56,58},{64,6... | collective-permute-start | bytes 786440 | tf_op jit(solution)/shard_map/ppermute | solution.py:35
  29.2 4.6 %collective-permute-start.5 = (bf16[512,256]{1,0:T(8,128)(2,1)S(1)}, bf16[512,256]{1,0:T(8,128)(2,1)S(1)}, u32[]{:S(2)}, u32[]{:S(2)}) collective-permute-start(bf16[512,256]{1,0:T(8,128)(2,1)S(1)} %collective-permute-done.3.refs_4_), channel_id=1, source_target_pairs={{0,6},{8,14},{16,22},{24,30},{32,38},{40,46},{48,54},{56,62},{64,7... | collective-permute-start | bytes 786440 | tf_op jit(solution)/shard_map/ppermute | solution.py:35
  33.7 0.0 collective-permute-done.refs_1_
  33.8 2.4 %collective-permute-start.6 = (bf16[512,256]{1,0:T(8,128)(2,1)S(1)}, bf16[512,256]{1,0:T(8,128)(2,1)S(1)}, u32[]{:S(2)}, u32[]{:S(2)}) collective-permute-start(bf16[512,256]{1,0:T(8,128)(2,1)S(1)} %collective-permute-done.3.refs_4_), channel_id=1, source_target_pairs={{0,4},{8,12},{16,20},{24,28},{32,36},{40,44},{48,52},{56,60},{64,6... | collective-permute-start | bytes 786440 | tf_op jit(solution)/shard_map/ppermute | solution.py:35
  36.2 2.3 %copy.10 = bf16[2048,2,384]{2,0,1:T(8,128)(2,1)S(1)} copy(bf16[2048,2,384]{2,1,0:T(2,128)(2,1)} %param.9) | data formatting | bytes 6291456 | tf_op args[2]
  38.5 0.0 collective-permute-done.1.refs_2_
  38.5 0.0 collective-permute-done.2.refs_3_
  38.5 2.3 %collective-permute-done.4.refs_5_ = bf16[512,256]{1,0:T(8,128)(2,1)S(1)} collective-permute-done((bf16[512,256]{1,0:T(8,128)(2,1)S(1)}, bf16[512,256]{1,0:T(8,128)(2,1)S(1)}, u32[]{:S(2)}, u32[]{:S(2)}) %collective-permute-start.4) | collective-permute-done | bytes 262176 | tf_op jit(solution)/shard_map/ppermute | solution.py:35
  40.8 1.1 collective-permute-done.5.refs_6_
  41.9 3.1 %collective-permute-done.6.refs_7_ = bf16[512,256]{1,0:T(8,128)(2,1)S(1)} collective-permute-done((bf16[512,256]{1,0:T(8,128)(2,1)S(1)}, bf16[512,256]{1,0:T(8,128)(2,1)S(1)}, u32[]{:S(2)}, u32[]{:S(2)}) %collective-permute-start.6) | collective-permute-done | bytes 262176 | tf_op jit(solution)/shard_map/ppermute | solution.py:35
  45.0 0.0 copy-done.1
  45.0 0.0 copy-done.2
  45.0 0.0 copy-done.3
  45.0 5.3 %project.1 = (bf16[512,384]{1,0:T(8,128)(2,1)S(1)}, bf16[512,512]{1,0:T(8,128)(2,1)S(1)}, bf16[384,512]{1,0:T(8,128)(2,1)S(1)}, f32[160,128]{1,0:T(8,128)S(1)}, ...) custom-call(bf16[512,256]{1,0:T(8,128)(2,1)S(1)} %copy-done.2, ...), custom_call_target="tpu_custom_call" | custom-call | tf_op jit(solution)/shard_map/project/pallas_call | solution.py:301
  50.3 0.0 copy-start.4
  50.3 14.6 %collective-permute-start.9 = (bf16[160,128]{1,0:T(8,128)(2,1)S(1)}, bf16[160,128]{1,0:T(8,128)(2,1)S(1)}, u32[]{:S(2)}, u32[]{:S(2)}) collective-permute-start(bf16[160,128]{1,0:T(8,128)(2,1)S(1)} %get-tuple-element.42), channel_id=1, source_target_pairs={{0,16},{8,24},{16,0},{24,8},{32,48},{40,56},{48,32},{56,40},{64,80... | collective-permute-start | bytes 122888 | tf_op jit(solution)/shard_map/ppermute | solution.py:35
  65.0 1.9 %collective-permute-start.8 = (bf16[160,128]{1,0:T(8,128)(2,1)S(1)}, bf16[160,128]{1,0:T(8,128)(2,1)S(1)}, u32[]{:S(2)}, u32[]{:S(2)}) collective-permute-start(bf16[160,128]{1,0:T(8,128)(2,1)S(1)} %get-tuple-element.41), channel_id=1, source_target_pairs={{0,24},{8,16},{16,8},{24,0},{32,56},{40,48},{48,40},{56,32},{64,88... | collective-permute-start | bytes 122888 | tf_op jit(solution)/shard_map/ppermute | solution.py:35
  66.9 2.0 %collective-permute-start.7 = (bf16[160,128]{1,0:T(8,128)(2,1)S(1)}, bf16[160,128]{1,0:T(8,128)(2,1)S(1)}, u32[]{:S(2)}, u32[]{:S(2)}) collective-permute-start(bf16[160,128]{1,0:T(8,128)(2,1)S(1)} %get-tuple-element.41), channel_id=1, source_target_pairs={{0,8},{8,0},{16,24},{24,16},{32,40},{40,32},{48,56},{56,48},{64,72... | collective-permute-start | bytes 122888 | tf_op jit(solution)/shard_map/ppermute | solution.py:35
  69.0 0.0 collective-permute-done.9
  69.0 1.3 collective-permute-done.8
  70.3 0.0 collective-permute-done.7
  70.3 1.9 %collective-permute-start.10 = (bf16[160,128]{1,0:T(8,128)(2,1)S(1)}, bf16[160,128]{1,0:T(8,128)(2,1)S(1)}, u32[]{:S(2)}, u32[]{:S(2)}) collective-permute-start(bf16[160,128]{1,0:T(8,128)(2,1)S(1)} %convert_element_type.72), channel_id=1, source_target_pairs={{0,32},{8,40},{16,48},{24,56},{32,0},{40,8},{48,16},{56,24},{64,96... | collective-permute-start | bytes 122888 | tf_op jit(solution)/shard_map/ppermute | solution.py:35
  72.3 5.3 %collective-permute-done.10 = bf16[160,128]{1,0:T(8,128)(2,1)S(1)} collective-permute-done((bf16[160,128]{1,0:T(8,128)(2,1)S(1)}, bf16[160,128]{1,0:T(8,128)(2,1)S(1)}, u32[]{:S(2)}, u32[]{:S(2)}) %collective-permute-start.10) | collective-permute-done | bytes 40992 | tf_op jit(solution)/shard_map/ppermute | solution.py:35
  77.6 0.0 copy-start
  77.6 6.6 %collective-permute-start.11 = (bf16[160,128]{1,0:T(8,128)(2,1)S(1)}, bf16[160,128]{1,0:T(8,128)(2,1)S(1)}, u32[]{:S(2)}, u32[]{:S(2)}) collective-permute-start(bf16[160,128]{1,0:T(8,128)(2,1)S(1)} %convert_element_type.74), channel_id=1, source_target_pairs={{0,64},{8,72},{16,80},{24,88},{32,96},{40,104},{48,112},{56,120},{... | collective-permute-start | bytes 122888 | tf_op jit(solution)/shard_map/ppermute | solution.py:35
  84.2 1.9 %collective-permute-start.16 = (bf16[384,512]{1,0:T(8,128)(2,1)S(1)}, bf16[384,512]{1,0:T(8,128)(2,1)S(1)}, u32[]{:S(2)}, u32[]{:S(2)}) collective-permute-start(bf16[384,512]{1,0:T(8,128)(2,1)S(1)} %get-tuple-element.60), channel_id=1, source_target_pairs={{0,8},{8,16},{16,24},{24,32},{32,40},{40,48},{48,56},{56,64},{64,7... | collective-permute-start | bytes 1179656 | tf_op jit(solution)/shard_map/ppermute | solution.py:35
  86.1 2.1 %near.1 = (f32[512,256]{1,0:T(8,128)S(1)}, bf16[2,512,160]{2,1,0:T(8,128)(2,1)S(1)}, bf16[2,512,160]{2,1,0:T(8,128)(2,1)S(1)}) custom-call(bf16[512,384]{1,0:T(8,128)(2,1)S(1)} %get-tuple-element.48.qf_ref, bf16[512,512]{1,0:T(8,128)(2,1)S(1)} %get-tuple-element.49.kv_ref, bf16[2,4,160,128]{3,2,1,0:T(8,128)(2,1)S(1)} %copy-done.1), custom_call_target="tpu_custom_call" | custom-call | tf_op jit(solution)/shard_map/near/pallas_call | solution.py:327
  88.2 0.8 collective-permute-done.11
  89.0 0.7 collective-permute-start.14
  89.7 1.3 collective-permute-start.13
  91.0 3.8 %collective-permute-start.12 = (bf16[160,128]{1,0:T(8,128)(2,1)S(1)}, bf16[160,128]{1,0:T(8,128)(2,1)S(1)}, u32[]{:S(2)}, u32[]{:S(2)}) collective-permute-start(bf16[160,128]{1,0:T(8,128)(2,1)S(1)} %convert_add_fusion.1), channel_id=1, source_target_pairs={{0,128},{8,136},{16,144},{24,152},{32,160},{40,168},{48,176},{56,1... | collective-permute-start | bytes 122888 | tf_op jit(solution)/shard_map/ppermute | solution.py:35
  94.8 0.0 collective-permute-done.14
  94.8 6.6 %collective-permute-done.13 = bf16[160,128]{1,0:T(8,128)(2,1)S(1)} collective-permute-done((bf16[160,128]{1,0:T(8,128)(2,1)S(1)}, bf16[160,128]{1,0:T(8,128)(2,1)S(1)}, u32[]{:S(2)}, u32[]{:S(2)}) %collective-permute-start.13) | collective-permute-done | bytes 40992 | tf_op jit(solution)/shard_map/ppermute | solution.py:35
  101.5 0.6 collective-permute-done.12
  102.2 1.9 %collective-permute-start.15 = (bf16[160,128]{1,0:T(8,128)(2,1)S(1)}, bf16[160,128]{1,0:T(8,128)(2,1)S(1)}, u32[]{:S(2)}, u32[]{:S(2)}) collective-permute-start(bf16[160,128]{1,0:T(8,128)(2,1)S(1)} %get-tuple-element.75), channel_id=1, source_target_pairs={{0,8},{8,0},{16,24},{24,16},{32,40},{40,32},{48,56},{56,48},{64,72... | collective-permute-start | bytes 122888 | tf_op jit(solution)/shard_map/ppermute | solution.py:35
  104.1 0.0 collective-permute-done.16.halo_ref
  104.1 0.0 copy-done.4
  104.1 2.4 %window.1.win_ref = f32[512,256]{1,0:T(8,128)S(1)} custom-call(s32[2]{0:T(128)S(1)} %copy-done.4, bf16[512,384]{1,0:T(8,128)(2,1)S(1)} %get-tuple-element.48.qf_ref, bf16[512,512]{1,0:T(8,128)(2,1)S(1)} %get-tuple-element.49.kv_ref, bf16[384,512]{1,0:T(8,128)(2,1)S(1)} %collective-permute-done.16.halo_ref), custom_call_target="tpu_custom_call" | custom-call | tf_op jit(solution)/shard_map/window/pallas_call | solution.py:343
  106.6 0.0 collective-permute-done.15.theirs
  106.6 0.7 hidden.1
  107.3 0.4 product.2
  107.7 3.7 %collective-permute-start.19 = (bf16[64,2048]{1,0:T(8,128)(2,1)S(1)}, bf16[64,2048]{1,0:T(8,128)(2,1)S(1)}, u32[]{:S(2)}, u32[]{:S(2)}) collective-permute-start(bf16[64,2048]{1,0:T(8,128)(2,1)S(1)} %get-tuple-element.67), channel_id=1, source_target_pairs={{0,4},{8,12},{16,20},{24,28},{32,36},{40,44},{48,52},{56,60},{64,6... | collective-permute-start | bytes 786440 | tf_op jit(solution)/shard_map/ppermute | solution.py:35
  111.4 5.6 %collective-permute-start.18 = (bf16[64,2048]{1,0:T(8,128)(2,1)S(1)}, bf16[64,2048]{1,0:T(8,128)(2,1)S(1)}, u32[]{:S(2)}, u32[]{:S(2)}) collective-permute-start(bf16[64,2048]{1,0:T(8,128)(2,1)S(1)} %get-tuple-element.66), channel_id=1, source_target_pairs={{0,6},{8,14},{16,22},{24,30},{32,38},{40,46},{48,54},{56,62},{64,7... | collective-permute-start | bytes 786440 | tf_op jit(solution)/shard_map/ppermute | solution.py:35
  117.1 1.9 %collective-permute-start.17 = (bf16[64,2048]{1,0:T(8,128)(2,1)S(1)}, bf16[64,2048]{1,0:T(8,128)(2,1)S(1)}, u32[]{:S(2)}, u32[]{:S(2)}) collective-permute-start(bf16[64,2048]{1,0:T(8,128)(2,1)S(1)} %get-tuple-element.65), channel_id=1, source_target_pairs={{0,2},{8,10},{16,18},{24,26},{32,34},{40,42},{48,50},{56,58},{64,6... | collective-permute-start | bytes 786440 | tf_op jit(solution)/shard_map/ppermute | solution.py:35
  119.0 0.8 collective-permute-done.19
  119.8 6.6 %collective-permute-done.18 = bf16[64,2048]{1,0:T(8,128)(2,1)S(1)} collective-permute-done((bf16[64,2048]{1,0:T(8,128)(2,1)S(1)}, bf16[64,2048]{1,0:T(8,128)(2,1)S(1)}, u32[]{:S(2)}, u32[]{:S(2)}) %collective-permute-start.18) | collective-permute-done | bytes 262176 | tf_op jit(solution)/shard_map/ppermute | solution.py:35
  126.5 1.8 %collective-permute-done.17 = bf16[64,2048]{1,0:T(8,128)(2,1)S(1)} collective-permute-done((bf16[64,2048]{1,0:T(8,128)(2,1)S(1)}, bf16[64,2048]{1,0:T(8,128)(2,1)S(1)}, u32[]{:S(2)}, u32[]{:S(2)}) %collective-permute-start.17) | collective-permute-done | bytes 262176 | tf_op jit(solution)/shard_map/ppermute | solution.py:35
  128.3 0.1 add_convert_fusion.1
  128.4 9.1 %collective-permute-start.20 = (bf16[64,2048]{1,0:T(8,128)(2,1)S(1)}, bf16[64,2048]{1,0:T(8,128)(2,1)S(1)}, u32[]{:S(2)}, u32[]{:S(2)}) collective-permute-start(bf16[64,2048]{1,0:T(8,128)(2,1)S(1)} %add_convert_fusion.1), channel_id=1, source_target_pairs={{0,1},{8,9},{16,17},{24,25},{32,33},{40,41},{48,49},{56,57},{64,65... | collective-permute-start | bytes 786440 | tf_op jit(solution)/shard_map/ppermute | solution.py:35
  137.6 0.4 product.3
  138.0 2.5 %collective-permute-start.23 = (bf16[64,2048]{1,0:T(8,128)(2,1)S(1)}, bf16[64,2048]{1,0:T(8,128)(2,1)S(1)}, u32[]{:S(2)}, u32[]{:S(2)}) collective-permute-start(bf16[64,2048]{1,0:T(8,128)(2,1)S(1)} %get-tuple-element.74), channel_id=1, source_target_pairs={{0,4},{8,12},{16,20},{24,28},{32,36},{40,44},{48,52},{56,60},{64,6... | collective-permute-start | bytes 786440 | tf_op jit(solution)/shard_map/ppermute | solution.py:35
  140.5 3.9 %collective-permute-start.22 = (bf16[64,2048]{1,0:T(8,128)(2,1)S(1)}, bf16[64,2048]{1,0:T(8,128)(2,1)S(1)}, u32[]{:S(2)}, u32[]{:S(2)}) collective-permute-start(bf16[64,2048]{1,0:T(8,128)(2,1)S(1)} %get-tuple-element.73), channel_id=1, source_target_pairs={{0,6},{8,14},{16,22},{24,30},{32,38},{40,46},{48,54},{56,62},{64,7... | collective-permute-start | bytes 786440 | tf_op jit(solution)/shard_map/ppermute | solution.py:35
  144.5 1.9 %collective-permute-start.21 = (bf16[64,2048]{1,0:T(8,128)(2,1)S(1)}, bf16[64,2048]{1,0:T(8,128)(2,1)S(1)}, u32[]{:S(2)}, u32[]{:S(2)}) collective-permute-start(bf16[64,2048]{1,0:T(8,128)(2,1)S(1)} %get-tuple-element.72), channel_id=1, source_target_pairs={{0,2},{8,10},{16,18},{24,26},{32,34},{40,42},{48,50},{56,58},{64,6... | collective-permute-start | bytes 786440 | tf_op jit(solution)/shard_map/ppermute | solution.py:35
  146.4 16.8 %collective-permute-done.20 = bf16[64,2048]{1,0:T(8,128)(2,1)S(1)} collective-permute-done((bf16[64,2048]{1,0:T(8,128)(2,1)S(1)}, bf16[64,2048]{1,0:T(8,128)(2,1)S(1)}, u32[]{:S(2)}, u32[]{:S(2)}) %collective-permute-start.20) | collective-permute-done | bytes 262176 | tf_op jit(solution)/shard_map/ppermute | solution.py:35
  163.3 0.1 convert_add_fusion
  163.3 0.0 collective-permute-done.23
  163.3 0.0 collective-permute-done.22
  163.4 0.0 collective-permute-done.21
  163.4 0.8 add_convert_fusion
  (11 shorter events, 0.1 us)
Async XLA Ops:
  0.0 45.0 %copy-start.1 = (bf16[2,4,160,128]{3,2,1,0:T(8,128)(2,1)S(1)}, bf16[2,4,160,128]{3,2,1,0:T(8,128)(2,1)}, u32[]{:S(2)}) copy-start(bf16[2,4,160,128]{3,2,1,0:T(8,128)(2,1)} %constant.52.clone.refs_10_.table) | copy-start | bytes 983044
  0.0 45.0 %copy-start.2 = (bf16[512,256]{1,0:T(8,128)(2,1)S(1)}, bf16[512,256]{1,0:T(8,128)(2,1)}, u32[]{:S(2)}) copy-start(bf16[512,256]{1,0:T(8,128)(2,1)} %refs_0_.1) | copy-start | bytes 786436
  0.0 45.0 %copy-start.3 = (bf16[2048,2,32]{0,2,1:T(8,128)(2,1)S(1)}, bf16[2048,2,32]{0,2,1:T(8,128)(2,1)}, u32[]{:S(2)}) copy-start(bf16[2048,2,32]{0,2,1:T(8,128)(2,1)} %param.8) | copy-start | bytes 786436
  0.0 26.7 %collective-permute-start.3 = (bf16[512,256]{1,0:T(8,128)(2,1)}, bf16[512,256]{1,0:T(8,128)(2,1)S(1)}, u32[]{:S(2)}, u32[]{:S(2)}) collective-permute-start(bf16[512,256]{1,0:T(8,128)(2,1)} %refs_0_.1), channel_id=1, source_target_pairs={{0,1},{8,9},{16,17},{24,25},{32,33},{40,41},{48,49},{56,57},{64,65... | collective-permute-start | bytes 786440 | tf_op jit(solution)/shard_map/ppermute | solution.py:35
  15.9 17.9 %collective-permute-start = (bf16[512,256]{1,0:T(8,128)(2,1)}, bf16[512,256]{1,0:T(8,128)(2,1)S(1)}, u32[]{:S(2)}, u32[]{:S(2)}) collective-permute-start(bf16[512,256]{1,0:T(8,128)(2,1)} %refs_0_.1), channel_id=1, source_target_pairs={{0,2},{8,10},{16,18},{24,26},{32,34},{40,42},{48,50},{56,58},{64,6... | collective-permute-start | bytes 786440 | tf_op jit(solution)/shard_map/ppermute | solution.py:35
  19.3 19.2 %collective-permute-start.1 = (bf16[512,256]{1,0:T(8,128)(2,1)}, bf16[512,256]{1,0:T(8,128)(2,1)S(1)}, u32[]{:S(2)}, u32[]{:S(2)}) collective-permute-start(bf16[512,256]{1,0:T(8,128)(2,1)} %refs_0_.1), channel_id=1, source_target_pairs={{0,6},{8,14},{16,22},{24,30},{32,38},{40,46},{48,54},{56,62},{64,7... | collective-permute-start | bytes 786440 | tf_op jit(solution)/shard_map/ppermute | solution.py:35
  22.9 15.6 %collective-permute-start.2 = (bf16[512,256]{1,0:T(8,128)(2,1)}, bf16[512,256]{1,0:T(8,128)(2,1)S(1)}, u32[]{:S(2)}, u32[]{:S(2)}) collective-permute-start(bf16[512,256]{1,0:T(8,128)(2,1)} %refs_0_.1), channel_id=1, source_target_pairs={{0,4},{8,12},{16,20},{24,28},{32,36},{40,44},{48,52},{56,60},{64,6... | collective-permute-start | bytes 786440 | tf_op jit(solution)/shard_map/ppermute | solution.py:35
  26.7 14.1 %collective-permute-start.4 = (bf16[512,256]{1,0:T(8,128)(2,1)S(1)}, bf16[512,256]{1,0:T(8,128)(2,1)S(1)}, u32[]{:S(2)}, u32[]{:S(2)}) collective-permute-start(bf16[512,256]{1,0:T(8,128)(2,1)S(1)} %collective-permute-done.3.refs_4_), channel_id=1, source_target_pairs={{0,2},{8,10},{16,18},{24,26},{32,34},{40,42},{48,50},{56,58},{64,6... | collective-permute-start | bytes 786440 | tf_op jit(solution)/shard_map/ppermute | solution.py:35
  29.2 12.7 %collective-permute-start.5 = (bf16[512,256]{1,0:T(8,128)(2,1)S(1)}, bf16[512,256]{1,0:T(8,128)(2,1)S(1)}, u32[]{:S(2)}, u32[]{:S(2)}) collective-permute-start(bf16[512,256]{1,0:T(8,128)(2,1)S(1)} %collective-permute-done.3.refs_4_), channel_id=1, source_target_pairs={{0,6},{8,14},{16,22},{24,30},{32,38},{40,46},{48,54},{56,62},{64,7... | collective-permute-start | bytes 786440 | tf_op jit(solution)/shard_map/ppermute | solution.py:35
  33.8 11.2 %collective-permute-start.6 = (bf16[512,256]{1,0:T(8,128)(2,1)S(1)}, bf16[512,256]{1,0:T(8,128)(2,1)S(1)}, u32[]{:S(2)}, u32[]{:S(2)}) collective-permute-start(bf16[512,256]{1,0:T(8,128)(2,1)S(1)} %collective-permute-done.3.refs_4_), channel_id=1, source_target_pairs={{0,4},{8,12},{16,20},{24,28},{32,36},{40,44},{48,52},{56,60},{64,6... | collective-permute-start | bytes 786440 | tf_op jit(solution)/shard_map/ppermute | solution.py:35
  50.3 53.8 %copy-start.4 = (s32[2]{0:T(128)S(1)}, s32[2]{0:T(128)}, u32[]{:S(2)}) copy-start(s32[2]{0:T(128)} %win.1) | copy-start | bytes 28
  50.3 18.6 %collective-permute-start.9 = (bf16[160,128]{1,0:T(8,128)(2,1)S(1)}, bf16[160,128]{1,0:T(8,128)(2,1)S(1)}, u32[]{:S(2)}, u32[]{:S(2)}) collective-permute-start(bf16[160,128]{1,0:T(8,128)(2,1)S(1)} %get-tuple-element.42), channel_id=1, source_target_pairs={{0,16},{8,24},{16,0},{24,8},{32,48},{40,56},{48,32},{56,40},{64,80... | collective-permute-start | bytes 122888 | tf_op jit(solution)/shard_map/ppermute | solution.py:35
  65.0 5.3 %collective-permute-start.8 = (bf16[160,128]{1,0:T(8,128)(2,1)S(1)}, bf16[160,128]{1,0:T(8,128)(2,1)S(1)}, u32[]{:S(2)}, u32[]{:S(2)}) collective-permute-start(bf16[160,128]{1,0:T(8,128)(2,1)S(1)} %get-tuple-element.41), channel_id=1, source_target_pairs={{0,24},{8,16},{16,8},{24,0},{32,56},{40,48},{48,40},{56,32},{64,88... | collective-permute-start | bytes 122888 | tf_op jit(solution)/shard_map/ppermute | solution.py:35
  66.9 3.4 %collective-permute-start.7 = (bf16[160,128]{1,0:T(8,128)(2,1)S(1)}, bf16[160,128]{1,0:T(8,128)(2,1)S(1)}, u32[]{:S(2)}, u32[]{:S(2)}) collective-permute-start(bf16[160,128]{1,0:T(8,128)(2,1)S(1)} %get-tuple-element.41), channel_id=1, source_target_pairs={{0,8},{8,0},{16,24},{24,16},{32,40},{40,32},{48,56},{56,48},{64,72... | collective-permute-start | bytes 122888 | tf_op jit(solution)/shard_map/ppermute | solution.py:35
  70.3 7.2 %collective-permute-start.10 = (bf16[160,128]{1,0:T(8,128)(2,1)S(1)}, bf16[160,128]{1,0:T(8,128)(2,1)S(1)}, u32[]{:S(2)}, u32[]{:S(2)}) collective-permute-start(bf16[160,128]{1,0:T(8,128)(2,1)S(1)} %convert_element_type.72), channel_id=1, source_target_pairs={{0,32},{8,40},{16,48},{24,56},{32,0},{40,8},{48,16},{56,24},{64,96... | collective-permute-start | bytes 122888 | tf_op jit(solution)/shard_map/ppermute | solution.py:35
  77.6 29.7 %copy-start = (bf16[2,128,2048]{2,1,0:T(8,128)(2,1)S(1)}, bf16[2,128,2048]{2,1,0:T(8,128)(2,1)}, u32[]{:S(2)}) copy-start(bf16[2,128,2048]{2,1,0:T(8,128)(2,1)} %param.10) | copy-start | bytes 3145732
  77.6 11.4 %collective-permute-start.11 = (bf16[160,128]{1,0:T(8,128)(2,1)S(1)}, bf16[160,128]{1,0:T(8,128)(2,1)S(1)}, u32[]{:S(2)}, u32[]{:S(2)}) collective-permute-start(bf16[160,128]{1,0:T(8,128)(2,1)S(1)} %convert_element_type.74), channel_id=1, source_target_pairs={{0,64},{8,72},{16,80},{24,88},{32,96},{40,104},{48,112},{56,120},{... | collective-permute-start | bytes 122888 | tf_op jit(solution)/shard_map/ppermute | solution.py:35
  84.2 19.9 %collective-permute-start.16 = (bf16[384,512]{1,0:T(8,128)(2,1)S(1)}, bf16[384,512]{1,0:T(8,128)(2,1)S(1)}, u32[]{:S(2)}, u32[]{:S(2)}) collective-permute-start(bf16[384,512]{1,0:T(8,128)(2,1)S(1)} %get-tuple-element.60), channel_id=1, source_target_pairs={{0,8},{8,16},{16,24},{24,32},{32,40},{40,48},{48,56},{56,64},{64,7... | collective-permute-start | bytes 1179656 | tf_op jit(solution)/shard_map/ppermute | solution.py:35
  89.0 5.8 %collective-permute-start.14 = (bf16[160,128]{1,0:T(8,128)(2,1)S(1)}, bf16[160,128]{1,0:T(8,128)(2,1)S(1)}, u32[]{:S(2)}, u32[]{:S(2)}) collective-permute-start(bf16[160,128]{1,0:T(8,128)(2,1)S(1)} %convert_add_fusion.1), channel_id=1, source_target_pairs={{0,384},{8,392},{16,400},{24,408},{32,416},{40,424},{48,432},{56,4... | collective-permute-start | bytes 122888 | tf_op jit(solution)/shard_map/ppermute | solution.py:35
  89.7 11.8 %collective-permute-start.13 = (bf16[160,128]{1,0:T(8,128)(2,1)S(1)}, bf16[160,128]{1,0:T(8,128)(2,1)S(1)}, u32[]{:S(2)}, u32[]{:S(2)}) collective-permute-start(bf16[160,128]{1,0:T(8,128)(2,1)S(1)} %convert_add_fusion.1), channel_id=1, source_target_pairs={{0,256},{8,264},{16,272},{24,280},{32,288},{40,296},{48,304},{56,3... | collective-permute-start | bytes 122888 | tf_op jit(solution)/shard_map/ppermute | solution.py:35
  91.0 11.1 %collective-permute-start.12 = (bf16[160,128]{1,0:T(8,128)(2,1)S(1)}, bf16[160,128]{1,0:T(8,128)(2,1)S(1)}, u32[]{:S(2)}, u32[]{:S(2)}) collective-permute-start(bf16[160,128]{1,0:T(8,128)(2,1)S(1)} %convert_add_fusion.1), channel_id=1, source_target_pairs={{0,128},{8,136},{16,144},{24,152},{32,160},{40,168},{48,176},{56,1... | collective-permute-start | bytes 122888 | tf_op jit(solution)/shard_map/ppermute | solution.py:35
  102.2 4.4 %collective-permute-start.15 = (bf16[160,128]{1,0:T(8,128)(2,1)S(1)}, bf16[160,128]{1,0:T(8,128)(2,1)S(1)}, u32[]{:S(2)}, u32[]{:S(2)}) collective-permute-start(bf16[160,128]{1,0:T(8,128)(2,1)S(1)} %get-tuple-element.75), channel_id=1, source_target_pairs={{0,8},{8,0},{16,24},{24,16},{32,40},{40,32},{48,56},{56,48},{64,72... | collective-permute-start | bytes 122888 | tf_op jit(solution)/shard_map/ppermute | solution.py:35
  107.7 12.1 %collective-permute-start.19 = (bf16[64,2048]{1,0:T(8,128)(2,1)S(1)}, bf16[64,2048]{1,0:T(8,128)(2,1)S(1)}, u32[]{:S(2)}, u32[]{:S(2)}) collective-permute-start(bf16[64,2048]{1,0:T(8,128)(2,1)S(1)} %get-tuple-element.67), channel_id=1, source_target_pairs={{0,4},{8,12},{16,20},{24,28},{32,36},{40,44},{48,52},{56,60},{64,6... | collective-permute-start | bytes 786440 | tf_op jit(solution)/shard_map/ppermute | solution.py:35
  111.4 15.0 %collective-permute-start.18 = (bf16[64,2048]{1,0:T(8,128)(2,1)S(1)}, bf16[64,2048]{1,0:T(8,128)(2,1)S(1)}, u32[]{:S(2)}, u32[]{:S(2)}) collective-permute-start(bf16[64,2048]{1,0:T(8,128)(2,1)S(1)} %get-tuple-element.66), channel_id=1, source_target_pairs={{0,6},{8,14},{16,22},{24,30},{32,38},{40,46},{48,54},{56,62},{64,7... | collective-permute-start | bytes 786440 | tf_op jit(solution)/shard_map/ppermute | solution.py:35
  117.1 11.2 %collective-permute-start.17 = (bf16[64,2048]{1,0:T(8,128)(2,1)S(1)}, bf16[64,2048]{1,0:T(8,128)(2,1)S(1)}, u32[]{:S(2)}, u32[]{:S(2)}) collective-permute-start(bf16[64,2048]{1,0:T(8,128)(2,1)S(1)} %get-tuple-element.65), channel_id=1, source_target_pairs={{0,2},{8,10},{16,18},{24,26},{32,34},{40,42},{48,50},{56,58},{64,6... | collective-permute-start | bytes 786440 | tf_op jit(solution)/shard_map/ppermute | solution.py:35
  128.4 34.8 %collective-permute-start.20 = (bf16[64,2048]{1,0:T(8,128)(2,1)S(1)}, bf16[64,2048]{1,0:T(8,128)(2,1)S(1)}, u32[]{:S(2)}, u32[]{:S(2)}) collective-permute-start(bf16[64,2048]{1,0:T(8,128)(2,1)S(1)} %add_convert_fusion.1), channel_id=1, source_target_pairs={{0,1},{8,9},{16,17},{24,25},{32,33},{40,41},{48,49},{56,57},{64,65... | collective-permute-start | bytes 786440 | tf_op jit(solution)/shard_map/ppermute | solution.py:35
  138.0 25.3 %collective-permute-start.23 = (bf16[64,2048]{1,0:T(8,128)(2,1)S(1)}, bf16[64,2048]{1,0:T(8,128)(2,1)S(1)}, u32[]{:S(2)}, u32[]{:S(2)}) collective-permute-start(bf16[64,2048]{1,0:T(8,128)(2,1)S(1)} %get-tuple-element.74), channel_id=1, source_target_pairs={{0,4},{8,12},{16,20},{24,28},{32,36},{40,44},{48,52},{56,60},{64,6... | collective-permute-start | bytes 786440 | tf_op jit(solution)/shard_map/ppermute | solution.py:35
  140.5 22.8 %collective-permute-start.22 = (bf16[64,2048]{1,0:T(8,128)(2,1)S(1)}, bf16[64,2048]{1,0:T(8,128)(2,1)S(1)}, u32[]{:S(2)}, u32[]{:S(2)}) collective-permute-start(bf16[64,2048]{1,0:T(8,128)(2,1)S(1)} %get-tuple-element.73), channel_id=1, source_target_pairs={{0,6},{8,14},{16,22},{24,30},{32,38},{40,46},{48,54},{56,62},{64,7... | collective-permute-start | bytes 786440 | tf_op jit(solution)/shard_map/ppermute | solution.py:35
  144.5 18.9 %collective-permute-start.21 = (bf16[64,2048]{1,0:T(8,128)(2,1)S(1)}, bf16[64,2048]{1,0:T(8,128)(2,1)S(1)}, u32[]{:S(2)}, u32[]{:S(2)}) collective-permute-start(bf16[64,2048]{1,0:T(8,128)(2,1)S(1)} %get-tuple-element.72), channel_id=1, source_target_pairs={{0,2},{8,10},{16,18},{24,26},{32,34},{40,42},{48,50},{56,58},{64,6... | collective-permute-start | bytes 786440 | tf_op jit(solution)/shard_map/ppermute | solution.py:35

commit v9 on v8

--- a/solution.py
+++ b/solution.py
@@ -114,35 +114,46 @@
     return lax.div(tp, 2), lax.rem(tp, 2), lax.rem(seq, 2), seq
 
 
-def project_kernel(*refs):
-    parts = refs[:N_TP]
-    wf, ww, table, qf_ref, kv_ref, tail_ref, mine_ref, short_ref, other_ref, held, held_wf, qf, tail, sems = refs[N_TP:]
-    x, half, core, _ = position()
-    owners = [lax.rem(x + NX - s, NX) * 2 + side for side in (half, 1 - half) for s in (0, 1, 3, 2)]
+def contract(parts, wf, ww, mine):
+    x, half, _, _ = position()
+    side = half if mine else 1 - half
     width = parts[0].shape[1]
     head = ww.shape[2] // 3
-    copies = [
-        pltpu.make_async_copy(part, held.at[:, pl.ds(pl.multiple_of(owner * width, width), width)], sems.at[k])
-        for k, (part, owner) in enumerate(zip(parts, owners))
-    ]
-    copies.append(pltpu.make_async_copy(wf, held_wf, sems.at[N_TP]))
-    for copy in copies:
-        copy.start()
-    for copy in copies:
-        copy.wait()
-    tokens = held[...]
-
-    def columns(weight):
-        return dot(tokens, weight).astype(bf16)
-
-    feats = dot_t(tokens, held_wf[...]).astype(bf16)
+    tokens = jnp.concatenate([part[...] for part in parts], axis=1)
+    owners = [lax.rem(x + NX - s, NX) * 2 + side for s in (0, 1, 3, 2)]
+    rows = [pl.ds(pl.multiple_of(owner * width, width), width) for owner in owners]
+
+    def columns(kind):
+        cols = slice(kind * head, (kind + 1) * head)
+        weight = [jnp.concatenate([ww[h, r, cols] for h in range(2)], axis=1) for r in rows]
+        return dot(tokens, jnp.concatenate(weight, axis=0))
+
+    return dot_t(tokens, jnp.concatenate([wf[:, r] for r in rows], axis=1)), columns
+
+
+def own_kernel(*refs):
+    parts = refs[:NX]
+    wf, ww, feats_ref, sums_ref = refs[NX:]
+    feats, columns = contract(parts, wf, ww, True)
+    feats_ref[...] = feats
+    for kind in range(3):
+        sums_ref[kind] = columns(kind)
+
+
+def project_kernel(*refs):
+    parts = refs[:NX]
+    wf, ww, table, own_feats, own_sums, qf_ref, kv_ref, tail_ref, mine_ref, short_ref, other_ref, qf, tail, sems = refs[NX:]
+    core = position()[2]
+    head = ww.shape[2] // 3
+    feats, columns = contract(parts, wf, ww, False)
+    feats = (feats + own_feats[...]).astype(bf16)
     ones = lax.broadcasted_iota(jnp.int32, feats.shape, 1) == 0
     feats = jnp.concatenate([feats, jnp.where(ones, 1.0, 0.0).astype(bf16)], axis=1)
     qf[:, 2 * head :] = feats
     first_tail = kv_ref.shape[0] - tail.shape[0]
     leave = [pltpu.make_async_copy(tail, tail_ref, sems.at[0]), pltpu.make_async_copy(qf, qf_ref, sems.at[1])]
     for kind in (2, 1, 0):
-        out = columns(jnp.concatenate([ww[h, :, kind * head : (kind + 1) * head] for h in range(2)], axis=1))
+        out = (columns(kind) + own_sums[kind]).astype(bf16)
         if kind == 2:
             values = out
             kv_ref[:, 2 * head :] = out
@@ -293,7 +304,19 @@
     return jax.ShapeDtypeStruct(dims, kind)
 
 
-def project(parts, wf, ww, tables):
+def own_products(parts, wf, ww):
+    tok_rows = parts[0].shape[0]
+    return pl.pallas_call(
+        own_kernel,
+        out_shape=(shape((tok_rows, wf.shape[0]), f32), shape((3, tok_rows, 2 * ww.shape[2] // 3), f32)),
+        in_specs=[VMEM] * (NX + 2),
+        out_specs=(VMEM,) * 2,
+        name="own",
+        compiler_params=pltpu.CompilerParams(vmem_limit_bytes=LIMIT),
+    )(*parts, wf, ww)
+
+
+def project(parts, wf, ww, tables, own):
     tok_rows = parts[0].shape[0]
     wide = 2 * ww.shape[2] // 3
     queries = shape((tok_rows, wide + 2 * wf.shape[0]), bf16)
@@ -308,18 +331,16 @@
             shape((ROWS, wide // 2), bf16),
             shape((ROWS, wide // 2), bf16),
         ),
-        in_specs=[HBM] * (N_TP + 1) + [VMEM] * 2,
+        in_specs=[VMEM] * (NX + 5),
         out_specs=(HBM, VMEM, HBM, VMEM, VMEM, VMEM),
         scratch_shapes=[
-            pltpu.VMEM((tok_rows, wf.shape[1]), bf16),
-            pltpu.VMEM(wf.shape, bf16),
             pltpu.VMEM(queries.shape, bf16),
             pltpu.VMEM(tail.shape, bf16),
-            pltpu.SemaphoreType.DMA((N_TP + 1,)),
+            pltpu.SemaphoreType.DMA((2,)),
         ],
         name="project",
         compiler_params=pltpu.CompilerParams(vmem_limit_bytes=LIMIT),
-    )(*parts, wf, ww, tables.astype(bf16))
+    )(*parts, wf, ww, tables.astype(bf16), *own)
 
 
 def near(qf, kv, tables):
@@ -389,9 +410,9 @@
     w_out = w_out.reshape(-1, model_width)
     parts += [other] + [send(other, to_x(s)) for s in (1, 3, 2)]
     tables = feature_maps(feat_dim, head_count)
-    qf, kv, tail, mine, short, theirs = project(
-        parts, w_feature.transpose(1, 2, 0).reshape(-1, model_width), w_window.transpose(1, 0, 2), tables
-    )
+    wf, ww = w_feature.transpose(1, 2, 0).reshape(-1, model_width), w_window.transpose(1, 0, 2)
+    own = own_products(parts[:NX], wf, ww)
+    qf, kv, tail, mine, short, theirs = project(parts[NX:], wf, ww, tables, own)
 
     def beside(total):
         early, kept, _ = lax.optimization_barrier((qf, tail, total))

time: 165 us -> 163 us (0.988)
    pallas_call x1, Pallas kernels: 5.32 us -> 3.24 us  [project(): pl.pallas_call(project_kernel, out_shape=(queries, shape((tok_rows, 2 * w...]
  transfers between devices with their start and end apart: 24 -> 24, of which waited for: 12 -> 12; matrix products, arithmetic and copies ran while one was open for 1% -> 1% of each run, Pallas kernels for 3% -> 4%
where the time goes in v9:
time: 163 us; the launch traced here: 162 us
  starting transfers between devices  102 us (63%)
  waiting for transfers between devices  46.1 us (28%)
  Pallas kernels  10.5 us (6%)
  local copies, waits for them, and re-layouts  2.32 us (1%)
    ppermute x24, starting transfers between devices, send(): return lax.ppermute(value, ('seq', 'tp'), pairs(move))  102 us
    ppermute x24, waiting for transfers between devices, send(): return lax.ppermute(value, ('seq', 'tp'), pairs(move))  46.1 us
  transfers between devices with their start and end apart: 24, of which 12 were waited for; matrix products, arithmetic and copies ran while one was open for 1% of the time, Pallas kernels for 4%

profile of v9, /device:TPU:16, one launch (start us, length us, event | category | flops | bytes accessed | tf_op | source)
XLA Modules:
  0.0 162.1 jit_solution(4143382559148819969)
XLA Ops:
  0.0 15.8 %collective-permute-start = (bf16[512,256]{1,0:T(8,128)(2,1)}, bf16[512,256]{1,0:T(8,128)(2,1)S(1)}, u32[]{:S(2)}, u32[]{:S(2)}) collective-permute-start(bf16[512,256]{1,0:T(8,128)(2,1)} %refs_0_.1), channel_id=1, source_target_pairs={{0,1},{8,9},{16,17},{24,25},{32,33},{40,41},{48,49},{56,57},{64,65... | collective-permute-start | bytes 786440 | tf_op jit(solution)/shard_map/ppermute | solution.py:35
  15.9 3.4 %collective-permute-start.4 = (bf16[512,256]{1,0:T(8,128)(2,1)}, bf16[512,256]{1,0:T(8,128)(2,1)S(1)}, u32[]{:S(2)}, u32[]{:S(2)}) collective-permute-start(bf16[512,256]{1,0:T(8,128)(2,1)} %refs_0_.1), channel_id=1, source_target_pairs={{0,2},{8,10},{16,18},{24,26},{32,34},{40,42},{48,50},{56,58},{64,6... | collective-permute-start | bytes 786440 | tf_op jit(solution)/shard_map/ppermute | solution.py:35
  19.3 3.7 %collective-permute-start.5 = (bf16[512,256]{1,0:T(8,128)(2,1)}, bf16[512,256]{1,0:T(8,128)(2,1)S(1)}, u32[]{:S(2)}, u32[]{:S(2)}) collective-permute-start(bf16[512,256]{1,0:T(8,128)(2,1)} %refs_0_.1), channel_id=1, source_target_pairs={{0,6},{8,14},{16,22},{24,30},{32,38},{40,46},{48,54},{56,62},{64,7... | collective-permute-start | bytes 786440 | tf_op jit(solution)/shard_map/ppermute | solution.py:35
  22.9 3.7 %collective-permute-start.6 = (bf16[512,256]{1,0:T(8,128)(2,1)}, bf16[512,256]{1,0:T(8,128)(2,1)S(1)}, u32[]{:S(2)}, u32[]{:S(2)}) collective-permute-start(bf16[512,256]{1,0:T(8,128)(2,1)} %refs_0_.1), channel_id=1, source_target_pairs={{0,4},{8,12},{16,20},{24,28},{32,36},{40,44},{48,52},{56,60},{64,6... | collective-permute-start | bytes 786440 | tf_op jit(solution)/shard_map/ppermute | solution.py:35
  26.7 0.0 collective-permute-done.refs_0_
  26.7 2.5 %collective-permute-start.1 = (bf16[512,256]{1,0:T(8,128)(2,1)S(1)}, bf16[512,256]{1,0:T(8,128)(2,1)S(1)}, u32[]{:S(2)}, u32[]{:S(2)}) collective-permute-start(bf16[512,256]{1,0:T(8,128)(2,1)S(1)} %collective-permute-done.refs_0_), channel_id=1, source_target_pairs={{0,2},{8,10},{16,18},{24,26},{32,34},{40,42},{48,50},{56,58},{64,6... | collective-permute-start | bytes 786440 | tf_op jit(solution)/shard_map/ppermute | solution.py:35
  29.2 4.6 %collective-permute-start.2 = (bf16[512,256]{1,0:T(8,128)(2,1)S(1)}, bf16[512,256]{1,0:T(8,128)(2,1)S(1)}, u32[]{:S(2)}, u32[]{:S(2)}) collective-permute-start(bf16[512,256]{1,0:T(8,128)(2,1)S(1)} %collective-permute-done.refs_0_), channel_id=1, source_target_pairs={{0,6},{8,14},{16,22},{24,30},{32,38},{40,46},{48,54},{56,62},{64,7... | collective-permute-start | bytes 786440 | tf_op jit(solution)/shard_map/ppermute | solution.py:35
  33.7 0.0 collective-permute-done.4.refs_1_
  33.7 2.4 %collective-permute-start.3 = (bf16[512,256]{1,0:T(8,128)(2,1)S(1)}, bf16[512,256]{1,0:T(8,128)(2,1)S(1)}, u32[]{:S(2)}, u32[]{:S(2)}) collective-permute-start(bf16[512,256]{1,0:T(8,128)(2,1)S(1)} %collective-permute-done.refs_0_), channel_id=1, source_target_pairs={{0,4},{8,12},{16,20},{24,28},{32,36},{40,44},{48,52},{56,60},{64,6... | collective-permute-start | bytes 786440 | tf_op jit(solution)/shard_map/ppermute | solution.py:35
  36.2 2.3 %copy.10 = bf16[2048,2,384]{2,0,1:T(8,128)(2,1)S(1)} copy(bf16[2048,2,384]{2,1,0:T(2,128)(2,1)} %param.9) | data formatting | bytes 6291456 | tf_op args[2]
  38.5 0.0 copy-start.1
  38.5 0.0 collective-permute-done.5.refs_2_
  38.5 0.0 collective-permute-done.6.refs_3_
  38.5 1.3 own.1
  39.8 1.0 collective-permute-done.1.refs_1_
  40.8 1.1 collective-permute-done.2.refs_2_
  41.9 3.1 %collective-permute-done.3.refs_3_ = bf16[512,256]{1,0:T(8,128)(2,1)S(1)} collective-permute-done((bf16[512,256]{1,0:T(8,128)(2,1)S(1)}, bf16[512,256]{1,0:T(8,128)(2,1)S(1)}, u32[]{:S(2)}, u32[]{:S(2)}) %collective-permute-start.3) | collective-permute-done | bytes 262176 | tf_op jit(solution)/shard_map/ppermute | solution.py:35
  45.0 0.0 copy-done.1
  45.0 3.2 %project.1 = (bf16[512,384]{1,0:T(8,128)(2,1)S(1)}, bf16[512,512]{1,0:T(8,128)(2,1)S(1)}, bf16[384,512]{1,0:T(8,128)(2,1)S(1)}, f32[160,128]{1,0:T(8,128)S(1)}, ...) custom-call(bf16[512,256]{1,0:T(8,128)(2,1)S(1)} %collective-permute-done.refs_0_, ...), custom_call_target="tpu_custom_call" | custom-call | tf_op jit(solution)/shard_map/project/pallas_call | solution.py:324
  48.2 0.0 copy-start.4
  48.2 14.6 %collective-permute-start.9 = (bf16[160,128]{1,0:T(8,128)(2,1)S(1)}, bf16[160,128]{1,0:T(8,128)(2,1)S(1)}, u32[]{:S(2)}, u32[]{:S(2)}) collective-permute-start(bf16[160,128]{1,0:T(8,128)(2,1)S(1)} %get-tuple-element.46), channel_id=1, source_target_pairs={{0,16},{8,24},{16,0},{24,8},{32,48},{40,56},{48,32},{56,40},{64,80... | collective-permute-start | bytes 122888 | tf_op jit(solution)/shard_map/ppermute | solution.py:35
  62.9 1.9 %collective-permute-start.8 = (bf16[160,128]{1,0:T(8,128)(2,1)S(1)}, bf16[160,128]{1,0:T(8,128)(2,1)S(1)}, u32[]{:S(2)}, u32[]{:S(2)}) collective-permute-start(bf16[160,128]{1,0:T(8,128)(2,1)S(1)} %get-tuple-element.45), channel_id=1, source_target_pairs={{0,24},{8,16},{16,8},{24,0},{32,56},{40,48},{48,40},{56,32},{64,88... | collective-permute-start | bytes 122888 | tf_op jit(solution)/shard_map/ppermute | solution.py:35
  64.8 2.0 %collective-permute-start.7 = (bf16[160,128]{1,0:T(8,128)(2,1)S(1)}, bf16[160,128]{1,0:T(8,128)(2,1)S(1)}, u32[]{:S(2)}, u32[]{:S(2)}) collective-permute-start(bf16[160,128]{1,0:T(8,128)(2,1)S(1)} %get-tuple-element.45), channel_id=1, source_target_pairs={{0,8},{8,0},{16,24},{24,16},{32,40},{40,32},{48,56},{56,48},{64,72... | collective-permute-start | bytes 122888 | tf_op jit(solution)/shard_map/ppermute | solution.py:35
  66.9 0.0 collective-permute-done.9
  66.9 1.3 collective-permute-done.8
  68.2 0.0 collective-permute-done.7
  68.2 1.9 %collective-permute-start.10 = (bf16[160,128]{1,0:T(8,128)(2,1)S(1)}, bf16[160,128]{1,0:T(8,128)(2,1)S(1)}, u32[]{:S(2)}, u32[]{:S(2)}) collective-permute-start(bf16[160,128]{1,0:T(8,128)(2,1)S(1)} %convert_element_type.72), channel_id=1, source_target_pairs={{0,32},{8,40},{16,48},{24,56},{32,0},{40,8},{48,16},{56,24},{64,96... | collective-permute-start | bytes 122888 | tf_op jit(solution)/shard_map/ppermute | solution.py:35
  70.2 5.3 %collective-permute-done.10 = bf16[160,128]{1,0:T(8,128)(2,1)S(1)} collective-permute-done((bf16[160,128]{1,0:T(8,128)(2,1)S(1)}, bf16[160,128]{1,0:T(8,128)(2,1)S(1)}, u32[]{:S(2)}, u32[]{:S(2)}) %collective-permute-start.10) | collective-permute-done | bytes 40992 | tf_op jit(solution)/shard_map/ppermute | solution.py:35
  75.5 0.0 copy-start
  75.5 6.6 %collective-permute-start.11 = (bf16[160,128]{1,0:T(8,128)(2,1)S(1)}, bf16[160,128]{1,0:T(8,128)(2,1)S(1)}, u32[]{:S(2)}, u32[]{:S(2)}) collective-permute-start(bf16[160,128]{1,0:T(8,128)(2,1)S(1)} %convert_element_type.74), channel_id=1, source_target_pairs={{0,64},{8,72},{16,80},{24,88},{32,96},{40,104},{48,112},{56,120},{... | collective-permute-start | bytes 122888 | tf_op jit(solution)/shard_map/ppermute | solution.py:35
  82.1 1.9 %collective-permute-start.16 = (bf16[384,512]{1,0:T(8,128)(2,1)S(1)}, bf16[384,512]{1,0:T(8,128)(2,1)S(1)}, u32[]{:S(2)}, u32[]{:S(2)}) collective-permute-start(bf16[384,512]{1,0:T(8,128)(2,1)S(1)} %get-tuple-element.64), channel_id=1, source_target_pairs={{0,8},{8,16},{16,24},{24,32},{32,40},{40,48},{48,56},{56,64},{64,7... | collective-permute-start | bytes 1179656 | tf_op jit(solution)/shard_map/ppermute | solution.py:35
  84.0 2.0 %near.1 = (f32[512,256]{1,0:T(8,128)S(1)}, bf16[2,512,160]{2,1,0:T(8,128)(2,1)S(1)}, bf16[2,512,160]{2,1,0:T(8,128)(2,1)S(1)}) custom-call(bf16[512,384]{1,0:T(8,128)(2,1)S(1)} %get-tuple-element.52.qf_ref, bf16[512,512]{1,0:T(8,128)(2,1)S(1)} %get-tuple-element.53.kv_ref, bf16[2,4,160,128]{3,2,1,0:T(8,128)(2,1)S(1)} %copy-done.1), custom_call_target="tpu_custom_call" | custom-call | tf_op jit(solution)/shard_map/near/pallas_call | solution.py:348
  86.1 0.8 collective-permute-done.11
  86.9 0.7 collective-permute-start.14
  87.6 1.3 collective-permute-start.13
  88.9 3.8 %collective-permute-start.12 = (bf16[160,128]{1,0:T(8,128)(2,1)S(1)}, bf16[160,128]{1,0:T(8,128)(2,1)S(1)}, u32[]{:S(2)}, u32[]{:S(2)}) collective-permute-start(bf16[160,128]{1,0:T(8,128)(2,1)S(1)} %convert_add_fusion.1), channel_id=1, source_target_pairs={{0,128},{8,136},{16,144},{24,152},{32,160},{40,168},{48,176},{56,1... | collective-permute-start | bytes 122888 | tf_op jit(solution)/shard_map/ppermute | solution.py:35
  92.7 0.0 collective-permute-done.14
  92.7 6.6 %collective-permute-done.13 = bf16[160,128]{1,0:T(8,128)(2,1)S(1)} collective-permute-done((bf16[160,128]{1,0:T(8,128)(2,1)S(1)}, bf16[160,128]{1,0:T(8,128)(2,1)S(1)}, u32[]{:S(2)}, u32[]{:S(2)}) %collective-permute-start.13) | collective-permute-done | bytes 40992 | tf_op jit(solution)/shard_map/ppermute | solution.py:35
  99.4 0.6 collective-permute-done.12
  100.1 1.9 %collective-permute-start.15 = (bf16[160,128]{1,0:T(8,128)(2,1)S(1)}, bf16[160,128]{1,0:T(8,128)(2,1)S(1)}, u32[]{:S(2)}, u32[]{:S(2)}) collective-permute-start(bf16[160,128]{1,0:T(8,128)(2,1)S(1)} %get-tuple-element.79), channel_id=1, source_target_pairs={{0,8},{8,0},{16,24},{24,16},{32,40},{40,32},{48,56},{56,48},{64,72... | collective-permute-start | bytes 122888 | tf_op jit(solution)/shard_map/ppermute | solution.py:35
  102.0 0.0 collective-permute-done.16.halo_ref
  102.0 2.4 %window.1.win_ref = f32[512,256]{1,0:T(8,128)S(1)} custom-call(s32[2]{0:T(128)S(1)} %copy-done.4, bf16[512,384]{1,0:T(8,128)(2,1)S(1)} %get-tuple-element.52.qf_ref, bf16[512,512]{1,0:T(8,128)(2,1)S(1)} %get-tuple-element.53.kv_ref, bf16[384,512]{1,0:T(8,128)(2,1)S(1)} %collective-permute-done.16.halo_ref), custom_call_target="tpu_custom_call" | custom-call | tf_op jit(solution)/shard_map/window/pallas_call | solution.py:364
  104.5 0.0 collective-permute-done.15.theirs
  104.5 0.7 hidden.1
  105.2 0.0 copy-done
  105.2 0.5 product.2
  105.6 3.7 %collective-permute-start.19 = (bf16[64,2048]{1,0:T(8,128)(2,1)S(1)}, bf16[64,2048]{1,0:T(8,128)(2,1)S(1)}, u32[]{:S(2)}, u32[]{:S(2)}) collective-permute-start(bf16[64,2048]{1,0:T(8,128)(2,1)S(1)} %get-tuple-element.71), channel_id=1, source_target_pairs={{0,4},{8,12},{16,20},{24,28},{32,36},{40,44},{48,52},{56,60},{64,6... | collective-permute-start | bytes 786440 | tf_op jit(solution)/shard_map/ppermute | solution.py:35
  109.3 5.6 %collective-permute-start.18 = (bf16[64,2048]{1,0:T(8,128)(2,1)S(1)}, bf16[64,2048]{1,0:T(8,128)(2,1)S(1)}, u32[]{:S(2)}, u32[]{:S(2)}) collective-permute-start(bf16[64,2048]{1,0:T(8,128)(2,1)S(1)} %get-tuple-element.70), channel_id=1, source_target_pairs={{0,6},{8,14},{16,22},{24,30},{32,38},{40,46},{48,54},{56,62},{64,7... | collective-permute-start | bytes 786440 | tf_op jit(solution)/shard_map/ppermute | solution.py:35
  115.0 1.9 %collective-permute-start.17 = (bf16[64,2048]{1,0:T(8,128)(2,1)S(1)}, bf16[64,2048]{1,0:T(8,128)(2,1)S(1)}, u32[]{:S(2)}, u32[]{:S(2)}) collective-permute-start(bf16[64,2048]{1,0:T(8,128)(2,1)S(1)} %get-tuple-element.69), channel_id=1, source_target_pairs={{0,2},{8,10},{16,18},{24,26},{32,34},{40,42},{48,50},{56,58},{64,6... | collective-permute-start | bytes 786440 | tf_op jit(solution)/shard_map/ppermute | solution.py:35
  116.9 0.8 collective-permute-done.19
  117.7 6.6 %collective-permute-done.18 = bf16[64,2048]{1,0:T(8,128)(2,1)S(1)} collective-permute-done((bf16[64,2048]{1,0:T(8,128)(2,1)S(1)}, bf16[64,2048]{1,0:T(8,128)(2,1)S(1)}, u32[]{:S(2)}, u32[]{:S(2)}) %collective-permute-start.18) | collective-permute-done | bytes 262176 | tf_op jit(solution)/shard_map/ppermute | solution.py:35
  124.4 1.8 %collective-permute-done.17 = bf16[64,2048]{1,0:T(8,128)(2,1)S(1)} collective-permute-done((bf16[64,2048]{1,0:T(8,128)(2,1)S(1)}, bf16[64,2048]{1,0:T(8,128)(2,1)S(1)}, u32[]{:S(2)}, u32[]{:S(2)}) %collective-permute-start.17) | collective-permute-done | bytes 262176 | tf_op jit(solution)/shard_map/ppermute | solution.py:35
  126.2 0.1 add_convert_fusion.1
  126.3 9.1 %collective-permute-start.20 = (bf16[64,2048]{1,0:T(8,128)(2,1)S(1)}, bf16[64,2048]{1,0:T(8,128)(2,1)S(1)}, u32[]{:S(2)}, u32[]{:S(2)}) collective-permute-start(bf16[64,2048]{1,0:T(8,128)(2,1)S(1)} %add_convert_fusion.1), channel_id=1, source_target_pairs={{0,1},{8,9},{16,17},{24,25},{32,33},{40,41},{48,49},{56,57},{64,65... | collective-permute-start | bytes 786440 | tf_op jit(solution)/shard_map/ppermute | solution.py:35
  135.5 0.4 product.3
  135.9 2.5 %collective-permute-start.23 = (bf16[64,2048]{1,0:T(8,128)(2,1)S(1)}, bf16[64,2048]{1,0:T(8,128)(2,1)S(1)}, u32[]{:S(2)}, u32[]{:S(2)}) collective-permute-start(bf16[64,2048]{1,0:T(8,128)(2,1)S(1)} %get-tuple-element.78), channel_id=1, source_target_pairs={{0,4},{8,12},{16,20},{24,28},{32,36},{40,44},{48,52},{56,60},{64,6... | collective-permute-start | bytes 786440 | tf_op jit(solution)/shard_map/ppermute | solution.py:35
  138.4 3.9 %collective-permute-start.22 = (bf16[64,2048]{1,0:T(8,128)(2,1)S(1)}, bf16[64,2048]{1,0:T(8,128)(2,1)S(1)}, u32[]{:S(2)}, u32[]{:S(2)}) collective-permute-start(bf16[64,2048]{1,0:T(8,128)(2,1)S(1)} %get-tuple-element.77), channel_id=1, source_target_pairs={{0,6},{8,14},{16,22},{24,30},{32,38},{40,46},{48,54},{56,62},{64,7... | collective-permute-start | bytes 786440 | tf_op jit(solution)/shard_map/ppermute | solution.py:35
  142.4 1.9 %collective-permute-start.21 = (bf16[64,2048]{1,0:T(8,128)(2,1)S(1)}, bf16[64,2048]{1,0:T(8,128)(2,1)S(1)}, u32[]{:S(2)}, u32[]{:S(2)}) collective-permute-start(bf16[64,2048]{1,0:T(8,128)(2,1)S(1)} %get-tuple-element.76), channel_id=1, source_target_pairs={{0,2},{8,10},{16,18},{24,26},{32,34},{40,42},{48,50},{56,58},{64,6... | collective-permute-start | bytes 786440 | tf_op jit(solution)/shard_map/ppermute | solution.py:35
  144.3 16.9 %collective-permute-done.20 = bf16[64,2048]{1,0:T(8,128)(2,1)S(1)} collective-permute-done((bf16[64,2048]{1,0:T(8,128)(2,1)S(1)}, bf16[64,2048]{1,0:T(8,128)(2,1)S(1)}, u32[]{:S(2)}, u32[]{:S(2)}) %collective-permute-start.20) | collective-permute-done | bytes 262176 | tf_op jit(solution)/shard_map/ppermute | solution.py:35
  161.2 0.1 convert_add_fusion
  161.2 0.0 collective-permute-done.23
  161.2 0.0 collective-permute-done.22
  161.3 0.0 collective-permute-done.21
  161.3 0.8 add_convert_fusion
  (12 shorter events, 0.1 us)
Async XLA Ops:
  0.0 38.5 %copy-start.3 = (bf16[512,256]{1,0:T(8,128)(2,1)S(1)}, bf16[512,256]{1,0:T(8,128)(2,1)}, u32[]{:S(2)}) copy-start(bf16[512,256]{1,0:T(8,128)(2,1)} %refs_0_.1) | copy-start | bytes 786436
  0.0 38.5 %copy-start.2 = (bf16[2048,2,32]{0,2,1:T(8,128)(2,1)S(1)}, bf16[2048,2,32]{0,2,1:T(8,128)(2,1)}, u32[]{:S(2)}) copy-start(bf16[2048,2,32]{0,2,1:T(8,128)(2,1)} %param.8) | copy-start | bytes 786436
  0.0 26.6 %collective-permute-start = (bf16[512,256]{1,0:T(8,128)(2,1)}, bf16[512,256]{1,0:T(8,128)(2,1)S(1)}, u32[]{:S(2)}, u32[]{:S(2)}) collective-permute-start(bf16[512,256]{1,0:T(8,128)(2,1)} %refs_0_.1), channel_id=1, source_target_pairs={{0,1},{8,9},{16,17},{24,25},{32,33},{40,41},{48,49},{56,57},{64,65... | collective-permute-start | bytes 786440 | tf_op jit(solution)/shard_map/ppermute | solution.py:35
  15.9 17.9 %collective-permute-start.4 = (bf16[512,256]{1,0:T(8,128)(2,1)}, bf16[512,256]{1,0:T(8,128)(2,1)S(1)}, u32[]{:S(2)}, u32[]{:S(2)}) collective-permute-start(bf16[512,256]{1,0:T(8,128)(2,1)} %refs_0_.1), channel_id=1, source_target_pairs={{0,2},{8,10},{16,18},{24,26},{32,34},{40,42},{48,50},{56,58},{64,6... | collective-permute-start | bytes 786440 | tf_op jit(solution)/shard_map/ppermute | solution.py:35
  19.3 19.2 %collective-permute-start.5 = (bf16[512,256]{1,0:T(8,128)(2,1)}, bf16[512,256]{1,0:T(8,128)(2,1)S(1)}, u32[]{:S(2)}, u32[]{:S(2)}) collective-permute-start(bf16[512,256]{1,0:T(8,128)(2,1)} %refs_0_.1), channel_id=1, source_target_pairs={{0,6},{8,14},{16,22},{24,30},{32,38},{40,46},{48,54},{56,62},{64,7... | collective-permute-start | bytes 786440 | tf_op jit(solution)/shard_map/ppermute | solution.py:35
  22.9 15.6 %collective-permute-start.6 = (bf16[512,256]{1,0:T(8,128)(2,1)}, bf16[512,256]{1,0:T(8,128)(2,1)S(1)}, u32[]{:S(2)}, u32[]{:S(2)}) collective-permute-start(bf16[512,256]{1,0:T(8,128)(2,1)} %refs_0_.1), channel_id=1, source_target_pairs={{0,4},{8,12},{16,20},{24,28},{32,36},{40,44},{48,52},{56,60},{64,6... | collective-permute-start | bytes 786440 | tf_op jit(solution)/shard_map/ppermute | solution.py:35
  26.7 14.1 %collective-permute-start.1 = (bf16[512,256]{1,0:T(8,128)(2,1)S(1)}, bf16[512,256]{1,0:T(8,128)(2,1)S(1)}, u32[]{:S(2)}, u32[]{:S(2)}) collective-permute-start(bf16[512,256]{1,0:T(8,128)(2,1)S(1)} %collective-permute-done.refs_0_), channel_id=1, source_target_pairs={{0,2},{8,10},{16,18},{24,26},{32,34},{40,42},{48,50},{56,58},{64,6... | collective-permute-start | bytes 786440 | tf_op jit(solution)/shard_map/ppermute | solution.py:35
  29.2 12.7 %collective-permute-start.2 = (bf16[512,256]{1,0:T(8,128)(2,1)S(1)}, bf16[512,256]{1,0:T(8,128)(2,1)S(1)}, u32[]{:S(2)}, u32[]{:S(2)}) collective-permute-start(bf16[512,256]{1,0:T(8,128)(2,1)S(1)} %collective-permute-done.refs_0_), channel_id=1, source_target_pairs={{0,6},{8,14},{16,22},{24,30},{32,38},{40,46},{48,54},{56,62},{64,7... | collective-permute-start | bytes 786440 | tf_op jit(solution)/shard_map/ppermute | solution.py:35
  33.7 11.2 %collective-permute-start.3 = (bf16[512,256]{1,0:T(8,128)(2,1)S(1)}, bf16[512,256]{1,0:T(8,128)(2,1)S(1)}, u32[]{:S(2)}, u32[]{:S(2)}) collective-permute-start(bf16[512,256]{1,0:T(8,128)(2,1)S(1)} %collective-permute-done.refs_0_), channel_id=1, source_target_pairs={{0,4},{8,12},{16,20},{24,28},{32,36},{40,44},{48,52},{56,60},{64,6... | collective-permute-start | bytes 786440 | tf_op jit(solution)/shard_map/ppermute | solution.py:35
  38.5 6.5 %copy-start.1 = (bf16[2,4,160,128]{3,2,1,0:T(8,128)(2,1)S(1)}, bf16[2,4,160,128]{3,2,1,0:T(8,128)(2,1)}, u32[]{:S(2)}) copy-start(bf16[2,4,160,128]{3,2,1,0:T(8,128)(2,1)} %constant.52.clone.refs_6_.table) | copy-start | bytes 983044
  48.2 53.8 %copy-start.4 = (s32[2]{0:T(128)S(1)}, s32[2]{0:T(128)}, u32[]{:S(2)}) copy-start(s32[2]{0:T(128)} %win.1) | copy-start | bytes 28
  48.2 18.6 %collective-permute-start.9 = (bf16[160,128]{1,0:T(8,128)(2,1)S(1)}, bf16[160,128]{1,0:T(8,128)(2,1)S(1)}, u32[]{:S(2)}, u32[]{:S(2)}) collective-permute-start(bf16[160,128]{1,0:T(8,128)(2,1)S(1)} %get-tuple-element.46), channel_id=1, source_target_pairs={{0,16},{8,24},{16,0},{24,8},{32,48},{40,56},{48,32},{56,40},{64,80... | collective-permute-start | bytes 122888 | tf_op jit(solution)/shard_map/ppermute | solution.py:35
  62.9 5.3 %collective-permute-start.8 = (bf16[160,128]{1,0:T(8,128)(2,1)S(1)}, bf16[160,128]{1,0:T(8,128)(2,1)S(1)}, u32[]{:S(2)}, u32[]{:S(2)}) collective-permute-start(bf16[160,128]{1,0:T(8,128)(2,1)S(1)} %get-tuple-element.45), channel_id=1, source_target_pairs={{0,24},{8,16},{16,8},{24,0},{32,56},{40,48},{48,40},{56,32},{64,88... | collective-permute-start | bytes 122888 | tf_op jit(solution)/shard_map/ppermute | solution.py:35
  64.8 3.4 %collective-permute-start.7 = (bf16[160,128]{1,0:T(8,128)(2,1)S(1)}, bf16[160,128]{1,0:T(8,128)(2,1)S(1)}, u32[]{:S(2)}, u32[]{:S(2)}) collective-permute-start(bf16[160,128]{1,0:T(8,128)(2,1)S(1)} %get-tuple-element.45), channel_id=1, source_target_pairs={{0,8},{8,0},{16,24},{24,16},{32,40},{40,32},{48,56},{56,48},{64,72... | collective-permute-start | bytes 122888 | tf_op jit(solution)/shard_map/ppermute | solution.py:35
  68.2 7.2 %collective-permute-start.10 = (bf16[160,128]{1,0:T(8,128)(2,1)S(1)}, bf16[160,128]{1,0:T(8,128)(2,1)S(1)}, u32[]{:S(2)}, u32[]{:S(2)}) collective-permute-start(bf16[160,128]{1,0:T(8,128)(2,1)S(1)} %convert_element_type.72), channel_id=1, source_target_pairs={{0,32},{8,40},{16,48},{24,56},{32,0},{40,8},{48,16},{56,24},{64,96... | collective-permute-start | bytes 122888 | tf_op jit(solution)/shard_map/ppermute | solution.py:35
  75.5 29.7 %copy-start = (bf16[2,128,2048]{2,1,0:T(8,128)(2,1)S(1)}, bf16[2,128,2048]{2,1,0:T(8,128)(2,1)}, u32[]{:S(2)}) copy-start(bf16[2,128,2048]{2,1,0:T(8,128)(2,1)} %param.10) | copy-start | bytes 3145732
  75.5 11.4 %collective-permute-start.11 = (bf16[160,128]{1,0:T(8,128)(2,1)S(1)}, bf16[160,128]{1,0:T(8,128)(2,1)S(1)}, u32[]{:S(2)}, u32[]{:S(2)}) collective-permute-start(bf16[160,128]{1,0:T(8,128)(2,1)S(1)} %convert_element_type.74), channel_id=1, source_target_pairs={{0,64},{8,72},{16,80},{24,88},{32,96},{40,104},{48,112},{56,120},{... | collective-permute-start | bytes 122888 | tf_op jit(solution)/shard_map/ppermute | solution.py:35
  82.1 19.9 %collective-permute-start.16 = (bf16[384,512]{1,0:T(8,128)(2,1)S(1)}, bf16[384,512]{1,0:T(8,128)(2,1)S(1)}, u32[]{:S(2)}, u32[]{:S(2)}) collective-permute-start(bf16[384,512]{1,0:T(8,128)(2,1)S(1)} %get-tuple-element.64), channel_id=1, source_target_pairs={{0,8},{8,16},{16,24},{24,32},{32,40},{40,48},{48,56},{56,64},{64,7... | collective-permute-start | bytes 1179656 | tf_op jit(solution)/shard_map/ppermute | solution.py:35
  86.9 5.8 %collective-permute-start.14 = (bf16[160,128]{1,0:T(8,128)(2,1)S(1)}, bf16[160,128]{1,0:T(8,128)(2,1)S(1)}, u32[]{:S(2)}, u32[]{:S(2)}) collective-permute-start(bf16[160,128]{1,0:T(8,128)(2,1)S(1)} %convert_add_fusion.1), channel_id=1, source_target_pairs={{0,384},{8,392},{16,400},{24,408},{32,416},{40,424},{48,432},{56,4... | collective-permute-start | bytes 122888 | tf_op jit(solution)/shard_map/ppermute | solution.py:35
  87.6 11.8 %collective-permute-start.13 = (bf16[160,128]{1,0:T(8,128)(2,1)S(1)}, bf16[160,128]{1,0:T(8,128)(2,1)S(1)}, u32[]{:S(2)}, u32[]{:S(2)}) collective-permute-start(bf16[160,128]{1,0:T(8,128)(2,1)S(1)} %convert_add_fusion.1), channel_id=1, source_target_pairs={{0,256},{8,264},{16,272},{24,280},{32,288},{40,296},{48,304},{56,3... | collective-permute-start | bytes 122888 | tf_op jit(solution)/shard_map/ppermute | solution.py:35
  88.9 11.1 %collective-permute-start.12 = (bf16[160,128]{1,0:T(8,128)(2,1)S(1)}, bf16[160,128]{1,0:T(8,128)(2,1)S(1)}, u32[]{:S(2)}, u32[]{:S(2)}) collective-permute-start(bf16[160,128]{1,0:T(8,128)(2,1)S(1)} %convert_add_fusion.1), channel_id=1, source_target_pairs={{0,128},{8,136},{16,144},{24,152},{32,160},{40,168},{48,176},{56,1... | collective-permute-start | bytes 122888 | tf_op jit(solution)/shard_map/ppermute | solution.py:35
  100.1 4.4 %collective-permute-start.15 = (bf16[160,128]{1,0:T(8,128)(2,1)S(1)}, bf16[160,128]{1,0:T(8,128)(2,1)S(1)}, u32[]{:S(2)}, u32[]{:S(2)}) collective-permute-start(bf16[160,128]{1,0:T(8,128)(2,1)S(1)} %get-tuple-element.79), channel_id=1, source_target_pairs={{0,8},{8,0},{16,24},{24,16},{32,40},{40,32},{48,56},{56,48},{64,72... | collective-permute-start | bytes 122888 | tf_op jit(solution)/shard_map/ppermute | solution.py:35
  105.6 12.1 %collective-permute-start.19 = (bf16[64,2048]{1,0:T(8,128)(2,1)S(1)}, bf16[64,2048]{1,0:T(8,128)(2,1)S(1)}, u32[]{:S(2)}, u32[]{:S(2)}) collective-permute-start(bf16[64,2048]{1,0:T(8,128)(2,1)S(1)} %get-tuple-element.71), channel_id=1, source_target_pairs={{0,4},{8,12},{16,20},{24,28},{32,36},{40,44},{48,52},{56,60},{64,6... | collective-permute-start | bytes 786440 | tf_op jit(solution)/shard_map/ppermute | solution.py:35
  109.3 15.0 %collective-permute-start.18 = (bf16[64,2048]{1,0:T(8,128)(2,1)S(1)}, bf16[64,2048]{1,0:T(8,128)(2,1)S(1)}, u32[]{:S(2)}, u32[]{:S(2)}) collective-permute-start(bf16[64,2048]{1,0:T(8,128)(2,1)S(1)} %get-tuple-element.70), channel_id=1, source_target_pairs={{0,6},{8,14},{16,22},{24,30},{32,38},{40,46},{48,54},{56,62},{64,7... | collective-permute-start | bytes 786440 | tf_op jit(solution)/shard_map/ppermute | solution.py:35
  115.0 11.2 %collective-permute-start.17 = (bf16[64,2048]{1,0:T(8,128)(2,1)S(1)}, bf16[64,2048]{1,0:T(8,128)(2,1)S(1)}, u32[]{:S(2)}, u32[]{:S(2)}) collective-permute-start(bf16[64,2048]{1,0:T(8,128)(2,1)S(1)} %get-tuple-element.69), channel_id=1, source_target_pairs={{0,2},{8,10},{16,18},{24,26},{32,34},{40,42},{48,50},{56,58},{64,6... | collective-permute-start | bytes 786440 | tf_op jit(solution)/shard_map/ppermute | solution.py:35
  126.3 34.8 %collective-permute-start.20 = (bf16[64,2048]{1,0:T(8,128)(2,1)S(1)}, bf16[64,2048]{1,0:T(8,128)(2,1)S(1)}, u32[]{:S(2)}, u32[]{:S(2)}) collective-permute-start(bf16[64,2048]{1,0:T(8,128)(2,1)S(1)} %add_convert_fusion.1), channel_id=1, source_target_pairs={{0,1},{8,9},{16,17},{24,25},{32,33},{40,41},{48,49},{56,57},{64,65... | collective-permute-start | bytes 786440 | tf_op jit(solution)/shard_map/ppermute | solution.py:35
  135.9 25.3 %collective-permute-start.23 = (bf16[64,2048]{1,0:T(8,128)(2,1)S(1)}, bf16[64,2048]{1,0:T(8,128)(2,1)S(1)}, u32[]{:S(2)}, u32[]{:S(2)}) collective-permute-start(bf16[64,2048]{1,0:T(8,128)(2,1)S(1)} %get-tuple-element.78), channel_id=1, source_target_pairs={{0,4},{8,12},{16,20},{24,28},{32,36},{40,44},{48,52},{56,60},{64,6... | collective-permute-start | bytes 786440 | tf_op jit(solution)/shard_map/ppermute | solution.py:35
  138.4 22.8 %collective-permute-start.22 = (bf16[64,2048]{1,0:T(8,128)(2,1)S(1)}, bf16[64,2048]{1,0:T(8,128)(2,1)S(1)}, u32[]{:S(2)}, u32[]{:S(2)}) collective-permute-start(bf16[64,2048]{1,0:T(8,128)(2,1)S(1)} %get-tuple-element.77), channel_id=1, source_target_pairs={{0,6},{8,14},{16,22},{24,30},{32,38},{40,46},{48,54},{56,62},{64,7... | collective-permute-start | bytes 786440 | tf_op jit(solution)/shard_map/ppermute | solution.py:35
  142.4 18.9 %collective-permute-start.21 = (bf16[64,2048]{1,0:T(8,128)(2,1)S(1)}, bf16[64,2048]{1,0:T(8,128)(2,1)S(1)}, u32[]{:S(2)}, u32[]{:S(2)}) collective-permute-start(bf16[64,2048]{1,0:T(8,128)(2,1)S(1)} %get-tuple-element.76), channel_id=1, source_target_pairs={{0,2},{8,10},{16,18},{24,26},{32,34},{40,42},{48,50},{56,58},{64,6... | collective-permute-start | bytes 786440 | tf_op jit(solution)/shard_map/ppermute | solution.py:35

commit v10 on v9

--- a/solution.py
+++ b/solution.py
@@ -183,7 +183,7 @@
         copy.wait()
 
 
-def near_kernel(qf_ref, kv_ref, table, near_ref, high_ref, low_ref, qn_ref, sem):
+def near_kernel(qf_ref, kv_ref, table, near_ref, map_ref, qn_ref, sem):
     copy = pltpu.make_async_copy(qf_ref, qn_ref, sem)
     copy.start()
     copy.wait()
@@ -199,9 +199,7 @@
         vcols = slice((heads + h) * head, (heads + h + 1) * head)
         left = dot_t(feats, table[h, 0])
         right = dot_t(feats, table[h, 1])
-        high, low = halves(left * right)
-        high_ref[h] = high
-        low_ref[h] = low
+        map_ref[h] = (left * right).astype(bf16)
         key = lax.broadcasted_iota(jnp.int32, (feats.shape[1], feats.shape[1]), 0)
         lane = lax.broadcasted_iota(jnp.int32, (feats.shape[1], feats.shape[1]), 1)
         first = h * 2 * feat
@@ -245,7 +243,7 @@
             win_ref[at, cols] = unit(dot(weights, values[b * BLOCK : b * BLOCK + span]))
 
 
-def hidden_kernel(ours, theirs, near_ref, win_ref, high_ref, low_ref, keep_ref, away_ref, hidden):
+def hidden_kernel(ours, theirs, near_ref, win_ref, map_ref, keep_ref, away_ref, hidden):
     x, half, core, _ = position()
     mine, other = ours[...], theirs[...].astype(f32)
     head = mine.shape[1]
@@ -253,8 +251,7 @@
     for h in range(2):
         cols = slice(h * head, (h + 1) * head)
         state_high, state_low = halves(jnp.where(core == h, mine, other))
-        high = high_ref[h]
-        far = dot(high, state_high) + dot(low_ref[h], state_high) + dot(high, state_low)
+        far = dot(map_ref[h], state_high) + dot(map_ref[h], state_low)
         out = (unit(near_ref[:, cols] + far) + win_ref[:, cols]).astype(bf16)
         for g in range(N_TP):
             hidden[g, :, cols] = out[g * rows : (g + 1) * rows]
@@ -271,7 +268,7 @@
         out[...] = product[s * rows : (s + 1) * rows]
 
 
-def prefix(mine, short, other, place, beside):
+def prefix(mine, short, other, place, attend, hand_on):
     x, h, y, z, c = place
     across = send(other, lambda x, h, y, z, c: (x, h, y, z ^ 1, 1 - c)).astype(f32)
     beyond = send(short, to_z(1)).astype(f32)
@@ -280,24 +277,21 @@
     add = (jnp.where(c == 0, mine, 0.0), jnp.where(c == 1, got, 0.0))
     before = jnp.where(z % 2 == 1, across + beyond, 0.0)
     total, before, add = lax.optimization_barrier((total, before, add))
-    done = None
     for flip in (2, 4):
         part = send(total.astype(bf16), to_z(flip))
-        if flip == 4:
-            *behind, halo = done
-            part, *behind = lax.optimization_barrier((part, *behind))
-            done = (*behind, halo)
+        if flip == 2:
+            part, *behind = lax.optimization_barrier((part, *attend(total)))
+        else:
+            halo = hand_on(total)
         part = part.astype(f32)
         before = before + jnp.where((z ^ flip) < z, part, 0.0)
         total, before = lax.optimization_barrier((total + part, before))
-        if flip == 2:
-            done = beside(total)
     short = total.astype(bf16)
     for steps in (1, 2, 3):
         before = before + send(short, to_y(steps)).astype(f32)
     theirs = send((before + add[0]).astype(bf16), to_core)
     ours = before + add[1]
-    return ours, theirs, done
+    return ours, theirs, behind, halo
 
 
 def shape(dims, kind):
@@ -350,10 +344,9 @@
         out_shape=(
             shape((tok_rows, wide), f32),
             shape((2, tok_rows, ROWS), bf16),
-            shape((2, tok_rows, ROWS), bf16),
         ),
         in_specs=[HBM, VMEM, VMEM],
-        out_specs=(VMEM,) * 3,
+        out_specs=(VMEM,) * 2,
         scratch_shapes=[pltpu.VMEM(qf.shape, bf16), pltpu.SemaphoreType.DMA],
         name="near",
         compiler_params=pltpu.CompilerParams(vmem_limit_bytes=LIMIT),
@@ -372,17 +365,17 @@
     )(win_blocks, qf, kv, halo)
 
 
-def hidden_rows(ours, theirs, near_out, win_out, high, low):
+def hidden_rows(ours, theirs, near_out, win_out, query_map):
     tok_rows, wide = near_out.shape
     return pl.pallas_call(
         hidden_kernel,
         out_shape=(shape((tok_rows // 2, wide), bf16),) * 2,
-        in_specs=[VMEM] * 6,
+        in_specs=[VMEM] * 5,
         out_specs=(VMEM,) * 2,
         scratch_shapes=[pltpu.VMEM((N_TP, tok_rows // N_TP, wide), bf16)],
         name="hidden",
         compiler_params=pltpu.CompilerParams(vmem_limit_bytes=LIMIT),
-    )(ours, theirs, near_out, win_out, high, low)
+    )(ours, theirs, near_out, win_out, query_map)
 
 
 def product(hidden, w_out):
@@ -414,16 +407,18 @@
     own = own_products(parts[:NX], wf, ww)
     qf, kv, tail, mine, short, theirs = project(parts[NX:], wf, ww, tables, own)
 
-    def beside(total):
-        early, kept, _ = lax.optimization_barrier((qf, tail, total))
-        return *near(early, kv, tables), send(kept, to_next)
-
-    ours, theirs, (near_out, high, low, halo) = prefix(mine, short, theirs, (x, h, y, z, c), beside)
+    def attend(total):
+        return near(lax.optimization_barrier((qf, total))[0], kv, tables)
+
+    def hand_on(total):
+        return send(lax.optimization_barrier((tail, total))[0], to_next)
+
+    ours, theirs, (near_out, query_map), halo = prefix(mine, short, theirs, (x, h, y, z, c), attend, hand_on)
     win_out = window(win_blocks, qf, kv, halo)
-    keep, away = hidden_rows(ours, theirs, near_out, win_out, high, low)
+    keep, away = hidden_rows(ours, theirs, near_out, win_out, query_map)
 
     def summed(total, group):
-        for steps in (1, 3, 2):
+        for steps in (2, 3, 1):
             total = total + send(group[steps], to_x(steps)).astype(f32)
         return total.astype(bf16)
 

time: 163 us -> 166 us (1.018)
  the two profiles are of different devices: /device:TPU:16 before, /device:TPU:18 now
where the time goes in v10:
time: 166 us
  starting transfers between devices  99.8 us (60%)
  waiting for transfers between devices  48.3 us (29%)
  Pallas kernels  10.4 us (6%)
  other arithmetic  3.49 us (2%)
  local copies, waits for them, and re-layouts  3.07 us (2%)
    ppermute x24, starting transfers between devices, send(): return lax.ppermute(value, ('seq', 'tp'), pairs(move))  99.8 us
    ppermute x24, waiting for transfers between devices, send(): return lax.ppermute(value, ('seq', 'tp'), pairs(move))  48.3 us
  transfers between devices with their start and end apart: 24, of which 12 were waited for; matrix products, arithmetic and copies ran while one was open for 2% of the time, Pallas kernels for 4%

profile of v10, /device:TPU:18, one launch (start us, length us, event | category | flops | bytes accessed | tf_op | source)
XLA Modules:
  0.0 165.6 jit_solution(12796734983028277933)
XLA Ops:
  0.0 15.8 %collective-permute-start = (bf16[512,256]{1,0:T(8,128)(2,1)}, bf16[512,256]{1,0:T(8,128)(2,1)S(1)}, u32[]{:S(2)}, u32[]{:S(2)}) collective-permute-start(bf16[512,256]{1,0:T(8,128)(2,1)} %refs_0_.1), channel_id=1, source_target_pairs={{0,1},{8,9},{16,17},{24,25},{32,33},{40,41},{48,49},{56,57},{64,65... | collective-permute-start | bytes 786440 | tf_op jit(solution)/shard_map/ppermute | solution.py:35
  15.9 3.4 %collective-permute-start.4 = (bf16[512,256]{1,0:T(8,128)(2,1)}, bf16[512,256]{1,0:T(8,128)(2,1)S(1)}, u32[]{:S(2)}, u32[]{:S(2)}) collective-permute-start(bf16[512,256]{1,0:T(8,128)(2,1)} %refs_0_.1), channel_id=1, source_target_pairs={{0,2},{8,10},{16,18},{24,26},{32,34},{40,42},{48,50},{56,58},{64,6... | collective-permute-start | bytes 786440 | tf_op jit(solution)/shard_map/ppermute | solution.py:35
  19.3 2.4 %collective-permute-start.5 = (bf16[512,256]{1,0:T(8,128)(2,1)}, bf16[512,256]{1,0:T(8,128)(2,1)S(1)}, u32[]{:S(2)}, u32[]{:S(2)}) collective-permute-start(bf16[512,256]{1,0:T(8,128)(2,1)} %refs_0_.1), channel_id=1, source_target_pairs={{0,6},{8,14},{16,22},{24,30},{32,38},{40,46},{48,54},{56,62},{64,7... | collective-permute-start | bytes 786440 | tf_op jit(solution)/shard_map/ppermute | solution.py:35
  21.7 4.0 %collective-permute-start.6 = (bf16[512,256]{1,0:T(8,128)(2,1)}, bf16[512,256]{1,0:T(8,128)(2,1)S(1)}, u32[]{:S(2)}, u32[]{:S(2)}) collective-permute-start(bf16[512,256]{1,0:T(8,128)(2,1)} %refs_0_.1), channel_id=1, source_target_pairs={{0,4},{8,12},{16,20},{24,28},{32,36},{40,44},{48,52},{56,60},{64,6... | collective-permute-start | bytes 786440 | tf_op jit(solution)/shard_map/ppermute | solution.py:35
  25.8 0.0 collective-permute-done.refs_0_
  25.8 3.0 %collective-permute-start.1 = (bf16[512,256]{1,0:T(8,128)(2,1)S(1)}, bf16[512,256]{1,0:T(8,128)(2,1)S(1)}, u32[]{:S(2)}, u32[]{:S(2)}) collective-permute-start(bf16[512,256]{1,0:T(8,128)(2,1)S(1)} %collective-permute-done.refs_0_), channel_id=1, source_target_pairs={{0,2},{8,10},{16,18},{24,26},{32,34},{40,42},{48,50},{56,58},{64,6... | collective-permute-start | bytes 786440 | tf_op jit(solution)/shard_map/ppermute | solution.py:35
  28.8 2.9 %collective-permute-start.2 = (bf16[512,256]{1,0:T(8,128)(2,1)S(1)}, bf16[512,256]{1,0:T(8,128)(2,1)S(1)}, u32[]{:S(2)}, u32[]{:S(2)}) collective-permute-start(bf16[512,256]{1,0:T(8,128)(2,1)S(1)} %collective-permute-done.refs_0_), channel_id=1, source_target_pairs={{0,6},{8,14},{16,22},{24,30},{32,38},{40,46},{48,54},{56,62},{64,7... | collective-permute-start | bytes 786440 | tf_op jit(solution)/shard_map/ppermute | solution.py:35
  31.6 0.0 collective-permute-done.4.refs_1_
  31.6 3.4 %collective-permute-start.3 = (bf16[512,256]{1,0:T(8,128)(2,1)S(1)}, bf16[512,256]{1,0:T(8,128)(2,1)S(1)}, u32[]{:S(2)}, u32[]{:S(2)}) collective-permute-start(bf16[512,256]{1,0:T(8,128)(2,1)S(1)} %collective-permute-done.refs_0_), channel_id=1, source_target_pairs={{0,4},{8,12},{16,20},{24,28},{32,36},{40,44},{48,52},{56,60},{64,6... | collective-permute-start | bytes 786440 | tf_op jit(solution)/shard_map/ppermute | solution.py:35
  35.0 2.3 %copy.10 = bf16[2048,2,384]{2,0,1:T(8,128)(2,1)S(1)} copy(bf16[2048,2,384]{2,1,0:T(2,128)(2,1)} %param.9) | data formatting | bytes 6291456 | tf_op args[2]
  37.3 0.0 copy-start.1
  37.3 0.0 collective-permute-done.5.refs_2_
  37.4 0.0 collective-permute-done.6.refs_3_
  37.4 1.3 own.1
  38.7 1.6 collective-permute-done.1.refs_1_
  40.3 2.2 %collective-permute-done.2.refs_2_ = bf16[512,256]{1,0:T(8,128)(2,1)S(1)} collective-permute-done((bf16[512,256]{1,0:T(8,128)(2,1)S(1)}, bf16[512,256]{1,0:T(8,128)(2,1)S(1)}, u32[]{:S(2)}, u32[]{:S(2)}) %collective-permute-start.2) | collective-permute-done | bytes 262176 | tf_op jit(solution)/shard_map/ppermute | solution.py:35
  42.5 3.9 %collective-permute-done.3.refs_3_ = bf16[512,256]{1,0:T(8,128)(2,1)S(1)} collective-permute-done((bf16[512,256]{1,0:T(8,128)(2,1)S(1)}, bf16[512,256]{1,0:T(8,128)(2,1)S(1)}, u32[]{:S(2)}, u32[]{:S(2)}) %collective-permute-start.3) | collective-permute-done | bytes 262176 | tf_op jit(solution)/shard_map/ppermute | solution.py:35
  46.4 3.2 %project.1 = (bf16[512,384]{1,0:T(8,128)(2,1)S(1)}, bf16[512,512]{1,0:T(8,128)(2,1)S(1)}, bf16[384,512]{1,0:T(8,128)(2,1)S(1)}, f32[160,128]{1,0:T(8,128)S(1)}, ...) custom-call(bf16[512,256]{1,0:T(8,128)(2,1)S(1)} %collective-permute-done.refs_0_, ...), custom_call_target="tpu_custom_call" | custom-call | tf_op jit(solution)/shard_map/project/pallas_call | solution.py:318
  49.6 0.8 copy-done.5
  50.4 14.7 %collective-permute-start.9 = (bf16[160,128]{1,0:T(8,128)(2,1)S(1)}, bf16[160,128]{1,0:T(8,128)(2,1)S(1)}, u32[]{:S(2)}, u32[]{:S(2)}) collective-permute-start(bf16[160,128]{1,0:T(8,128)(2,1)S(1)} %get-tuple-element.44), channel_id=1, source_target_pairs={{0,16},{8,24},{16,0},{24,8},{32,48},{40,56},{48,32},{56,40},{64,80... | collective-permute-start | bytes 122888 | tf_op jit(solution)/shard_map/ppermute | solution.py:35
  65.1 1.9 %collective-permute-start.8 = (bf16[160,128]{1,0:T(8,128)(2,1)S(1)}, bf16[160,128]{1,0:T(8,128)(2,1)S(1)}, u32[]{:S(2)}, u32[]{:S(2)}) collective-permute-start(bf16[160,128]{1,0:T(8,128)(2,1)S(1)} %get-tuple-element.43), channel_id=1, source_target_pairs={{0,24},{8,16},{16,8},{24,0},{32,56},{40,48},{48,40},{56,32},{64,88... | collective-permute-start | bytes 122888 | tf_op jit(solution)/shard_map/ppermute | solution.py:35
  67.0 2.0 %collective-permute-start.7 = (bf16[160,128]{1,0:T(8,128)(2,1)S(1)}, bf16[160,128]{1,0:T(8,128)(2,1)S(1)}, u32[]{:S(2)}, u32[]{:S(2)}) collective-permute-start(bf16[160,128]{1,0:T(8,128)(2,1)S(1)} %get-tuple-element.43), channel_id=1, source_target_pairs={{0,8},{8,0},{16,24},{24,16},{32,40},{40,32},{48,56},{56,48},{64,72... | collective-permute-start | bytes 122888 | tf_op jit(solution)/shard_map/ppermute | solution.py:35
  69.1 0.0 collective-permute-done.9
  69.1 1.3 collective-permute-done.8
  70.4 0.0 collective-permute-done.7
  70.4 0.7 broadcast_select_fusion
  71.1 2.1 %collective-permute-start.10 = (bf16[160,128]{1,0:T(8,128)(2,1)S(1)}, bf16[160,128]{1,0:T(8,128)(2,1)}, u32[]{:S(2)}, u32[]{:S(2)}) collective-permute-start(bf16[160,128]{1,0:T(8,128)(2,1)S(1)} %convert_element_type.72), channel_id=1, source_target_pairs={{0,32},{8,40},{16,48},{24,56},{32,0},{40,8},{48,16},{56,24},{64,96... | collective-permute-start | bytes 122888 | tf_op jit(solution)/shard_map/ppermute | solution.py:35
  73.2 2.0 %near.1 = (f32[512,256]{1,0:T(8,128)S(1)}, bf16[2,512,160]{2,1,0:T(8,128)(2,1)S(1)}) custom-call(bf16[512,384]{1,0:T(8,128)(2,1)S(1)} %get-tuple-element.47.qf_ref, bf16[512,512]{1,0:T(8,128)(2,1)S(1)} %get-tuple-element.48.kv_ref, bf16[2,4,160,128]{3,2,1,0:T(8,128)(2,1)S(1)} %copy-done.1), custom_call_target="tpu_custom_call" | custom-call | tf_op jit(solution)/shard_map/near/pallas_call | solution.py:342
  75.2 3.3 %collective-permute-done.10 = bf16[160,128]{1,0:T(8,128)(2,1)} collective-permute-done((bf16[160,128]{1,0:T(8,128)(2,1)S(1)}, bf16[160,128]{1,0:T(8,128)(2,1)}, u32[]{:S(2)}, u32[]{:S(2)}) %collective-permute-start.10) | collective-permute-done | bytes 40992 | tf_op jit(solution)/shard_map/ppermute | solution.py:35
  78.6 0.8 fusion.1
  79.4 6.5 %collective-permute-start.11 = (bf16[160,128]{1,0:T(8,128)(2,1)S(1)}, bf16[160,128]{1,0:T(8,128)(2,1)S(1)}, u32[]{:S(2)}, u32[]{:S(2)}) collective-permute-start(bf16[160,128]{1,0:T(8,128)(2,1)S(1)} %convert_element_type.74), channel_id=1, source_target_pairs={{0,64},{8,72},{16,80},{24,88},{32,96},{40,104},{48,112},{56,120},{... | collective-permute-start | bytes 122888 | tf_op jit(solution)/shard_map/ppermute | solution.py:35
  85.8 1.9 %collective-permute-start.16 = (bf16[384,512]{1,0:T(8,128)(2,1)}, bf16[384,512]{1,0:T(8,128)(2,1)S(1)}, u32[]{:S(2)}, u32[]{:S(2)}) collective-permute-start(bf16[384,512]{1,0:T(8,128)(2,1)} %copy-done.5), channel_id=1, source_target_pairs={{0,8},{8,16},{16,24},{24,32},{32,40},{40,48},{48,56},{56,64},{64,7... | collective-permute-start | bytes 1179656 | tf_op jit(solution)/shard_map/ppermute | solution.py:35
  87.8 2.9 %collective-permute-done.11 = bf16[160,128]{1,0:T(8,128)(2,1)S(1)} collective-permute-done((bf16[160,128]{1,0:T(8,128)(2,1)S(1)}, bf16[160,128]{1,0:T(8,128)(2,1)S(1)}, u32[]{:S(2)}, u32[]{:S(2)}) %collective-permute-start.11) | collective-permute-done | bytes 40992 | tf_op jit(solution)/shard_map/ppermute | solution.py:35
  90.7 0.7 collective-permute-start.14
  91.3 1.3 collective-permute-start.13
  92.6 3.8 %collective-permute-start.12 = (bf16[160,128]{1,0:T(8,128)(2,1)S(1)}, bf16[160,128]{1,0:T(8,128)(2,1)S(1)}, u32[]{:S(2)}, u32[]{:S(2)}) collective-permute-start(bf16[160,128]{1,0:T(8,128)(2,1)S(1)} %convert_add_fusion.1), channel_id=1, source_target_pairs={{0,128},{8,136},{16,144},{24,152},{32,160},{40,168},{48,176},{56,1... | collective-permute-start | bytes 122888 | tf_op jit(solution)/shard_map/ppermute | solution.py:35
  96.5 0.0 collective-permute-done.14
  96.5 6.7 %collective-permute-done.13 = bf16[160,128]{1,0:T(8,128)(2,1)S(1)} collective-permute-done((bf16[160,128]{1,0:T(8,128)(2,1)S(1)}, bf16[160,128]{1,0:T(8,128)(2,1)S(1)}, u32[]{:S(2)}, u32[]{:S(2)}) %collective-permute-start.13) | collective-permute-done | bytes 40992 | tf_op jit(solution)/shard_map/ppermute | solution.py:35
  103.2 0.3 collective-permute-done.12
  103.5 1.0 add_convert_fusion.2
  104.5 1.9 %collective-permute-start.15 = (bf16[160,128]{1,0:T(8,128)(2,1)S(1)}, bf16[160,128]{1,0:T(8,128)(2,1)S(1)}, u32[]{:S(2)}, u32[]{:S(2)}) collective-permute-start(bf16[160,128]{1,0:T(8,128)(2,1)S(1)} %get-tuple-element.75), channel_id=1, source_target_pairs={{0,8},{8,0},{16,24},{24,16},{32,40},{40,32},{48,56},{56,48},{64,72... | collective-permute-start | bytes 122888 | tf_op jit(solution)/shard_map/ppermute | solution.py:35
  106.4 0.0 collective-permute-done.16.halo_ref
  106.4 2.4 %window.1.win_ref = f32[512,256]{1,0:T(8,128)S(1)} custom-call(s32[2]{0:T(128)S(1)} %copy-done.4, bf16[512,384]{1,0:T(8,128)(2,1)S(1)} %get-tuple-element.47.qf_ref, bf16[512,512]{1,0:T(8,128)(2,1)S(1)} %get-tuple-element.48.kv_ref, bf16[384,512]{1,0:T(8,128)(2,1)S(1)} %collective-permute-done.16.halo_ref), custom_call_target="tpu_custom_call" | custom-call | tf_op jit(solution)/shard_map/window/pallas_call | solution.py:357
  108.9 0.0 collective-permute-done.15.theirs
  108.9 0.6 hidden.1
  109.5 0.4 product.2
  109.9 1.9 %collective-permute-start.19 = (bf16[64,2048]{1,0:T(8,128)(2,1)S(1)}, bf16[64,2048]{1,0:T(8,128)(2,1)S(1)}, u32[]{:S(2)}, u32[]{:S(2)}) collective-permute-start(bf16[64,2048]{1,0:T(8,128)(2,1)S(1)} %get-tuple-element.67), channel_id=1, source_target_pairs={{0,2},{8,10},{16,18},{24,26},{32,34},{40,42},{48,50},{56,58},{64,6... | collective-permute-start | bytes 786440 | tf_op jit(solution)/shard_map/ppermute | solution.py:35
  111.8 3.9 %collective-permute-start.18 = (bf16[64,2048]{1,0:T(8,128)(2,1)S(1)}, bf16[64,2048]{1,0:T(8,128)(2,1)S(1)}, u32[]{:S(2)}, u32[]{:S(2)}) collective-permute-start(bf16[64,2048]{1,0:T(8,128)(2,1)S(1)} %get-tuple-element.66), channel_id=1, source_target_pairs={{0,6},{8,14},{16,22},{24,30},{32,38},{40,46},{48,54},{56,62},{64,7... | collective-permute-start | bytes 786440 | tf_op jit(solution)/shard_map/ppermute | solution.py:35
  115.8 3.6 %collective-permute-start.17 = (bf16[64,2048]{1,0:T(8,128)(2,1)S(1)}, bf16[64,2048]{1,0:T(8,128)(2,1)S(1)}, u32[]{:S(2)}, u32[]{:S(2)}) collective-permute-start(bf16[64,2048]{1,0:T(8,128)(2,1)S(1)} %get-tuple-element.65), channel_id=1, source_target_pairs={{0,4},{8,12},{16,20},{24,28},{32,36},{40,44},{48,52},{56,60},{64,6... | collective-permute-start | bytes 786440 | tf_op jit(solution)/shard_map/ppermute | solution.py:35
  119.4 1.1 collective-permute-done.19
  120.5 2.2 %collective-permute-done.18 = bf16[64,2048]{1,0:T(8,128)(2,1)S(1)} collective-permute-done((bf16[64,2048]{1,0:T(8,128)(2,1)S(1)}, bf16[64,2048]{1,0:T(8,128)(2,1)S(1)}, u32[]{:S(2)}, u32[]{:S(2)}) %collective-permute-start.18) | collective-permute-done | bytes 262176 | tf_op jit(solution)/shard_map/ppermute | solution.py:35
  122.7 6.8 %collective-permute-done.17 = bf16[64,2048]{1,0:T(8,128)(2,1)S(1)} collective-permute-done((bf16[64,2048]{1,0:T(8,128)(2,1)S(1)}, bf16[64,2048]{1,0:T(8,128)(2,1)S(1)}, u32[]{:S(2)}, u32[]{:S(2)}) %collective-permute-start.17) | collective-permute-done | bytes 262176 | tf_op jit(solution)/shard_map/ppermute | solution.py:35
  129.5 0.1 add_convert_fusion.1
  129.6 9.3 %collective-permute-start.20 = (bf16[64,2048]{1,0:T(8,128)(2,1)S(1)}, bf16[64,2048]{1,0:T(8,128)(2,1)S(1)}, u32[]{:S(2)}, u32[]{:S(2)}) collective-permute-start(bf16[64,2048]{1,0:T(8,128)(2,1)S(1)} %add_convert_fusion.1), channel_id=1, source_target_pairs={{0,1},{8,9},{16,17},{24,25},{32,33},{40,41},{48,49},{56,57},{64,65... | collective-permute-start | bytes 786440 | tf_op jit(solution)/shard_map/ppermute | solution.py:35
  138.9 0.4 product.3
  139.4 1.9 %collective-permute-start.23 = (bf16[64,2048]{1,0:T(8,128)(2,1)S(1)}, bf16[64,2048]{1,0:T(8,128)(2,1)S(1)}, u32[]{:S(2)}, u32[]{:S(2)}) collective-permute-start(bf16[64,2048]{1,0:T(8,128)(2,1)S(1)} %get-tuple-element.74), channel_id=1, source_target_pairs={{0,2},{8,10},{16,18},{24,26},{32,34},{40,42},{48,50},{56,58},{64,6... | collective-permute-start | bytes 786440 | tf_op jit(solution)/shard_map/ppermute | solution.py:35
  141.3 3.9 %collective-permute-start.22 = (bf16[64,2048]{1,0:T(8,128)(2,1)S(1)}, bf16[64,2048]{1,0:T(8,128)(2,1)S(1)}, u32[]{:S(2)}, u32[]{:S(2)}) collective-permute-start(bf16[64,2048]{1,0:T(8,128)(2,1)S(1)} %get-tuple-element.73), channel_id=1, source_target_pairs={{0,6},{8,14},{16,22},{24,30},{32,38},{40,46},{48,54},{56,62},{64,7... | collective-permute-start | bytes 786440 | tf_op jit(solution)/shard_map/ppermute | solution.py:35
  145.2 3.5 %collective-permute-start.21 = (bf16[64,2048]{1,0:T(8,128)(2,1)S(1)}, bf16[64,2048]{1,0:T(8,128)(2,1)S(1)}, u32[]{:S(2)}, u32[]{:S(2)}) collective-permute-start(bf16[64,2048]{1,0:T(8,128)(2,1)S(1)} %get-tuple-element.72), channel_id=1, source_target_pairs={{0,4},{8,12},{16,20},{24,28},{32,36},{40,44},{48,52},{56,60},{64,6... | collective-permute-start | bytes 786440 | tf_op jit(solution)/shard_map/ppermute | solution.py:35
  148.8 15.9 %collective-permute-done.20 = bf16[64,2048]{1,0:T(8,128)(2,1)S(1)} collective-permute-done((bf16[64,2048]{1,0:T(8,128)(2,1)S(1)}, bf16[64,2048]{1,0:T(8,128)(2,1)S(1)}, u32[]{:S(2)}, u32[]{:S(2)}) %collective-permute-start.20) | collective-permute-done | bytes 262176 | tf_op jit(solution)/shard_map/ppermute | solution.py:35
  164.7 0.1 convert_add_fusion
  164.7 0.0 collective-permute-done.23
  164.7 0.0 collective-permute-done.22
  164.7 0.0 collective-permute-done.21
  164.8 0.8 add_convert_fusion
  (14 shorter events, 0.1 us)
Async XLA Ops:
  0.0 37.4 %copy-start.3 = (bf16[512,256]{1,0:T(8,128)(2,1)S(1)}, bf16[512,256]{1,0:T(8,128)(2,1)}, u32[]{:S(2)}) copy-start(bf16[512,256]{1,0:T(8,128)(2,1)} %refs_0_.1) | copy-start | bytes 786436
  0.0 37.4 %copy-start.2 = (bf16[2048,2,32]{0,2,1:T(8,128)(2,1)S(1)}, bf16[2048,2,32]{0,2,1:T(8,128)(2,1)}, u32[]{:S(2)}) copy-start(bf16[2048,2,32]{0,2,1:T(8,128)(2,1)} %param.8) | copy-start | bytes 786436
  0.0 25.8 %collective-permute-start = (bf16[512,256]{1,0:T(8,128)(2,1)}, bf16[512,256]{1,0:T(8,128)(2,1)S(1)}, u32[]{:S(2)}, u32[]{:S(2)}) collective-permute-start(bf16[512,256]{1,0:T(8,128)(2,1)} %refs_0_.1), channel_id=1, source_target_pairs={{0,1},{8,9},{16,17},{24,25},{32,33},{40,41},{48,49},{56,57},{64,65... | collective-permute-start | bytes 786440 | tf_op jit(solution)/shard_map/ppermute | solution.py:35
  15.9 15.8 %collective-permute-start.4 = (bf16[512,256]{1,0:T(8,128)(2,1)}, bf16[512,256]{1,0:T(8,128)(2,1)S(1)}, u32[]{:S(2)}, u32[]{:S(2)}) collective-permute-start(bf16[512,256]{1,0:T(8,128)(2,1)} %refs_0_.1), channel_id=1, source_target_pairs={{0,2},{8,10},{16,18},{24,26},{32,34},{40,42},{48,50},{56,58},{64,6... | collective-permute-start | bytes 786440 | tf_op jit(solution)/shard_map/ppermute | solution.py:35
  19.3 18.1 %collective-permute-start.5 = (bf16[512,256]{1,0:T(8,128)(2,1)}, bf16[512,256]{1,0:T(8,128)(2,1)S(1)}, u32[]{:S(2)}, u32[]{:S(2)}) collective-permute-start(bf16[512,256]{1,0:T(8,128)(2,1)} %refs_0_.1), channel_id=1, source_target_pairs={{0,6},{8,14},{16,22},{24,30},{32,38},{40,46},{48,54},{56,62},{64,7... | collective-permute-start | bytes 786440 | tf_op jit(solution)/shard_map/ppermute | solution.py:35
  21.7 15.6 %collective-permute-start.6 = (bf16[512,256]{1,0:T(8,128)(2,1)}, bf16[512,256]{1,0:T(8,128)(2,1)S(1)}, u32[]{:S(2)}, u32[]{:S(2)}) collective-permute-start(bf16[512,256]{1,0:T(8,128)(2,1)} %refs_0_.1), channel_id=1, source_target_pairs={{0,4},{8,12},{16,20},{24,28},{32,36},{40,44},{48,52},{56,60},{64,6... | collective-permute-start | bytes 786440 | tf_op jit(solution)/shard_map/ppermute | solution.py:35
  25.8 14.5 %collective-permute-start.1 = (bf16[512,256]{1,0:T(8,128)(2,1)S(1)}, bf16[512,256]{1,0:T(8,128)(2,1)S(1)}, u32[]{:S(2)}, u32[]{:S(2)}) collective-permute-start(bf16[512,256]{1,0:T(8,128)(2,1)S(1)} %collective-permute-done.refs_0_), channel_id=1, source_target_pairs={{0,2},{8,10},{16,18},{24,26},{32,34},{40,42},{48,50},{56,58},{64,6... | collective-permute-start | bytes 786440 | tf_op jit(solution)/shard_map/ppermute | solution.py:35
  28.8 13.7 %collective-permute-start.2 = (bf16[512,256]{1,0:T(8,128)(2,1)S(1)}, bf16[512,256]{1,0:T(8,128)(2,1)S(1)}, u32[]{:S(2)}, u32[]{:S(2)}) collective-permute-start(bf16[512,256]{1,0:T(8,128)(2,1)S(1)} %collective-permute-done.refs_0_), channel_id=1, source_target_pairs={{0,6},{8,14},{16,22},{24,30},{32,38},{40,46},{48,54},{56,62},{64,7... | collective-permute-start | bytes 786440 | tf_op jit(solution)/shard_map/ppermute | solution.py:35
  31.6 14.7 %collective-permute-start.3 = (bf16[512,256]{1,0:T(8,128)(2,1)S(1)}, bf16[512,256]{1,0:T(8,128)(2,1)S(1)}, u32[]{:S(2)}, u32[]{:S(2)}) collective-permute-start(bf16[512,256]{1,0:T(8,128)(2,1)S(1)} %collective-permute-done.refs_0_), channel_id=1, source_target_pairs={{0,4},{8,12},{16,20},{24,28},{32,36},{40,44},{48,52},{56,60},{64,6... | collective-permute-start | bytes 786440 | tf_op jit(solution)/shard_map/ppermute | solution.py:35
  37.3 9.0 %copy-start.1 = (bf16[2,4,160,128]{3,2,1,0:T(8,128)(2,1)S(1)}, bf16[2,4,160,128]{3,2,1,0:T(8,128)(2,1)}, u32[]{:S(2)}) copy-start(bf16[2,4,160,128]{3,2,1,0:T(8,128)(2,1)} %constant.52.clone.refs_6_.table) | copy-start | bytes 983044
  49.6 0.8 copy-start.5
  50.4 56.1 %copy-start.4 = (s32[2]{0:T(128)S(1)}, s32[2]{0:T(128)}, u32[]{:S(2)}) copy-start(s32[2]{0:T(128)} %win.1) | copy-start | bytes 28
  50.4 18.7 %collective-permute-start.9 = (bf16[160,128]{1,0:T(8,128)(2,1)S(1)}, bf16[160,128]{1,0:T(8,128)(2,1)S(1)}, u32[]{:S(2)}, u32[]{:S(2)}) collective-permute-start(bf16[160,128]{1,0:T(8,128)(2,1)S(1)} %get-tuple-element.44), channel_id=1, source_target_pairs={{0,16},{8,24},{16,0},{24,8},{32,48},{40,56},{48,32},{56,40},{64,80... | collective-permute-start | bytes 122888 | tf_op jit(solution)/shard_map/ppermute | solution.py:35
  65.1 5.3 %collective-permute-start.8 = (bf16[160,128]{1,0:T(8,128)(2,1)S(1)}, bf16[160,128]{1,0:T(8,128)(2,1)S(1)}, u32[]{:S(2)}, u32[]{:S(2)}) collective-permute-start(bf16[160,128]{1,0:T(8,128)(2,1)S(1)} %get-tuple-element.43), channel_id=1, source_target_pairs={{0,24},{8,16},{16,8},{24,0},{32,56},{40,48},{48,40},{56,32},{64,88... | collective-permute-start | bytes 122888 | tf_op jit(solution)/shard_map/ppermute | solution.py:35
  67.0 3.4 %collective-permute-start.7 = (bf16[160,128]{1,0:T(8,128)(2,1)S(1)}, bf16[160,128]{1,0:T(8,128)(2,1)S(1)}, u32[]{:S(2)}, u32[]{:S(2)}) collective-permute-start(bf16[160,128]{1,0:T(8,128)(2,1)S(1)} %get-tuple-element.43), channel_id=1, source_target_pairs={{0,8},{8,0},{16,24},{24,16},{32,40},{40,32},{48,56},{56,48},{64,72... | collective-permute-start | bytes 122888 | tf_op jit(solution)/shard_map/ppermute | solution.py:35
  71.1 38.4 %copy-start = (bf16[2,128,2048]{2,1,0:T(8,128)(2,1)S(1)}, bf16[2,128,2048]{2,1,0:T(8,128)(2,1)}, u32[]{:S(2)}) copy-start(bf16[2,128,2048]{2,1,0:T(8,128)(2,1)} %param.10) | copy-start | bytes 3145732
  71.1 7.5 %collective-permute-start.10 = (bf16[160,128]{1,0:T(8,128)(2,1)S(1)}, bf16[160,128]{1,0:T(8,128)(2,1)}, u32[]{:S(2)}, u32[]{:S(2)}) collective-permute-start(bf16[160,128]{1,0:T(8,128)(2,1)S(1)} %convert_element_type.72), channel_id=1, source_target_pairs={{0,32},{8,40},{16,48},{24,56},{32,0},{40,8},{48,16},{56,24},{64,96... | collective-permute-start | bytes 122888 | tf_op jit(solution)/shard_map/ppermute | solution.py:35
  79.4 11.3 %collective-permute-start.11 = (bf16[160,128]{1,0:T(8,128)(2,1)S(1)}, bf16[160,128]{1,0:T(8,128)(2,1)S(1)}, u32[]{:S(2)}, u32[]{:S(2)}) collective-permute-start(bf16[160,128]{1,0:T(8,128)(2,1)S(1)} %convert_element_type.74), channel_id=1, source_target_pairs={{0,64},{8,72},{16,80},{24,88},{32,96},{40,104},{48,112},{56,120},{... | collective-permute-start | bytes 122888 | tf_op jit(solution)/shard_map/ppermute | solution.py:35
  85.8 20.6 %collective-permute-start.16 = (bf16[384,512]{1,0:T(8,128)(2,1)}, bf16[384,512]{1,0:T(8,128)(2,1)S(1)}, u32[]{:S(2)}, u32[]{:S(2)}) collective-permute-start(bf16[384,512]{1,0:T(8,128)(2,1)} %copy-done.5), channel_id=1, source_target_pairs={{0,8},{8,16},{16,24},{24,32},{32,40},{40,48},{48,56},{56,64},{64,7... | collective-permute-start | bytes 1179656 | tf_op jit(solution)/shard_map/ppermute | solution.py:35
  90.7 5.8 %collective-permute-start.14 = (bf16[160,128]{1,0:T(8,128)(2,1)S(1)}, bf16[160,128]{1,0:T(8,128)(2,1)S(1)}, u32[]{:S(2)}, u32[]{:S(2)}) collective-permute-start(bf16[160,128]{1,0:T(8,128)(2,1)S(1)} %convert_add_fusion.1), channel_id=1, source_target_pairs={{0,384},{8,392},{16,400},{24,408},{32,416},{40,424},{48,432},{56,4... | collective-permute-start | bytes 122888 | tf_op jit(solution)/shard_map/ppermute | solution.py:35
  91.3 11.9 %collective-permute-start.13 = (bf16[160,128]{1,0:T(8,128)(2,1)S(1)}, bf16[160,128]{1,0:T(8,128)(2,1)S(1)}, u32[]{:S(2)}, u32[]{:S(2)}) collective-permute-start(bf16[160,128]{1,0:T(8,128)(2,1)S(1)} %convert_add_fusion.1), channel_id=1, source_target_pairs={{0,256},{8,264},{16,272},{24,280},{32,288},{40,296},{48,304},{56,3... | collective-permute-start | bytes 122888 | tf_op jit(solution)/shard_map/ppermute | solution.py:35
  92.6 10.9 %collective-permute-start.12 = (bf16[160,128]{1,0:T(8,128)(2,1)S(1)}, bf16[160,128]{1,0:T(8,128)(2,1)S(1)}, u32[]{:S(2)}, u32[]{:S(2)}) collective-permute-start(bf16[160,128]{1,0:T(8,128)(2,1)S(1)} %convert_add_fusion.1), channel_id=1, source_target_pairs={{0,128},{8,136},{16,144},{24,152},{32,160},{40,168},{48,176},{56,1... | collective-permute-start | bytes 122888 | tf_op jit(solution)/shard_map/ppermute | solution.py:35
  104.5 4.4 %collective-permute-start.15 = (bf16[160,128]{1,0:T(8,128)(2,1)S(1)}, bf16[160,128]{1,0:T(8,128)(2,1)S(1)}, u32[]{:S(2)}, u32[]{:S(2)}) collective-permute-start(bf16[160,128]{1,0:T(8,128)(2,1)S(1)} %get-tuple-element.75), channel_id=1, source_target_pairs={{0,8},{8,0},{16,24},{24,16},{32,40},{40,32},{48,56},{56,48},{64,72... | collective-permute-start | bytes 122888 | tf_op jit(solution)/shard_map/ppermute | solution.py:35
  109.9 10.6 %collective-permute-start.19 = (bf16[64,2048]{1,0:T(8,128)(2,1)S(1)}, bf16[64,2048]{1,0:T(8,128)(2,1)S(1)}, u32[]{:S(2)}, u32[]{:S(2)}) collective-permute-start(bf16[64,2048]{1,0:T(8,128)(2,1)S(1)} %get-tuple-element.67), channel_id=1, source_target_pairs={{0,2},{8,10},{16,18},{24,26},{32,34},{40,42},{48,50},{56,58},{64,6... | collective-permute-start | bytes 786440 | tf_op jit(solution)/shard_map/ppermute | solution.py:35
  111.8 10.8 %collective-permute-start.18 = (bf16[64,2048]{1,0:T(8,128)(2,1)S(1)}, bf16[64,2048]{1,0:T(8,128)(2,1)S(1)}, u32[]{:S(2)}, u32[]{:S(2)}) collective-permute-start(bf16[64,2048]{1,0:T(8,128)(2,1)S(1)} %get-tuple-element.66), channel_id=1, source_target_pairs={{0,6},{8,14},{16,22},{24,30},{32,38},{40,46},{48,54},{56,62},{64,7... | collective-permute-start | bytes 786440 | tf_op jit(solution)/shard_map/ppermute | solution.py:35
  115.8 13.7 %collective-permute-start.17 = (bf16[64,2048]{1,0:T(8,128)(2,1)S(1)}, bf16[64,2048]{1,0:T(8,128)(2,1)S(1)}, u32[]{:S(2)}, u32[]{:S(2)}) collective-permute-start(bf16[64,2048]{1,0:T(8,128)(2,1)S(1)} %get-tuple-element.65), channel_id=1, source_target_pairs={{0,4},{8,12},{16,20},{24,28},{32,36},{40,44},{48,52},{56,60},{64,6... | collective-permute-start | bytes 786440 | tf_op jit(solution)/shard_map/ppermute | solution.py:35
  129.6 35.1 %collective-permute-start.20 = (bf16[64,2048]{1,0:T(8,128)(2,1)S(1)}, bf16[64,2048]{1,0:T(8,128)(2,1)S(1)}, u32[]{:S(2)}, u32[]{:S(2)}) collective-permute-start(bf16[64,2048]{1,0:T(8,128)(2,1)S(1)} %add_convert_fusion.1), channel_id=1, source_target_pairs={{0,1},{8,9},{16,17},{24,25},{32,33},{40,41},{48,49},{56,57},{64,65... | collective-permute-start | bytes 786440 | tf_op jit(solution)/shard_map/ppermute | solution.py:35
  139.4 25.4 %collective-permute-start.23 = (bf16[64,2048]{1,0:T(8,128)(2,1)S(1)}, bf16[64,2048]{1,0:T(8,128)(2,1)S(1)}, u32[]{:S(2)}, u32[]{:S(2)}) collective-permute-start(bf16[64,2048]{1,0:T(8,128)(2,1)S(1)} %get-tuple-element.74), channel_id=1, source_target_pairs={{0,2},{8,10},{16,18},{24,26},{32,34},{40,42},{48,50},{56,58},{64,6... | collective-permute-start | bytes 786440 | tf_op jit(solution)/shard_map/ppermute | solution.py:35
  141.3 23.4 %collective-permute-start.22 = (bf16[64,2048]{1,0:T(8,128)(2,1)S(1)}, bf16[64,2048]{1,0:T(8,128)(2,1)S(1)}, u32[]{:S(2)}, u32[]{:S(2)}) collective-permute-start(bf16[64,2048]{1,0:T(8,128)(2,1)S(1)} %get-tuple-element.73), channel_id=1, source_target_pairs={{0,6},{8,14},{16,22},{24,30},{32,38},{40,46},{48,54},{56,62},{64,7... | collective-permute-start | bytes 786440 | tf_op jit(solution)/shard_map/ppermute | solution.py:35
  145.2 19.5 %collective-permute-start.21 = (bf16[64,2048]{1,0:T(8,128)(2,1)S(1)}, bf16[64,2048]{1,0:T(8,128)(2,1)S(1)}, u32[]{:S(2)}, u32[]{:S(2)}) collective-permute-start(bf16[64,2048]{1,0:T(8,128)(2,1)S(1)} %get-tuple-element.72), channel_id=1, source_target_pairs={{0,4},{8,12},{16,20},{24,28},{32,36},{40,44},{48,52},{56,60},{64,6... | collective-permute-start | bytes 786440 | tf_op jit(solution)/shard_map/ppermute | solution.py:35

commit v11 on v10

--- a/solution.py
+++ b/solution.py
@@ -268,7 +268,7 @@
         out[...] = product[s * rows : (s + 1) * rows]
 
 
-def prefix(mine, short, other, place, attend, hand_on):
+def prefix(mine, short, other, place, beside, attend):
     x, h, y, z, c = place
     across = send(other, lambda x, h, y, z, c: (x, h, y, z ^ 1, 1 - c)).astype(f32)
     beyond = send(short, to_z(1)).astype(f32)
@@ -277,21 +277,25 @@
     add = (jnp.where(c == 0, mine, 0.0), jnp.where(c == 1, got, 0.0))
     before = jnp.where(z % 2 == 1, across + beyond, 0.0)
     total, before, add = lax.optimization_barrier((total, before, add))
+    done = None
     for flip in (2, 4):
         part = send(total.astype(bf16), to_z(flip))
-        if flip == 2:
-            part, *behind = lax.optimization_barrier((part, *attend(total)))
-        else:
-            halo = hand_on(total)
+        if flip == 4:
+            *behind, halo = done
+            part, *behind = lax.optimization_barrier((part, *behind))
         part = part.astype(f32)
         before = before + jnp.where((z ^ flip) < z, part, 0.0)
         total, before = lax.optimization_barrier((total + part, before))
+        if flip == 2:
+            done = beside(total)
     short = total.astype(bf16)
-    for steps in (1, 2, 3):
-        before = before + send(short, to_y(steps)).astype(f32)
+    earlier = [send(short, to_y(steps)) for steps in (1, 2, 3)]
+    *earlier, attended = lax.optimization_barrier((*earlier, attend(halo)))
+    for part in earlier:
+        before = before + part.astype(f32)
     theirs = send((before + add[0]).astype(bf16), to_core)
     ours = before + add[1]
-    return ours, theirs, behind, halo
+    return ours, theirs, behind, attended
 
 
 def shape(dims, kind):
@@ -407,18 +411,18 @@
     own = own_products(parts[:NX], wf, ww)
     qf, kv, tail, mine, short, theirs = project(parts[NX:], wf, ww, tables, own)
 
-    def attend(total):
-        return near(lax.optimization_barrier((qf, total))[0], kv, tables)
-
-    def hand_on(total):
-        return send(lax.optimization_barrier((tail, total))[0], to_next)
-
-    ours, theirs, (near_out, query_map), halo = prefix(mine, short, theirs, (x, h, y, z, c), attend, hand_on)
-    win_out = window(win_blocks, qf, kv, halo)
+    def beside(total):
+        early, kept, _ = lax.optimization_barrier((qf, tail, total))
+        return *near(early, kv, tables), send(kept, to_next)
+
+    def attend(halo):
+        return window(win_blocks, qf, kv, halo)
+
+    ours, theirs, (near_out, query_map), win_out = prefix(mine, short, theirs, (x, h, y, z, c), beside, attend)
     keep, away = hidden_rows(ours, theirs, near_out, win_out, query_map)
 
     def summed(total, group):
-        for steps in (2, 3, 1):
+        for steps in (1, 3, 2):
             total = total + send(group[steps], to_x(steps)).astype(f32)
         return total.astype(bf16)
 

time: 166 us -> 162 us (0.976)
  the two profiles are of different devices: /device:TPU:18 before, /device:TPU:16 now
where the time goes in v11:
time: 162 us; the launch traced here: 161 us
  starting transfers between devices  101 us (62%)
  waiting for transfers between devices  45.9 us (28%)
  Pallas kernels  10.4 us (6%)
  local copies, waits for them, and re-layouts  2.32 us (1%)
    ppermute x24, starting transfers between devices, send(): return lax.ppermute(value, ('seq', 'tp'), pairs(move))  101 us
    ppermute x24, waiting for transfers between devices, send(): return lax.ppermute(value, ('seq', 'tp'), pairs(move))  45.9 us
  transfers between devices with their start and end apart: 24, of which 12 were waited for; matrix products, arithmetic and copies ran while one was open for 1% of the time, Pallas kernels for 4%

profile of v11, /device:TPU:16, one launch (start us, length us, event | category | flops | bytes accessed | tf_op | source)
XLA Modules:
  0.0 161.2 jit_solution(6262215567908363343)
XLA Ops:
  0.0 15.8 %collective-permute-start = (bf16[512,256]{1,0:T(8,128)(2,1)}, bf16[512,256]{1,0:T(8,128)(2,1)S(1)}, u32[]{:S(2)}, u32[]{:S(2)}) collective-permute-start(bf16[512,256]{1,0:T(8,128)(2,1)} %refs_0_.1), channel_id=1, source_target_pairs={{0,1},{8,9},{16,17},{24,25},{32,33},{40,41},{48,49},{56,57},{64,65... | collective-permute-start | bytes 786440 | tf_op jit(solution)/shard_map/ppermute | solution.py:35
  15.9 3.4 %collective-permute-start.4 = (bf16[512,256]{1,0:T(8,128)(2,1)}, bf16[512,256]{1,0:T(8,128)(2,1)S(1)}, u32[]{:S(2)}, u32[]{:S(2)}) collective-permute-start(bf16[512,256]{1,0:T(8,128)(2,1)} %refs_0_.1), channel_id=1, source_target_pairs={{0,2},{8,10},{16,18},{24,26},{32,34},{40,42},{48,50},{56,58},{64,6... | collective-permute-start | bytes 786440 | tf_op jit(solution)/shard_map/ppermute | solution.py:35
  19.3 3.7 %collective-permute-start.5 = (bf16[512,256]{1,0:T(8,128)(2,1)}, bf16[512,256]{1,0:T(8,128)(2,1)S(1)}, u32[]{:S(2)}, u32[]{:S(2)}) collective-permute-start(bf16[512,256]{1,0:T(8,128)(2,1)} %refs_0_.1), channel_id=1, source_target_pairs={{0,6},{8,14},{16,22},{24,30},{32,38},{40,46},{48,54},{56,62},{64,7... | collective-permute-start | bytes 786440 | tf_op jit(solution)/shard_map/ppermute | solution.py:35
  22.9 3.7 %collective-permute-start.6 = (bf16[512,256]{1,0:T(8,128)(2,1)}, bf16[512,256]{1,0:T(8,128)(2,1)S(1)}, u32[]{:S(2)}, u32[]{:S(2)}) collective-permute-start(bf16[512,256]{1,0:T(8,128)(2,1)} %refs_0_.1), channel_id=1, source_target_pairs={{0,4},{8,12},{16,20},{24,28},{32,36},{40,44},{48,52},{56,60},{64,6... | collective-permute-start | bytes 786440 | tf_op jit(solution)/shard_map/ppermute | solution.py:35
  26.7 0.0 collective-permute-done.refs_0_
  26.7 2.5 %collective-permute-start.1 = (bf16[512,256]{1,0:T(8,128)(2,1)S(1)}, bf16[512,256]{1,0:T(8,128)(2,1)S(1)}, u32[]{:S(2)}, u32[]{:S(2)}) collective-permute-start(bf16[512,256]{1,0:T(8,128)(2,1)S(1)} %collective-permute-done.refs_0_), channel_id=1, source_target_pairs={{0,2},{8,10},{16,18},{24,26},{32,34},{40,42},{48,50},{56,58},{64,6... | collective-permute-start | bytes 786440 | tf_op jit(solution)/shard_map/ppermute | solution.py:35
  29.2 4.6 %collective-permute-start.2 = (bf16[512,256]{1,0:T(8,128)(2,1)S(1)}, bf16[512,256]{1,0:T(8,128)(2,1)S(1)}, u32[]{:S(2)}, u32[]{:S(2)}) collective-permute-start(bf16[512,256]{1,0:T(8,128)(2,1)S(1)} %collective-permute-done.refs_0_), channel_id=1, source_target_pairs={{0,6},{8,14},{16,22},{24,30},{32,38},{40,46},{48,54},{56,62},{64,7... | collective-permute-start | bytes 786440 | tf_op jit(solution)/shard_map/ppermute | solution.py:35
  33.7 0.0 collective-permute-done.4.refs_1_
  33.7 2.4 %collective-permute-start.3 = (bf16[512,256]{1,0:T(8,128)(2,1)S(1)}, bf16[512,256]{1,0:T(8,128)(2,1)S(1)}, u32[]{:S(2)}, u32[]{:S(2)}) collective-permute-start(bf16[512,256]{1,0:T(8,128)(2,1)S(1)} %collective-permute-done.refs_0_), channel_id=1, source_target_pairs={{0,4},{8,12},{16,20},{24,28},{32,36},{40,44},{48,52},{56,60},{64,6... | collective-permute-start | bytes 786440 | tf_op jit(solution)/shard_map/ppermute | solution.py:35
  36.2 2.3 %copy.10 = bf16[2048,2,384]{2,0,1:T(8,128)(2,1)S(1)} copy(bf16[2048,2,384]{2,1,0:T(2,128)(2,1)} %param.9) | data formatting | bytes 6291456 | tf_op args[2]
  38.5 0.0 copy-start.1
  38.5 0.0 collective-permute-done.5.refs_2_
  38.5 0.0 collective-permute-done.6.refs_3_
  38.5 0.0 copy-done.3
  38.5 1.3 own.1
  39.8 1.0 collective-permute-done.1.refs_1_
  40.8 1.1 collective-permute-done.2.refs_2_
  41.9 3.1 %collective-permute-done.3.refs_3_ = bf16[512,256]{1,0:T(8,128)(2,1)S(1)} collective-permute-done((bf16[512,256]{1,0:T(8,128)(2,1)S(1)}, bf16[512,256]{1,0:T(8,128)(2,1)S(1)}, u32[]{:S(2)}, u32[]{:S(2)}) %collective-permute-start.3) | collective-permute-done | bytes 262176 | tf_op jit(solution)/shard_map/ppermute | solution.py:35
  45.0 0.0 copy-done.1
  45.0 3.2 %project.1 = (bf16[512,384]{1,0:T(8,128)(2,1)S(1)}, bf16[512,512]{1,0:T(8,128)(2,1)S(1)}, bf16[384,512]{1,0:T(8,128)(2,1)S(1)}, f32[160,128]{1,0:T(8,128)S(1)}, ...) custom-call(bf16[512,256]{1,0:T(8,128)(2,1)S(1)} %collective-permute-done.refs_0_, ...), custom_call_target="tpu_custom_call" | custom-call | tf_op jit(solution)/shard_map/project/pallas_call | solution.py:322
  48.2 14.6 %collective-permute-start.9 = (bf16[160,128]{1,0:T(8,128)(2,1)S(1)}, bf16[160,128]{1,0:T(8,128)(2,1)S(1)}, u32[]{:S(2)}, u32[]{:S(2)}) collective-permute-start(bf16[160,128]{1,0:T(8,128)(2,1)S(1)} %get-tuple-element.48), channel_id=1, source_target_pairs={{0,16},{8,24},{16,0},{24,8},{32,48},{40,56},{48,32},{56,40},{64,80... | collective-permute-start | bytes 122888 | tf_op jit(solution)/shard_map/ppermute | solution.py:35
  62.8 1.9 %collective-permute-start.8 = (bf16[160,128]{1,0:T(8,128)(2,1)S(1)}, bf16[160,128]{1,0:T(8,128)(2,1)S(1)}, u32[]{:S(2)}, u32[]{:S(2)}) collective-permute-start(bf16[160,128]{1,0:T(8,128)(2,1)S(1)} %get-tuple-element.47), channel_id=1, source_target_pairs={{0,24},{8,16},{16,8},{24,0},{32,56},{40,48},{48,40},{56,32},{64,88... | collective-permute-start | bytes 122888 | tf_op jit(solution)/shard_map/ppermute | solution.py:35
  64.8 2.0 %collective-permute-start.7 = (bf16[160,128]{1,0:T(8,128)(2,1)S(1)}, bf16[160,128]{1,0:T(8,128)(2,1)S(1)}, u32[]{:S(2)}, u32[]{:S(2)}) collective-permute-start(bf16[160,128]{1,0:T(8,128)(2,1)S(1)} %get-tuple-element.47), channel_id=1, source_target_pairs={{0,8},{8,0},{16,24},{24,16},{32,40},{40,32},{48,56},{56,48},{64,72... | collective-permute-start | bytes 122888 | tf_op jit(solution)/shard_map/ppermute | solution.py:35
  66.9 0.0 collective-permute-done.9
  66.9 1.3 collective-permute-done.8
  68.2 0.0 collective-permute-done.7
  68.2 0.0 copy-start
  68.2 2.1 %collective-permute-start.10 = (bf16[160,128]{1,0:T(8,128)(2,1)S(1)}, bf16[160,128]{1,0:T(8,128)(2,1)S(1)}, u32[]{:S(2)}, u32[]{:S(2)}) collective-permute-start(bf16[160,128]{1,0:T(8,128)(2,1)S(1)} %convert_element_type.72), channel_id=1, source_target_pairs={{0,32},{8,40},{16,48},{24,56},{32,0},{40,8},{48,16},{56,24},{64,96... | collective-permute-start | bytes 122888 | tf_op jit(solution)/shard_map/ppermute | solution.py:35
  70.3 5.3 %collective-permute-done.10 = bf16[160,128]{1,0:T(8,128)(2,1)S(1)} collective-permute-done((bf16[160,128]{1,0:T(8,128)(2,1)S(1)}, bf16[160,128]{1,0:T(8,128)(2,1)S(1)}, u32[]{:S(2)}, u32[]{:S(2)}) %collective-permute-start.10) | collective-permute-done | bytes 40992 | tf_op jit(solution)/shard_map/ppermute | solution.py:35
  75.6 6.5 %collective-permute-start.11 = (bf16[160,128]{1,0:T(8,128)(2,1)S(1)}, bf16[160,128]{1,0:T(8,128)(2,1)S(1)}, u32[]{:S(2)}, u32[]{:S(2)}) collective-permute-start(bf16[160,128]{1,0:T(8,128)(2,1)S(1)} %convert_element_type.74), channel_id=1, source_target_pairs={{0,64},{8,72},{16,80},{24,88},{32,96},{40,104},{48,112},{56,120},{... | collective-permute-start | bytes 122888 | tf_op jit(solution)/shard_map/ppermute | solution.py:35
  82.1 1.9 %collective-permute-start.15 = (bf16[384,512]{1,0:T(8,128)(2,1)S(1)}, bf16[384,512]{1,0:T(8,128)(2,1)S(1)}, u32[]{:S(2)}, u32[]{:S(2)}) collective-permute-start(bf16[384,512]{1,0:T(8,128)(2,1)S(1)} %get-tuple-element.62), channel_id=1, source_target_pairs={{0,8},{8,16},{16,24},{24,32},{32,40},{40,48},{48,56},{56,64},{64,7... | collective-permute-start | bytes 1179656 | tf_op jit(solution)/shard_map/ppermute | solution.py:35
  84.0 2.1 %near.1 = (f32[512,256]{1,0:T(8,128)S(1)}, bf16[2,512,160]{2,1,0:T(8,128)(2,1)S(1)}) custom-call(bf16[512,384]{1,0:T(8,128)(2,1)S(1)} %get-tuple-element.54.qf_ref, bf16[512,512]{1,0:T(8,128)(2,1)S(1)} %get-tuple-element.55.kv_ref, bf16[2,4,160,128]{3,2,1,0:T(8,128)(2,1)S(1)} %copy-done.1), custom_call_target="tpu_custom_call" | custom-call | tf_op jit(solution)/shard_map/near/pallas_call | solution.py:346
  86.1 0.8 collective-permute-done.11
  86.9 3.2 %collective-permute-start.12 = (bf16[160,128]{1,0:T(8,128)(2,1)S(1)}, bf16[160,128]{1,0:T(8,128)(2,1)S(1)}, u32[]{:S(2)}, u32[]{:S(2)}) collective-permute-start(bf16[160,128]{1,0:T(8,128)(2,1)S(1)} %convert_add_fusion.1), channel_id=1, source_target_pairs={{0,128},{8,136},{16,144},{24,152},{32,160},{40,168},{48,176},{56,1... | collective-permute-start | bytes 122888 | tf_op jit(solution)/shard_map/ppermute | solution.py:35
  90.1 1.3 collective-permute-start.13
  91.4 0.7 collective-permute-start.14
  92.1 6.7 %collective-permute-done.15.halo_ref = bf16[384,512]{1,0:T(8,128)(2,1)S(1)} collective-permute-done((bf16[384,512]{1,0:T(8,128)(2,1)S(1)}, bf16[384,512]{1,0:T(8,128)(2,1)S(1)}, u32[]{:S(2)}, u32[]{:S(2)}) %collective-permute-start.15) | collective-permute-done | bytes 393248 | tf_op jit(solution)/shard_map/ppermute | solution.py:35
  98.8 0.0 copy-done.4
  98.8 2.4 %window.1.win_ref = f32[512,256]{1,0:T(8,128)S(1)} custom-call(s32[2]{0:T(128)S(1)} %copy-done.4, bf16[512,384]{1,0:T(8,128)(2,1)S(1)} %get-tuple-element.54.qf_ref, bf16[512,512]{1,0:T(8,128)(2,1)S(1)} %get-tuple-element.55.kv_ref, bf16[384,512]{1,0:T(8,128)(2,1)S(1)} %collective-permute-done.15.halo_ref), custom_call_target="tpu_custom_call" | custom-call | tf_op jit(solution)/shard_map/window/pallas_call | solution.py:361
  101.3 0.0 collective-permute-done.12
  101.3 0.0 collective-permute-done.13
  101.3 0.0 collective-permute-done.14
  101.3 1.9 %collective-permute-start.16 = (bf16[160,128]{1,0:T(8,128)(2,1)S(1)}, bf16[160,128]{1,0:T(8,128)(2,1)S(1)}, u32[]{:S(2)}, u32[]{:S(2)}) collective-permute-start(bf16[160,128]{1,0:T(8,128)(2,1)S(1)} %get-tuple-element.83), channel_id=1, source_target_pairs={{0,8},{8,0},{16,24},{24,16},{32,40},{40,32},{48,56},{56,48},{64,72... | collective-permute-start | bytes 122888 | tf_op jit(solution)/shard_map/ppermute | solution.py:35
  103.3 1.2 collective-permute-done.16.theirs
  104.4 0.5 hidden.1
  105.0 0.4 product.2
  105.4 3.7 %collective-permute-start.19 = (bf16[64,2048]{1,0:T(8,128)(2,1)S(1)}, bf16[64,2048]{1,0:T(8,128)(2,1)S(1)}, u32[]{:S(2)}, u32[]{:S(2)}) collective-permute-start(bf16[64,2048]{1,0:T(8,128)(2,1)S(1)} %get-tuple-element.75), channel_id=1, source_target_pairs={{0,4},{8,12},{16,20},{24,28},{32,36},{40,44},{48,52},{56,60},{64,6... | collective-permute-start | bytes 786440 | tf_op jit(solution)/shard_map/ppermute | solution.py:35
  109.2 5.6 %collective-permute-start.18 = (bf16[64,2048]{1,0:T(8,128)(2,1)S(1)}, bf16[64,2048]{1,0:T(8,128)(2,1)S(1)}, u32[]{:S(2)}, u32[]{:S(2)}) collective-permute-start(bf16[64,2048]{1,0:T(8,128)(2,1)S(1)} %get-tuple-element.74), channel_id=1, source_target_pairs={{0,6},{8,14},{16,22},{24,30},{32,38},{40,46},{48,54},{56,62},{64,7... | collective-permute-start | bytes 786440 | tf_op jit(solution)/shard_map/ppermute | solution.py:35
  114.8 1.9 %collective-permute-start.17 = (bf16[64,2048]{1,0:T(8,128)(2,1)S(1)}, bf16[64,2048]{1,0:T(8,128)(2,1)S(1)}, u32[]{:S(2)}, u32[]{:S(2)}) collective-permute-start(bf16[64,2048]{1,0:T(8,128)(2,1)S(1)} %get-tuple-element.73), channel_id=1, source_target_pairs={{0,2},{8,10},{16,18},{24,26},{32,34},{40,42},{48,50},{56,58},{64,6... | collective-permute-start | bytes 786440 | tf_op jit(solution)/shard_map/ppermute | solution.py:35
  116.7 0.5 collective-permute-done.19
  117.2 6.7 %collective-permute-done.18 = bf16[64,2048]{1,0:T(8,128)(2,1)S(1)} collective-permute-done((bf16[64,2048]{1,0:T(8,128)(2,1)S(1)}, bf16[64,2048]{1,0:T(8,128)(2,1)S(1)}, u32[]{:S(2)}, u32[]{:S(2)}) %collective-permute-start.18) | collective-permute-done | bytes 262176 | tf_op jit(solution)/shard_map/ppermute | solution.py:35
  123.9 1.8 %collective-permute-done.17 = bf16[64,2048]{1,0:T(8,128)(2,1)S(1)} collective-permute-done((bf16[64,2048]{1,0:T(8,128)(2,1)S(1)}, bf16[64,2048]{1,0:T(8,128)(2,1)S(1)}, u32[]{:S(2)}, u32[]{:S(2)}) %collective-permute-start.17) | collective-permute-done | bytes 262176 | tf_op jit(solution)/shard_map/ppermute | solution.py:35
  125.7 0.1 add_convert_fusion.1
  125.8 9.1 %collective-permute-start.20 = (bf16[64,2048]{1,0:T(8,128)(2,1)S(1)}, bf16[64,2048]{1,0:T(8,128)(2,1)S(1)}, u32[]{:S(2)}, u32[]{:S(2)}) collective-permute-start(bf16[64,2048]{1,0:T(8,128)(2,1)S(1)} %add_convert_fusion.1), channel_id=1, source_target_pairs={{0,1},{8,9},{16,17},{24,25},{32,33},{40,41},{48,49},{56,57},{64,65... | collective-permute-start | bytes 786440 | tf_op jit(solution)/shard_map/ppermute | solution.py:35
  135.0 0.4 product.3
  135.4 2.5 %collective-permute-start.23 = (bf16[64,2048]{1,0:T(8,128)(2,1)S(1)}, bf16[64,2048]{1,0:T(8,128)(2,1)S(1)}, u32[]{:S(2)}, u32[]{:S(2)}) collective-permute-start(bf16[64,2048]{1,0:T(8,128)(2,1)S(1)} %get-tuple-element.82), channel_id=1, source_target_pairs={{0,4},{8,12},{16,20},{24,28},{32,36},{40,44},{48,52},{56,60},{64,6... | collective-permute-start | bytes 786440 | tf_op jit(solution)/shard_map/ppermute | solution.py:35
  138.0 3.9 %collective-permute-start.22 = (bf16[64,2048]{1,0:T(8,128)(2,1)S(1)}, bf16[64,2048]{1,0:T(8,128)(2,1)S(1)}, u32[]{:S(2)}, u32[]{:S(2)}) collective-permute-start(bf16[64,2048]{1,0:T(8,128)(2,1)S(1)} %get-tuple-element.81), channel_id=1, source_target_pairs={{0,6},{8,14},{16,22},{24,30},{32,38},{40,46},{48,54},{56,62},{64,7... | collective-permute-start | bytes 786440 | tf_op jit(solution)/shard_map/ppermute | solution.py:35
  141.9 1.9 %collective-permute-start.21 = (bf16[64,2048]{1,0:T(8,128)(2,1)S(1)}, bf16[64,2048]{1,0:T(8,128)(2,1)S(1)}, u32[]{:S(2)}, u32[]{:S(2)}) collective-permute-start(bf16[64,2048]{1,0:T(8,128)(2,1)S(1)} %get-tuple-element.80), channel_id=1, source_target_pairs={{0,2},{8,10},{16,18},{24,26},{32,34},{40,42},{48,50},{56,58},{64,6... | collective-permute-start | bytes 786440 | tf_op jit(solution)/shard_map/ppermute | solution.py:35
  143.8 16.4 %collective-permute-done.20 = bf16[64,2048]{1,0:T(8,128)(2,1)S(1)} collective-permute-done((bf16[64,2048]{1,0:T(8,128)(2,1)S(1)}, bf16[64,2048]{1,0:T(8,128)(2,1)S(1)}, u32[]{:S(2)}, u32[]{:S(2)}) %collective-permute-start.20) | collective-permute-done | bytes 262176 | tf_op jit(solution)/shard_map/ppermute | solution.py:35
  160.3 0.1 convert_add_fusion
  160.3 0.0 collective-permute-done.23
  160.3 0.0 collective-permute-done.22
  160.3 0.0 collective-permute-done.21
  160.3 0.8 add_convert_fusion
  (12 shorter events, 0.1 us)
Async XLA Ops:
  0.0 38.5 %copy-start.3 = (bf16[512,256]{1,0:T(8,128)(2,1)S(1)}, bf16[512,256]{1,0:T(8,128)(2,1)}, u32[]{:S(2)}) copy-start(bf16[512,256]{1,0:T(8,128)(2,1)} %refs_0_.1) | copy-start | bytes 786436
  0.0 38.5 %copy-start.2 = (bf16[2048,2,32]{0,2,1:T(8,128)(2,1)S(1)}, bf16[2048,2,32]{0,2,1:T(8,128)(2,1)}, u32[]{:S(2)}) copy-start(bf16[2048,2,32]{0,2,1:T(8,128)(2,1)} %param.8) | copy-start | bytes 786436
  0.0 26.6 %collective-permute-start = (bf16[512,256]{1,0:T(8,128)(2,1)}, bf16[512,256]{1,0:T(8,128)(2,1)S(1)}, u32[]{:S(2)}, u32[]{:S(2)}) collective-permute-start(bf16[512,256]{1,0:T(8,128)(2,1)} %refs_0_.1), channel_id=1, source_target_pairs={{0,1},{8,9},{16,17},{24,25},{32,33},{40,41},{48,49},{56,57},{64,65... | collective-permute-start | bytes 786440 | tf_op jit(solution)/shard_map/ppermute | solution.py:35
  15.9 17.9 %collective-permute-start.4 = (bf16[512,256]{1,0:T(8,128)(2,1)}, bf16[512,256]{1,0:T(8,128)(2,1)S(1)}, u32[]{:S(2)}, u32[]{:S(2)}) collective-permute-start(bf16[512,256]{1,0:T(8,128)(2,1)} %refs_0_.1), channel_id=1, source_target_pairs={{0,2},{8,10},{16,18},{24,26},{32,34},{40,42},{48,50},{56,58},{64,6... | collective-permute-start | bytes 786440 | tf_op jit(solution)/shard_map/ppermute | solution.py:35
  19.3 19.2 %collective-permute-start.5 = (bf16[512,256]{1,0:T(8,128)(2,1)}, bf16[512,256]{1,0:T(8,128)(2,1)S(1)}, u32[]{:S(2)}, u32[]{:S(2)}) collective-permute-start(bf16[512,256]{1,0:T(8,128)(2,1)} %refs_0_.1), channel_id=1, source_target_pairs={{0,6},{8,14},{16,22},{24,30},{32,38},{40,46},{48,54},{56,62},{64,7... | collective-permute-start | bytes 786440 | tf_op jit(solution)/shard_map/ppermute | solution.py:35
  22.9 15.6 %collective-permute-start.6 = (bf16[512,256]{1,0:T(8,128)(2,1)}, bf16[512,256]{1,0:T(8,128)(2,1)S(1)}, u32[]{:S(2)}, u32[]{:S(2)}) collective-permute-start(bf16[512,256]{1,0:T(8,128)(2,1)} %refs_0_.1), channel_id=1, source_target_pairs={{0,4},{8,12},{16,20},{24,28},{32,36},{40,44},{48,52},{56,60},{64,6... | collective-permute-start | bytes 786440 | tf_op jit(solution)/shard_map/ppermute | solution.py:35
  26.7 14.1 %collective-permute-start.1 = (bf16[512,256]{1,0:T(8,128)(2,1)S(1)}, bf16[512,256]{1,0:T(8,128)(2,1)S(1)}, u32[]{:S(2)}, u32[]{:S(2)}) collective-permute-start(bf16[512,256]{1,0:T(8,128)(2,1)S(1)} %collective-permute-done.refs_0_), channel_id=1, source_target_pairs={{0,2},{8,10},{16,18},{24,26},{32,34},{40,42},{48,50},{56,58},{64,6... | collective-permute-start | bytes 786440 | tf_op jit(solution)/shard_map/ppermute | solution.py:35
  29.2 12.7 %collective-permute-start.2 = (bf16[512,256]{1,0:T(8,128)(2,1)S(1)}, bf16[512,256]{1,0:T(8,128)(2,1)S(1)}, u32[]{:S(2)}, u32[]{:S(2)}) collective-permute-start(bf16[512,256]{1,0:T(8,128)(2,1)S(1)} %collective-permute-done.refs_0_), channel_id=1, source_target_pairs={{0,6},{8,14},{16,22},{24,30},{32,38},{40,46},{48,54},{56,62},{64,7... | collective-permute-start | bytes 786440 | tf_op jit(solution)/shard_map/ppermute | solution.py:35
  33.7 11.2 %collective-permute-start.3 = (bf16[512,256]{1,0:T(8,128)(2,1)S(1)}, bf16[512,256]{1,0:T(8,128)(2,1)S(1)}, u32[]{:S(2)}, u32[]{:S(2)}) collective-permute-start(bf16[512,256]{1,0:T(8,128)(2,1)S(1)} %collective-permute-done.refs_0_), channel_id=1, source_target_pairs={{0,4},{8,12},{16,20},{24,28},{32,36},{40,44},{48,52},{56,60},{64,6... | collective-permute-start | bytes 786440 | tf_op jit(solution)/shard_map/ppermute | solution.py:35
  38.5 6.5 %copy-start.1 = (bf16[2,4,160,128]{3,2,1,0:T(8,128)(2,1)S(1)}, bf16[2,4,160,128]{3,2,1,0:T(8,128)(2,1)}, u32[]{:S(2)}) copy-start(bf16[2,4,160,128]{3,2,1,0:T(8,128)(2,1)} %constant.52.clone.refs_6_.table) | copy-start | bytes 983044
  45.0 53.9 %copy-start.4 = (s32[2]{0:T(128)S(1)}, s32[2]{0:T(128)}, u32[]{:S(2)}) copy-start(s32[2]{0:T(128)} %win.1) | copy-start | bytes 28
  48.2 18.6 %collective-permute-start.9 = (bf16[160,128]{1,0:T(8,128)(2,1)S(1)}, bf16[160,128]{1,0:T(8,128)(2,1)S(1)}, u32[]{:S(2)}, u32[]{:S(2)}) collective-permute-start(bf16[160,128]{1,0:T(8,128)(2,1)S(1)} %get-tuple-element.48), channel_id=1, source_target_pairs={{0,16},{8,24},{16,0},{24,8},{32,48},{40,56},{48,32},{56,40},{64,80... | collective-permute-start | bytes 122888 | tf_op jit(solution)/shard_map/ppermute | solution.py:35
  62.8 5.3 %collective-permute-start.8 = (bf16[160,128]{1,0:T(8,128)(2,1)S(1)}, bf16[160,128]{1,0:T(8,128)(2,1)S(1)}, u32[]{:S(2)}, u32[]{:S(2)}) collective-permute-start(bf16[160,128]{1,0:T(8,128)(2,1)S(1)} %get-tuple-element.47), channel_id=1, source_target_pairs={{0,24},{8,16},{16,8},{24,0},{32,56},{40,48},{48,40},{56,32},{64,88... | collective-permute-start | bytes 122888 | tf_op jit(solution)/shard_map/ppermute | solution.py:35
  64.8 3.4 %collective-permute-start.7 = (bf16[160,128]{1,0:T(8,128)(2,1)S(1)}, bf16[160,128]{1,0:T(8,128)(2,1)S(1)}, u32[]{:S(2)}, u32[]{:S(2)}) collective-permute-start(bf16[160,128]{1,0:T(8,128)(2,1)S(1)} %get-tuple-element.47), channel_id=1, source_target_pairs={{0,8},{8,0},{16,24},{24,16},{32,40},{40,32},{48,56},{56,48},{64,72... | collective-permute-start | bytes 122888 | tf_op jit(solution)/shard_map/ppermute | solution.py:35
  68.2 36.8 %copy-start = (bf16[2,128,2048]{2,1,0:T(8,128)(2,1)S(1)}, bf16[2,128,2048]{2,1,0:T(8,128)(2,1)}, u32[]{:S(2)}) copy-start(bf16[2,128,2048]{2,1,0:T(8,128)(2,1)} %param.10) | copy-start | bytes 3145732
  68.2 7.4 %collective-permute-start.10 = (bf16[160,128]{1,0:T(8,128)(2,1)S(1)}, bf16[160,128]{1,0:T(8,128)(2,1)S(1)}, u32[]{:S(2)}, u32[]{:S(2)}) collective-permute-start(bf16[160,128]{1,0:T(8,128)(2,1)S(1)} %convert_element_type.72), channel_id=1, source_target_pairs={{0,32},{8,40},{16,48},{24,56},{32,0},{40,8},{48,16},{56,24},{64,96... | collective-permute-start | bytes 122888 | tf_op jit(solution)/shard_map/ppermute | solution.py:35
  75.6 11.3 %collective-permute-start.11 = (bf16[160,128]{1,0:T(8,128)(2,1)S(1)}, bf16[160,128]{1,0:T(8,128)(2,1)S(1)}, u32[]{:S(2)}, u32[]{:S(2)}) collective-permute-start(bf16[160,128]{1,0:T(8,128)(2,1)S(1)} %convert_element_type.74), channel_id=1, source_target_pairs={{0,64},{8,72},{16,80},{24,88},{32,96},{40,104},{48,112},{56,120},{... | collective-permute-start | bytes 122888 | tf_op jit(solution)/shard_map/ppermute | solution.py:35
  82.1 16.7 %collective-permute-start.15 = (bf16[384,512]{1,0:T(8,128)(2,1)S(1)}, bf16[384,512]{1,0:T(8,128)(2,1)S(1)}, u32[]{:S(2)}, u32[]{:S(2)}) collective-permute-start(bf16[384,512]{1,0:T(8,128)(2,1)S(1)} %get-tuple-element.62), channel_id=1, source_target_pairs={{0,8},{8,16},{16,24},{24,32},{32,40},{40,48},{48,56},{56,64},{64,7... | collective-permute-start | bytes 1179656 | tf_op jit(solution)/shard_map/ppermute | solution.py:35
  86.9 14.3 %collective-permute-start.12 = (bf16[160,128]{1,0:T(8,128)(2,1)S(1)}, bf16[160,128]{1,0:T(8,128)(2,1)S(1)}, u32[]{:S(2)}, u32[]{:S(2)}) collective-permute-start(bf16[160,128]{1,0:T(8,128)(2,1)S(1)} %convert_add_fusion.1), channel_id=1, source_target_pairs={{0,128},{8,136},{16,144},{24,152},{32,160},{40,168},{48,176},{56,1... | collective-permute-start | bytes 122888 | tf_op jit(solution)/shard_map/ppermute | solution.py:35
  90.1 11.1 %collective-permute-start.13 = (bf16[160,128]{1,0:T(8,128)(2,1)S(1)}, bf16[160,128]{1,0:T(8,128)(2,1)S(1)}, u32[]{:S(2)}, u32[]{:S(2)}) collective-permute-start(bf16[160,128]{1,0:T(8,128)(2,1)S(1)} %convert_add_fusion.1), channel_id=1, source_target_pairs={{0,256},{8,264},{16,272},{24,280},{32,288},{40,296},{48,304},{56,3... | collective-permute-start | bytes 122888 | tf_op jit(solution)/shard_map/ppermute | solution.py:35
  91.4 9.9 %collective-permute-start.14 = (bf16[160,128]{1,0:T(8,128)(2,1)S(1)}, bf16[160,128]{1,0:T(8,128)(2,1)S(1)}, u32[]{:S(2)}, u32[]{:S(2)}) collective-permute-start(bf16[160,128]{1,0:T(8,128)(2,1)S(1)} %convert_add_fusion.1), channel_id=1, source_target_pairs={{0,384},{8,392},{16,400},{24,408},{32,416},{40,424},{48,432},{56,4... | collective-permute-start | bytes 122888 | tf_op jit(solution)/shard_map/ppermute | solution.py:35
  101.3 3.1 %collective-permute-start.16 = (bf16[160,128]{1,0:T(8,128)(2,1)S(1)}, bf16[160,128]{1,0:T(8,128)(2,1)S(1)}, u32[]{:S(2)}, u32[]{:S(2)}) collective-permute-start(bf16[160,128]{1,0:T(8,128)(2,1)S(1)} %get-tuple-element.83), channel_id=1, source_target_pairs={{0,8},{8,0},{16,24},{24,16},{32,40},{40,32},{48,56},{56,48},{64,72... | collective-permute-start | bytes 122888 | tf_op jit(solution)/shard_map/ppermute | solution.py:35
  105.4 11.8 %collective-permute-start.19 = (bf16[64,2048]{1,0:T(8,128)(2,1)S(1)}, bf16[64,2048]{1,0:T(8,128)(2,1)S(1)}, u32[]{:S(2)}, u32[]{:S(2)}) collective-permute-start(bf16[64,2048]{1,0:T(8,128)(2,1)S(1)} %get-tuple-element.75), channel_id=1, source_target_pairs={{0,4},{8,12},{16,20},{24,28},{32,36},{40,44},{48,52},{56,60},{64,6... | collective-permute-start | bytes 786440 | tf_op jit(solution)/shard_map/ppermute | solution.py:35
  109.2 14.7 %collective-permute-start.18 = (bf16[64,2048]{1,0:T(8,128)(2,1)S(1)}, bf16[64,2048]{1,0:T(8,128)(2,1)S(1)}, u32[]{:S(2)}, u32[]{:S(2)}) collective-permute-start(bf16[64,2048]{1,0:T(8,128)(2,1)S(1)} %get-tuple-element.74), channel_id=1, source_target_pairs={{0,6},{8,14},{16,22},{24,30},{32,38},{40,46},{48,54},{56,62},{64,7... | collective-permute-start | bytes 786440 | tf_op jit(solution)/shard_map/ppermute | solution.py:35
  114.8 10.9 %collective-permute-start.17 = (bf16[64,2048]{1,0:T(8,128)(2,1)S(1)}, bf16[64,2048]{1,0:T(8,128)(2,1)S(1)}, u32[]{:S(2)}, u32[]{:S(2)}) collective-permute-start(bf16[64,2048]{1,0:T(8,128)(2,1)S(1)} %get-tuple-element.73), channel_id=1, source_target_pairs={{0,2},{8,10},{16,18},{24,26},{32,34},{40,42},{48,50},{56,58},{64,6... | collective-permute-start | bytes 786440 | tf_op jit(solution)/shard_map/ppermute | solution.py:35
  125.8 34.4 %collective-permute-start.20 = (bf16[64,2048]{1,0:T(8,128)(2,1)S(1)}, bf16[64,2048]{1,0:T(8,128)(2,1)S(1)}, u32[]{:S(2)}, u32[]{:S(2)}) collective-permute-start(bf16[64,2048]{1,0:T(8,128)(2,1)S(1)} %add_convert_fusion.1), channel_id=1, source_target_pairs={{0,1},{8,9},{16,17},{24,25},{32,33},{40,41},{48,49},{56,57},{64,65... | collective-permute-start | bytes 786440 | tf_op jit(solution)/shard_map/ppermute | solution.py:35
  135.4 24.9 %collective-permute-start.23 = (bf16[64,2048]{1,0:T(8,128)(2,1)S(1)}, bf16[64,2048]{1,0:T(8,128)(2,1)S(1)}, u32[]{:S(2)}, u32[]{:S(2)}) collective-permute-start(bf16[64,2048]{1,0:T(8,128)(2,1)S(1)} %get-tuple-element.82), channel_id=1, source_target_pairs={{0,4},{8,12},{16,20},{24,28},{32,36},{40,44},{48,52},{56,60},{64,6... | collective-permute-start | bytes 786440 | tf_op jit(solution)/shard_map/ppermute | solution.py:35
  138.0 22.4 %collective-permute-start.22 = (bf16[64,2048]{1,0:T(8,128)(2,1)S(1)}, bf16[64,2048]{1,0:T(8,128)(2,1)S(1)}, u32[]{:S(2)}, u32[]{:S(2)}) collective-permute-start(bf16[64,2048]{1,0:T(8,128)(2,1)S(1)} %get-tuple-element.81), channel_id=1, source_target_pairs={{0,6},{8,14},{16,22},{24,30},{32,38},{40,46},{48,54},{56,62},{64,7... | collective-permute-start | bytes 786440 | tf_op jit(solution)/shard_map/ppermute | solution.py:35
  141.9 18.4 %collective-permute-start.21 = (bf16[64,2048]{1,0:T(8,128)(2,1)S(1)}, bf16[64,2048]{1,0:T(8,128)(2,1)S(1)}, u32[]{:S(2)}, u32[]{:S(2)}) collective-permute-start(bf16[64,2048]{1,0:T(8,128)(2,1)S(1)} %get-tuple-element.80), channel_id=1, source_target_pairs={{0,2},{8,10},{16,18},{24,26},{32,34},{40,42},{48,50},{56,58},{64,6... | collective-permute-start | bytes 786440 | tf_op jit(solution)/shard_map/ppermute | solution.py:35

commit v12 on v11

--- a/solution.py
+++ b/solution.py
@@ -243,7 +243,8 @@
             win_ref[at, cols] = unit(dot(weights, values[b * BLOCK : b * BLOCK + span]))
 
 
-def hidden_kernel(ours, theirs, near_ref, win_ref, map_ref, keep_ref, away_ref, hidden):
+def hidden_kernel(ours, theirs, near_ref, win_ref, map_ref, w_ref, keep_ref, *refs):
+    outs, hidden = refs[:-1], refs[-1]
     x, half, core, _ = position()
     mine, other = ours[...], theirs[...].astype(f32)
     head = mine.shape[1]
@@ -258,7 +259,10 @@
     for s in range(NX):
         group = lax.rem(x + s, NX) * 2
         keep_ref[s * rows : (s + 1) * rows] = hidden[group + half]
-        away_ref[s * rows : (s + 1) * rows] = hidden[group + 1 - half]
+    groups = [hidden[lax.rem(x + s, NX) * 2 + 1 - half] for s in range(NX)]
+    product = dot(jnp.concatenate(groups, axis=0), w_ref[...]).astype(bf16)
+    for s, out in enumerate(outs):
+        out[...] = product[s * rows : (s + 1) * rows]
 
 
 def product_kernel(hidden_ref, w_ref, *outs):
@@ -369,17 +373,17 @@
     )(win_blocks, qf, kv, halo)
 
 
-def hidden_rows(ours, theirs, near_out, win_out, query_map):
+def hidden_rows(ours, theirs, near_out, win_out, query_map, w_out):
     tok_rows, wide = near_out.shape
     return pl.pallas_call(
         hidden_kernel,
-        out_shape=(shape((tok_rows // 2, wide), bf16),) * 2,
-        in_specs=[VMEM] * 5,
-        out_specs=(VMEM,) * 2,
+        out_shape=(shape((tok_rows // 2, wide), bf16),) + (shape((tok_rows // N_TP, w_out.shape[1]), bf16),) * NX,
+        in_specs=[VMEM] * 6,
+        out_specs=(VMEM,) * (NX + 1),
         scratch_shapes=[pltpu.VMEM((N_TP, tok_rows // N_TP, wide), bf16)],
         name="hidden",
         compiler_params=pltpu.CompilerParams(vmem_limit_bytes=LIMIT),
-    )(ours, theirs, near_out, win_out, query_map)
+    )(ours, theirs, near_out, win_out, query_map, w_out)
 
 
 def product(hidden, w_out):
@@ -419,14 +423,13 @@
         return window(win_blocks, qf, kv, halo)
 
     ours, theirs, (near_out, query_map), win_out = prefix(mine, short, theirs, (x, h, y, z, c), beside, attend)
-    keep, away = hidden_rows(ours, theirs, near_out, win_out, query_map)
+    keep, *group = hidden_rows(ours, theirs, near_out, win_out, query_map, w_out)
 
     def summed(total, group):
         for steps in (1, 3, 2):
             total = total + send(group[steps], to_x(steps)).astype(f32)
         return total.astype(bf16)
 
-    group = product(away, w_out)
     away, keep = lax.optimization_barrier((summed(group[0].astype(f32), group), keep))
     group = product(keep, w_out)
     total = lax.optimization_barrier(group[0].astype(f32) + send(away, to_half).astype(f32))

time: 162 us -> 162 us (level)
  no operation moved by 1% of the time
where the time goes in v12:
time: 162 us; the launch traced here: 161 us
  starting transfers between devices  101 us (62%)
  waiting for transfers between devices  45.9 us (28%)
  Pallas kernels  10.4 us (6%)
  local copies, waits for them, and re-layouts  2.32 us (1%)
    ppermute x24, starting transfers between devices, send(): return lax.ppermute(value, ('seq', 'tp'), pairs(move))  101 us
    ppermute x24, waiting for transfers between devices, send(): return lax.ppermute(value, ('seq', 'tp'), pairs(move))  45.9 us
  transfers between devices with their start and end apart: 24, of which 12 were waited for; matrix products, arithmetic and copies ran while one was open for 1% of the time, Pallas kernels for 4%

profile of v12, /device:TPU:16, one launch (start us, length us, event | category | flops | bytes accessed | tf_op | source)
XLA Modules:
  0.0 161.1 jit_solution(13795638374005637055)
XLA Ops:
  0.0 15.8 %collective-permute-start = (bf16[512,256]{1,0:T(8,128)(2,1)}, bf16[512,256]{1,0:T(8,128)(2,1)S(1)}, u32[]{:S(2)}, u32[]{:S(2)}) collective-permute-start(bf16[512,256]{1,0:T(8,128)(2,1)} %refs_0_.1), channel_id=1, source_target_pairs={{0,1},{8,9},{16,17},{24,25},{32,33},{40,41},{48,49},{56,57},{64,65... | collective-permute-start | bytes 786440 | tf_op jit(solution)/shard_map/ppermute | solution.py:35
  15.9 3.4 %collective-permute-start.4 = (bf16[512,256]{1,0:T(8,128)(2,1)}, bf16[512,256]{1,0:T(8,128)(2,1)S(1)}, u32[]{:S(2)}, u32[]{:S(2)}) collective-permute-start(bf16[512,256]{1,0:T(8,128)(2,1)} %refs_0_.1), channel_id=1, source_target_pairs={{0,2},{8,10},{16,18},{24,26},{32,34},{40,42},{48,50},{56,58},{64,6... | collective-permute-start | bytes 786440 | tf_op jit(solution)/shard_map/ppermute | solution.py:35
  19.3 3.7 %collective-permute-start.5 = (bf16[512,256]{1,0:T(8,128)(2,1)}, bf16[512,256]{1,0:T(8,128)(2,1)S(1)}, u32[]{:S(2)}, u32[]{:S(2)}) collective-permute-start(bf16[512,256]{1,0:T(8,128)(2,1)} %refs_0_.1), channel_id=1, source_target_pairs={{0,6},{8,14},{16,22},{24,30},{32,38},{40,46},{48,54},{56,62},{64,7... | collective-permute-start | bytes 786440 | tf_op jit(solution)/shard_map/ppermute | solution.py:35
  22.9 3.7 %collective-permute-start.6 = (bf16[512,256]{1,0:T(8,128)(2,1)}, bf16[512,256]{1,0:T(8,128)(2,1)S(1)}, u32[]{:S(2)}, u32[]{:S(2)}) collective-permute-start(bf16[512,256]{1,0:T(8,128)(2,1)} %refs_0_.1), channel_id=1, source_target_pairs={{0,4},{8,12},{16,20},{24,28},{32,36},{40,44},{48,52},{56,60},{64,6... | collective-permute-start | bytes 786440 | tf_op jit(solution)/shard_map/ppermute | solution.py:35
  26.7 0.0 collective-permute-done.refs_0_
  26.7 2.5 %collective-permute-start.1 = (bf16[512,256]{1,0:T(8,128)(2,1)S(1)}, bf16[512,256]{1,0:T(8,128)(2,1)S(1)}, u32[]{:S(2)}, u32[]{:S(2)}) collective-permute-start(bf16[512,256]{1,0:T(8,128)(2,1)S(1)} %collective-permute-done.refs_0_), channel_id=1, source_target_pairs={{0,2},{8,10},{16,18},{24,26},{32,34},{40,42},{48,50},{56,58},{64,6... | collective-permute-start | bytes 786440 | tf_op jit(solution)/shard_map/ppermute | solution.py:35
  29.2 4.6 %collective-permute-start.2 = (bf16[512,256]{1,0:T(8,128)(2,1)S(1)}, bf16[512,256]{1,0:T(8,128)(2,1)S(1)}, u32[]{:S(2)}, u32[]{:S(2)}) collective-permute-start(bf16[512,256]{1,0:T(8,128)(2,1)S(1)} %collective-permute-done.refs_0_), channel_id=1, source_target_pairs={{0,6},{8,14},{16,22},{24,30},{32,38},{40,46},{48,54},{56,62},{64,7... | collective-permute-start | bytes 786440 | tf_op jit(solution)/shard_map/ppermute | solution.py:35
  33.7 0.0 collective-permute-done.4.refs_1_
  33.7 2.4 %collective-permute-start.3 = (bf16[512,256]{1,0:T(8,128)(2,1)S(1)}, bf16[512,256]{1,0:T(8,128)(2,1)S(1)}, u32[]{:S(2)}, u32[]{:S(2)}) collective-permute-start(bf16[512,256]{1,0:T(8,128)(2,1)S(1)} %collective-permute-done.refs_0_), channel_id=1, source_target_pairs={{0,4},{8,12},{16,20},{24,28},{32,36},{40,44},{48,52},{56,60},{64,6... | collective-permute-start | bytes 786440 | tf_op jit(solution)/shard_map/ppermute | solution.py:35
  36.2 2.3 %copy.10 = bf16[2048,2,384]{2,0,1:T(8,128)(2,1)S(1)} copy(bf16[2048,2,384]{2,1,0:T(2,128)(2,1)} %param.9) | data formatting | bytes 6291456 | tf_op args[2]
  38.5 0.0 copy-start.1
  38.5 0.0 collective-permute-done.5.refs_2_
  38.5 0.0 collective-permute-done.6.refs_3_
  38.5 0.0 copy-done.3
  38.5 0.0 copy-done.2
  38.5 1.3 own.1
  39.8 1.0 collective-permute-done.1.refs_1_
  40.8 1.1 collective-permute-done.2.refs_2_
  41.9 3.1 %collective-permute-done.3.refs_3_ = bf16[512,256]{1,0:T(8,128)(2,1)S(1)} collective-permute-done((bf16[512,256]{1,0:T(8,128)(2,1)S(1)}, bf16[512,256]{1,0:T(8,128)(2,1)S(1)}, u32[]{:S(2)}, u32[]{:S(2)}) %collective-permute-start.3) | collective-permute-done | bytes 262176 | tf_op jit(solution)/shard_map/ppermute | solution.py:35
  45.0 0.0 copy-done.1
  45.0 3.2 %project.1 = (bf16[512,384]{1,0:T(8,128)(2,1)S(1)}, bf16[512,512]{1,0:T(8,128)(2,1)S(1)}, bf16[384,512]{1,0:T(8,128)(2,1)S(1)}, f32[160,128]{1,0:T(8,128)S(1)}, ...) custom-call(bf16[512,256]{1,0:T(8,128)(2,1)S(1)} %collective-permute-done.refs_0_, ...), custom_call_target="tpu_custom_call" | custom-call | tf_op jit(solution)/shard_map/project/pallas_call | solution.py:326
  48.2 0.0 copy-start
  48.2 14.7 %collective-permute-start.9 = (bf16[160,128]{1,0:T(8,128)(2,1)S(1)}, bf16[160,128]{1,0:T(8,128)(2,1)S(1)}, u32[]{:S(2)}, u32[]{:S(2)}) collective-permute-start(bf16[160,128]{1,0:T(8,128)(2,1)S(1)} %get-tuple-element.47), channel_id=1, source_target_pairs={{0,16},{8,24},{16,0},{24,8},{32,48},{40,56},{48,32},{56,40},{64,80... | collective-permute-start | bytes 122888 | tf_op jit(solution)/shard_map/ppermute | solution.py:35
  63.0 1.9 %collective-permute-start.8 = (bf16[160,128]{1,0:T(8,128)(2,1)S(1)}, bf16[160,128]{1,0:T(8,128)(2,1)S(1)}, u32[]{:S(2)}, u32[]{:S(2)}) collective-permute-start(bf16[160,128]{1,0:T(8,128)(2,1)S(1)} %get-tuple-element.46), channel_id=1, source_target_pairs={{0,24},{8,16},{16,8},{24,0},{32,56},{40,48},{48,40},{56,32},{64,88... | collective-permute-start | bytes 122888 | tf_op jit(solution)/shard_map/ppermute | solution.py:35
  64.9 2.0 %collective-permute-start.7 = (bf16[160,128]{1,0:T(8,128)(2,1)S(1)}, bf16[160,128]{1,0:T(8,128)(2,1)S(1)}, u32[]{:S(2)}, u32[]{:S(2)}) collective-permute-start(bf16[160,128]{1,0:T(8,128)(2,1)S(1)} %get-tuple-element.46), channel_id=1, source_target_pairs={{0,8},{8,0},{16,24},{24,16},{32,40},{40,32},{48,56},{56,48},{64,72... | collective-permute-start | bytes 122888 | tf_op jit(solution)/shard_map/ppermute | solution.py:35
  67.0 0.0 collective-permute-done.9
  67.0 1.3 collective-permute-done.8
  68.3 0.0 collective-permute-done.7
  68.4 1.9 %collective-permute-start.10 = (bf16[160,128]{1,0:T(8,128)(2,1)S(1)}, bf16[160,128]{1,0:T(8,128)(2,1)S(1)}, u32[]{:S(2)}, u32[]{:S(2)}) collective-permute-start(bf16[160,128]{1,0:T(8,128)(2,1)S(1)} %convert_element_type.72), channel_id=1, source_target_pairs={{0,32},{8,40},{16,48},{24,56},{32,0},{40,8},{48,16},{56,24},{64,96... | collective-permute-start | bytes 122888 | tf_op jit(solution)/shard_map/ppermute | solution.py:35
  70.3 5.3 %collective-permute-done.10 = bf16[160,128]{1,0:T(8,128)(2,1)S(1)} collective-permute-done((bf16[160,128]{1,0:T(8,128)(2,1)S(1)}, bf16[160,128]{1,0:T(8,128)(2,1)S(1)}, u32[]{:S(2)}, u32[]{:S(2)}) %collective-permute-start.10) | collective-permute-done | bytes 40992 | tf_op jit(solution)/shard_map/ppermute | solution.py:35
  75.6 6.5 %collective-permute-start.11 = (bf16[160,128]{1,0:T(8,128)(2,1)S(1)}, bf16[160,128]{1,0:T(8,128)(2,1)S(1)}, u32[]{:S(2)}, u32[]{:S(2)}) collective-permute-start(bf16[160,128]{1,0:T(8,128)(2,1)S(1)} %convert_element_type.74), channel_id=1, source_target_pairs={{0,64},{8,72},{16,80},{24,88},{32,96},{40,104},{48,112},{56,120},{... | collective-permute-start | bytes 122888 | tf_op jit(solution)/shard_map/ppermute | solution.py:35
  82.1 1.9 %collective-permute-start.15 = (bf16[384,512]{1,0:T(8,128)(2,1)S(1)}, bf16[384,512]{1,0:T(8,128)(2,1)S(1)}, u32[]{:S(2)}, u32[]{:S(2)}) collective-permute-start(bf16[384,512]{1,0:T(8,128)(2,1)S(1)} %get-tuple-element.61), channel_id=1, source_target_pairs={{0,8},{8,16},{16,24},{24,32},{32,40},{40,48},{48,56},{56,64},{64,7... | collective-permute-start | bytes 1179656 | tf_op jit(solution)/shard_map/ppermute | solution.py:35
  84.0 2.1 %near.1 = (f32[512,256]{1,0:T(8,128)S(1)}, bf16[2,512,160]{2,1,0:T(8,128)(2,1)S(1)}) custom-call(bf16[512,384]{1,0:T(8,128)(2,1)S(1)} %get-tuple-element.53.qf_ref, bf16[512,512]{1,0:T(8,128)(2,1)S(1)} %get-tuple-element.54.kv_ref, bf16[2,4,160,128]{3,2,1,0:T(8,128)(2,1)S(1)} %copy-done.1), custom_call_target="tpu_custom_call" | custom-call | tf_op jit(solution)/shard_map/near/pallas_call | solution.py:350
  86.1 0.8 collective-permute-done.11
  86.9 3.2 %collective-permute-start.12 = (bf16[160,128]{1,0:T(8,128)(2,1)S(1)}, bf16[160,128]{1,0:T(8,128)(2,1)S(1)}, u32[]{:S(2)}, u32[]{:S(2)}) collective-permute-start(bf16[160,128]{1,0:T(8,128)(2,1)S(1)} %convert_add_fusion.1), channel_id=1, source_target_pairs={{0,128},{8,136},{16,144},{24,152},{32,160},{40,168},{48,176},{56,1... | collective-permute-start | bytes 122888 | tf_op jit(solution)/shard_map/ppermute | solution.py:35
  90.1 1.3 collective-permute-start.13
  91.4 0.7 collective-permute-start.14
  92.1 6.7 %collective-permute-done.15.halo_ref = bf16[384,512]{1,0:T(8,128)(2,1)S(1)} collective-permute-done((bf16[384,512]{1,0:T(8,128)(2,1)S(1)}, bf16[384,512]{1,0:T(8,128)(2,1)S(1)}, u32[]{:S(2)}, u32[]{:S(2)}) %collective-permute-start.15) | collective-permute-done | bytes 393248 | tf_op jit(solution)/shard_map/ppermute | solution.py:35
  98.8 2.4 %window.1.win_ref = f32[512,256]{1,0:T(8,128)S(1)} custom-call(s32[2]{0:T(128)S(1)} %copy-done.4, bf16[512,384]{1,0:T(8,128)(2,1)S(1)} %get-tuple-element.53.qf_ref, bf16[512,512]{1,0:T(8,128)(2,1)S(1)} %get-tuple-element.54.kv_ref, bf16[384,512]{1,0:T(8,128)(2,1)S(1)} %collective-permute-done.15.halo_ref), custom_call_target="tpu_custom_call" | custom-call | tf_op jit(solution)/shard_map/window/pallas_call | solution.py:365
  101.3 0.0 collective-permute-done.12
  101.3 0.0 collective-permute-done.13
  101.3 0.0 collective-permute-done.14
  101.3 1.9 %collective-permute-start.16 = (bf16[160,128]{1,0:T(8,128)(2,1)S(1)}, bf16[160,128]{1,0:T(8,128)(2,1)S(1)}, u32[]{:S(2)}, u32[]{:S(2)}) collective-permute-start(bf16[160,128]{1,0:T(8,128)(2,1)S(1)} %get-tuple-element.81), channel_id=1, source_target_pairs={{0,8},{8,0},{16,24},{24,16},{32,40},{40,32},{48,56},{56,48},{64,72... | collective-permute-start | bytes 122888 | tf_op jit(solution)/shard_map/ppermute | solution.py:35
  103.3 1.2 collective-permute-done.16.theirs
  104.4 0.0 copy-done
  104.4 0.9 hidden.1
  105.4 3.7 %collective-permute-start.19 = (bf16[64,2048]{1,0:T(8,128)(2,1)S(1)}, bf16[64,2048]{1,0:T(8,128)(2,1)S(1)}, u32[]{:S(2)}, u32[]{:S(2)}) collective-permute-start(bf16[64,2048]{1,0:T(8,128)(2,1)S(1)} %get-tuple-element.73), channel_id=1, source_target_pairs={{0,4},{8,12},{16,20},{24,28},{32,36},{40,44},{48,52},{56,60},{64,6... | collective-permute-start | bytes 786440 | tf_op jit(solution)/shard_map/ppermute | solution.py:35
  109.1 5.6 %collective-permute-start.18 = (bf16[64,2048]{1,0:T(8,128)(2,1)S(1)}, bf16[64,2048]{1,0:T(8,128)(2,1)S(1)}, u32[]{:S(2)}, u32[]{:S(2)}) collective-permute-start(bf16[64,2048]{1,0:T(8,128)(2,1)S(1)} %get-tuple-element.72), channel_id=1, source_target_pairs={{0,6},{8,14},{16,22},{24,30},{32,38},{40,46},{48,54},{56,62},{64,7... | collective-permute-start | bytes 786440 | tf_op jit(solution)/shard_map/ppermute | solution.py:35
  114.7 1.9 %collective-permute-start.17 = (bf16[64,2048]{1,0:T(8,128)(2,1)S(1)}, bf16[64,2048]{1,0:T(8,128)(2,1)S(1)}, u32[]{:S(2)}, u32[]{:S(2)}) collective-permute-start(bf16[64,2048]{1,0:T(8,128)(2,1)S(1)} %get-tuple-element.71), channel_id=1, source_target_pairs={{0,2},{8,10},{16,18},{24,26},{32,34},{40,42},{48,50},{56,58},{64,6... | collective-permute-start | bytes 786440 | tf_op jit(solution)/shard_map/ppermute | solution.py:35
  116.7 0.5 collective-permute-done.19
  117.2 6.7 %collective-permute-done.18 = bf16[64,2048]{1,0:T(8,128)(2,1)S(1)} collective-permute-done((bf16[64,2048]{1,0:T(8,128)(2,1)S(1)}, bf16[64,2048]{1,0:T(8,128)(2,1)S(1)}, u32[]{:S(2)}, u32[]{:S(2)}) %collective-permute-start.18) | collective-permute-done | bytes 262176 | tf_op jit(solution)/shard_map/ppermute | solution.py:35
  123.8 1.8 %collective-permute-done.17 = bf16[64,2048]{1,0:T(8,128)(2,1)S(1)} collective-permute-done((bf16[64,2048]{1,0:T(8,128)(2,1)S(1)}, bf16[64,2048]{1,0:T(8,128)(2,1)S(1)}, u32[]{:S(2)}, u32[]{:S(2)}) %collective-permute-start.17) | collective-permute-done | bytes 262176 | tf_op jit(solution)/shard_map/ppermute | solution.py:35
  125.7 0.1 add_convert_fusion.1
  125.8 9.1 %collective-permute-start.20 = (bf16[64,2048]{1,0:T(8,128)(2,1)S(1)}, bf16[64,2048]{1,0:T(8,128)(2,1)S(1)}, u32[]{:S(2)}, u32[]{:S(2)}) collective-permute-start(bf16[64,2048]{1,0:T(8,128)(2,1)S(1)} %add_convert_fusion.1), channel_id=1, source_target_pairs={{0,1},{8,9},{16,17},{24,25},{32,33},{40,41},{48,49},{56,57},{64,65... | collective-permute-start | bytes 786440 | tf_op jit(solution)/shard_map/ppermute | solution.py:35
  134.9 0.5 product.1
  135.4 2.5 %collective-permute-start.23 = (bf16[64,2048]{1,0:T(8,128)(2,1)S(1)}, bf16[64,2048]{1,0:T(8,128)(2,1)S(1)}, u32[]{:S(2)}, u32[]{:S(2)}) collective-permute-start(bf16[64,2048]{1,0:T(8,128)(2,1)S(1)} %get-tuple-element.80), channel_id=1, source_target_pairs={{0,4},{8,12},{16,20},{24,28},{32,36},{40,44},{48,52},{56,60},{64,6... | collective-permute-start | bytes 786440 | tf_op jit(solution)/shard_map/ppermute | solution.py:35
  137.9 3.9 %collective-permute-start.22 = (bf16[64,2048]{1,0:T(8,128)(2,1)S(1)}, bf16[64,2048]{1,0:T(8,128)(2,1)S(1)}, u32[]{:S(2)}, u32[]{:S(2)}) collective-permute-start(bf16[64,2048]{1,0:T(8,128)(2,1)S(1)} %get-tuple-element.79), channel_id=1, source_target_pairs={{0,6},{8,14},{16,22},{24,30},{32,38},{40,46},{48,54},{56,62},{64,7... | collective-permute-start | bytes 786440 | tf_op jit(solution)/shard_map/ppermute | solution.py:35
  141.9 1.9 %collective-permute-start.21 = (bf16[64,2048]{1,0:T(8,128)(2,1)S(1)}, bf16[64,2048]{1,0:T(8,128)(2,1)S(1)}, u32[]{:S(2)}, u32[]{:S(2)}) collective-permute-start(bf16[64,2048]{1,0:T(8,128)(2,1)S(1)} %get-tuple-element.78), channel_id=1, source_target_pairs={{0,2},{8,10},{16,18},{24,26},{32,34},{40,42},{48,50},{56,58},{64,6... | collective-permute-start | bytes 786440 | tf_op jit(solution)/shard_map/ppermute | solution.py:35
  143.8 16.4 %collective-permute-done.20 = bf16[64,2048]{1,0:T(8,128)(2,1)S(1)} collective-permute-done((bf16[64,2048]{1,0:T(8,128)(2,1)S(1)}, bf16[64,2048]{1,0:T(8,128)(2,1)S(1)}, u32[]{:S(2)}, u32[]{:S(2)}) %collective-permute-start.20) | collective-permute-done | bytes 262176 | tf_op jit(solution)/shard_map/ppermute | solution.py:35
  160.2 0.1 convert_add_fusion
  160.3 0.0 collective-permute-done.23
  160.3 0.0 collective-permute-done.22
  160.3 0.0 collective-permute-done.21
  160.3 0.8 add_convert_fusion
  (11 shorter events, 0.1 us)
Async XLA Ops:
  0.0 38.5 %copy-start.3 = (bf16[512,256]{1,0:T(8,128)(2,1)S(1)}, bf16[512,256]{1,0:T(8,128)(2,1)}, u32[]{:S(2)}) copy-start(bf16[512,256]{1,0:T(8,128)(2,1)} %refs_0_.1) | copy-start | bytes 786436
  0.0 38.5 %copy-start.2 = (bf16[2048,2,32]{0,2,1:T(8,128)(2,1)S(1)}, bf16[2048,2,32]{0,2,1:T(8,128)(2,1)}, u32[]{:S(2)}) copy-start(bf16[2048,2,32]{0,2,1:T(8,128)(2,1)} %param.8) | copy-start | bytes 786436
  0.0 26.6 %collective-permute-start = (bf16[512,256]{1,0:T(8,128)(2,1)}, bf16[512,256]{1,0:T(8,128)(2,1)S(1)}, u32[]{:S(2)}, u32[]{:S(2)}) collective-permute-start(bf16[512,256]{1,0:T(8,128)(2,1)} %refs_0_.1), channel_id=1, source_target_pairs={{0,1},{8,9},{16,17},{24,25},{32,33},{40,41},{48,49},{56,57},{64,65... | collective-permute-start | bytes 786440 | tf_op jit(solution)/shard_map/ppermute | solution.py:35
  15.9 17.9 %collective-permute-start.4 = (bf16[512,256]{1,0:T(8,128)(2,1)}, bf16[512,256]{1,0:T(8,128)(2,1)S(1)}, u32[]{:S(2)}, u32[]{:S(2)}) collective-permute-start(bf16[512,256]{1,0:T(8,128)(2,1)} %refs_0_.1), channel_id=1, source_target_pairs={{0,2},{8,10},{16,18},{24,26},{32,34},{40,42},{48,50},{56,58},{64,6... | collective-permute-start | bytes 786440 | tf_op jit(solution)/shard_map/ppermute | solution.py:35
  19.3 19.2 %collective-permute-start.5 = (bf16[512,256]{1,0:T(8,128)(2,1)}, bf16[512,256]{1,0:T(8,128)(2,1)S(1)}, u32[]{:S(2)}, u32[]{:S(2)}) collective-permute-start(bf16[512,256]{1,0:T(8,128)(2,1)} %refs_0_.1), channel_id=1, source_target_pairs={{0,6},{8,14},{16,22},{24,30},{32,38},{40,46},{48,54},{56,62},{64,7... | collective-permute-start | bytes 786440 | tf_op jit(solution)/shard_map/ppermute | solution.py:35
  22.9 15.6 %collective-permute-start.6 = (bf16[512,256]{1,0:T(8,128)(2,1)}, bf16[512,256]{1,0:T(8,128)(2,1)S(1)}, u32[]{:S(2)}, u32[]{:S(2)}) collective-permute-start(bf16[512,256]{1,0:T(8,128)(2,1)} %refs_0_.1), channel_id=1, source_target_pairs={{0,4},{8,12},{16,20},{24,28},{32,36},{40,44},{48,52},{56,60},{64,6... | collective-permute-start | bytes 786440 | tf_op jit(solution)/shard_map/ppermute | solution.py:35
  26.7 14.1 %collective-permute-start.1 = (bf16[512,256]{1,0:T(8,128)(2,1)S(1)}, bf16[512,256]{1,0:T(8,128)(2,1)S(1)}, u32[]{:S(2)}, u32[]{:S(2)}) collective-permute-start(bf16[512,256]{1,0:T(8,128)(2,1)S(1)} %collective-permute-done.refs_0_), channel_id=1, source_target_pairs={{0,2},{8,10},{16,18},{24,26},{32,34},{40,42},{48,50},{56,58},{64,6... | collective-permute-start | bytes 786440 | tf_op jit(solution)/shard_map/ppermute | solution.py:35
  29.2 12.7 %collective-permute-start.2 = (bf16[512,256]{1,0:T(8,128)(2,1)S(1)}, bf16[512,256]{1,0:T(8,128)(2,1)S(1)}, u32[]{:S(2)}, u32[]{:S(2)}) collective-permute-start(bf16[512,256]{1,0:T(8,128)(2,1)S(1)} %collective-permute-done.refs_0_), channel_id=1, source_target_pairs={{0,6},{8,14},{16,22},{24,30},{32,38},{40,46},{48,54},{56,62},{64,7... | collective-permute-start | bytes 786440 | tf_op jit(solution)/shard_map/ppermute | solution.py:35
  33.7 11.2 %collective-permute-start.3 = (bf16[512,256]{1,0:T(8,128)(2,1)S(1)}, bf16[512,256]{1,0:T(8,128)(2,1)S(1)}, u32[]{:S(2)}, u32[]{:S(2)}) collective-permute-start(bf16[512,256]{1,0:T(8,128)(2,1)S(1)} %collective-permute-done.refs_0_), channel_id=1, source_target_pairs={{0,4},{8,12},{16,20},{24,28},{32,36},{40,44},{48,52},{56,60},{64,6... | collective-permute-start | bytes 786440 | tf_op jit(solution)/shard_map/ppermute | solution.py:35
  38.5 6.5 %copy-start.1 = (bf16[2,4,160,128]{3,2,1,0:T(8,128)(2,1)S(1)}, bf16[2,4,160,128]{3,2,1,0:T(8,128)(2,1)}, u32[]{:S(2)}) copy-start(bf16[2,4,160,128]{3,2,1,0:T(8,128)(2,1)} %constant.52.clone.refs_6_.table) | copy-start | bytes 983044
  45.0 53.9 %copy-start.4 = (s32[2]{0:T(128)S(1)}, s32[2]{0:T(128)}, u32[]{:S(2)}) copy-start(s32[2]{0:T(128)} %win.1) | copy-start | bytes 28
  48.2 56.2 %copy-start = (bf16[2,128,2048]{2,1,0:T(8,128)(2,1)S(1)}, bf16[2,128,2048]{2,1,0:T(8,128)(2,1)}, u32[]{:S(2)}) copy-start(bf16[2,128,2048]{2,1,0:T(8,128)(2,1)} %param.10) | copy-start | bytes 3145732
  48.2 18.8 %collective-permute-start.9 = (bf16[160,128]{1,0:T(8,128)(2,1)S(1)}, bf16[160,128]{1,0:T(8,128)(2,1)S(1)}, u32[]{:S(2)}, u32[]{:S(2)}) collective-permute-start(bf16[160,128]{1,0:T(8,128)(2,1)S(1)} %get-tuple-element.47), channel_id=1, source_target_pairs={{0,16},{8,24},{16,0},{24,8},{32,48},{40,56},{48,32},{56,40},{64,80... | collective-permute-start | bytes 122888 | tf_op jit(solution)/shard_map/ppermute | solution.py:35
  63.0 5.3 %collective-permute-start.8 = (bf16[160,128]{1,0:T(8,128)(2,1)S(1)}, bf16[160,128]{1,0:T(8,128)(2,1)S(1)}, u32[]{:S(2)}, u32[]{:S(2)}) collective-permute-start(bf16[160,128]{1,0:T(8,128)(2,1)S(1)} %get-tuple-element.46), channel_id=1, source_target_pairs={{0,24},{8,16},{16,8},{24,0},{32,56},{40,48},{48,40},{56,32},{64,88... | collective-permute-start | bytes 122888 | tf_op jit(solution)/shard_map/ppermute | solution.py:35
  64.9 3.4 %collective-permute-start.7 = (bf16[160,128]{1,0:T(8,128)(2,1)S(1)}, bf16[160,128]{1,0:T(8,128)(2,1)S(1)}, u32[]{:S(2)}, u32[]{:S(2)}) collective-permute-start(bf16[160,128]{1,0:T(8,128)(2,1)S(1)} %get-tuple-element.46), channel_id=1, source_target_pairs={{0,8},{8,0},{16,24},{24,16},{32,40},{40,32},{48,56},{56,48},{64,72... | collective-permute-start | bytes 122888 | tf_op jit(solution)/shard_map/ppermute | solution.py:35
  68.4 7.2 %collective-permute-start.10 = (bf16[160,128]{1,0:T(8,128)(2,1)S(1)}, bf16[160,128]{1,0:T(8,128)(2,1)S(1)}, u32[]{:S(2)}, u32[]{:S(2)}) collective-permute-start(bf16[160,128]{1,0:T(8,128)(2,1)S(1)} %convert_element_type.72), channel_id=1, source_target_pairs={{0,32},{8,40},{16,48},{24,56},{32,0},{40,8},{48,16},{56,24},{64,96... | collective-permute-start | bytes 122888 | tf_op jit(solution)/shard_map/ppermute | solution.py:35
  75.6 11.3 %collective-permute-start.11 = (bf16[160,128]{1,0:T(8,128)(2,1)S(1)}, bf16[160,128]{1,0:T(8,128)(2,1)S(1)}, u32[]{:S(2)}, u32[]{:S(2)}) collective-permute-start(bf16[160,128]{1,0:T(8,128)(2,1)S(1)} %convert_element_type.74), channel_id=1, source_target_pairs={{0,64},{8,72},{16,80},{24,88},{32,96},{40,104},{48,112},{56,120},{... | collective-permute-start | bytes 122888 | tf_op jit(solution)/shard_map/ppermute | solution.py:35
  82.1 16.7 %collective-permute-start.15 = (bf16[384,512]{1,0:T(8,128)(2,1)S(1)}, bf16[384,512]{1,0:T(8,128)(2,1)S(1)}, u32[]{:S(2)}, u32[]{:S(2)}) collective-permute-start(bf16[384,512]{1,0:T(8,128)(2,1)S(1)} %get-tuple-element.61), channel_id=1, source_target_pairs={{0,8},{8,16},{16,24},{24,32},{32,40},{40,48},{48,56},{56,64},{64,7... | collective-permute-start | bytes 1179656 | tf_op jit(solution)/shard_map/ppermute | solution.py:35
  86.9 14.3 %collective-permute-start.12 = (bf16[160,128]{1,0:T(8,128)(2,1)S(1)}, bf16[160,128]{1,0:T(8,128)(2,1)S(1)}, u32[]{:S(2)}, u32[]{:S(2)}) collective-permute-start(bf16[160,128]{1,0:T(8,128)(2,1)S(1)} %convert_add_fusion.1), channel_id=1, source_target_pairs={{0,128},{8,136},{16,144},{24,152},{32,160},{40,168},{48,176},{56,1... | collective-permute-start | bytes 122888 | tf_op jit(solution)/shard_map/ppermute | solution.py:35
  90.1 11.1 %collective-permute-start.13 = (bf16[160,128]{1,0:T(8,128)(2,1)S(1)}, bf16[160,128]{1,0:T(8,128)(2,1)S(1)}, u32[]{:S(2)}, u32[]{:S(2)}) collective-permute-start(bf16[160,128]{1,0:T(8,128)(2,1)S(1)} %convert_add_fusion.1), channel_id=1, source_target_pairs={{0,256},{8,264},{16,272},{24,280},{32,288},{40,296},{48,304},{56,3... | collective-permute-start | bytes 122888 | tf_op jit(solution)/shard_map/ppermute | solution.py:35
  91.4 9.9 %collective-permute-start.14 = (bf16[160,128]{1,0:T(8,128)(2,1)S(1)}, bf16[160,128]{1,0:T(8,128)(2,1)S(1)}, u32[]{:S(2)}, u32[]{:S(2)}) collective-permute-start(bf16[160,128]{1,0:T(8,128)(2,1)S(1)} %convert_add_fusion.1), channel_id=1, source_target_pairs={{0,384},{8,392},{16,400},{24,408},{32,416},{40,424},{48,432},{56,4... | collective-permute-start | bytes 122888 | tf_op jit(solution)/shard_map/ppermute | solution.py:35
  101.3 3.1 %collective-permute-start.16 = (bf16[160,128]{1,0:T(8,128)(2,1)S(1)}, bf16[160,128]{1,0:T(8,128)(2,1)S(1)}, u32[]{:S(2)}, u32[]{:S(2)}) collective-permute-start(bf16[160,128]{1,0:T(8,128)(2,1)S(1)} %get-tuple-element.81), channel_id=1, source_target_pairs={{0,8},{8,0},{16,24},{24,16},{32,40},{40,32},{48,56},{56,48},{64,72... | collective-permute-start | bytes 122888 | tf_op jit(solution)/shard_map/ppermute | solution.py:35
  105.4 11.8 %collective-permute-start.19 = (bf16[64,2048]{1,0:T(8,128)(2,1)S(1)}, bf16[64,2048]{1,0:T(8,128)(2,1)S(1)}, u32[]{:S(2)}, u32[]{:S(2)}) collective-permute-start(bf16[64,2048]{1,0:T(8,128)(2,1)S(1)} %get-tuple-element.73), channel_id=1, source_target_pairs={{0,4},{8,12},{16,20},{24,28},{32,36},{40,44},{48,52},{56,60},{64,6... | collective-permute-start | bytes 786440 | tf_op jit(solution)/shard_map/ppermute | solution.py:35
  109.1 14.7 %collective-permute-start.18 = (bf16[64,2048]{1,0:T(8,128)(2,1)S(1)}, bf16[64,2048]{1,0:T(8,128)(2,1)S(1)}, u32[]{:S(2)}, u32[]{:S(2)}) collective-permute-start(bf16[64,2048]{1,0:T(8,128)(2,1)S(1)} %get-tuple-element.72), channel_id=1, source_target_pairs={{0,6},{8,14},{16,22},{24,30},{32,38},{40,46},{48,54},{56,62},{64,7... | collective-permute-start | bytes 786440 | tf_op jit(solution)/shard_map/ppermute | solution.py:35
  114.7 10.9 %collective-permute-start.17 = (bf16[64,2048]{1,0:T(8,128)(2,1)S(1)}, bf16[64,2048]{1,0:T(8,128)(2,1)S(1)}, u32[]{:S(2)}, u32[]{:S(2)}) collective-permute-start(bf16[64,2048]{1,0:T(8,128)(2,1)S(1)} %get-tuple-element.71), channel_id=1, source_target_pairs={{0,2},{8,10},{16,18},{24,26},{32,34},{40,42},{48,50},{56,58},{64,6... | collective-permute-start | bytes 786440 | tf_op jit(solution)/shard_map/ppermute | solution.py:35
  125.8 34.4 %collective-permute-start.20 = (bf16[64,2048]{1,0:T(8,128)(2,1)S(1)}, bf16[64,2048]{1,0:T(8,128)(2,1)S(1)}, u32[]{:S(2)}, u32[]{:S(2)}) collective-permute-start(bf16[64,2048]{1,0:T(8,128)(2,1)S(1)} %add_convert_fusion.1), channel_id=1, source_target_pairs={{0,1},{8,9},{16,17},{24,25},{32,33},{40,41},{48,49},{56,57},{64,65... | collective-permute-start | bytes 786440 | tf_op jit(solution)/shard_map/ppermute | solution.py:35
  135.4 24.9 %collective-permute-start.23 = (bf16[64,2048]{1,0:T(8,128)(2,1)S(1)}, bf16[64,2048]{1,0:T(8,128)(2,1)S(1)}, u32[]{:S(2)}, u32[]{:S(2)}) collective-permute-start(bf16[64,2048]{1,0:T(8,128)(2,1)S(1)} %get-tuple-element.80), channel_id=1, source_target_pairs={{0,4},{8,12},{16,20},{24,28},{32,36},{40,44},{48,52},{56,60},{64,6... | collective-permute-start | bytes 786440 | tf_op jit(solution)/shard_map/ppermute | solution.py:35
  137.9 22.3 %collective-permute-start.22 = (bf16[64,2048]{1,0:T(8,128)(2,1)S(1)}, bf16[64,2048]{1,0:T(8,128)(2,1)S(1)}, u32[]{:S(2)}, u32[]{:S(2)}) collective-permute-start(bf16[64,2048]{1,0:T(8,128)(2,1)S(1)} %get-tuple-element.79), channel_id=1, source_target_pairs={{0,6},{8,14},{16,22},{24,30},{32,38},{40,46},{48,54},{56,62},{64,7... | collective-permute-start | bytes 786440 | tf_op jit(solution)/shard_map/ppermute | solution.py:35
  141.9 18.4 %collective-permute-start.21 = (bf16[64,2048]{1,0:T(8,128)(2,1)S(1)}, bf16[64,2048]{1,0:T(8,128)(2,1)S(1)}, u32[]{:S(2)}, u32[]{:S(2)}) collective-permute-start(bf16[64,2048]{1,0:T(8,128)(2,1)S(1)} %get-tuple-element.78), channel_id=1, source_target_pairs={{0,2},{8,10},{16,18},{24,26},{32,34},{40,42},{48,50},{56,58},{64,6... | collective-permute-start | bytes 786440 | tf_op jit(solution)/shard_map/ppermute | solution.py:35
